TPU v7x, 32 devices: a whole 2x2x4 slice. The times are simulated.
32 devices in a mesh: elec: 4 (over z), cell: 8 (over y, x, core).
Axes of the slice: x: 2, y: 2, z: 4, core: 2. Of those that a mesh axis runs over, the one named last changes fastest.
Arguments:
- grads: bfloat16 [3, 1024, 1024], P(None, 'elec', 'cell'), may hold values from -6 to 6
- quads: int32 [16384, 4], P('elec'), may hold values from 0 to 1023, all different within a row
- volume: float32 [1024], P('cell'), may hold values from 0.5 to 2
- weight: float32 [16384], P('elec'), may hold values from 0.5 to 2
Outputs:
- hessian: float32 [1024, 1024], P('elec', 'cell')
Inputs may be any that keep to these rules, and one draw needn't show every extreme that they name: `quads`: each row names four different electrodes; every electrode appears in some row.
All inputs are finite; a program needn't handle non-finite values.
Results may differ from a plain program's by a relative error of at most 0.00096.
Values may be sent and summed in bfloat16 or wider, within the bound.
No kernel may reach another device: no remote copies, remote signals or barrier semaphores. Data moves between devices by JAX's collectives and lax.ppermute only.
A program may use at most 64 MiB of HBM per device.

v0:
```python
import jax
import jax.numpy as jnp
from jax import lax
from jax.sharding import PartitionSpec as P


def inner_rows(left, right):
    return lax.dot_general(
        left, right, (((0,), (0,)), ((), ())), preferred_element_type=jnp.float32
    )


def per_device(grads, quads, volume, weight):
    measured_rows = quads.shape[0]
    piece = lax.all_gather(grads, "elec", axis=1, tiled=True)
    width = piece.shape[1]
    labels = lax.iota(jnp.int32, width)
    source_map = (
        (quads[:, 0:1] == labels).astype(jnp.float32)
        - (quads[:, 1:2] == labels).astype(jnp.float32)
    ).astype(jnp.bfloat16)
    receive_map = (
        (quads[:, 2:3] == labels).astype(jnp.float32)
        - (quads[:, 3:4] == labels).astype(jnp.float32)
    ).astype(jnp.bfloat16)
    source = jnp.einsum("me,kec->kmc", source_map, piece, preferred_element_type=jnp.float32)
    receiver = jnp.einsum("me,kec->kmc", receive_map, piece, preferred_element_type=jnp.float32)
    source, receiver = (source, receiver)
    dots = source[0] * receiver[0] + source[1] * receiver[1] + source[2] * receiver[2]
    scaled_rows = (weight[:, None] * -(volume[None, :] * dots)).astype(jnp.bfloat16)
    term = inner_rows(lax.all_gather(scaled_rows, "cell", axis=1, tiled=True), scaled_rows)
    summed_rows = lax.psum_scatter(term, "elec", scatter_dimension=0, tiled=True)
    return summed_rows / jnp.float32(measured_rows * lax.axis_size("elec"))


def solution(mesh):
    placed = (P(None, "elec", "cell"), P("elec", None), P("cell"), P("elec"))
    return jax.shard_map(
        per_device, mesh=mesh, in_specs=placed, out_specs=P("elec", "cell"), check_vma=False
    )
```

profile of v0, /device:TPU:0, one launch (start us, length us, event | category | flops | bytes accessed | tf_op | source)
XLA Modules:
  0.0 137.0 jit_solution(11653929246199119935)
XLA Ops:
  6.5 0.0 all-gather.2.cloned.1.call-start
  6.5 1.1 fusion.23
  7.6 21.5 %all_gather.6 = bf16[3,1024,128]{2,1,0:T(8,128)(2,1)S(1)} all-gather(bf16[3,256,128]{2,1,0:T(8,128)(2,1)} %param.4), channel_id=1, replica_groups=mesh['elec'=4,'cell'=8] {'elec'}, dimensions={1}, use_global_device_ids=true | all-gather | bytes 983040 | tf_op jit(solution)/shard_map/all_gather | solution.py:15
  29.1 6.9 %fusion.10 = f32[3,4096,128]{2,1,0:T(8,128)S(1)} fusion(bf16[3,1024,128]{2,1,0:T(8,128)(2,1)S(1)} %all_gather.6, s32[4096]{0:T(1024)S(1)} %bitcast.34, s32[4096]{0:T(1024)S(1)} %bitcast.35), kind=kOutput, calls=%fused_computation.14 | convolution fusion | flops 3246391296 | bytes 7110656 | tf_op jit(solution)/shard_map/me,kec->kmc/dot_general | solution.py:27
  36.0 0.0 copy-start
  36.0 0.0 copy-start.1
  36.1 6.9 %fusion.13 = f32[3,4096,128]{2,1,0:T(8,128)S(1)} fusion(bf16[3,1024,128]{2,1,0:T(8,128)(2,1)S(1)} %all_gather.6, s32[4096]{0:T(1024)S(1)} %bitcast.33, s32[4096]{0:T(1024)S(1)} %bitcast.32), kind=kOutput, calls=%fused_computation.15 | convolution fusion | flops 3246391296 | bytes 7110656 | tf_op jit(solution)/shard_map/me,kec->kmc/dot_general | solution.py:26
  43.0 0.0 copy-done
  43.0 0.0 copy-done.1
  43.0 1.6 %fusion.21 = bf16[4096,128]{1,0:T(8,128)(2,1)} fusion(f32[3,4096,128]{2,1,0:T(8,128)S(1)} %fusion.10, f32[3,4096,128]{2,1,0:T(8,128)S(1)} %fusion.13, f32[128]{0:T(128)S(1)} %copy-done.1, f32[4096]{0:T(1024)S(1)} %copy-done), kind=kLoop, calls=%fused_computation.22 | loop fusion | flops 4718592 | bytes 13648384 | tf_op jit(solution)/shard_map/convert_element_type | solution.py:30
  44.6 0.0 all-gather.2.cloned.1.call-update
  44.6 0.0 reduce-scatter.2.cloned.1.call-start
  44.7 55.4 %all-gather.2.cloned.1.call-done = bf16[4096,1024]{1,0:T(8,128)(2,1)} async-done(((bf16[4096,128]{1,0:T(8,128)(2,1)}), bf16[4096,1024]{1,0:T(8,128)(2,1)}) %all-gather.2.cloned.1.call-update) | async-done | bytes 8388624 | tf_op jit(solution)/shard_map/all_gather | solution.py:31
  100.1 6.8 %fusion.24 = f32[1024,128]{1,0:T(8,128)} fusion(bf16[4096,1024]{1,0:T(8,128)(2,1)} %all-gather.2.cloned.1.call-done, bf16[4096,128]{1,0:T(8,128)(2,1)} %fusion.21), kind=kOutput, calls=%fused_computation.28 | convolution fusion | flops 1073741824 | bytes 9961472 | tf_op jit(solution)/shard_map/dot_general | solution.py:8
  106.8 0.0 reduce-scatter.2.cloned.1.call-update
  106.9 21.8 %reduce-scatter.2.cloned.1.call-done = f32[256,128]{1,0:T(8,128)} async-done(((f32[1024,128]{1,0:T(8,128)}), f32[256,128]{1,0:T(8,128)}) %reduce-scatter.2.cloned.1.call-update) | async-done | bytes 131088 | tf_op jit(solution)/shard_map/reduce_scatter | solution.py:32
  128.6 1.6 %broadcast_multiply_fusion = f32[256,128]{1,0:T(8,128)} fusion(f32[256,128]{1,0:T(8,128)} %reduce-scatter.2.cloned.1.call-done), kind=kLoop, calls=%fused_computation.26 | loop fusion | flops 32768 | bytes 262144 | tf_op jit(solution)/shard_map/div | solution.py:33
Async XLA Ops:
  6.5 93.5 %all-gather.2.cloned.1.call-start = ((), (), s32[]{:S(2)}) async-start(), calls=%async_computation.1 | async-start | bytes 9437184 | tf_op jit(solution)/shard_map/all_gather | solution.py:31
  36.0 7.0 %copy-start = (f32[4096]{0:T(1024)S(1)}, f32[4096]{0:T(1024)}, u32[]{:S(2)}) copy-start(f32[4096]{0:T(1024)} %param.7) | copy-start | bytes 49156
  36.0 7.0 %copy-start.1 = (f32[128]{0:T(128)S(1)}, f32[128]{0:T(128)}, u32[]{:S(2)}) copy-start(f32[128]{0:T(128)} %param.6) | copy-start | bytes 1540
  44.6 84.0 %reduce-scatter.2.cloned.1.call-start = ((), (), s32[]{:S(2)}) async-start(), calls=%async_computation.2 | async-start | bytes 655360 | tf_op jit(solution)/shard_map/reduce_scatter | solution.py:32
Sparse Core Ops, SparseCore 0:
  44.7 55.2 all-gather.1
  107.0 21.6 reduce-scatter.1
where the time goes:
time: 137 us
  waiting for transfers between devices  77.2 us (56%)
  blocking collectives  21.5 us (16%)
  matrix products  20.6 us (15%)
  between operations  13.5 us (10%)
  other arithmetic  3.14 us (2%)
    all_gather x1, waiting for transfers between devices, per_device(): lax.all_gather(scaled_rows, 'cell', axis=1, tiled=True)  55.4 us
    reduce_scatter x1, waiting for transfers between devices, per_device(): lax.psum_scatter(term, 'elec', scatter_dimension=0, tiled=True)  21.8 us
    all_gather x1, blocking collectives, per_device(): piece = lax.all_gather(grads, 'elec', axis=1, tiled=True)  21.5 us
    dot_general x1, matrix products, per_device(): jnp.einsum('me,kec->kmc', source_map, piece, preferred_element_type=jnp.f...  6.94 us
    dot_general x1, matrix products, per_device(): jnp.einsum('me,kec->kmc', receive_map, piece, preferred_element_type=jnp....  6.92 us
    dot_general x1, matrix products, inner_rows(): lax.dot_general(left, right, (((0,), (0,)), ((), ())), preferred_element_...  6.76 us
  transfers between devices with their start and end apart: 2, of which 2 were waited for; matrix products, arithmetic and copies ran while one was open for 0% of the time, Pallas kernels for 0%

commit v1 on v0

v1 whole, which is shorter than its diff:
```python
import functools

import jax
import jax.numpy as jnp
from jax import lax
from jax.experimental import pallas as pl
from jax.experimental.pallas import tpu as pltpu
from jax.sharding import PartitionSpec as P

F32, BF16, I32 = jnp.float32, jnp.bfloat16, jnp.int32
TILES = 4
LIMIT = 24 * 1024 * 1024


def params():
    return pltpu.CompilerParams(vmem_limit_bytes=LIMIT)


def hop(x, axis, size, mask):
    return lax.ppermute(x, axis, [(i, i ^ mask) for i in range(size)])


def odd(d):
    return bin(d).count("1") % 2 == 1


def low_bit(d):
    return (d & -d).bit_length() - 1


def same_columns(left, right):
    return lax.dot_general(left, right, (((1,), (1,)), ((), ())), preferred_element_type=F32)


def difference_map(rows, at, base, depth):
    labels = lax.broadcasted_iota(jnp.int16, (depth, rows.shape[1]), 0)
    local = (rows - base).astype(jnp.int16)
    plus, minus = local[at : at + 1, :] == labels, local[at + 1 : at + 2, :] == labels
    one = jnp.ones((), BF16)
    return jnp.where(plus, one, jnp.where(minus, -one, jnp.zeros((), BF16)))


def turn(shards, turned, start=0):
    cells = shards[0].shape[2]
    for at, shard in enumerate(shards, start):
        for k in range(3):
            turned[at, k * cells : (k + 1) * cells, :] = shard[k].T


def turn_kernel(*refs):
    turn(refs[:-1], refs[-1])


def turn_shards(shards):
    _, depth, cells = shards[0].shape
    return pl.pallas_call(
        turn_kernel,
        out_shape=jax.ShapeDtypeStruct((len(shards), 3 * cells, depth), BF16),
        compiler_params=params(),
        cost_estimate=pl.CostEstimate(flops=1000, bytes_accessed=1000, transcendentals=0),
        name="turn_shards",
    )(*shards)


def sensitivity_kernel(ready, offsets, place, quads, weight, volume, *refs):
    shards, out, turned = refs[1 if ready else 0 : -2], refs[-2], refs[-1]
    cells, depth = out.shape[0], turned.shape[2]

    @pl.when(pl.program_id(0) == 0)
    def _():
        turn(shards, turned)

    rows = quads[...]
    source = receiver = None
    for at, offset in enumerate(offsets):
        base = jnp.bitwise_xor(place[0], offset) * depth
        left = refs[0][at] if at < ready else turned[at - ready]
        s = jnp.dot(left, difference_map(rows, 0, base, depth), preferred_element_type=F32)
        r = jnp.dot(left, difference_map(rows, 2, base, depth), preferred_element_type=F32)
        source = s if at == 0 else source + s
        receiver = r if at == 0 else receiver + r
    product = source * receiver
    dots = product[:cells] + product[cells : 2 * cells] + product[2 * cells :]
    out[...] = (weight[...] * -(volume[...] * dots)).astype(BF16)


def sensitivities(place, tiles, quads, weight, volume, shards, turned=None, ready=()):
    offsets = tuple(ready) + tuple(sorted(shards))
    held = [shards[k] for k in offsets[len(ready) :]]
    _, depth, cells = held[0].shape
    width = quads.shape[1] // TILES
    count = len(tiles)
    scalars = jnp.stack([place[0], *tiles]).astype(I32)
    spec = pltpu.PrefetchScalarGridSpec(
        num_scalar_prefetch=1,
        grid=(count,),
        in_specs=[
            pl.BlockSpec((4, width), lambda i, s: (0, s[1 + i])),
            pl.BlockSpec((1, width), lambda i, s: (0, s[1 + i])),
            pl.BlockSpec((cells, 1), lambda i, s: (0, 0)),
        ]
        + [pl.BlockSpec((len(ready), 3 * cells, depth), lambda i, s: (0, 0, 0))] * (1 if ready else 0)
        + [pl.BlockSpec((3, depth, cells), lambda i, s: (0, 0, 0))] * len(held),
        out_specs=pl.BlockSpec((cells, width), lambda i, s: (0, i)),
        scratch_shapes=[pltpu.VMEM((len(held), 3 * cells, depth), BF16)],
    )
    flops = 4 * count * width * len(offsets) * depth * 3 * cells
    return pl.pallas_call(
        functools.partial(sensitivity_kernel, len(ready), offsets),
        grid_spec=spec,
        out_shape=jax.ShapeDtypeStruct((cells, count * width), BF16),
        compiler_params=params(),
        cost_estimate=pl.CostEstimate(flops=flops, bytes_accessed=1, transcendentals=0),
        name="sensitivities",
    )(scalars, quads, weight, volume, *([turned] if ready else []), *held)


def pair_blocks(rows, own, other, core):
    return ((core, same_columns(rows, own)), (1 - core, same_columns(rows, other)))


def early_kernel(evens, place, own_send, own_keep, other_send, other_keep, *refs):
    recomputed, outs, every = refs[: len(evens)], refs[len(evens) : -1], refs[-1]
    core = place[2]
    sides = ((0, own_send, other_send), (1, own_keep, other_keep))

    def add(d, side, blocks):
        for column, block in blocks:
            if side == 0:
                every[d, column] = block
            else:
                every[d, column] += block

    for side, own, other in sides:
        add(0, side, pair_blocks(own[...], own[...], other[...], core))
    for at, d in enumerate(evens):
        part = own_send.shape[1] // 2
        for bit in range(2):

            @pl.when(jnp.bitwise_and(jnp.right_shift(place[1], low_bit(d)), 1) == bit)
            def _():
                lanes = slice(bit * part, (bit + 1) * part)
                for side, own, other in sides:
                    rows = recomputed[at][:, side * part : (side + 1) * part]
                    add(d, side, pair_blocks(rows, own[:, lanes], other[:, lanes], core))

    first = jnp.bitwise_xor(place[0], place[1])
    for k, out in enumerate(outs):
        out[...] = every[jnp.bitwise_xor(first, k)]


def late_kernel(odds, place, own_keep, other_keep, *refs):
    received, outs, every = refs[: len(odds)], refs[len(odds) : -1], refs[-1]
    for at, d in enumerate(odds):
        for column, block in pair_blocks(received[at][...], own_keep[...], other_keep[...], place[2]):
            every[d, column] = block
    first = jnp.bitwise_xor(place[0], place[1])
    for k, out in enumerate(outs):
        out[...] = every[jnp.bitwise_xor(first, k)]


def gather_kernel(width, place, own_early, own_late, *refs):
    received, mine, swap, mirror = refs[:-3], refs[-3], refs[-2], refs[-1]
    cells = own_early.shape[1]
    core = place[2]
    gap = jnp.bitwise_xor(place[0], place[1])
    late = functools.reduce(jnp.bitwise_xor, [jnp.bitwise_and(jnp.right_shift(gap, b), 1) for b in range(width)]) == 1

    def total(column):
        value = jnp.where(late, own_late[column], own_early[column])
        for part in received:
            value = value + part[column]
        return value

    mine[...] = total(core)
    swap[...] = total(1 - core).astype(BF16)
    for column in range(2):
        mirror[column * cells : (column + 1) * cells, :] = total(column).T.astype(BF16)


def final_kernel(amount, place, mine, swap, mirror, out):
    cells = mine.shape[0]
    core = place[2]
    here = pl.ds(pl.multiple_of(core * cells, cells), cells)
    there = pl.ds(pl.multiple_of((1 - core) * cells, cells), cells)
    out[here, :] = (mine[...] + mirror[here, :].astype(F32)) / amount
    out[there, :] = (swap[...].astype(F32) + mirror[there, :].astype(F32)) / amount


def whole_call(kernel, name, shapes, scratch, flops, place, *arrays):
    vmem = pl.BlockSpec(memory_space=pltpu.VMEM)
    many = isinstance(shapes, list)
    moved = sum(2 * a.size for a in arrays)
    return pl.pallas_call(
        kernel,
        in_specs=[pl.BlockSpec(memory_space=pltpu.SMEM)] + [vmem] * len(arrays),
        out_specs=[vmem] * len(shapes) if many else vmem,
        out_shape=shapes,
        scratch_shapes=scratch,
        compiler_params=params(),
        cost_estimate=pl.CostEstimate(flops=1, bytes_accessed=1, transcendentals=0),
        name=name,
    )(place, *arrays)


def to_group(x, k, late, groups, chips):
    pairs = [
        ((g * chips + p) * 2 + c, ((g ^ k) * chips + p) * 2 + c)
        for g in range(groups)
        for p in range(chips)
        for c in range(2)
        if odd(g ^ p ^ k) == late
    ]
    return lax.ppermute(x, ("elec", "cell"), pairs)


def per_device(grads, quads, volume, weight):
    groups, devices = lax.axis_size("elec"), lax.axis_size("cell")
    chips = devices // 2
    cells, measured = grads.shape[2], quads.shape[0]
    here = lax.axis_index("cell")
    group, chip, core = lax.axis_index("elec"), here // 2, here % 2
    place = jnp.stack([group, chip, core]).astype(I32)

    half, far = groups // 2, groups - 1
    shards = {0: grads, far: hop(grads, "elec", groups, far)}
    for j in range(1, half):
        shards[j] = hop(grads, "elec", groups, j)
    for j in range(1, half):
        shards[far ^ j] = hop(shards[far], "elec", groups, j)

    odds = [d for d in range(1, chips) if odd(d)]
    evens = [d for d in range(1, chips) if not odd(d)]
    columns, weights = quads.T, weight.reshape(1, measured)
    volumes = volume.reshape(cells, 1)
    volumes_across = {d: hop(volume, "cell", devices, 2 * d).reshape(cells, 1) for d in evens}
    bits = max(1, (chips - 1).bit_length())
    parity = functools.reduce(jnp.bitwise_xor, [(chip >> b) & 1 for b in range(bits)])
    keep, send = parity, 1 - parity
    keep_tiles, send_tiles = [2 * keep, 2 * keep + 1], [2 * send, 2 * send + 1]
    relayed = {far ^ j: shards[far ^ j] for j in range(1, half)}
    direct = {k: shards[k] for k in shards if k not in relayed}
    ready = tuple(sorted(direct))
    turned = turn_shards([direct[k] for k in ready])

    across = {}
    for d in evens:
        near, away = hop(grads, "cell", devices, 2 * d), hop(shards[far], "cell", devices, 2 * d)
        across[d] = {0: near, far: away}
        both = jnp.stack([near, away])
        both, relayed = lax.optimization_barrier((both, relayed))
        for j in range(1, half):
            moved = hop(both, "elec", groups, j)
            across[d][j], across[d][far ^ j] = moved[0], moved[1]

    form = functools.partial(sensitivities, place)
    own_send = form(send_tiles, columns, weights, volumes, relayed, turned, ready)
    received = [hop(own_send, "cell", devices, 2 * d) for d in odds]
    other_send = hop(own_send, "cell", devices, 1)
    columns, own_send = lax.optimization_barrier((columns, own_send))
    own_keep = form(keep_tiles, columns, weights, volumes, relayed, turned, ready)
    other_keep = hop(own_keep, "cell", devices, 1)
    recomputed = []
    for d in evens:
        bit = (chip >> low_bit(d)) & 1
        recomputed.append(form([2 * send + bit, 2 * keep + bit], columns, weights, volumes_across[d], across[d]))

    block = (2, cells, cells)
    shape = [jax.ShapeDtypeStruct(block, F32)] * groups
    every = [pltpu.VMEM((chips, *block), F32)]
    early = whole_call(
        functools.partial(early_kernel, evens), "early_blocks", shape, every, 1000,
        place, own_send, own_keep, other_send, other_keep, *recomputed,
    )
    late = whole_call(
        functools.partial(late_kernel, odds), "late_blocks", shape, every, 1000,
        place, own_keep, other_keep, *received,
    )
    arrived = [to_group(early[k], k, False, groups, chips) for k in range(1, groups)]
    arrived += [to_group(late[k], k, True, groups, chips) for k in range(1, groups)]
    mine, swap, mirror = whole_call(
        functools.partial(gather_kernel, bits),
        "sum_groups",
        [
            jax.ShapeDtypeStruct((cells, cells), F32),
            jax.ShapeDtypeStruct((cells, cells), BF16),
            jax.ShapeDtypeStruct((2 * cells, cells), BF16),
        ],
        [],
        1000,
        place, early[0], late[0], *arrived,
    )
    pairs = [
        (g * devices + 2 * p + c, p * devices + 2 * g + c)
        for g in range(groups)
        for p in range(chips)
        for c in range(2)
        if g != p
    ]
    mirrored = lax.ppermute(mirror, ("elec", "cell"), pairs)
    swapped = hop(swap, "cell", devices, 1)
    amount = float(measured * groups)
    return whole_call(
        functools.partial(final_kernel, amount),
        "finish",
        jax.ShapeDtypeStruct((2 * cells, cells), F32),
        [],
        1000,
        place, mine, swapped, mirrored,
    )


def solution(mesh):
    placed = (P(None, "elec", "cell"), P("elec", None), P("cell"), P("elec"))
    return jax.shard_map(
        per_device, mesh=mesh, in_specs=placed, out_specs=P("elec", "cell"), check_vma=False
    )
```

time: 137 us -> 69.5 us (0.51)
  the two profiles are of different devices: /device:TPU:0 before, /device:TPU:14 now
where the time goes in v1:
time: 69.5 us; the launch traced here: 69.3 us
  starting transfers between devices  29.6 us (43%)
  waiting for transfers between devices  19.6 us (28%)
  Pallas kernels  18.6 us (27%)
  local copies, waits for them, and re-layouts  0.91 us (1%)
    ppermute x6, starting transfers between devices, to_group(): return lax.ppermute(x, ('elec', 'cell'), pairs)  15 us
    pallas_call x3, Pallas kernels, sensitivities(): pl.pallas_call(functools.partial(sensitivity_kernel, len(ready), offsets)...  13.5 us
    ppermute x12, starting transfers between devices, hop(): return lax.ppermute(x, axis, [(i, i ^ mask) for i in range(size)])  12.3 us
    ppermute x12, waiting for transfers between devices, hop(): return lax.ppermute(x, axis, [(i, i ^ mask) for i in range(size)])  10.6 us
    pallas_call x4, Pallas kernels, whole_call(): pl.pallas_call(kernel, in_specs=[pl.BlockSpec(memory_space=pltpu.SMEM)] +...  4.89 us
    ppermute x6, waiting for transfers between devices, to_group(): return lax.ppermute(x, ('elec', 'cell'), pairs)  4.52 us
    ppermute x1, waiting for transfers between devices, per_device(): mirrored = lax.ppermute(mirror, ('elec', 'cell'), pairs)  4.43 us
    ppermute x1, starting transfers between devices, per_device(): mirrored = lax.ppermute(mirror, ('elec', 'cell'), pairs)  2.25 us
  transfers between devices with their start and end apart: 19, of which 6 were waited for; matrix products, arithmetic and copies ran while one was open for 2% of the time, Pallas kernels for 24%

profile of v1, /device:TPU:14, one launch (start us, length us, event | category | flops | bytes accessed | tf_op | source)
XLA Modules:
  0.0 69.3 jit_solution(6416698278415563035)
XLA Ops:
  0.0 0.4 collective-permute-start
  0.5 2.7 %collective-permute-start.1 = (bf16[3,256,128]{2,1,0:T(8,128)(2,1)}, bf16[3,256,128]{2,1,0:T(8,128)(2,1)S(1)}, u32[]{:S(2)}, u32[]{:S(2)}) collective-permute-start(bf16[3,256,128]{2,1,0:T(8,128)(2,1)} %refs_0_.1), channel_id=1, source_target_pairs={{0,24},{8,16},{16,8},{24,0},{1,25},{9,17},{17,9},{25,1},{2,26},{10... | collective-permute-start | bytes 589832 | tf_op jit(solution)/shard_map/ppermute | solution.py:20
  3.2 0.5 collective-permute-start.2
  3.6 2.4 %collective-permute-start.7 = (f32[128]{0:T(128)}, f32[128]{0:T(128)S(1)}, u32[]{:S(2)}, u32[]{:S(2)}) collective-permute-start(f32[128]{0:T(128)} %param.6), channel_id=1, source_target_pairs={{0,6},{1,7},{2,4},{3,5},{4,2},{5,3},{6,0},{7,1},{8,14},{9,15},{10,... | collective-permute-start | bytes 1544 | tf_op jit(solution)/shard_map/ppermute | solution.py:20
  6.2 6.0 %collective-permute-done.1.refs_2_ = bf16[3,256,128]{2,1,0:T(8,128)(2,1)S(1)} collective-permute-done((bf16[3,256,128]{2,1,0:T(8,128)(2,1)}, bf16[3,256,128]{2,1,0:T(8,128)(2,1)S(1)}, u32[]{:S(2)}, u32[]{:S(2)}) %collective-permute-start.1) | collective-permute-done | bytes 196640 | tf_op jit(solution)/shard_map/ppermute | solution.py:20
  12.2 0.5 collective-permute-start.3
  12.8 1.4 %collective-permute-start.4 = (bf16[3,256,128]{2,1,0:T(8,128)(2,1)S(1)}, bf16[3,256,128]{2,1,0:T(8,128)(2,1)S(1)}, u32[]{:S(2)}, u32[]{:S(2)}) collective-permute-start(bf16[3,256,128]{2,1,0:T(8,128)(2,1)S(1)} %collective-permute-done.1.refs_2_), channel_id=1, source_target_pairs={{0,8},{8,0},{16,24},{24,16},{1,9},{9,1},{17,25},{25,17},{2,10},{10... | collective-permute-start | bytes 589832 | tf_op jit(solution)/shard_map/ppermute | solution.py:20
  14.3 0.8 %copy.5.volume = f32[128,1]{1,0:T(8,128)S(1)} copy(f32[128,1]{0,1:T(1,128)} %bitcast.27) | data formatting | bytes 1024 | tf_op jit(solution)/shard_map/reshape | solution.py:235
  15.0 0.1 copy.7.volume
  15.2 0.2 turn_shards.1.refs_0_
  15.4 3.4 %collective-permute-done.3.refs_3_ = bf16[3,256,128]{2,1,0:T(8,128)(2,1)S(1)} collective-permute-done((bf16[3,256,128]{2,1,0:T(8,128)(2,1)S(1)}, bf16[3,256,128]{2,1,0:T(8,128)(2,1)S(1)}, u32[]{:S(2)}, u32[]{:S(2)}) %collective-permute-start.3) | collective-permute-done | bytes 196640 | tf_op jit(solution)/shard_map/ppermute | solution.py:20
  18.9 1.5 %collective-permute-start.8 = (bf16[2,3,256,128]{3,2,1,0:T(8,128)(2,1)S(1)}, bf16[2,3,256,128]{3,2,1,0:T(8,128)(2,1)S(1)}, u32[]{:S(2)}, u32[]{:S(2)}) collective-permute-start(bf16[2,3,256,128]{3,2,1,0:T(8,128)(2,1)S(1)} %pad_maximum_fusion), channel_id=1, source_target_pairs={{0,8},{8,0},{16,24},{24,16},{1,9},{9,1},{17,25},{25,17},{2,10},{10... | collective-permute-start | bytes 1179656 | tf_op jit(solution)/shard_map/ppermute | solution.py:20
  20.4 4.5 %sensitivities.3.own_send = bf16[128,2048]{1,0:T(8,128)(2,1)S(1)} custom-call(s32[3]{0:T(128)S(1)} %pad_add_fusion.1.place, s32[4,4096]{1,0:T(4,128)S(1)} %bitcast.21, f32[1,4096]{1,0:T(1,128)S(1)} %bitcast.24, f32[128,1]{1,0:T(8,128)S(1)} %copy.5.volume, bf16[3,384,256]{2,1,0:T(8,128)(2,1)S(1)} %turn_shards.1.refs_0_, ...), custom_call_target="tpu_custom_call" | custom-call | flops 3221225472 | bytes 1 | tf_op jit(solution)/shard_map/sensitivities/pallas_call | solution.py:108
  24.9 1.0 %collective-permute-start.9 = (bf16[128,2048]{1,0:T(8,128)(2,1)S(1)}, bf16[128,2048]{1,0:T(8,128)(2,1)S(1)}, u32[]{:S(2)}, u32[]{:S(2)}) collective-permute-start(bf16[128,2048]{1,0:T(8,128)(2,1)S(1)} %sensitivities.3.own_send), channel_id=1, source_target_pairs={{0,2},{1,3},{2,0},{3,1},{4,6},{5,7},{6,4},{7,5},{8,10},{9,11},{10,... | collective-permute-start | bytes 1572872 | tf_op jit(solution)/shard_map/ppermute | solution.py:20
  26.0 1.5 %collective-permute-start.10 = (bf16[128,2048]{1,0:T(8,128)(2,1)S(1)}, bf16[128,2048]{1,0:T(8,128)(2,1)S(1)}, u32[]{:S(2)}, u32[]{:S(2)}) collective-permute-start(bf16[128,2048]{1,0:T(8,128)(2,1)S(1)} %sensitivities.3.own_send), channel_id=1, source_target_pairs={{0,4},{1,5},{2,6},{3,7},{4,0},{5,1},{6,2},{7,3},{8,12},{9,13},{10,... | collective-permute-start | bytes 1572872 | tf_op jit(solution)/shard_map/ppermute | solution.py:20
  27.5 4.5 %sensitivities.4.own_keep = bf16[128,2048]{1,0:T(8,128)(2,1)S(1)} custom-call(s32[3]{0:T(128)S(1)} %pad_add_fusion.2.place, s32[4,4096]{1,0:T(4,128)S(1)} %bitcast.22, f32[1,4096]{1,0:T(1,128)S(1)} %bitcast.25, f32[128,1]{1,0:T(8,128)S(1)} %copy.5.volume, bf16[3,384,256]{2,1,0:T(8,128)(2,1)S(1)} %turn_shards.1.refs_0_, ...), custom_call_target="tpu_custom_call" | custom-call | flops 3221225472 | bytes 1 | tf_op jit(solution)/shard_map/sensitivities/pallas_call | solution.py:108
  32.1 4.6 %sensitivities.5.refs_0_ = bf16[128,2048]{1,0:T(8,128)(2,1)S(1)} custom-call(s32[3]{0:T(128)S(1)} %pad_add_fusion.3.place, s32[4,4096]{1,0:T(4,128)S(1)} %bitcast.23, f32[1,4096]{1,0:T(1,128)S(1)} %bitcast.26, f32[128,1]{1,0:T(8,128)S(1)} %copy.7.volume, bf16[3,256,128]{2,1,0:T(8,128)(2,1)S(1)} %collective-permute-done.2.refs_0_, ...), custom_call_target="tpu_custom_call" | custom-call | flops 3221225472 | bytes 1 | tf_op jit(solution)/shard_map/sensitivities/pallas_call | solution.py:108
  36.7 1.7 %early_blocks.1 = (f32[2,128,128]{2,1,0:T(8,128)S(1)}, f32[2,128,128]{2,1,0:T(8,128)S(1)}, f32[2,128,128]{2,1,0:T(8,128)S(1)}, f32[2,128,128]{2,1,0:T(8,128)S(1)}) custom-call(s32[3]{0:T(128)S(1)} %pad_add_fusion.place, bf16[128,2048]{1,0:T(8,128)(2,1)S(1)} %sensitivities.3.own_send, bf16[128,2048]{1,0:T(8,128)(2,1)S(1)} %sensitivities.4.own_keep, ...), custom_call_target="tpu_custom_call" | custom-call | flops 1 | bytes 1 | tf_op jit(solution)/shard_map/early_blocks/pallas_call | solution.py:194
  38.5 2.5 %collective-permute-start.11 = (f32[2,128,128]{2,1,0:T(8,128)S(1)}, f32[2,128,128]{2,1,0:T(8,128)S(1)}, u32[]{:S(2)}, u32[]{:S(2)}) collective-permute-start(f32[2,128,128]{2,1,0:T(8,128)S(1)} %get-tuple-element.26), channel_id=1, source_target_pairs={{2,10},{3,11},{4,12},{5,13},{8,0},{9,1},{14,6},{15,7},{16,24},{17,... | collective-permute-start | bytes 393224 | tf_op jit(solution)/shard_map/ppermute | solution.py:214
  41.0 3.7 %collective-permute-start.12 = (f32[2,128,128]{2,1,0:T(8,128)S(1)}, f32[2,128,128]{2,1,0:T(8,128)S(1)}, u32[]{:S(2)}, u32[]{:S(2)}) collective-permute-start(f32[2,128,128]{2,1,0:T(8,128)S(1)} %get-tuple-element.27), channel_id=1, source_target_pairs={{2,18},{3,19},{4,20},{5,21},{8,24},{9,25},{14,30},{15,31},{16,0},{... | collective-permute-start | bytes 393224 | tf_op jit(solution)/shard_map/ppermute | solution.py:214
  44.7 0.7 collective-permute-start.13
  45.4 1.3 %late_blocks.1 = (f32[2,128,128]{2,1,0:T(8,128)S(1)}, f32[2,128,128]{2,1,0:T(8,128)S(1)}, f32[2,128,128]{2,1,0:T(8,128)S(1)}, f32[2,128,128]{2,1,0:T(8,128)S(1)}) custom-call(s32[3]{0:T(128)S(1)} %pad_add_fusion.place, bf16[128,2048]{1,0:T(8,128)(2,1)S(1)} %sensitivities.4.own_keep, bf16[128,2048]{1,0:T(8,128)(2,1)S(1)} %collective-permute-done.6.other_keep, ...), custom_call_target="tpu_custom_call" | custom-call | flops 1 | bytes 1 | tf_op jit(solution)/shard_map/late_blocks/pallas_call | solution.py:194
  46.7 1.3 %collective-permute-start.14 = (f32[2,128,128]{2,1,0:T(8,128)S(1)}, f32[2,128,128]{2,1,0:T(8,128)S(1)}, u32[]{:S(2)}, u32[]{:S(2)}) collective-permute-start(f32[2,128,128]{2,1,0:T(8,128)S(1)} %get-tuple-element.29), channel_id=1, source_target_pairs={{0,8},{1,9},{6,14},{7,15},{10,2},{11,3},{12,4},{13,5},{18,26},{19,... | collective-permute-start | bytes 393224 | tf_op jit(solution)/shard_map/ppermute | solution.py:214
  48.0 1.3 %collective-permute-start.15 = (f32[2,128,128]{2,1,0:T(8,128)S(1)}, f32[2,128,128]{2,1,0:T(8,128)S(1)}, u32[]{:S(2)}, u32[]{:S(2)}) collective-permute-start(f32[2,128,128]{2,1,0:T(8,128)S(1)} %get-tuple-element.30), channel_id=1, source_target_pairs={{0,16},{1,17},{6,22},{7,23},{10,26},{11,27},{12,28},{13,29},{18,2}... | collective-permute-start | bytes 393224 | tf_op jit(solution)/shard_map/ppermute | solution.py:214
  49.3 5.6 %collective-permute-start.16 = (f32[2,128,128]{2,1,0:T(8,128)S(1)}, f32[2,128,128]{2,1,0:T(8,128)S(1)}, u32[]{:S(2)}, u32[]{:S(2)}) collective-permute-start(f32[2,128,128]{2,1,0:T(8,128)S(1)} %get-tuple-element.31), channel_id=1, source_target_pairs={{2,26},{3,27},{4,28},{5,29},{8,16},{9,17},{14,22},{15,23},{16,8},{... | collective-permute-start | bytes 393224 | tf_op jit(solution)/shard_map/ppermute | solution.py:214
  54.9 2.2 %collective-permute-done.15.refs_4_ = f32[2,128,128]{2,1,0:T(8,128)S(1)} collective-permute-done((f32[2,128,128]{2,1,0:T(8,128)S(1)}, f32[2,128,128]{2,1,0:T(8,128)S(1)}, u32[]{:S(2)}, u32[]{:S(2)}) %collective-permute-start.15) | collective-permute-done | bytes 131104 | tf_op jit(solution)/shard_map/ppermute | solution.py:214
  57.1 2.3 %collective-permute-done.16.refs_5_ = f32[2,128,128]{2,1,0:T(8,128)S(1)} collective-permute-done((f32[2,128,128]{2,1,0:T(8,128)S(1)}, f32[2,128,128]{2,1,0:T(8,128)S(1)}, u32[]{:S(2)}, u32[]{:S(2)}) %collective-permute-start.16) | collective-permute-done | bytes 131104 | tf_op jit(solution)/shard_map/ppermute | solution.py:214
  59.4 0.7 sum_groups.1
  60.1 2.2 %collective-permute-start.18 = (bf16[256,128]{1,0:T(8,128)(2,1)S(1)}, bf16[256,128]{1,0:T(8,128)(2,1)S(1)}, u32[]{:S(2)}, u32[]{:S(2)}) collective-permute-start(bf16[256,128]{1,0:T(8,128)(2,1)S(1)} %get-tuple-element.34), channel_id=1, source_target_pairs={{2,8},{3,9},{4,16},{5,17},{6,24},{7,25},{8,2},{9,3},{12,18},{13,19... | collective-permute-start | bytes 196616 | tf_op jit(solution)/shard_map/ppermute | solution.py:300
  62.4 1.2 %collective-permute-done.17.swap = bf16[128,128]{1,0:T(8,128)(2,1)S(1)} collective-permute-done((bf16[128,128]{1,0:T(8,128)(2,1)S(1)}, bf16[128,128]{1,0:T(8,128)(2,1)S(1)}, u32[]{:S(2)}, u32[]{:S(2)}) %collective-permute-start.17) | collective-permute-done | bytes 32800 | tf_op jit(solution)/shard_map/ppermute | solution.py:20
  63.6 4.4 %collective-permute-done.18.mirror = bf16[256,128]{1,0:T(8,128)(2,1)S(1)} collective-permute-done((bf16[256,128]{1,0:T(8,128)(2,1)S(1)}, bf16[256,128]{1,0:T(8,128)(2,1)S(1)}, u32[]{:S(2)}, u32[]{:S(2)}) %collective-permute-start.18) | collective-permute-done | bytes 65568 | tf_op jit(solution)/shard_map/ppermute | solution.py:300
  68.0 1.2 %finish.1 = f32[256,128]{1,0:T(8,128)} custom-call(s32[3]{0:T(128)S(1)} %pad_add_fusion.place, f32[128,128]{1,0:T(8,128)S(1)} %get-tuple-element.32.mine, bf16[128,128]{1,0:T(8,128)(2,1)S(1)} %collective-permute-done.17.swap, bf16[256,128]{1,0:T(8,128)(2,1)S(1)} %collective-permute-done.18.mirror), custom_call_target="tpu_custom_call" | custom-call | flops 1 | bytes 1 | tf_op jit(solution)/shard_map/finish/pallas_call | solution.py:194
  (28 shorter events, 0.6 us)
Async XLA Ops:
  0.0 15.2 %copy-start = (bf16[3,256,128]{2,1,0:T(8,128)(2,1)S(1)}, bf16[3,256,128]{2,1,0:T(8,128)(2,1)}, u32[]{:S(2)}) copy-start(bf16[3,256,128]{2,1,0:T(8,128)(2,1)} %refs_0_.1) | copy-start | bytes 589828
  0.0 15.2 %collective-permute-start = (bf16[3,256,128]{2,1,0:T(8,128)(2,1)}, bf16[3,256,128]{2,1,0:T(8,128)(2,1)S(1)}, u32[]{:S(2)}, u32[]{:S(2)}) collective-permute-start(bf16[3,256,128]{2,1,0:T(8,128)(2,1)} %refs_0_.1), channel_id=1, source_target_pairs={{0,8},{8,0},{16,24},{24,16},{1,9},{9,1},{17,25},{25,17},{2,10},{10... | collective-permute-start | bytes 589832 | tf_op jit(solution)/shard_map/ppermute | solution.py:20
  0.5 11.8 %collective-permute-start.1 = (bf16[3,256,128]{2,1,0:T(8,128)(2,1)}, bf16[3,256,128]{2,1,0:T(8,128)(2,1)S(1)}, u32[]{:S(2)}, u32[]{:S(2)}) collective-permute-start(bf16[3,256,128]{2,1,0:T(8,128)(2,1)} %refs_0_.1), channel_id=1, source_target_pairs={{0,24},{8,16},{16,8},{24,0},{1,25},{9,17},{17,9},{25,1},{2,26},{10... | collective-permute-start | bytes 589832 | tf_op jit(solution)/shard_map/ppermute | solution.py:20
  3.2 12.2 %collective-permute-start.2 = (bf16[3,256,128]{2,1,0:T(8,128)(2,1)}, bf16[3,256,128]{2,1,0:T(8,128)(2,1)S(1)}, u32[]{:S(2)}, u32[]{:S(2)}) collective-permute-start(bf16[3,256,128]{2,1,0:T(8,128)(2,1)} %refs_0_.1), channel_id=1, source_target_pairs={{0,6},{1,7},{2,4},{3,5},{4,2},{5,3},{6,0},{7,1},{8,14},{9,15},{10,... | collective-permute-start | bytes 589832 | tf_op jit(solution)/shard_map/ppermute | solution.py:20
  3.6 11.4 %collective-permute-start.7 = (f32[128]{0:T(128)}, f32[128]{0:T(128)S(1)}, u32[]{:S(2)}, u32[]{:S(2)}) collective-permute-start(f32[128]{0:T(128)} %param.6), channel_id=1, source_target_pairs={{0,6},{1,7},{2,4},{3,5},{4,2},{5,3},{6,0},{7,1},{8,14},{9,15},{10,... | collective-permute-start | bytes 1544 | tf_op jit(solution)/shard_map/ppermute | solution.py:20
  12.2 6.6 %collective-permute-start.3 = (bf16[3,256,128]{2,1,0:T(8,128)(2,1)S(1)}, bf16[3,256,128]{2,1,0:T(8,128)(2,1)S(1)}, u32[]{:S(2)}, u32[]{:S(2)}) collective-permute-start(bf16[3,256,128]{2,1,0:T(8,128)(2,1)S(1)} %collective-permute-done.1.refs_2_), channel_id=1, source_target_pairs={{0,6},{1,7},{2,4},{3,5},{4,2},{5,3},{6,0},{7,1},{8,14},{9,15},{10,... | collective-permute-start | bytes 589832 | tf_op jit(solution)/shard_map/ppermute | solution.py:20
  12.8 6.1 %collective-permute-start.4 = (bf16[3,256,128]{2,1,0:T(8,128)(2,1)S(1)}, bf16[3,256,128]{2,1,0:T(8,128)(2,1)S(1)}, u32[]{:S(2)}, u32[]{:S(2)}) collective-permute-start(bf16[3,256,128]{2,1,0:T(8,128)(2,1)S(1)} %collective-permute-done.1.refs_2_), channel_id=1, source_target_pairs={{0,8},{8,0},{16,24},{24,16},{1,9},{9,1},{17,25},{25,17},{2,10},{10... | collective-permute-start | bytes 589832 | tf_op jit(solution)/shard_map/ppermute | solution.py:20
  18.8 1.6 %copy-start.1 = (s32[4096,4]{0,1:T(4,128)S(1)}, s32[4096,4]{0,1:T(4,128)}, u32[]{:S(2)}) copy-start(s32[4096,4]{0,1:T(4,128)} %param.5) | copy-start | bytes 196612
  18.8 1.6 %copy-start.2 = (f32[4096]{0:T(1024)S(1)}, f32[4096]{0:T(1024)}, u32[]{:S(2)}) copy-start(f32[4096]{0:T(1024)} %param.7) | copy-start | bytes 49156
  18.9 13.2 %collective-permute-start.8 = (bf16[2,3,256,128]{3,2,1,0:T(8,128)(2,1)S(1)}, bf16[2,3,256,128]{3,2,1,0:T(8,128)(2,1)S(1)}, u32[]{:S(2)}, u32[]{:S(2)}) collective-permute-start(bf16[2,3,256,128]{3,2,1,0:T(8,128)(2,1)S(1)} %pad_maximum_fusion), channel_id=1, source_target_pairs={{0,8},{8,0},{16,24},{24,16},{1,9},{9,1},{17,25},{25,17},{2,10},{10... | collective-permute-start | bytes 1179656 | tf_op jit(solution)/shard_map/ppermute | solution.py:20
  24.9 11.9 %collective-permute-start.5 = (bf16[128,2048]{1,0:T(8,128)(2,1)S(1)}, bf16[128,2048]{1,0:T(8,128)(2,1)S(1)}, u32[]{:S(2)}, u32[]{:S(2)}) collective-permute-start(bf16[128,2048]{1,0:T(8,128)(2,1)S(1)} %sensitivities.3.own_send), channel_id=1, source_target_pairs={{0,1},{1,0},{2,3},{3,2},{4,5},{5,4},{6,7},{7,6},{8,9},{9,8},{10,11... | collective-permute-start | bytes 1572872 | tf_op jit(solution)/shard_map/ppermute | solution.py:20
  24.9 20.4 %collective-permute-start.9 = (bf16[128,2048]{1,0:T(8,128)(2,1)S(1)}, bf16[128,2048]{1,0:T(8,128)(2,1)S(1)}, u32[]{:S(2)}, u32[]{:S(2)}) collective-permute-start(bf16[128,2048]{1,0:T(8,128)(2,1)S(1)} %sensitivities.3.own_send), channel_id=1, source_target_pairs={{0,2},{1,3},{2,0},{3,1},{4,6},{5,7},{6,4},{7,5},{8,10},{9,11},{10,... | collective-permute-start | bytes 1572872 | tf_op jit(solution)/shard_map/ppermute | solution.py:20
  26.0 19.4 %collective-permute-start.10 = (bf16[128,2048]{1,0:T(8,128)(2,1)S(1)}, bf16[128,2048]{1,0:T(8,128)(2,1)S(1)}, u32[]{:S(2)}, u32[]{:S(2)}) collective-permute-start(bf16[128,2048]{1,0:T(8,128)(2,1)S(1)} %sensitivities.3.own_send), channel_id=1, source_target_pairs={{0,4},{1,5},{2,6},{3,7},{4,0},{5,1},{6,2},{7,3},{8,12},{9,13},{10,... | collective-permute-start | bytes 1572872 | tf_op jit(solution)/shard_map/ppermute | solution.py:20
  32.0 4.8 %collective-permute-start.6 = (bf16[128,2048]{1,0:T(8,128)(2,1)S(1)}, bf16[128,2048]{1,0:T(8,128)(2,1)S(1)}, u32[]{:S(2)}, u32[]{:S(2)}) collective-permute-start(bf16[128,2048]{1,0:T(8,128)(2,1)S(1)} %sensitivities.4.own_keep), channel_id=1, source_target_pairs={{0,1},{1,0},{2,3},{3,2},{4,5},{5,4},{6,7},{7,6},{8,9},{9,8},{10,11... | collective-permute-start | bytes 1572872 | tf_op jit(solution)/shard_map/ppermute | solution.py:20
  38.5 10.8 %collective-permute-start.11 = (f32[2,128,128]{2,1,0:T(8,128)S(1)}, f32[2,128,128]{2,1,0:T(8,128)S(1)}, u32[]{:S(2)}, u32[]{:S(2)}) collective-permute-start(f32[2,128,128]{2,1,0:T(8,128)S(1)} %get-tuple-element.26), channel_id=1, source_target_pairs={{2,10},{3,11},{4,12},{5,13},{8,0},{9,1},{14,6},{15,7},{16,24},{17,... | collective-permute-start | bytes 393224 | tf_op jit(solution)/shard_map/ppermute | solution.py:214
  41.0 13.9 %collective-permute-start.12 = (f32[2,128,128]{2,1,0:T(8,128)S(1)}, f32[2,128,128]{2,1,0:T(8,128)S(1)}, u32[]{:S(2)}, u32[]{:S(2)}) collective-permute-start(f32[2,128,128]{2,1,0:T(8,128)S(1)} %get-tuple-element.27), channel_id=1, source_target_pairs={{2,18},{3,19},{4,20},{5,21},{8,24},{9,25},{14,30},{15,31},{16,0},{... | collective-permute-start | bytes 393224 | tf_op jit(solution)/shard_map/ppermute | solution.py:214
  44.7 10.2 %collective-permute-start.13 = (f32[2,128,128]{2,1,0:T(8,128)S(1)}, f32[2,128,128]{2,1,0:T(8,128)S(1)}, u32[]{:S(2)}, u32[]{:S(2)}) collective-permute-start(f32[2,128,128]{2,1,0:T(8,128)S(1)} %get-tuple-element.28), channel_id=1, source_target_pairs={{0,24},{1,25},{6,30},{7,31},{10,18},{11,19},{12,20},{13,21},{18,10... | collective-permute-start | bytes 393224 | tf_op jit(solution)/shard_map/ppermute | solution.py:214
  46.7 8.2 %collective-permute-start.14 = (f32[2,128,128]{2,1,0:T(8,128)S(1)}, f32[2,128,128]{2,1,0:T(8,128)S(1)}, u32[]{:S(2)}, u32[]{:S(2)}) collective-permute-start(f32[2,128,128]{2,1,0:T(8,128)S(1)} %get-tuple-element.29), channel_id=1, source_target_pairs={{0,8},{1,9},{6,14},{7,15},{10,2},{11,3},{12,4},{13,5},{18,26},{19,... | collective-permute-start | bytes 393224 | tf_op jit(solution)/shard_map/ppermute | solution.py:214
  48.0 9.1 %collective-permute-start.15 = (f32[2,128,128]{2,1,0:T(8,128)S(1)}, f32[2,128,128]{2,1,0:T(8,128)S(1)}, u32[]{:S(2)}, u32[]{:S(2)}) collective-permute-start(f32[2,128,128]{2,1,0:T(8,128)S(1)} %get-tuple-element.30), channel_id=1, source_target_pairs={{0,16},{1,17},{6,22},{7,23},{10,26},{11,27},{12,28},{13,29},{18,2}... | collective-permute-start | bytes 393224 | tf_op jit(solution)/shard_map/ppermute | solution.py:214
  49.3 10.1 %collective-permute-start.16 = (f32[2,128,128]{2,1,0:T(8,128)S(1)}, f32[2,128,128]{2,1,0:T(8,128)S(1)}, u32[]{:S(2)}, u32[]{:S(2)}) collective-permute-start(f32[2,128,128]{2,1,0:T(8,128)S(1)} %get-tuple-element.31), channel_id=1, source_target_pairs={{2,26},{3,27},{4,28},{5,29},{8,16},{9,17},{14,22},{15,23},{16,8},{... | collective-permute-start | bytes 393224 | tf_op jit(solution)/shard_map/ppermute | solution.py:214
  60.1 8.0 %collective-permute-start.18 = (bf16[256,128]{1,0:T(8,128)(2,1)S(1)}, bf16[256,128]{1,0:T(8,128)(2,1)S(1)}, u32[]{:S(2)}, u32[]{:S(2)}) collective-permute-start(bf16[256,128]{1,0:T(8,128)(2,1)S(1)} %get-tuple-element.34), channel_id=1, source_target_pairs={{2,8},{3,9},{4,16},{5,17},{6,24},{7,25},{8,2},{9,3},{12,18},{13,19... | collective-permute-start | bytes 196616 | tf_op jit(solution)/shard_map/ppermute | solution.py:300
  62.3 1.3 %collective-permute-start.17 = (bf16[128,128]{1,0:T(8,128)(2,1)S(1)}, bf16[128,128]{1,0:T(8,128)(2,1)S(1)}, u32[]{:S(2)}, u32[]{:S(2)}) collective-permute-start(bf16[128,128]{1,0:T(8,128)(2,1)S(1)} %get-tuple-element.33), channel_id=1, source_target_pairs={{0,1},{1,0},{2,3},{3,2},{4,5},{5,4},{6,7},{7,6},{8,9},{9,8},{10,11... | collective-permute-start | bytes 98312 | tf_op jit(solution)/shard_map/ppermute | solution.py:20

commit v2 on v1

--- a/solution.py
+++ b/solution.py
@@ -120,16 +120,16 @@
 
 
 def early_kernel(evens, place, own_send, own_keep, other_send, other_keep, *refs):
-    recomputed, outs, every = refs[: len(evens)], refs[len(evens) : -1], refs[-1]
+    recomputed, out = refs[: len(evens)], refs[-1]
     core = place[2]
     sides = ((0, own_send, other_send), (1, own_keep, other_keep))
 
-    def add(d, side, blocks):
+    def add(at, side, blocks):
         for column, block in blocks:
             if side == 0:
-                every[d, column] = block
+                out[at, column] = block
             else:
-                every[d, column] += block
+                out[at, column] += block
 
     for side, own, other in sides:
         add(0, side, pair_blocks(own[...], own[...], other[...], core))
@@ -142,35 +142,45 @@
                 lanes = slice(bit * part, (bit + 1) * part)
                 for side, own, other in sides:
                     rows = recomputed[at][:, side * part : (side + 1) * part]
-                    add(d, side, pair_blocks(rows, own[:, lanes], other[:, lanes], core))
-
-    first = jnp.bitwise_xor(place[0], place[1])
-    for k, out in enumerate(outs):
-        out[...] = every[jnp.bitwise_xor(first, k)]
-
-
-def late_kernel(odds, place, own_keep, other_keep, *refs):
-    received, outs, every = refs[: len(odds)], refs[len(odds) : -1], refs[-1]
+                    add(1 + at, side, pair_blocks(rows, own[:, lanes], other[:, lanes], core))
+
+
+def diagonal(cells):
+    return lax.broadcasted_iota(I32, (cells, cells), 0) == lax.broadcasted_iota(I32, (cells, cells), 1)
+
+
+def late_kernel(evens, odds, place, early, own_keep, other_keep, *refs):
+    received, out_own, outs, every = refs[: len(odds)], refs[len(odds)], refs[len(odds) + 1 : -1], refs[-1]
+    cells, core = early.shape[-1], place[2]
+    every[0] = early[0]
+    for at, d in enumerate(evens):
+        every[d] = early[1 + at]
     for at, d in enumerate(odds):
-        for column, block in pair_blocks(received[at][...], own_keep[...], other_keep[...], place[2]):
+        for column, block in pair_blocks(received[at][...], own_keep[...], other_keep[...], core):
             every[d, column] = block
     first = jnp.bitwise_xor(place[0], place[1])
-    for k, out in enumerate(outs):
-        out[...] = every[jnp.bitwise_xor(first, k)]
-
-
-def gather_kernel(width, place, own_early, own_late, *refs):
+    out_own[...] = every[first]
+    for k, out in enumerate(outs, 1):
+        d = jnp.bitwise_xor(first, k)
+        for column in range(2):
+            out[column * cells : (column + 1) * cells, :] = every[d, column].astype(BF16)
+        square = every[d, core]
+        lost = jnp.where(diagonal(cells), square - square.astype(BF16).astype(F32), 0.0)
+        out[2 * cells :, :] = jnp.broadcast_to(jnp.sum(lost, axis=0, keepdims=True), (16, cells)).astype(BF16)
+
+
+def gather_kernel(place, own, *refs):
     received, mine, swap, mirror = refs[:-3], refs[-3], refs[-2], refs[-1]
-    cells = own_early.shape[1]
+    cells = own.shape[1]
     core = place[2]
-    gap = jnp.bitwise_xor(place[0], place[1])
-    late = functools.reduce(jnp.bitwise_xor, [jnp.bitwise_and(jnp.right_shift(gap, b), 1) for b in range(width)]) == 1
 
     def total(column):
-        value = jnp.where(late, own_late[column], own_early[column])
+        value = own[column]
+        here = pl.ds(pl.multiple_of(column * cells, cells), cells)
         for part in received:
-            value = value + part[column]
-        return value
+            value = value + part[here, :].astype(F32)
+        lost = functools.reduce(jnp.add, [part[2 * cells : 2 * cells + 1, :].astype(F32) for part in received])
+        return value + jnp.where(diagonal(cells) & (column == core), lost, 0.0)
 
     mine[...] = total(core)
     swap[...] = total(1 - core).astype(BF16)
@@ -203,17 +213,6 @@
     )(place, *arrays)
 
 
-def to_group(x, k, late, groups, chips):
-    pairs = [
-        ((g * chips + p) * 2 + c, ((g ^ k) * chips + p) * 2 + c)
-        for g in range(groups)
-        for p in range(chips)
-        for c in range(2)
-        if odd(g ^ p ^ k) == late
-    ]
-    return lax.ppermute(x, ("elec", "cell"), pairs)
-
-
 def per_device(grads, quads, volume, weight):
     groups, devices = lax.axis_size("elec"), lax.axis_size("cell")
     chips = devices // 2
@@ -223,20 +222,20 @@
     place = jnp.stack([group, chip, core]).astype(I32)
 
     half, far = groups // 2, groups - 1
-    shards = {0: grads, far: hop(grads, "elec", groups, far)}
+    odds = [d for d in range(1, chips) if odd(d)]
+    evens = [d for d in range(1, chips) if not odd(d)]
+    shards = {far: hop(grads, "elec", groups, far)}
+    volumes_across = {d: hop(volume, "cell", devices, 2 * d) for d in evens}
+    shards[0], volumes_across = lax.optimization_barrier((grads, volumes_across))
     for j in range(1, half):
-        shards[j] = hop(grads, "elec", groups, j)
+        shards[j] = hop(shards[0], "elec", groups, j)
     for j in range(1, half):
         shards[far ^ j] = hop(shards[far], "elec", groups, j)
-
-    odds = [d for d in range(1, chips) if odd(d)]
-    evens = [d for d in range(1, chips) if not odd(d)]
-    columns, weights = quads.T, weight.reshape(1, measured)
-    volumes = volume.reshape(cells, 1)
-    volumes_across = {d: hop(volume, "cell", devices, 2 * d).reshape(cells, 1) for d in evens}
     bits = max(1, (chips - 1).bit_length())
     parity = functools.reduce(jnp.bitwise_xor, [(chip >> b) & 1 for b in range(bits)])
     keep, send = parity, 1 - parity
+    columns, weights = quads.T, weight.reshape(1, measured)
+    volumes = volume.reshape(cells, 1)
     keep_tiles, send_tiles = [2 * keep, 2 * keep + 1], [2 * send, 2 * send + 1]
     relayed = {far ^ j: shards[far ^ j] for j in range(1, half)}
     direct = {k: shards[k] for k in shards if k not in relayed}
@@ -245,10 +244,9 @@
 
     across = {}
     for d in evens:
-        near, away = hop(grads, "cell", devices, 2 * d), hop(shards[far], "cell", devices, 2 * d)
+        near, away = hop(shards[0], "cell", devices, 2 * d), hop(shards[far], "cell", devices, 2 * d)
         across[d] = {0: near, far: away}
-        both = jnp.stack([near, away])
-        both, relayed = lax.optimization_barrier((both, relayed))
+        both, relayed, turned = lax.optimization_barrier((jnp.stack([near, away]), relayed, turned))
         for j in range(1, half):
             moved = hop(both, "elec", groups, j)
             across[d][j], across[d][far ^ j] = moved[0], moved[1]
@@ -263,23 +261,28 @@
     recomputed = []
     for d in evens:
         bit = (chip >> low_bit(d)) & 1
-        recomputed.append(form([2 * send + bit, 2 * keep + bit], columns, weights, volumes_across[d], across[d]))
+        recomputed.append(form([2 * send + bit, 2 * keep + bit], columns, weights, volumes_across[d].reshape(cells, 1), across[d]))
 
     block = (2, cells, cells)
-    shape = [jax.ShapeDtypeStruct(block, F32)] * groups
-    every = [pltpu.VMEM((chips, *block), F32)]
     early = whole_call(
-        functools.partial(early_kernel, evens), "early_blocks", shape, every, 1000,
+        functools.partial(early_kernel, evens),
+        "early_blocks",
+        jax.ShapeDtypeStruct((1 + len(evens), *block), F32),
+        [],
+        1000,
         place, own_send, own_keep, other_send, other_keep, *recomputed,
     )
-    late = whole_call(
-        functools.partial(late_kernel, odds), "late_blocks", shape, every, 1000,
-        place, own_keep, other_keep, *received,
-    )
-    arrived = [to_group(early[k], k, False, groups, chips) for k in range(1, groups)]
-    arrived += [to_group(late[k], k, True, groups, chips) for k in range(1, groups)]
+    parts = whole_call(
+        functools.partial(late_kernel, evens, odds),
+        "late_blocks",
+        [jax.ShapeDtypeStruct(block, F32)] + [jax.ShapeDtypeStruct((2 * cells + 16, cells), BF16)] * (groups - 1),
+        [pltpu.VMEM((chips, *block), F32)],
+        1000,
+        place, early, own_keep, other_keep, *received,
+    )
+    arrived = [hop(parts[k], "elec", groups, k) for k in range(1, groups)]
     mine, swap, mirror = whole_call(
-        functools.partial(gather_kernel, bits),
+        gather_kernel,
         "sum_groups",
         [
             jax.ShapeDtypeStruct((cells, cells), F32),
@@ -288,7 +291,7 @@
         ],
         [],
         1000,
-        place, early[0], late[0], *arrived,
+        place, parts[0], *arrived,
     )
     pairs = [
         (g * devices + 2 * p + c, p * devices + 2 * g + c)

time: 69.5 us -> 63.1 us (0.908)
  the two profiles are of different devices: /device:TPU:14 before, /device:TPU:6 now
where the time goes in v2:
time: 63.1 us; the launch traced here: 62.9 us
  starting transfers between devices  24.9 us (39%)
  Pallas kernels  18.6 us (29%)
  waiting for transfers between devices  17.9 us (28%)
  local copies, waits for them, and re-layouts  0.91 us (1%)
    ppermute x15, starting transfers between devices, hop(): return lax.ppermute(x, axis, [(i, i ^ mask) for i in range(size)])  20.5 us
    ppermute x15, waiting for transfers between devices, hop(): return lax.ppermute(x, axis, [(i, i ^ mask) for i in range(size)])  13.9 us
    pallas_call x3, Pallas kernels, sensitivities(): pl.pallas_call(functools.partial(sensitivity_kernel, len(ready), offsets)...  13.5 us
    pallas_call x4, Pallas kernels, whole_call(): pl.pallas_call(kernel, in_specs=[pl.BlockSpec(memory_space=pltpu.SMEM)] +...  4.92 us
    ppermute x1, starting transfers between devices, per_device(): mirrored = lax.ppermute(mirror, ('elec', 'cell'), pairs)  4.47 us
    ppermute x1, waiting for transfers between devices, per_device(): mirrored = lax.ppermute(mirror, ('elec', 'cell'), pairs)  4 us
  transfers between devices with their start and end apart: 16, of which 10 were waited for; matrix products, arithmetic and copies ran while one was open for 2% of the time, Pallas kernels for 25%

profile of v2, /device:TPU:6, one launch (start us, length us, event | category | flops | bytes accessed | tf_op | source)
XLA Modules:
  0.0 62.9 jit_solution(12429852668098333190)
XLA Ops:
  0.0 4.1 %collective-permute-start.2 = (bf16[3,256,128]{2,1,0:T(8,128)(2,1)}, bf16[3,256,128]{2,1,0:T(8,128)(2,1)S(1)}, u32[]{:S(2)}, u32[]{:S(2)}) collective-permute-start(bf16[3,256,128]{2,1,0:T(8,128)(2,1)} %refs_0_), channel_id=1, source_target_pairs={{0,24},{8,16},{16,8},{24,0},{1,25},{9,17},{17,9},{25,1},{2,26},{10... | collective-permute-start | bytes 589832 | tf_op jit(solution)/shard_map/ppermute | solution.py:20
  4.2 0.8 %copy.5.volume = f32[128,1]{1,0:T(8,128)S(1)} copy(f32[128,1]{0,1:T(1,128)} %bitcast.27) | data formatting | bytes 1024 | tf_op jit(solution)/shard_map/reshape | solution.py:238
  5.0 1.1 %collective-permute-start.5 = (bf16[3,256,128]{2,1,0:T(8,128)(2,1)}, bf16[3,256,128]{2,1,0:T(8,128)(2,1)S(1)}, u32[]{:S(2)}, u32[]{:S(2)}) collective-permute-start(bf16[3,256,128]{2,1,0:T(8,128)(2,1)} %refs_0_), channel_id=1, source_target_pairs={{0,8},{8,0},{16,24},{24,16},{1,9},{9,1},{17,25},{25,17},{2,10},{10... | collective-permute-start | bytes 589832 | tf_op jit(solution)/shard_map/ppermute | solution.py:20
  6.2 1.5 %collective-permute-start.1 = (bf16[3,256,128]{2,1,0:T(8,128)(2,1)}, bf16[3,256,128]{2,1,0:T(8,128)(2,1)S(1)}, u32[]{:S(2)}, u32[]{:S(2)}) collective-permute-start(bf16[3,256,128]{2,1,0:T(8,128)(2,1)} %refs_0_), channel_id=1, source_target_pairs={{0,6},{1,7},{2,4},{3,5},{4,2},{5,3},{6,0},{7,1},{8,14},{9,15},{10,... | collective-permute-start | bytes 589832 | tf_op jit(solution)/shard_map/ppermute | solution.py:20
  7.6 2.2 %collective-permute-done.2.refs_2_ = bf16[3,256,128]{2,1,0:T(8,128)(2,1)S(1)} collective-permute-done((bf16[3,256,128]{2,1,0:T(8,128)(2,1)}, bf16[3,256,128]{2,1,0:T(8,128)(2,1)S(1)}, u32[]{:S(2)}, u32[]{:S(2)}) %collective-permute-start.2) | collective-permute-done | bytes 196640 | tf_op jit(solution)/shard_map/ppermute | solution.py:20
  9.8 3.0 %collective-permute-start.3 = (bf16[3,256,128]{2,1,0:T(8,128)(2,1)S(1)}, bf16[3,256,128]{2,1,0:T(8,128)(2,1)S(1)}, u32[]{:S(2)}, u32[]{:S(2)}) collective-permute-start(bf16[3,256,128]{2,1,0:T(8,128)(2,1)S(1)} %collective-permute-done.2.refs_2_), channel_id=1, source_target_pairs={{0,6},{1,7},{2,4},{3,5},{4,2},{5,3},{6,0},{7,1},{8,14},{9,15},{10,... | collective-permute-start | bytes 589832 | tf_op jit(solution)/shard_map/ppermute | solution.py:20
  12.8 2.5 %collective-permute-start.4 = (bf16[3,256,128]{2,1,0:T(8,128)(2,1)S(1)}, bf16[3,256,128]{2,1,0:T(8,128)(2,1)S(1)}, u32[]{:S(2)}, u32[]{:S(2)}) collective-permute-start(bf16[3,256,128]{2,1,0:T(8,128)(2,1)S(1)} %collective-permute-done.2.refs_2_), channel_id=1, source_target_pairs={{0,8},{8,0},{16,24},{24,16},{1,9},{9,1},{17,25},{25,17},{2,10},{10... | collective-permute-start | bytes 589832 | tf_op jit(solution)/shard_map/ppermute | solution.py:20
  15.4 0.1 copy.7.volume
  15.6 0.2 turn_shards.1.refs_0_
  15.8 1.4 %collective-permute-done.3.refs_3_ = bf16[3,256,128]{2,1,0:T(8,128)(2,1)S(1)} collective-permute-done((bf16[3,256,128]{2,1,0:T(8,128)(2,1)S(1)}, bf16[3,256,128]{2,1,0:T(8,128)(2,1)S(1)}, u32[]{:S(2)}, u32[]{:S(2)}) %collective-permute-start.3) | collective-permute-done | bytes 196640 | tf_op jit(solution)/shard_map/ppermute | solution.py:20
  17.2 2.1 %collective-permute-done.4.refs_1_ = bf16[3,256,128]{2,1,0:T(8,128)(2,1)S(1)} collective-permute-done((bf16[3,256,128]{2,1,0:T(8,128)(2,1)S(1)}, bf16[3,256,128]{2,1,0:T(8,128)(2,1)S(1)}, u32[]{:S(2)}, u32[]{:S(2)}) %collective-permute-start.4) | collective-permute-done | bytes 196640 | tf_op jit(solution)/shard_map/ppermute | solution.py:20
  19.3 1.8 %collective-permute-start.8 = (bf16[2,3,256,128]{3,2,1,0:T(8,128)(2,1)S(1)}, bf16[2,3,256,128]{3,2,1,0:T(8,128)(2,1)S(1)}, u32[]{:S(2)}, u32[]{:S(2)}) collective-permute-start(bf16[2,3,256,128]{3,2,1,0:T(8,128)(2,1)S(1)} %pad_maximum_fusion), channel_id=1, source_target_pairs={{0,8},{8,0},{16,24},{24,16},{1,9},{9,1},{17,25},{25,17},{2,10},{10... | collective-permute-start | bytes 1179656 | tf_op jit(solution)/shard_map/ppermute | solution.py:20
  21.0 4.5 %sensitivities.3.own_send = bf16[128,2048]{1,0:T(8,128)(2,1)S(1)} custom-call(s32[3]{0:T(128)S(1)} %pad_add_fusion.1.place, s32[4,4096]{1,0:T(4,128)S(1)} %bitcast.21, f32[1,4096]{1,0:T(1,128)S(1)} %bitcast.24, f32[128,1]{1,0:T(8,128)S(1)} %copy.5.volume, bf16[3,384,256]{2,1,0:T(8,128)(2,1)S(1)} %turn_shards.1.refs_0_, ...), custom_call_target="tpu_custom_call" | custom-call | flops 3221225472 | bytes 1 | tf_op jit(solution)/shard_map/sensitivities/pallas_call | solution.py:108
  25.6 0.6 collective-permute-start.10
  26.2 1.2 %collective-permute-start.9 = (bf16[128,2048]{1,0:T(8,128)(2,1)S(1)}, bf16[128,2048]{1,0:T(8,128)(2,1)S(1)}, u32[]{:S(2)}, u32[]{:S(2)}) collective-permute-start(bf16[128,2048]{1,0:T(8,128)(2,1)S(1)} %sensitivities.3.own_send), channel_id=1, source_target_pairs={{0,2},{1,3},{2,0},{3,1},{4,6},{5,7},{6,4},{7,5},{8,10},{9,11},{10,... | collective-permute-start | bytes 1572872 | tf_op jit(solution)/shard_map/ppermute | solution.py:20
  27.4 4.5 %sensitivities.4.own_keep = bf16[128,2048]{1,0:T(8,128)(2,1)S(1)} custom-call(s32[3]{0:T(128)S(1)} %pad_add_fusion.2.place, s32[4,4096]{1,0:T(4,128)S(1)} %bitcast.22, f32[1,4096]{1,0:T(1,128)S(1)} %bitcast.25, f32[128,1]{1,0:T(8,128)S(1)} %copy.5.volume, bf16[3,384,256]{2,1,0:T(8,128)(2,1)S(1)} %turn_shards.1.refs_0_, ...), custom_call_target="tpu_custom_call" | custom-call | flops 3221225472 | bytes 1 | tf_op jit(solution)/shard_map/sensitivities/pallas_call | solution.py:108
  32.0 4.6 %sensitivities.5.refs_0_ = bf16[128,2048]{1,0:T(8,128)(2,1)S(1)} custom-call(s32[3]{0:T(128)S(1)} %pad_add_fusion.3.place, s32[4,4096]{1,0:T(4,128)S(1)} %bitcast.23, f32[1,4096]{1,0:T(1,128)S(1)} %bitcast.26, f32[128,1]{1,0:T(8,128)S(1)} %copy.7.volume, bf16[3,256,128]{2,1,0:T(8,128)(2,1)S(1)} %collective-permute-done.1.refs_0_, ...), custom_call_target="tpu_custom_call" | custom-call | flops 3221225472 | bytes 1 | tf_op jit(solution)/shard_map/sensitivities/pallas_call | solution.py:108
  36.6 1.7 %early_blocks.1.early = f32[2,2,128,128]{3,2,1,0:T(8,128)S(1)} custom-call(s32[3]{0:T(128)S(1)} %pad_add_fusion.place, bf16[128,2048]{1,0:T(8,128)(2,1)S(1)} %sensitivities.3.own_send, bf16[128,2048]{1,0:T(8,128)(2,1)S(1)} %sensitivities.4.own_keep, bf16[128,2048]{1,0:T(8,128)(2,1)S(1)} %collective-permute-done.6.other_send, ...), custom_call_target="tpu_custom_call" | custom-call | flops 1 | bytes 1 | tf_op jit(solution)/shard_map/early_blocks/pallas_call | solution.py:204
  38.3 1.6 %collective-permute-done.10.refs_1_ = bf16[128,2048]{1,0:T(8,128)(2,1)S(1)} collective-permute-done((bf16[128,2048]{1,0:T(8,128)(2,1)S(1)}, bf16[128,2048]{1,0:T(8,128)(2,1)S(1)}, u32[]{:S(2)}, u32[]{:S(2)}) %collective-permute-start.10) | collective-permute-done | bytes 524320 | tf_op jit(solution)/shard_map/ppermute | solution.py:20
  39.9 0.2 collective-permute-done.9.refs_0_
  40.2 1.3 %late_blocks.1 = (f32[2,128,128]{2,1,0:T(8,128)S(1)}, bf16[272,128]{1,0:T(8,128)(2,1)S(1)}, bf16[272,128]{1,0:T(8,128)(2,1)S(1)}, bf16[272,128]{1,0:T(8,128)(2,1)S(1)}) custom-call(s32[3]{0:T(128)S(1)} %pad_add_fusion.place, f32[2,2,128,128]{3,2,1,0:T(8,128)S(1)} %early_blocks.1.early, bf16[128,2048]{1,0:T(8,128)(2,1)S(1)} %sensitivities.4.own_keep, ...), custom_call_target="tpu_custom_call" | custom-call | flops 1 | bytes 1 | tf_op jit(solution)/shard_map/late_blocks/pallas_call | solution.py:204
  41.5 0.5 collective-permute-start.11
  42.0 3.1 %collective-permute-start.12 = (bf16[272,128]{1,0:T(8,128)(2,1)S(1)}, bf16[272,128]{1,0:T(8,128)(2,1)S(1)}, u32[]{:S(2)}, u32[]{:S(2)}) collective-permute-start(bf16[272,128]{1,0:T(8,128)(2,1)S(1)} %get-tuple-element.28), channel_id=1, source_target_pairs={{0,16},{8,24},{16,0},{24,8},{1,17},{9,25},{17,1},{25,9},{2,18},{10... | collective-permute-start | bytes 208904 | tf_op jit(solution)/shard_map/ppermute | solution.py:20
  45.1 0.8 %collective-permute-start.13 = (bf16[272,128]{1,0:T(8,128)(2,1)S(1)}, bf16[272,128]{1,0:T(8,128)(2,1)S(1)}, u32[]{:S(2)}, u32[]{:S(2)}) collective-permute-start(bf16[272,128]{1,0:T(8,128)(2,1)S(1)} %get-tuple-element.29), channel_id=1, source_target_pairs={{0,24},{8,16},{16,8},{24,0},{1,25},{9,17},{17,9},{25,1},{2,26},{10... | collective-permute-start | bytes 208904 | tf_op jit(solution)/shard_map/ppermute | solution.py:20
  45.9 0.6 collective-permute-done.11.refs_0_
  46.6 3.1 %collective-permute-done.12.refs_1_ = bf16[272,128]{1,0:T(8,128)(2,1)S(1)} collective-permute-done((bf16[272,128]{1,0:T(8,128)(2,1)S(1)}, bf16[272,128]{1,0:T(8,128)(2,1)S(1)}, u32[]{:S(2)}, u32[]{:S(2)}) %collective-permute-start.12) | collective-permute-done | bytes 69664 | tf_op jit(solution)/shard_map/ppermute | solution.py:20
  49.7 1.6 %collective-permute-done.13.refs_2_ = bf16[272,128]{1,0:T(8,128)(2,1)S(1)} collective-permute-done((bf16[272,128]{1,0:T(8,128)(2,1)S(1)}, bf16[272,128]{1,0:T(8,128)(2,1)S(1)}, u32[]{:S(2)}, u32[]{:S(2)}) %collective-permute-start.13) | collective-permute-done | bytes 69664 | tf_op jit(solution)/shard_map/ppermute | solution.py:20
  51.3 0.7 %sum_groups.1 = (f32[128,128]{1,0:T(8,128)S(1)}, bf16[128,128]{1,0:T(8,128)(2,1)S(1)}, bf16[256,128]{1,0:T(8,128)(2,1)S(1)}) custom-call(s32[3]{0:T(128)S(1)} %pad_add_fusion.place, f32[2,128,128]{2,1,0:T(8,128)S(1)} %get-tuple-element.26.own, bf16[272,128]{1,0:T(8,128)(2,1)S(1)} %collective-permute-done.11.refs_0_, ...), custom_call_target="tpu_custom_call" | custom-call | flops 1 | bytes 1 | tf_op jit(solution)/shard_map/sum_groups/pallas_call | solution.py:204
  51.9 4.5 %collective-permute-start.15 = (bf16[256,128]{1,0:T(8,128)(2,1)S(1)}, bf16[256,128]{1,0:T(8,128)(2,1)S(1)}, u32[]{:S(2)}, u32[]{:S(2)}) collective-permute-start(bf16[256,128]{1,0:T(8,128)(2,1)S(1)} %get-tuple-element.32), channel_id=1, source_target_pairs={{2,8},{3,9},{4,16},{5,17},{6,24},{7,25},{8,2},{9,3},{12,18},{13,19... | collective-permute-start | bytes 196616 | tf_op jit(solution)/shard_map/ppermute | solution.py:303
  56.5 1.2 %collective-permute-done.14.swap = bf16[128,128]{1,0:T(8,128)(2,1)S(1)} collective-permute-done((bf16[128,128]{1,0:T(8,128)(2,1)S(1)}, bf16[128,128]{1,0:T(8,128)(2,1)S(1)}, u32[]{:S(2)}, u32[]{:S(2)}) %collective-permute-start.14) | collective-permute-done | bytes 32800 | tf_op jit(solution)/shard_map/ppermute | solution.py:20
  57.7 4.0 %collective-permute-done.15.mirror = bf16[256,128]{1,0:T(8,128)(2,1)S(1)} collective-permute-done((bf16[256,128]{1,0:T(8,128)(2,1)S(1)}, bf16[256,128]{1,0:T(8,128)(2,1)S(1)}, u32[]{:S(2)}, u32[]{:S(2)}) %collective-permute-start.15) | collective-permute-done | bytes 65568 | tf_op jit(solution)/shard_map/ppermute | solution.py:303
  61.7 1.2 %finish.1 = f32[256,128]{1,0:T(8,128)} custom-call(s32[3]{0:T(128)S(1)} %pad_add_fusion.place, f32[128,128]{1,0:T(8,128)S(1)} %get-tuple-element.30.mine, bf16[128,128]{1,0:T(8,128)(2,1)S(1)} %collective-permute-done.14.swap, bf16[256,128]{1,0:T(8,128)(2,1)S(1)} %collective-permute-done.15.mirror), custom_call_target="tpu_custom_call" | custom-call | flops 1 | bytes 1 | tf_op jit(solution)/shard_map/finish/pallas_call | solution.py:204
  (22 shorter events, 0.6 us)
Async XLA Ops:
  0.0 15.6 %copy-start = (bf16[3,256,128]{2,1,0:T(8,128)(2,1)S(1)}, bf16[3,256,128]{2,1,0:T(8,128)(2,1)}, u32[]{:S(2)}) copy-start(bf16[3,256,128]{2,1,0:T(8,128)(2,1)} %refs_0_) | copy-start | bytes 589828
  0.0 5.0 %collective-permute-start = (f32[128]{0:T(128)}, f32[128]{0:T(128)S(1)}, u32[]{:S(2)}, u32[]{:S(2)}) collective-permute-start(f32[128]{0:T(128)} %param.6), channel_id=1, source_target_pairs={{0,6},{1,7},{2,4},{3,5},{4,2},{5,3},{6,0},{7,1},{8,14},{9,15},{10,... | collective-permute-start | bytes 1544 | tf_op jit(solution)/shard_map/ppermute | solution.py:20
  0.0 9.8 %collective-permute-start.2 = (bf16[3,256,128]{2,1,0:T(8,128)(2,1)}, bf16[3,256,128]{2,1,0:T(8,128)(2,1)S(1)}, u32[]{:S(2)}, u32[]{:S(2)}) collective-permute-start(bf16[3,256,128]{2,1,0:T(8,128)(2,1)} %refs_0_), channel_id=1, source_target_pairs={{0,24},{8,16},{16,8},{24,0},{1,25},{9,17},{17,9},{25,1},{2,26},{10... | collective-permute-start | bytes 589832 | tf_op jit(solution)/shard_map/ppermute | solution.py:20
  5.0 10.5 %collective-permute-start.5 = (bf16[3,256,128]{2,1,0:T(8,128)(2,1)}, bf16[3,256,128]{2,1,0:T(8,128)(2,1)S(1)}, u32[]{:S(2)}, u32[]{:S(2)}) collective-permute-start(bf16[3,256,128]{2,1,0:T(8,128)(2,1)} %refs_0_), channel_id=1, source_target_pairs={{0,8},{8,0},{16,24},{24,16},{1,9},{9,1},{17,25},{25,17},{2,10},{10... | collective-permute-start | bytes 589832 | tf_op jit(solution)/shard_map/ppermute | solution.py:20
  6.2 9.6 %collective-permute-start.1 = (bf16[3,256,128]{2,1,0:T(8,128)(2,1)}, bf16[3,256,128]{2,1,0:T(8,128)(2,1)S(1)}, u32[]{:S(2)}, u32[]{:S(2)}) collective-permute-start(bf16[3,256,128]{2,1,0:T(8,128)(2,1)} %refs_0_), channel_id=1, source_target_pairs={{0,6},{1,7},{2,4},{3,5},{4,2},{5,3},{6,0},{7,1},{8,14},{9,15},{10,... | collective-permute-start | bytes 589832 | tf_op jit(solution)/shard_map/ppermute | solution.py:20
  9.8 7.4 %collective-permute-start.3 = (bf16[3,256,128]{2,1,0:T(8,128)(2,1)S(1)}, bf16[3,256,128]{2,1,0:T(8,128)(2,1)S(1)}, u32[]{:S(2)}, u32[]{:S(2)}) collective-permute-start(bf16[3,256,128]{2,1,0:T(8,128)(2,1)S(1)} %collective-permute-done.2.refs_2_), channel_id=1, source_target_pairs={{0,6},{1,7},{2,4},{3,5},{4,2},{5,3},{6,0},{7,1},{8,14},{9,15},{10,... | collective-permute-start | bytes 589832 | tf_op jit(solution)/shard_map/ppermute | solution.py:20
  12.8 6.4 %collective-permute-start.4 = (bf16[3,256,128]{2,1,0:T(8,128)(2,1)S(1)}, bf16[3,256,128]{2,1,0:T(8,128)(2,1)S(1)}, u32[]{:S(2)}, u32[]{:S(2)}) collective-permute-start(bf16[3,256,128]{2,1,0:T(8,128)(2,1)S(1)} %collective-permute-done.2.refs_2_), channel_id=1, source_target_pairs={{0,8},{8,0},{16,24},{24,16},{1,9},{9,1},{17,25},{25,17},{2,10},{10... | collective-permute-start | bytes 589832 | tf_op jit(solution)/shard_map/ppermute | solution.py:20
  17.1 3.9 %copy-start.1 = (s32[4096,4]{0,1:T(4,128)S(1)}, s32[4096,4]{0,1:T(4,128)}, u32[]{:S(2)}) copy-start(s32[4096,4]{0,1:T(4,128)} %param.5) | copy-start | bytes 196612
  17.1 3.9 %copy-start.2 = (f32[4096]{0:T(1024)S(1)}, f32[4096]{0:T(1024)}, u32[]{:S(2)}) copy-start(f32[4096]{0:T(1024)} %param.7) | copy-start | bytes 49156
  19.3 12.7 %collective-permute-start.8 = (bf16[2,3,256,128]{3,2,1,0:T(8,128)(2,1)S(1)}, bf16[2,3,256,128]{3,2,1,0:T(8,128)(2,1)S(1)}, u32[]{:S(2)}, u32[]{:S(2)}) collective-permute-start(bf16[2,3,256,128]{3,2,1,0:T(8,128)(2,1)S(1)} %pad_maximum_fusion), channel_id=1, source_target_pairs={{0,8},{8,0},{16,24},{24,16},{1,9},{9,1},{17,25},{25,17},{2,10},{10... | collective-permute-start | bytes 1179656 | tf_op jit(solution)/shard_map/ppermute | solution.py:20
  25.5 11.1 %collective-permute-start.6 = (bf16[128,2048]{1,0:T(8,128)(2,1)S(1)}, bf16[128,2048]{1,0:T(8,128)(2,1)S(1)}, u32[]{:S(2)}, u32[]{:S(2)}) collective-permute-start(bf16[128,2048]{1,0:T(8,128)(2,1)S(1)} %sensitivities.3.own_send), channel_id=1, source_target_pairs={{0,1},{1,0},{2,3},{3,2},{4,5},{5,4},{6,7},{7,6},{8,9},{9,8},{10,11... | collective-permute-start | bytes 1572872 | tf_op jit(solution)/shard_map/ppermute | solution.py:20
  25.6 14.3 %collective-permute-start.10 = (bf16[128,2048]{1,0:T(8,128)(2,1)S(1)}, bf16[128,2048]{1,0:T(8,128)(2,1)S(1)}, u32[]{:S(2)}, u32[]{:S(2)}) collective-permute-start(bf16[128,2048]{1,0:T(8,128)(2,1)S(1)} %sensitivities.3.own_send), channel_id=1, source_target_pairs={{0,4},{1,5},{2,6},{3,7},{4,0},{5,1},{6,2},{7,3},{8,12},{9,13},{10,... | collective-permute-start | bytes 1572872 | tf_op jit(solution)/shard_map/ppermute | solution.py:20
  26.2 14.0 %collective-permute-start.9 = (bf16[128,2048]{1,0:T(8,128)(2,1)S(1)}, bf16[128,2048]{1,0:T(8,128)(2,1)S(1)}, u32[]{:S(2)}, u32[]{:S(2)}) collective-permute-start(bf16[128,2048]{1,0:T(8,128)(2,1)S(1)} %sensitivities.3.own_send), channel_id=1, source_target_pairs={{0,2},{1,3},{2,0},{3,1},{4,6},{5,7},{6,4},{7,5},{8,10},{9,11},{10,... | collective-permute-start | bytes 1572872 | tf_op jit(solution)/shard_map/ppermute | solution.py:20
  31.9 4.7 %collective-permute-start.7 = (bf16[128,2048]{1,0:T(8,128)(2,1)S(1)}, bf16[128,2048]{1,0:T(8,128)(2,1)S(1)}, u32[]{:S(2)}, u32[]{:S(2)}) collective-permute-start(bf16[128,2048]{1,0:T(8,128)(2,1)S(1)} %sensitivities.4.own_keep), channel_id=1, source_target_pairs={{0,1},{1,0},{2,3},{3,2},{4,5},{5,4},{6,7},{7,6},{8,9},{9,8},{10,11... | collective-permute-start | bytes 1572872 | tf_op jit(solution)/shard_map/ppermute | solution.py:20
  41.5 5.1 %collective-permute-start.11 = (bf16[272,128]{1,0:T(8,128)(2,1)S(1)}, bf16[272,128]{1,0:T(8,128)(2,1)S(1)}, u32[]{:S(2)}, u32[]{:S(2)}) collective-permute-start(bf16[272,128]{1,0:T(8,128)(2,1)S(1)} %get-tuple-element.27), channel_id=1, source_target_pairs={{0,8},{8,0},{16,24},{24,16},{1,9},{9,1},{17,25},{25,17},{2,10},{10... | collective-permute-start | bytes 208904 | tf_op jit(solution)/shard_map/ppermute | solution.py:20
  42.0 7.6 %collective-permute-start.12 = (bf16[272,128]{1,0:T(8,128)(2,1)S(1)}, bf16[272,128]{1,0:T(8,128)(2,1)S(1)}, u32[]{:S(2)}, u32[]{:S(2)}) collective-permute-start(bf16[272,128]{1,0:T(8,128)(2,1)S(1)} %get-tuple-element.28), channel_id=1, source_target_pairs={{0,16},{8,24},{16,0},{24,8},{1,17},{9,25},{17,1},{25,9},{2,18},{10... | collective-permute-start | bytes 208904 | tf_op jit(solution)/shard_map/ppermute | solution.py:20
  45.1 6.1 %collective-permute-start.13 = (bf16[272,128]{1,0:T(8,128)(2,1)S(1)}, bf16[272,128]{1,0:T(8,128)(2,1)S(1)}, u32[]{:S(2)}, u32[]{:S(2)}) collective-permute-start(bf16[272,128]{1,0:T(8,128)(2,1)S(1)} %get-tuple-element.29), channel_id=1, source_target_pairs={{0,24},{8,16},{16,8},{24,0},{1,25},{9,17},{17,9},{25,1},{2,26},{10... | collective-permute-start | bytes 208904 | tf_op jit(solution)/shard_map/ppermute | solution.py:20
  51.9 9.8 %collective-permute-start.15 = (bf16[256,128]{1,0:T(8,128)(2,1)S(1)}, bf16[256,128]{1,0:T(8,128)(2,1)S(1)}, u32[]{:S(2)}, u32[]{:S(2)}) collective-permute-start(bf16[256,128]{1,0:T(8,128)(2,1)S(1)} %get-tuple-element.32), channel_id=1, source_target_pairs={{2,8},{3,9},{4,16},{5,17},{6,24},{7,25},{8,2},{9,3},{12,18},{13,19... | collective-permute-start | bytes 196616 | tf_op jit(solution)/shard_map/ppermute | solution.py:303
  56.4 1.3 %collective-permute-start.14 = (bf16[128,128]{1,0:T(8,128)(2,1)S(1)}, bf16[128,128]{1,0:T(8,128)(2,1)S(1)}, u32[]{:S(2)}, u32[]{:S(2)}) collective-permute-start(bf16[128,128]{1,0:T(8,128)(2,1)S(1)} %get-tuple-element.31), channel_id=1, source_target_pairs={{0,1},{1,0},{2,3},{3,2},{4,5},{5,4},{6,7},{7,6},{8,9},{9,8},{10,11... | collective-permute-start | bytes 98312 | tf_op jit(solution)/shard_map/ppermute | solution.py:20

commit v3 on v2

v3 whole, which is shorter than its diff:
```python
import functools

import jax
import jax.numpy as jnp
from jax import lax
from jax.experimental import pallas as pl
from jax.experimental.pallas import tpu as pltpu
from jax.sharding import PartitionSpec as P

F32, BF16, I32 = jnp.float32, jnp.bfloat16, jnp.int32
TILES = 4
LIMIT = 24 * 1024 * 1024


def params():
    return pltpu.CompilerParams(vmem_limit_bytes=LIMIT)


def hop(x, axis, size, mask):
    return lax.ppermute(x, axis, [(i, i ^ mask) for i in range(size)])


def odd(d):
    return bin(d).count("1") % 2 == 1


def low_bit(d):
    return (d & -d).bit_length() - 1


def same_columns(left, right):
    return lax.dot_general(left, right, (((1,), (1,)), ((), ())), preferred_element_type=F32)


def difference_map(rows, at, base, depth):
    labels = lax.broadcasted_iota(jnp.int16, (depth, rows.shape[1]), 0)
    local = (rows - base).astype(jnp.int16)
    plus, minus = local[at : at + 1, :] == labels, local[at + 1 : at + 2, :] == labels
    one = jnp.ones((), BF16)
    return jnp.where(plus, one, jnp.where(minus, -one, jnp.zeros((), BF16)))


def turn(shards, turned, start=0):
    cells = shards[0].shape[2]
    for at, shard in enumerate(shards, start):
        for k in range(3):
            turned[at, k * cells : (k + 1) * cells, :] = shard[k].T


def turn_kernel(*refs):
    turn(refs[:-1], refs[-1])


def turn_shards(shards):
    _, depth, cells = shards[0].shape
    return pl.pallas_call(
        turn_kernel,
        out_shape=jax.ShapeDtypeStruct((len(shards), 3 * cells, depth), BF16),
        compiler_params=params(),
        cost_estimate=pl.CostEstimate(flops=1000, bytes_accessed=1000, transcendentals=0),
        name="turn_shards",
    )(*shards)


def pack_kernel(shard, volume, out):
    parts, depth, cells = shard.shape
    for k in range(parts):
        out[k * depth : (k + 1) * depth, :] = shard[k]
    rest = volume[...]
    rows = []
    for _ in range(3):
        rows.append(rest.astype(BF16).astype(F32))
        rest = rest - rows[-1]
    tail = jnp.concatenate(rows + [jnp.zeros((13, cells), F32)], axis=0)
    out[parts * depth :, :] = tail.astype(BF16)


def pack(shard, volume):
    parts, depth, cells = shard.shape
    return pl.pallas_call(
        pack_kernel,
        out_shape=jax.ShapeDtypeStruct((parts * depth + 16, cells), BF16),
        compiler_params=params(),
        cost_estimate=pl.CostEstimate(flops=1000, bytes_accessed=1000, transcendentals=0),
        name="pack",
    )(shard, volume.reshape(1, cells))


def sensitivity_kernel(ready, offsets, place, quads, weight, volume, *refs):
    shards, out, turned = refs[1 if ready else 0 : -2], refs[-2], refs[-1]
    cells, depth = out.shape[0], turned.shape[2]

    @pl.when(pl.program_id(0) == 0)
    def _():
        turn(shards, turned)

    rows = quads[...]
    source = receiver = None
    for at, offset in enumerate(offsets):
        base = jnp.bitwise_xor(place[0], offset) * depth
        left = refs[0][at] if at < ready else turned[at - ready]
        s = jnp.dot(left, difference_map(rows, 0, base, depth), preferred_element_type=F32)
        r = jnp.dot(left, difference_map(rows, 2, base, depth), preferred_element_type=F32)
        source = s if at == 0 else source + s
        receiver = r if at == 0 else receiver + r
    product = source * receiver
    dots = product[:cells] + product[cells : 2 * cells] + product[2 * cells :]
    terms = volume[...].astype(F32)
    column = jnp.sum(jnp.broadcast_to(terms[:, None, :], (terms.shape[0], 8, cells)), axis=0).T[:, :1]
    out[...] = (weight[...] * -(column * dots)).astype(BF16)


def sensitivities(place, tiles, quads, weight, volume, shards, turned=None, ready=()):
    offsets = tuple(ready) + tuple(sorted(shards))
    held = [shards[k] for k in offsets[len(ready) :]]
    _, depth, cells = held[0].shape
    width = quads.shape[1] // TILES
    count = len(tiles)
    scalars = jnp.stack([place[0], *tiles]).astype(I32)
    spec = pltpu.PrefetchScalarGridSpec(
        num_scalar_prefetch=1,
        grid=(count,),
        in_specs=[
            pl.BlockSpec((4, width), lambda i, s: (0, s[1 + i])),
            pl.BlockSpec((1, width), lambda i, s: (0, s[1 + i])),
            pl.BlockSpec(volume.shape, lambda i, s: (0, 0)),
        ]
        + [pl.BlockSpec((len(ready), 3 * cells, depth), lambda i, s: (0, 0, 0))] * (1 if ready else 0)
        + [pl.BlockSpec((3, depth, cells), lambda i, s: (0, 0, 0))] * len(held),
        out_specs=pl.BlockSpec((cells, width), lambda i, s: (0, i)),
        scratch_shapes=[pltpu.VMEM((len(held), 3 * cells, depth), BF16)],
    )
    flops = 4 * count * width * len(offsets) * depth * 3 * cells
    return pl.pallas_call(
        functools.partial(sensitivity_kernel, len(ready), offsets),
        grid_spec=spec,
        out_shape=jax.ShapeDtypeStruct((cells, count * width), BF16),
        compiler_params=params(),
        cost_estimate=pl.CostEstimate(flops=flops, bytes_accessed=1, transcendentals=0),
        name="sensitivities",
    )(scalars, quads, weight, volume, *([turned] if ready else []), *held)


def rows_of(core, cells):
    return pl.ds(pl.multiple_of(core * cells, cells), cells)


def early_kernel(evens, place, own_send, own_keep, other_send, other_keep, *refs):
    count, core = len(evens), place[2]
    recomputed, own_block, mine, swap = refs[:count], *refs[count : count + 3]
    mirrors, pair = refs[count + 3 : -1], refs[-1]
    cells = own_send.shape[0]
    here, there = rows_of(core, cells), rows_of(1 - core, cells)
    sides = ((0, own_send, other_send), (1, own_keep, other_keep))
    own_block[here, :] = functools.reduce(jnp.add, [same_columns(own[...], own[...]) for _, own, _ in sides])
    own_block[there, :] = functools.reduce(jnp.add, [same_columns(other[...], own[...]) for _, own, other in sides])
    for at, d in enumerate(evens):
        part = own_send.shape[1] // 2
        for bit in range(2):

            @pl.when(jnp.bitwise_and(jnp.right_shift(place[1], low_bit(d)), 1) == bit)
            def _():
                lanes = slice(bit * part, (bit + 1) * part)
                for side, own, other in sides:
                    rows = recomputed[at][:, side * part : (side + 1) * part]
                    for which, columns in enumerate((own, other)):
                        block = same_columns(rows, columns[:, lanes])
                        pair[which] = block if side == 0 else pair[which] + block

        mine[at] = pair[0]
        swap[at] = pair[1].astype(BF16)
        mirrors[at][here, :] = pair[0].T.astype(BF16)
        mirrors[at][there, :] = pair[1].T.astype(BF16)


def late_kernel(odds, place, own_keep, other_keep, *refs):
    count, core = len(odds), place[2]
    received, mine, swap, mirrors = refs[:count], refs[count], refs[count + 1], refs[count + 2 :]
    cells = own_keep.shape[0]
    here, there = rows_of(core, cells), rows_of(1 - core, cells)
    for at in range(count):
        rows = received[at][...]
        block, across = same_columns(rows, own_keep[...]), same_columns(rows, other_keep[...])
        mine[at] = block
        swap[at] = across.astype(BF16)
        mirrors[at][here, :] = block.T.astype(BF16)
        mirrors[at][there, :] = across.T.astype(BF16)


def diagonal(cells):
    return lax.broadcasted_iota(I32, (cells, cells), 0) == lax.broadcasted_iota(I32, (cells, cells), 1)


def combine_kernel(evens, odds, place, own_block, *refs):
    core, every = place[2], refs[-1]
    cells = own_block.shape[1]
    here, there = rows_of(core, cells), rows_of(1 - core, cells)
    every[0] = own_block[...]
    at = 0
    for group in (evens, odds):
        mine, swapped, mirrored = refs[at], refs[at + 1], refs[at + 2 : at + 2 + len(group)]
        at += 2 + len(group)
        for i, d in enumerate(group):
            every[d, here, :] = mine[i] + mirrored[i][here, :].astype(F32)
            every[d, there, :] = swapped[i].astype(F32) + mirrored[i][there, :].astype(F32)
    out_own, outs = refs[at], refs[at + 1 : -1]
    first = jnp.bitwise_xor(place[0], place[1])
    out_own[...] = every[first]
    for k, out in enumerate(outs, 1):
        d = jnp.bitwise_xor(first, k)
        out[: 2 * cells, :] = every[d].astype(BF16)
        square = every[d, here, :]
        lost = jnp.where(diagonal(cells), square - square.astype(BF16).astype(F32), 0.0)
        out[2 * cells :, :] = jnp.broadcast_to(jnp.sum(lost, axis=0, keepdims=True), (16, cells)).astype(BF16)


def final_kernel(amount, place, own, *refs):
    received, out = refs[:-1], refs[-1]
    cells = own.shape[1]
    total = own[...]
    for part in received:
        total = total + part[: 2 * cells, :].astype(F32)
    out[...] = total / amount
    lost = functools.reduce(jnp.add, [part[2 * cells : 2 * cells + 1, :].astype(F32) for part in received])
    here = rows_of(place[2], cells)
    out[here, :] += jnp.where(diagonal(cells), lost / amount, 0.0)


def whole_call(kernel, name, shapes, scratch, place, *arrays):
    vmem = pl.BlockSpec(memory_space=pltpu.VMEM)
    many = isinstance(shapes, list)
    return pl.pallas_call(
        kernel,
        in_specs=[pl.BlockSpec(memory_space=pltpu.SMEM)] + [vmem] * len(arrays),
        out_specs=[vmem] * len(shapes) if many else vmem,
        out_shape=shapes,
        scratch_shapes=scratch,
        compiler_params=params(),
        cost_estimate=pl.CostEstimate(flops=1, bytes_accessed=1, transcendentals=0),
        name=name,
    )(place, *arrays)


def per_device(grads, quads, volume, weight):
    groups, devices = lax.axis_size("elec"), lax.axis_size("cell")
    chips = devices // 2
    cells, measured = grads.shape[2], quads.shape[0]
    here = lax.axis_index("cell")
    group, chip, core = lax.axis_index("elec"), here // 2, here % 2
    place = jnp.stack([group, chip, core]).astype(I32)

    half, far = groups // 2, groups - 1
    odds = [d for d in range(1, chips) if odd(d)]
    evens = [d for d in range(1, chips) if not odd(d)]
    packed = pack(grads, volume)
    shape = grads.shape
    gradients = lambda x: x[: 3 * shape[1], :].reshape(shape)
    shards = {0: grads, far: hop(grads, "elec", groups, far)}
    for j in range(1, half):
        shards[j] = gradients(hop(packed, "elec", groups, j))
    for j in range(1, half):
        shards[far ^ j] = hop(shards[far], "elec", groups, j)

    bits = max(1, (chips - 1).bit_length())
    parity = functools.reduce(jnp.bitwise_xor, [(chip >> b) & 1 for b in range(bits)])
    keep, send = parity, 1 - parity
    columns, weights = quads.T, weight.reshape(1, measured)
    volumes = volume.reshape(1, cells)
    keep_tiles, send_tiles = [2 * keep, 2 * keep + 1], [2 * send, 2 * send + 1]
    relayed = {far ^ j: shards[far ^ j] for j in range(1, half)}
    direct = {k: shards[k] for k in shards if k not in relayed}
    ready = tuple(sorted(direct))
    turned = turn_shards([direct[k] for k in ready])

    across, volumes_across = {}, {}
    for d in evens:
        near, away = hop(packed, "cell", devices, 2 * d), hop(shards[far], "cell", devices, 2 * d)
        near, volumes_across[d] = gradients(near), near[3 * shape[1] :, :]
        across[d] = {0: near, far: away}
        both, relayed, turned = lax.optimization_barrier((jnp.stack([near, away]), relayed, turned))
        for j in range(1, half):
            moved = hop(both, "elec", groups, j)
            across[d][j], across[d][far ^ j] = moved[0], moved[1]

    form = functools.partial(sensitivities, place)
    own_send = form(send_tiles, columns, weights, volumes, relayed, turned, ready)
    received = [hop(own_send, "cell", devices, 2 * d) for d in odds]
    other_send = hop(own_send, "cell", devices, 1)
    columns, own_send = lax.optimization_barrier((columns, own_send))
    own_keep = form(keep_tiles, columns, weights, volumes, relayed, turned, ready)
    other_keep = hop(own_keep, "cell", devices, 1)
    recomputed = []
    for d in evens:
        bit = (chip >> low_bit(d)) & 1
        recomputed.append(form([2 * send + bit, 2 * keep + bit], columns, weights, volumes_across[d], across[d]))

    whole, small = (2 * cells, cells), (cells, cells)
    outputs = lambda group: [
        jax.ShapeDtypeStruct((len(group), *small), F32),
        jax.ShapeDtypeStruct((len(group), *small), BF16),
    ] + [jax.ShapeDtypeStruct(whole, BF16)] * len(group)
    own_block, *early = whole_call(
        functools.partial(early_kernel, evens),
        "early_blocks",
        [jax.ShapeDtypeStruct(whole, F32)] + outputs(evens),
        [pltpu.VMEM((2, *small), F32)],
        place, own_send, own_keep, other_send, other_keep, *recomputed,
    )
    late = whole_call(functools.partial(late_kernel, odds), "late_blocks", outputs(odds), [], place, own_keep, other_keep, *received)

    def exchange(group, mine, swap, *mirrors):
        moved = [hop(m, "cell", devices, 2 * d) for d, m in zip(group, mirrors)]
        return [mine, hop(swap, "cell", devices, 1)] + moved

    parts = whole_call(
        functools.partial(combine_kernel, evens, odds),
        "combine",
        [jax.ShapeDtypeStruct(whole, F32)] + [jax.ShapeDtypeStruct((2 * cells + 16, cells), BF16)] * (groups - 1),
        [pltpu.VMEM((chips, *whole), F32)],
        place, own_block, *exchange(evens, *early), *exchange(odds, *late),
    )
    arrived = [hop(parts[k], "elec", groups, k) for k in range(1, groups)]
    return whole_call(
        functools.partial(final_kernel, float(measured * groups)),
        "finish",
        jax.ShapeDtypeStruct(whole, F32),
        [],
        place, parts[0], *arrived,
    )


def solution(mesh):
    placed = (P(None, "elec", "cell"), P("elec", None), P("cell"), P("elec"))
    return jax.shard_map(
        per_device, mesh=mesh, in_specs=placed, out_specs=P("elec", "cell"), check_vma=False
    )
```

time: 63.1 us -> 60.1 us (0.952)
  the two profiles are of different devices: /device:TPU:6 before, /device:TPU:0 now
where the time goes in v3:
time: 60.1 us; the launch traced here: 59.9 us
  starting transfers between devices  25.4 us (42%)
  Pallas kernels  19.1 us (32%)
  waiting for transfers between devices  12.9 us (21%)
  local copies, waits for them, and re-layouts  1.94 us (3%)
    ppermute x18, starting transfers between devices, hop(): return lax.ppermute(x, axis, [(i, i ^ mask) for i in range(size)])  25.4 us
    pallas_call x3, Pallas kernels, sensitivities(): pl.pallas_call(functools.partial(sensitivity_kernel, len(ready), offsets)...  13.9 us
    ppermute x18, waiting for transfers between devices, hop(): return lax.ppermute(x, axis, [(i, i ^ mask) for i in range(size)])  12.9 us
    pallas_call x4, Pallas kernels, whole_call(): pl.pallas_call(kernel, in_specs=[pl.BlockSpec(memory_space=pltpu.SMEM)] +...  5.01 us
    unnamed x10, local copies, waits for them, and re-layouts  1.88 us
  transfers between devices with their start and end apart: 18, of which 7 were waited for; matrix products, arithmetic and copies ran while one was open for 1% of the time, Pallas kernels for 29%

profile of v3, /device:TPU:0, one launch (start us, length us, event | category | flops | bytes accessed | tf_op | source)
XLA Modules:
  0.0 59.9 jit_solution(4355354599687701562)
XLA Ops:
  0.0 5.0 %collective-permute-start.1 = (bf16[3,256,128]{2,1,0:T(8,128)(2,1)}, bf16[3,256,128]{2,1,0:T(8,128)(2,1)S(1)}, u32[]{:S(2)}, u32[]{:S(2)}) collective-permute-start(bf16[3,256,128]{2,1,0:T(8,128)(2,1)} %refs_0_.1), channel_id=1, source_target_pairs={{0,24},{8,16},{16,8},{24,0},{1,25},{9,17},{17,9},{25,1},{2,26},{10... | collective-permute-start | bytes 589832 | tf_op jit(solution)/shard_map/ppermute | solution.py:20
  5.1 1.0 %copy-done = bf16[3,256,128]{2,1,0:T(8,128)(2,1)S(1)} copy-done((bf16[3,256,128]{2,1,0:T(8,128)(2,1)S(1)}, bf16[3,256,128]{2,1,0:T(8,128)(2,1)}, u32[]{:S(2)}) %copy-start) | copy-done | bytes 196632
  6.0 2.5 %collective-permute-start = (bf16[784,128]{1,0:T(8,128)(2,1)S(1)}, bf16[784,128]{1,0:T(8,128)(2,1)S(1)}, u32[]{:S(2)}, u32[]{:S(2)}) collective-permute-start(bf16[784,128]{1,0:T(8,128)(2,1)S(1)} %pack.1), channel_id=1, source_target_pairs={{0,6},{1,7},{2,4},{3,5},{4,2},{5,3},{6,0},{7,1},{8,14},{9,15},{10,... | collective-permute-start | bytes 602120 | tf_op jit(solution)/shard_map/ppermute | solution.py:20
  8.6 0.1 pad_add_fusion.place
  8.7 2.0 %collective-permute-done.1.refs_2_ = bf16[3,256,128]{2,1,0:T(8,128)(2,1)S(1)} collective-permute-done((bf16[3,256,128]{2,1,0:T(8,128)(2,1)}, bf16[3,256,128]{2,1,0:T(8,128)(2,1)S(1)}, u32[]{:S(2)}, u32[]{:S(2)}) %collective-permute-start.1) | collective-permute-done | bytes 196640 | tf_op jit(solution)/shard_map/ppermute | solution.py:20
  10.7 3.0 %collective-permute-start.2 = (bf16[3,256,128]{2,1,0:T(8,128)(2,1)S(1)}, bf16[3,256,128]{2,1,0:T(8,128)(2,1)S(1)}, u32[]{:S(2)}, u32[]{:S(2)}) collective-permute-start(bf16[3,256,128]{2,1,0:T(8,128)(2,1)S(1)} %collective-permute-done.1.refs_2_), channel_id=1, source_target_pairs={{0,6},{1,7},{2,4},{3,5},{4,2},{5,3},{6,0},{7,1},{8,14},{9,15},{10,... | collective-permute-start | bytes 589832 | tf_op jit(solution)/shard_map/ppermute | solution.py:20
  13.8 2.9 %collective-permute-start.3 = (bf16[3,256,128]{2,1,0:T(8,128)(2,1)S(1)}, bf16[3,256,128]{2,1,0:T(8,128)(2,1)S(1)}, u32[]{:S(2)}, u32[]{:S(2)}) collective-permute-start(bf16[3,256,128]{2,1,0:T(8,128)(2,1)S(1)} %collective-permute-done.1.refs_2_), channel_id=1, source_target_pairs={{0,8},{8,0},{16,24},{24,16},{1,9},{9,1},{17,25},{25,17},{2,10},{10... | collective-permute-start | bytes 589832 | tf_op jit(solution)/shard_map/ppermute | solution.py:20
  16.7 0.9 %copy-done.1 = bf16[3,256,128]{2,1,0:T(8,128)(2,1)S(1)} copy-done((bf16[3,256,128]{2,1,0:T(8,128)(2,1)S(1)}, bf16[3,256,128]{2,1,0:T(8,128)(2,1)}, u32[]{:S(2)}) %copy-start.1) | copy-done | bytes 196632
  17.6 0.2 turn_shards.1.refs_0_
  18.0 2.6 %collective-permute-done.3.refs_1_ = bf16[3,256,128]{2,1,0:T(8,128)(2,1)S(1)} collective-permute-done((bf16[3,256,128]{2,1,0:T(8,128)(2,1)S(1)}, bf16[3,256,128]{2,1,0:T(8,128)(2,1)S(1)}, u32[]{:S(2)}, u32[]{:S(2)}) %collective-permute-start.3) | collective-permute-done | bytes 196640 | tf_op jit(solution)/shard_map/ppermute | solution.py:20
  20.6 1.7 %collective-permute-start.7 = (bf16[2,3,256,128]{3,2,1,0:T(8,128)(2,1)S(1)}, bf16[2,3,256,128]{3,2,1,0:T(8,128)(2,1)S(1)}, u32[]{:S(2)}, u32[]{:S(2)}) collective-permute-start(bf16[2,3,256,128]{3,2,1,0:T(8,128)(2,1)S(1)} %pad_maximum_fusion), channel_id=1, source_target_pairs={{0,8},{8,0},{16,24},{24,16},{1,9},{9,1},{17,25},{25,17},{2,10},{10... | collective-permute-start | bytes 1179656 | tf_op jit(solution)/shard_map/ppermute | solution.py:20
  22.3 4.6 %sensitivities.3.own_send = bf16[128,2048]{1,0:T(8,128)(2,1)S(1)} custom-call(s32[3]{0:T(128)S(1)} %pad_add_fusion.1.place, s32[4,4096]{1,0:T(4,128)S(1)} %bitcast.27, f32[1,4096]{1,0:T(1,128)S(1)} %bitcast.30, f32[1,128]{1,0:T(1,128)S(1)} %bitcast.25, bf16[3,384,256]{2,1,0:T(8,128)(2,1)S(1)} %turn_shards.1.refs_0_, ...), custom_call_target="tpu_custom_call" | custom-call | flops 3221225472 | bytes 1 | tf_op jit(solution)/shard_map/sensitivities/pallas_call | solution.py:134
  27.0 0.6 %collective-permute-start.10 = (bf16[128,2048]{1,0:T(8,128)(2,1)S(1)}, bf16[128,2048]{1,0:T(8,128)(2,1)S(1)}, u32[]{:S(2)}, u32[]{:S(2)}) collective-permute-start(bf16[128,2048]{1,0:T(8,128)(2,1)S(1)} %sensitivities.3.own_send), channel_id=1, source_target_pairs={{0,2},{1,3},{2,0},{3,1},{4,6},{5,7},{6,4},{7,5},{8,10},{9,11},{10,... | collective-permute-start | bytes 1572872 | tf_op jit(solution)/shard_map/ppermute | solution.py:20
  27.6 1.2 %collective-permute-start.11 = (bf16[128,2048]{1,0:T(8,128)(2,1)S(1)}, bf16[128,2048]{1,0:T(8,128)(2,1)S(1)}, u32[]{:S(2)}, u32[]{:S(2)}) collective-permute-start(bf16[128,2048]{1,0:T(8,128)(2,1)S(1)} %sensitivities.3.own_send), channel_id=1, source_target_pairs={{0,4},{1,5},{2,6},{3,7},{4,0},{5,1},{6,2},{7,3},{8,12},{9,13},{10,... | collective-permute-start | bytes 1572872 | tf_op jit(solution)/shard_map/ppermute | solution.py:20
  28.8 4.6 %sensitivities.4.own_keep = bf16[128,2048]{1,0:T(8,128)(2,1)S(1)} custom-call(s32[3]{0:T(128)S(1)} %pad_add_fusion.2.place, s32[4,4096]{1,0:T(4,128)S(1)} %bitcast.28, f32[1,4096]{1,0:T(1,128)S(1)} %bitcast.31, f32[1,128]{1,0:T(1,128)S(1)} %bitcast.26, bf16[3,384,256]{2,1,0:T(8,128)(2,1)S(1)} %turn_shards.1.refs_0_, ...), custom_call_target="tpu_custom_call" | custom-call | flops 3221225472 | bytes 1 | tf_op jit(solution)/shard_map/sensitivities/pallas_call | solution.py:134
  33.6 4.7 %sensitivities.5.refs_0_ = bf16[128,2048]{1,0:T(8,128)(2,1)S(1)} custom-call(s32[3]{0:T(128)S(1)} %pad_add_fusion.3.place, s32[4,4096]{1,0:T(4,128)S(1)} %bitcast.29, f32[1,4096]{1,0:T(1,128)S(1)} %bitcast.32, bf16[16,128]{1,0:T(8,128)(2,1)S(1)} %slice.22.volume, bf16[3,256,128]{2,1,0:T(8,128)(2,1)S(1)} %bitcast.22, ...), custom_call_target="tpu_custom_call" | custom-call | flops 3221225472 | bytes 1 | tf_op jit(solution)/shard_map/sensitivities/pallas_call | solution.py:134
  38.3 1.8 %early_blocks.1 = (f32[256,128]{1,0:T(8,128)S(1)}, f32[1,128,128]{2,1,0:T(8,128)S(1)}, bf16[1,128,128]{2,1,0:T(8,128)(2,1)S(1)}, bf16[256,128]{1,0:T(8,128)(2,1)S(1)}) custom-call(s32[3]{0:T(128)S(1)} %pad_add_fusion.place, bf16[128,2048]{1,0:T(8,128)(2,1)S(1)} %sensitivities.3.own_send, bf16[128,2048]{1,0:T(8,128)(2,1)S(1)} %sensitivities.4.own_keep, ...), custom_call_target="tpu_custom_call" | custom-call | flops 1 | bytes 1 | tf_op jit(solution)/shard_map/early_blocks/pallas_call | solution.py:232
  40.1 1.8 %collective-permute-start.9 = (bf16[256,128]{1,0:T(8,128)(2,1)S(1)}, bf16[256,128]{1,0:T(8,128)(2,1)S(1)}, u32[]{:S(2)}, u32[]{:S(2)}) collective-permute-start(bf16[256,128]{1,0:T(8,128)(2,1)S(1)} %get-tuple-element.30), channel_id=1, source_target_pairs={{0,6},{1,7},{2,4},{3,5},{4,2},{5,3},{6,0},{7,1},{8,14},{9,15},{10,... | collective-permute-start | bytes 196616 | tf_op jit(solution)/shard_map/ppermute | solution.py:20
  41.9 1.3 %late_blocks.1 = (f32[2,128,128]{2,1,0:T(8,128)S(1)}, bf16[2,128,128]{2,1,0:T(8,128)(2,1)S(1)}, bf16[256,128]{1,0:T(8,128)(2,1)S(1)}, bf16[256,128]{1,0:T(8,128)(2,1)S(1)}) custom-call(s32[3]{0:T(128)S(1)} %pad_add_fusion.place, bf16[128,2048]{1,0:T(8,128)(2,1)S(1)} %sensitivities.4.own_keep, bf16[128,2048]{1,0:T(8,128)(2,1)S(1)} %collective-permute-done.6.other_keep, ...), custom_call_target="tpu_custom_call" | custom-call | flops 1 | bytes 1 | tf_op jit(solution)/shard_map/late_blocks/pallas_call | solution.py:232
  43.2 0.3 collective-permute-start.12
  43.5 1.0 %collective-permute-start.13 = (bf16[256,128]{1,0:T(8,128)(2,1)S(1)}, bf16[256,128]{1,0:T(8,128)(2,1)S(1)}, u32[]{:S(2)}, u32[]{:S(2)}) collective-permute-start(bf16[256,128]{1,0:T(8,128)(2,1)S(1)} %get-tuple-element.33), channel_id=1, source_target_pairs={{0,2},{1,3},{2,0},{3,1},{4,6},{5,7},{6,4},{7,5},{8,10},{9,11},{10,... | collective-permute-start | bytes 196616 | tf_op jit(solution)/shard_map/ppermute | solution.py:20
  44.5 0.7 %collective-permute-start.14 = (bf16[256,128]{1,0:T(8,128)(2,1)S(1)}, bf16[256,128]{1,0:T(8,128)(2,1)S(1)}, u32[]{:S(2)}, u32[]{:S(2)}) collective-permute-start(bf16[256,128]{1,0:T(8,128)(2,1)S(1)} %get-tuple-element.34), channel_id=1, source_target_pairs={{0,4},{1,5},{2,6},{3,7},{4,0},{5,1},{6,2},{7,3},{8,12},{9,13},{10,... | collective-permute-start | bytes 196616 | tf_op jit(solution)/shard_map/ppermute | solution.py:20
  45.3 1.2 %collective-permute-done.8.refs_1_ = bf16[1,128,128]{2,1,0:T(8,128)(2,1)S(1)} collective-permute-done((bf16[1,128,128]{2,1,0:T(8,128)(2,1)S(1)}, bf16[1,128,128]{2,1,0:T(8,128)(2,1)S(1)}, u32[]{:S(2)}, u32[]{:S(2)}) %collective-permute-start.8) | collective-permute-done | bytes 32800 | tf_op jit(solution)/shard_map/ppermute | solution.py:20
  46.5 1.3 %collective-permute-done.13.refs_5_ = bf16[256,128]{1,0:T(8,128)(2,1)S(1)} collective-permute-done((bf16[256,128]{1,0:T(8,128)(2,1)S(1)}, bf16[256,128]{1,0:T(8,128)(2,1)S(1)}, u32[]{:S(2)}, u32[]{:S(2)}) %collective-permute-start.13) | collective-permute-done | bytes 65568 | tf_op jit(solution)/shard_map/ppermute | solution.py:20
  47.8 1.0 %collective-permute-done.14.refs_6_ = bf16[256,128]{1,0:T(8,128)(2,1)S(1)} collective-permute-done((bf16[256,128]{1,0:T(8,128)(2,1)S(1)}, bf16[256,128]{1,0:T(8,128)(2,1)S(1)}, u32[]{:S(2)}, u32[]{:S(2)}) %collective-permute-start.14) | collective-permute-done | bytes 65568 | tf_op jit(solution)/shard_map/ppermute | solution.py:20
  48.8 0.7 %combine.1 = (f32[256,128]{1,0:T(8,128)S(1)}, bf16[272,128]{1,0:T(8,128)(2,1)S(1)}, bf16[272,128]{1,0:T(8,128)(2,1)S(1)}, bf16[272,128]{1,0:T(8,128)(2,1)S(1)}) custom-call(s32[3]{0:T(128)S(1)} %pad_add_fusion.place, f32[256,128]{1,0:T(8,128)S(1)} %get-tuple-element.27.own_block, f32[1,128,128]{2,1,0:T(8,128)S(1)} %get-tuple-element.28.refs_0_, ...), custom_call_target="tpu_custom_call" | custom-call | flops 1 | bytes 1 | tf_op jit(solution)/shard_map/combine/pallas_call | solution.py:232
  49.5 0.4 collective-permute-start.15
  49.8 2.8 %collective-permute-start.16 = (bf16[272,128]{1,0:T(8,128)(2,1)S(1)}, bf16[272,128]{1,0:T(8,128)(2,1)S(1)}, u32[]{:S(2)}, u32[]{:S(2)}) collective-permute-start(bf16[272,128]{1,0:T(8,128)(2,1)S(1)} %get-tuple-element.37), channel_id=1, source_target_pairs={{0,16},{8,24},{16,0},{24,8},{1,17},{9,25},{17,1},{25,9},{2,18},{10... | collective-permute-start | bytes 208904 | tf_op jit(solution)/shard_map/ppermute | solution.py:20
  52.6 1.3 %collective-permute-start.17 = (bf16[272,128]{1,0:T(8,128)(2,1)S(1)}, bf16[272,128]{1,0:T(8,128)(2,1)S(1)}, u32[]{:S(2)}, u32[]{:S(2)}) collective-permute-start(bf16[272,128]{1,0:T(8,128)(2,1)S(1)} %get-tuple-element.38), channel_id=1, source_target_pairs={{0,24},{8,16},{16,8},{24,0},{1,25},{9,17},{17,9},{25,1},{2,26},{10... | collective-permute-start | bytes 208904 | tf_op jit(solution)/shard_map/ppermute | solution.py:20
  53.9 1.6 %collective-permute-done.16.refs_1_ = bf16[272,128]{1,0:T(8,128)(2,1)S(1)} collective-permute-done((bf16[272,128]{1,0:T(8,128)(2,1)S(1)}, bf16[272,128]{1,0:T(8,128)(2,1)S(1)}, u32[]{:S(2)}, u32[]{:S(2)}) %collective-permute-start.16) | collective-permute-done | bytes 69664 | tf_op jit(solution)/shard_map/ppermute | solution.py:20
  55.6 3.1 %collective-permute-done.17.refs_2_ = bf16[272,128]{1,0:T(8,128)(2,1)S(1)} collective-permute-done((bf16[272,128]{1,0:T(8,128)(2,1)S(1)}, bf16[272,128]{1,0:T(8,128)(2,1)S(1)}, u32[]{:S(2)}, u32[]{:S(2)}) %collective-permute-start.17) | collective-permute-done | bytes 69664 | tf_op jit(solution)/shard_map/ppermute | solution.py:20
  58.7 1.2 %finish.1 = f32[256,128]{1,0:T(8,128)} custom-call(s32[3]{0:T(128)S(1)} %pad_add_fusion.place, f32[256,128]{1,0:T(8,128)S(1)} %get-tuple-element.35.own, bf16[272,128]{1,0:T(8,128)(2,1)S(1)} %collective-permute-done.15.refs_0_, bf16[272,128]{1,0:T(8,128)(2,1)S(1)} %collective-permute-done.16.refs_1_, bf16[272,128]{1,0:T(8,128)(2,1)S(1)} %collective-permute-done.17.refs_2_), custom_call_target="tpu_custom_call" | custom-call | flops 1 | bytes 1 | tf_op jit(solution)/shard_map/finish/pallas_call | solution.py:232
  (32 shorter events, 0.5 us)
Async XLA Ops:
  0.0 5.1 %copy-start.2 = (f32[128]{0:T(128)S(1)}, f32[128]{0:T(128)}, u32[]{:S(2)}) copy-start(f32[128]{0:T(128)} %param.6) | copy-start | bytes 1540
  0.0 10.7 %collective-permute-start.1 = (bf16[3,256,128]{2,1,0:T(8,128)(2,1)}, bf16[3,256,128]{2,1,0:T(8,128)(2,1)S(1)}, u32[]{:S(2)}, u32[]{:S(2)}) collective-permute-start(bf16[3,256,128]{2,1,0:T(8,128)(2,1)} %refs_0_.1), channel_id=1, source_target_pairs={{0,24},{8,16},{16,8},{24,0},{1,25},{9,17},{17,9},{25,1},{2,26},{10... | collective-permute-start | bytes 589832 | tf_op jit(solution)/shard_map/ppermute | solution.py:20
  5.1 1.0 %copy-start = (bf16[3,256,128]{2,1,0:T(8,128)(2,1)S(1)}, bf16[3,256,128]{2,1,0:T(8,128)(2,1)}, u32[]{:S(2)}) copy-start(bf16[3,256,128]{2,1,0:T(8,128)(2,1)} %refs_0_.1) | copy-start | bytes 589828
  6.0 11.8 %collective-permute-start = (bf16[784,128]{1,0:T(8,128)(2,1)S(1)}, bf16[784,128]{1,0:T(8,128)(2,1)S(1)}, u32[]{:S(2)}, u32[]{:S(2)}) collective-permute-start(bf16[784,128]{1,0:T(8,128)(2,1)S(1)} %pack.1), channel_id=1, source_target_pairs={{0,6},{1,7},{2,4},{3,5},{4,2},{5,3},{6,0},{7,1},{8,14},{9,15},{10,... | collective-permute-start | bytes 602120 | tf_op jit(solution)/shard_map/ppermute | solution.py:20
  8.5 8.1 %collective-permute-start.4 = (bf16[784,128]{1,0:T(8,128)(2,1)S(1)}, bf16[784,128]{1,0:T(8,128)(2,1)S(1)}, u32[]{:S(2)}, u32[]{:S(2)}) collective-permute-start(bf16[784,128]{1,0:T(8,128)(2,1)S(1)} %pack.1), channel_id=1, source_target_pairs={{0,8},{8,0},{16,24},{24,16},{1,9},{9,1},{17,25},{25,17},{2,10},{10... | collective-permute-start | bytes 602120 | tf_op jit(solution)/shard_map/ppermute | solution.py:20
  10.7 7.2 %collective-permute-start.2 = (bf16[3,256,128]{2,1,0:T(8,128)(2,1)S(1)}, bf16[3,256,128]{2,1,0:T(8,128)(2,1)S(1)}, u32[]{:S(2)}, u32[]{:S(2)}) collective-permute-start(bf16[3,256,128]{2,1,0:T(8,128)(2,1)S(1)} %collective-permute-done.1.refs_2_), channel_id=1, source_target_pairs={{0,6},{1,7},{2,4},{3,5},{4,2},{5,3},{6,0},{7,1},{8,14},{9,15},{10,... | collective-permute-start | bytes 589832 | tf_op jit(solution)/shard_map/ppermute | solution.py:20
  13.8 6.8 %collective-permute-start.3 = (bf16[3,256,128]{2,1,0:T(8,128)(2,1)S(1)}, bf16[3,256,128]{2,1,0:T(8,128)(2,1)S(1)}, u32[]{:S(2)}, u32[]{:S(2)}) collective-permute-start(bf16[3,256,128]{2,1,0:T(8,128)(2,1)S(1)} %collective-permute-done.1.refs_2_), channel_id=1, source_target_pairs={{0,8},{8,0},{16,24},{24,16},{1,9},{9,1},{17,25},{25,17},{2,10},{10... | collective-permute-start | bytes 589832 | tf_op jit(solution)/shard_map/ppermute | solution.py:20
  16.7 0.9 %copy-start.1 = (bf16[3,256,128]{2,1,0:T(8,128)(2,1)S(1)}, bf16[3,256,128]{2,1,0:T(8,128)(2,1)}, u32[]{:S(2)}) copy-start(bf16[3,256,128]{2,1,0:T(8,128)(2,1)} %refs_0_.1) | copy-start | bytes 589828
  17.9 4.4 %copy-start.3 = (s32[4096,4]{0,1:T(4,128)S(1)}, s32[4096,4]{0,1:T(4,128)}, u32[]{:S(2)}) copy-start(s32[4096,4]{0,1:T(4,128)} %param.5) | copy-start | bytes 196612
  17.9 4.4 %copy-start.4 = (f32[4096]{0:T(1024)S(1)}, f32[4096]{0:T(1024)}, u32[]{:S(2)}) copy-start(f32[4096]{0:T(1024)} %param.7) | copy-start | bytes 49156
  20.6 13.0 %collective-permute-start.7 = (bf16[2,3,256,128]{3,2,1,0:T(8,128)(2,1)S(1)}, bf16[2,3,256,128]{3,2,1,0:T(8,128)(2,1)S(1)}, u32[]{:S(2)}, u32[]{:S(2)}) collective-permute-start(bf16[2,3,256,128]{3,2,1,0:T(8,128)(2,1)S(1)} %pad_maximum_fusion), channel_id=1, source_target_pairs={{0,8},{8,0},{16,24},{24,16},{1,9},{9,1},{17,25},{25,17},{2,10},{10... | collective-permute-start | bytes 1179656 | tf_op jit(solution)/shard_map/ppermute | solution.py:20
  26.9 11.4 %collective-permute-start.5 = (bf16[128,2048]{1,0:T(8,128)(2,1)S(1)}, bf16[128,2048]{1,0:T(8,128)(2,1)S(1)}, u32[]{:S(2)}, u32[]{:S(2)}) collective-permute-start(bf16[128,2048]{1,0:T(8,128)(2,1)S(1)} %sensitivities.3.own_send), channel_id=1, source_target_pairs={{0,1},{1,0},{2,3},{3,2},{4,5},{5,4},{6,7},{7,6},{8,9},{9,8},{10,11... | collective-permute-start | bytes 1572872 | tf_op jit(solution)/shard_map/ppermute | solution.py:20
  27.0 14.9 %collective-permute-start.10 = (bf16[128,2048]{1,0:T(8,128)(2,1)S(1)}, bf16[128,2048]{1,0:T(8,128)(2,1)S(1)}, u32[]{:S(2)}, u32[]{:S(2)}) collective-permute-start(bf16[128,2048]{1,0:T(8,128)(2,1)S(1)} %sensitivities.3.own_send), channel_id=1, source_target_pairs={{0,2},{1,3},{2,0},{3,1},{4,6},{5,7},{6,4},{7,5},{8,10},{9,11},{10,... | collective-permute-start | bytes 1572872 | tf_op jit(solution)/shard_map/ppermute | solution.py:20
  27.6 14.3 %collective-permute-start.11 = (bf16[128,2048]{1,0:T(8,128)(2,1)S(1)}, bf16[128,2048]{1,0:T(8,128)(2,1)S(1)}, u32[]{:S(2)}, u32[]{:S(2)}) collective-permute-start(bf16[128,2048]{1,0:T(8,128)(2,1)S(1)} %sensitivities.3.own_send), channel_id=1, source_target_pairs={{0,4},{1,5},{2,6},{3,7},{4,0},{5,1},{6,2},{7,3},{8,12},{9,13},{10,... | collective-permute-start | bytes 1572872 | tf_op jit(solution)/shard_map/ppermute | solution.py:20
  33.4 4.9 %collective-permute-start.6 = (bf16[128,2048]{1,0:T(8,128)(2,1)S(1)}, bf16[128,2048]{1,0:T(8,128)(2,1)S(1)}, u32[]{:S(2)}, u32[]{:S(2)}) collective-permute-start(bf16[128,2048]{1,0:T(8,128)(2,1)S(1)} %sensitivities.4.own_keep), channel_id=1, source_target_pairs={{0,1},{1,0},{2,3},{3,2},{4,5},{5,4},{6,7},{7,6},{8,9},{9,8},{10,11... | collective-permute-start | bytes 1572872 | tf_op jit(solution)/shard_map/ppermute | solution.py:20
  40.1 6.4 %collective-permute-start.9 = (bf16[256,128]{1,0:T(8,128)(2,1)S(1)}, bf16[256,128]{1,0:T(8,128)(2,1)S(1)}, u32[]{:S(2)}, u32[]{:S(2)}) collective-permute-start(bf16[256,128]{1,0:T(8,128)(2,1)S(1)} %get-tuple-element.30), channel_id=1, source_target_pairs={{0,6},{1,7},{2,4},{3,5},{4,2},{5,3},{6,0},{7,1},{8,14},{9,15},{10,... | collective-permute-start | bytes 196616 | tf_op jit(solution)/shard_map/ppermute | solution.py:20
  43.2 3.3 %collective-permute-start.12 = (bf16[2,128,128]{2,1,0:T(8,128)(2,1)S(1)}, bf16[2,128,128]{2,1,0:T(8,128)(2,1)S(1)}, u32[]{:S(2)}, u32[]{:S(2)}) collective-permute-start(bf16[2,128,128]{2,1,0:T(8,128)(2,1)S(1)} %get-tuple-element.32), channel_id=1, source_target_pairs={{0,1},{1,0},{2,3},{3,2},{4,5},{5,4},{6,7},{7,6},{8,9},{9,8},{10,11... | collective-permute-start | bytes 196616 | tf_op jit(solution)/shard_map/ppermute | solution.py:20
  43.5 4.3 %collective-permute-start.13 = (bf16[256,128]{1,0:T(8,128)(2,1)S(1)}, bf16[256,128]{1,0:T(8,128)(2,1)S(1)}, u32[]{:S(2)}, u32[]{:S(2)}) collective-permute-start(bf16[256,128]{1,0:T(8,128)(2,1)S(1)} %get-tuple-element.33), channel_id=1, source_target_pairs={{0,2},{1,3},{2,0},{3,1},{4,6},{5,7},{6,4},{7,5},{8,10},{9,11},{10,... | collective-permute-start | bytes 196616 | tf_op jit(solution)/shard_map/ppermute | solution.py:20
  44.5 4.3 %collective-permute-start.14 = (bf16[256,128]{1,0:T(8,128)(2,1)S(1)}, bf16[256,128]{1,0:T(8,128)(2,1)S(1)}, u32[]{:S(2)}, u32[]{:S(2)}) collective-permute-start(bf16[256,128]{1,0:T(8,128)(2,1)S(1)} %get-tuple-element.34), channel_id=1, source_target_pairs={{0,4},{1,5},{2,6},{3,7},{4,0},{5,1},{6,2},{7,3},{8,12},{9,13},{10,... | collective-permute-start | bytes 196616 | tf_op jit(solution)/shard_map/ppermute | solution.py:20
  45.3 1.2 %collective-permute-start.8 = (bf16[1,128,128]{2,1,0:T(8,128)(2,1)S(1)}, bf16[1,128,128]{2,1,0:T(8,128)(2,1)S(1)}, u32[]{:S(2)}, u32[]{:S(2)}) collective-permute-start(bf16[1,128,128]{2,1,0:T(8,128)(2,1)S(1)} %get-tuple-element.29), channel_id=1, source_target_pairs={{0,1},{1,0},{2,3},{3,2},{4,5},{5,4},{6,7},{7,6},{8,9},{9,8},{10,11... | collective-permute-start | bytes 98312 | tf_op jit(solution)/shard_map/ppermute | solution.py:20
  49.5 4.5 %collective-permute-start.15 = (bf16[272,128]{1,0:T(8,128)(2,1)S(1)}, bf16[272,128]{1,0:T(8,128)(2,1)S(1)}, u32[]{:S(2)}, u32[]{:S(2)}) collective-permute-start(bf16[272,128]{1,0:T(8,128)(2,1)S(1)} %get-tuple-element.36), channel_id=1, source_target_pairs={{0,8},{8,0},{16,24},{24,16},{1,9},{9,1},{17,25},{25,17},{2,10},{10... | collective-permute-start | bytes 208904 | tf_op jit(solution)/shard_map/ppermute | solution.py:20
  49.8 5.7 %collective-permute-start.16 = (bf16[272,128]{1,0:T(8,128)(2,1)S(1)}, bf16[272,128]{1,0:T(8,128)(2,1)S(1)}, u32[]{:S(2)}, u32[]{:S(2)}) collective-permute-start(bf16[272,128]{1,0:T(8,128)(2,1)S(1)} %get-tuple-element.37), channel_id=1, source_target_pairs={{0,16},{8,24},{16,0},{24,8},{1,17},{9,25},{17,1},{25,9},{2,18},{10... | collective-permute-start | bytes 208904 | tf_op jit(solution)/shard_map/ppermute | solution.py:20
  52.6 6.1 %collective-permute-start.17 = (bf16[272,128]{1,0:T(8,128)(2,1)S(1)}, bf16[272,128]{1,0:T(8,128)(2,1)S(1)}, u32[]{:S(2)}, u32[]{:S(2)}) collective-permute-start(bf16[272,128]{1,0:T(8,128)(2,1)S(1)} %get-tuple-element.38), channel_id=1, source_target_pairs={{0,24},{8,16},{16,8},{24,0},{1,25},{9,17},{17,9},{25,1},{2,26},{10... | collective-permute-start | bytes 208904 | tf_op jit(solution)/shard_map/ppermute | solution.py:20

commit v4 on v3

--- a/solution.py
+++ b/solution.py
@@ -8,6 +8,7 @@
 from jax.sharding import PartitionSpec as P
 
 F32, BF16, I32 = jnp.float32, jnp.bfloat16, jnp.int32
+WEIGH = 4
 TILES = 4
 LIMIT = 24 * 1024 * 1024
 
@@ -28,23 +29,18 @@
     return (d & -d).bit_length() - 1
 
 
-def same_columns(left, right):
-    return lax.dot_general(left, right, (((1,), (1,)), ((), ())), preferred_element_type=F32)
-
-
-def difference_map(rows, at, base, depth):
-    labels = lax.broadcasted_iota(jnp.int16, (depth, rows.shape[1]), 0)
-    local = (rows - base).astype(jnp.int16)
-    plus, minus = local[at : at + 1, :] == labels, local[at + 1 : at + 2, :] == labels
+def difference_map(places, at, total):
+    labels = lax.broadcasted_iota(jnp.int16, (total, places.shape[1]), 0)
+    plus, minus = places[at : at + 1, :] == labels, places[at + 1 : at + 2, :] == labels
     one = jnp.ones((), BF16)
     return jnp.where(plus, one, jnp.where(minus, -one, jnp.zeros((), BF16)))
 
 
 def turn(shards, turned, start=0):
-    cells = shards[0].shape[2]
+    _, depth, cells = shards[0].shape
     for at, shard in enumerate(shards, start):
         for k in range(3):
-            turned[at, k * cells : (k + 1) * cells, :] = shard[k].T
+            turned[k * cells : (k + 1) * cells, at * depth : (at + 1) * depth] = shard[k].T
 
 
 def turn_kernel(*refs):
@@ -55,7 +51,7 @@
     _, depth, cells = shards[0].shape
     return pl.pallas_call(
         turn_kernel,
-        out_shape=jax.ShapeDtypeStruct((len(shards), 3 * cells, depth), BF16),
+        out_shape=jax.ShapeDtypeStruct((3 * cells, len(shards) * depth), BF16),
         compiler_params=params(),
         cost_estimate=pl.CostEstimate(flops=1000, bytes_accessed=1000, transcendentals=0),
         name="turn_shards",
@@ -86,59 +82,60 @@
     )(shard, volume.reshape(1, cells))
 
 
-def sensitivity_kernel(ready, offsets, place, quads, weight, volume, *refs):
-    shards, out, turned = refs[1 if ready else 0 : -2], refs[-2], refs[-1]
-    cells, depth = out.shape[0], turned.shape[2]
-
-    @pl.when(pl.program_id(0) == 0)
-    def _():
-        turn(shards, turned)
-
-    rows = quads[...]
-    source = receiver = None
-    for at, offset in enumerate(offsets):
-        base = jnp.bitwise_xor(place[0], offset) * depth
-        left = refs[0][at] if at < ready else turned[at - ready]
-        s = jnp.dot(left, difference_map(rows, 0, base, depth), preferred_element_type=F32)
-        r = jnp.dot(left, difference_map(rows, 2, base, depth), preferred_element_type=F32)
-        source = s if at == 0 else source + s
-        receiver = r if at == 0 else receiver + r
-    product = source * receiver
-    dots = product[:cells] + product[cells : 2 * cells] + product[2 * cells :]
+def sensitivity_kernel(offsets, ready, count, place, *refs):
+    quads, weights, volume = refs[:count], refs[count : 2 * count], refs[2 * count]
+    shards, out, turned = refs[2 * count + (2 if ready else 1) : -2], refs[-2], refs[-1]
+    cells, width = out.shape[0], quads[0].shape[1]
+    depth = turned.shape[1] // len(offsets)
+    if ready:
+        turned[:, : ready * depth] = refs[2 * count + 1][...]
+    turn(shards, turned, ready)
     terms = volume[...].astype(F32)
     column = jnp.sum(jnp.broadcast_to(terms[:, None, :], (terms.shape[0], 8, cells)), axis=0).T[:, :1]
-    out[...] = (weight[...] * -(column * dots)).astype(BF16)
-
-
-def sensitivities(place, tiles, quads, weight, volume, shards, turned=None, ready=()):
+    for tile in range(count):
+        rows = quads[tile][...]
+        owner = rows // depth
+        slot = jnp.bitwise_xor(owner, place[0])
+        if offsets != tuple(range(len(offsets))):
+            slot = functools.reduce(jnp.add, [jnp.where(slot == k, at, 0) for at, k in enumerate(offsets)])
+        places = (slot * depth + (rows - owner * depth)).astype(jnp.int16)
+        source = jnp.dot(turned[...], difference_map(places, 0, turned.shape[1]), preferred_element_type=F32)
+        receiver = jnp.dot(turned[...], difference_map(places, 2, turned.shape[1]), preferred_element_type=F32)
+        product = source * receiver
+        dots = product[:cells] + product[cells : 2 * cells] + product[2 * cells :]
+        out[:, tile * width : (tile + 1) * width] = (weights[tile][...] * -(column * dots)).astype(BF16)
+
+
+def sensitivities(place, tiles, quads, weight, volume, shards, turned=None, ready=(), weigh=1):
     offsets = tuple(ready) + tuple(sorted(shards))
     held = [shards[k] for k in offsets[len(ready) :]]
     _, depth, cells = held[0].shape
     width = quads.shape[1] // TILES
     count = len(tiles)
     scalars = jnp.stack([place[0], *tiles]).astype(I32)
+    whole = lambda a: pl.BlockSpec(a.shape, lambda i, s: (0,) * a.ndim)
+    tile_of = lambda rows, t: pl.BlockSpec((rows, width), lambda i, s: (0, s[1 + t]))
+    rest = [volume] + ([turned] if ready else []) + held
     spec = pltpu.PrefetchScalarGridSpec(
         num_scalar_prefetch=1,
-        grid=(count,),
-        in_specs=[
-            pl.BlockSpec((4, width), lambda i, s: (0, s[1 + i])),
-            pl.BlockSpec((1, width), lambda i, s: (0, s[1 + i])),
-            pl.BlockSpec(volume.shape, lambda i, s: (0, 0)),
-        ]
-        + [pl.BlockSpec((len(ready), 3 * cells, depth), lambda i, s: (0, 0, 0))] * (1 if ready else 0)
-        + [pl.BlockSpec((3, depth, cells), lambda i, s: (0, 0, 0))] * len(held),
-        out_specs=pl.BlockSpec((cells, width), lambda i, s: (0, i)),
-        scratch_shapes=[pltpu.VMEM((len(held), 3 * cells, depth), BF16)],
-    )
-    flops = 4 * count * width * len(offsets) * depth * 3 * cells
+        grid=(1,),
+        in_specs=[tile_of(4, t) for t in range(count)] + [tile_of(1, t) for t in range(count)] + [whole(a) for a in rest],
+        out_specs=pl.BlockSpec((cells, count * width), lambda i, s: (0, 0)),
+        scratch_shapes=[pltpu.VMEM((3 * cells, len(offsets) * depth), BF16)],
+    )
+    flops = weigh * 4 * count * width * len(offsets) * depth * 3 * cells
     return pl.pallas_call(
-        functools.partial(sensitivity_kernel, len(ready), offsets),
+        functools.partial(sensitivity_kernel, offsets, len(ready), count),
         grid_spec=spec,
         out_shape=jax.ShapeDtypeStruct((cells, count * width), BF16),
         compiler_params=params(),
         cost_estimate=pl.CostEstimate(flops=flops, bytes_accessed=1, transcendentals=0),
         name="sensitivities",
-    )(scalars, quads, weight, volume, *([turned] if ready else []), *held)
+    )(scalars, *[quads] * count, *[weight] * count, *rest)
+
+
+def same_columns(left, right):
+    return lax.dot_general(left, right, (((1,), (1,)), ((), ())), preferred_element_type=F32)
 
 
 def rows_of(core, cells):
@@ -147,13 +144,11 @@
 
 def early_kernel(evens, place, own_send, own_keep, other_send, other_keep, *refs):
     count, core = len(evens), place[2]
-    recomputed, own_block, mine, swap = refs[:count], *refs[count : count + 3]
-    mirrors, pair = refs[count + 3 : -1], refs[-1]
+    recomputed, mine, swap = refs[:count], *refs[count : count + 2]
+    mirrors, pair = refs[count + 2 : -1], refs[-1]
     cells = own_send.shape[0]
     here, there = rows_of(core, cells), rows_of(1 - core, cells)
     sides = ((0, own_send, other_send), (1, own_keep, other_keep))
-    own_block[here, :] = functools.reduce(jnp.add, [same_columns(own[...], own[...]) for _, own, _ in sides])
-    own_block[there, :] = functools.reduce(jnp.add, [same_columns(other[...], own[...]) for _, own, other in sides])
     for at, d in enumerate(evens):
         part = own_send.shape[1] // 2
         for bit in range(2):
@@ -171,6 +166,13 @@
         swap[at] = pair[1].astype(BF16)
         mirrors[at][here, :] = pair[0].T.astype(BF16)
         mirrors[at][there, :] = pair[1].T.astype(BF16)
+
+
+def own_kernel(place, own_send, own_keep, other_send, other_keep, out):
+    cells = own_send.shape[0]
+    sides = ((own_send[...], other_send[...]), (own_keep[...], other_keep[...]))
+    out[rows_of(place[2], cells), :] = functools.reduce(jnp.add, [same_columns(own, own) for own, _ in sides])
+    out[rows_of(1 - place[2], cells), :] = functools.reduce(jnp.add, [same_columns(other, own) for own, other in sides])
 
 
 def late_kernel(odds, place, own_keep, other_keep, *refs):
@@ -274,39 +276,45 @@
 
     across, volumes_across = {}, {}
     for d in evens:
-        near, away = hop(packed, "cell", devices, 2 * d), hop(shards[far], "cell", devices, 2 * d)
+        near = hop(packed, "cell", devices, 2 * d)
         near, volumes_across[d] = gradients(near), near[3 * shape[1] :, :]
-        across[d] = {0: near, far: away}
-        both, relayed, turned = lax.optimization_barrier((jnp.stack([near, away]), relayed, turned))
-        for j in range(1, half):
-            moved = hop(both, "elec", groups, j)
-            across[d][j], across[d][far ^ j] = moved[0], moved[1]
+        across[d] = {0: near}
+        for k in [far, *range(1, half)]:
+            across[d][k] = hop(shards[k], "cell", devices, 2 * d)
 
     form = functools.partial(sensitivities, place)
     own_send = form(send_tiles, columns, weights, volumes, relayed, turned, ready)
     received = [hop(own_send, "cell", devices, 2 * d) for d in odds]
     other_send = hop(own_send, "cell", devices, 1)
-    columns, own_send = lax.optimization_barrier((columns, own_send))
+    columns, own_send, across = lax.optimization_barrier((columns, own_send, across))
+    for d in evens:
+        for j in range(1, half):
+            across[d][far ^ j] = hop(across[d][far], "elec", groups, j)
     own_keep = form(keep_tiles, columns, weights, volumes, relayed, turned, ready)
     other_keep = hop(own_keep, "cell", devices, 1)
     recomputed = []
     for d in evens:
         bit = (chip >> low_bit(d)) & 1
-        recomputed.append(form([2 * send + bit, 2 * keep + bit], columns, weights, volumes_across[d], across[d]))
+        recomputed.append(form([2 * send + bit, 2 * keep + bit], columns, weights, volumes_across[d], across[d], weigh=WEIGH))
 
     whole, small = (2 * cells, cells), (cells, cells)
     outputs = lambda group: [
         jax.ShapeDtypeStruct((len(group), *small), F32),
         jax.ShapeDtypeStruct((len(group), *small), BF16),
     ] + [jax.ShapeDtypeStruct(whole, BF16)] * len(group)
-    own_block, *early = whole_call(
+    early = whole_call(
         functools.partial(early_kernel, evens),
         "early_blocks",
-        [jax.ShapeDtypeStruct(whole, F32)] + outputs(evens),
+        outputs(evens),
         [pltpu.VMEM((2, *small), F32)],
         place, own_send, own_keep, other_send, other_keep, *recomputed,
     )
     late = whole_call(functools.partial(late_kernel, odds), "late_blocks", outputs(odds), [], place, own_keep, other_keep, *received)
+
+    own_keep, late = lax.optimization_barrier((own_keep, late))
+    own_block = whole_call(
+        own_kernel, "own_block", jax.ShapeDtypeStruct(whole, F32), [], place, own_send, own_keep, other_send, other_keep
+    )
 
     def exchange(group, mine, swap, *mirrors):
         moved = [hop(m, "cell", devices, 2 * d) for d, m in zip(group, mirrors)]
@@ -319,7 +327,7 @@
         [pltpu.VMEM((chips, *whole), F32)],
         place, own_block, *exchange(evens, *early), *exchange(odds, *late),
     )
-    arrived = [hop(parts[k], "elec", groups, k) for k in range(1, groups)]
+    arrived = [hop(parts[k], "elec", groups, k) for k in reversed(range(1, groups))]
     return whole_call(
         functools.partial(final_kernel, float(measured * groups)),
         "finish",

time: 60.1 us -> 56.9 us (0.947)
  waiting for transfers between devices: 12.9 us -> 10.2 us
  starting transfers between devices: 25.4 us -> 27 us
  Pallas kernels: 19.1 us -> 18 us
  local copies, waits for them, and re-layouts: 1.94 us -> 1.01 us
    ppermute x18 -> x19, waiting for transfers between devices: 12.9 us -> 10.2 us  [hop(): return lax.ppermute(x, axis, [(i, i ^ mask) for i in range(size)])]
    pallas_call x4, Pallas kernels: 14.1 us -> 12.4 us  [the longest x3 12.2 us: sensitivities(): pl.pallas_call(functools.partial(sensitivity_kernel, offsets, len(ready),...]
    ppermute x18 -> x19, starting transfers between devices: 25.4 us -> 27 us  [hop(): return lax.ppermute(x, axis, [(i, i ^ mask) for i in range(size)])]
    unnamed x10, local copies, waits for them, and re-layouts: 1.88 us -> 0.98 us
    pallas_call x4 -> x5, Pallas kernels: 5.01 us -> 5.53 us  [whole_call(): pl.pallas_call(kernel, in_specs=[pl.BlockSpec(memory_space=pltpu.SMEM)] +...]
  transfers between devices with their start and end apart: 18 -> 19, of which waited for: 7 -> 7; matrix products, arithmetic and copies ran while one was open for 1% -> 1% of each run, Pallas kernels for 29% -> 28%
where the time goes in v4:
time: 56.9 us; the launch traced here: 56.7 us
  starting transfers between devices  27 us (47%)
  Pallas kernels  18 us (32%)
  waiting for transfers between devices  10.2 us (18%)
  local copies, waits for them, and re-layouts  1.01 us (2%)
    ppermute x19, starting transfers between devices, hop(): return lax.ppermute(x, axis, [(i, i ^ mask) for i in range(size)])  27 us
    pallas_call x3, Pallas kernels, sensitivities(): pl.pallas_call(functools.partial(sensitivity_kernel, offsets, len(ready),...  12.2 us
    ppermute x19, waiting for transfers between devices, hop(): return lax.ppermute(x, axis, [(i, i ^ mask) for i in range(size)])  10.2 us
    pallas_call x5, Pallas kernels, whole_call(): pl.pallas_call(kernel, in_specs=[pl.BlockSpec(memory_space=pltpu.SMEM)] +...  5.53 us
  transfers between devices with their start and end apart: 19, of which 7 were waited for; matrix products, arithmetic and copies ran while one was open for 1% of the time, Pallas kernels for 28%

profile of v4, /device:TPU:0, one launch (start us, length us, event | category | flops | bytes accessed | tf_op | source)
XLA Modules:
  0.0 56.7 jit_solution(10343244073982866371)
XLA Ops:
  0.0 5.0 %collective-permute-start.1 = (bf16[3,256,128]{2,1,0:T(8,128)(2,1)}, bf16[3,256,128]{2,1,0:T(8,128)(2,1)S(1)}, u32[]{:S(2)}, u32[]{:S(2)}) collective-permute-start(bf16[3,256,128]{2,1,0:T(8,128)(2,1)} %refs_0_.1), channel_id=1, source_target_pairs={{0,24},{8,16},{16,8},{24,0},{1,25},{9,17},{17,9},{25,1},{2,26},{10... | collective-permute-start | bytes 589832 | tf_op jit(solution)/shard_map/ppermute | solution.py:21
  5.1 1.0 %copy-done = bf16[3,256,128]{2,1,0:T(8,128)(2,1)S(1)} copy-done((bf16[3,256,128]{2,1,0:T(8,128)(2,1)S(1)}, bf16[3,256,128]{2,1,0:T(8,128)(2,1)}, u32[]{:S(2)}) %copy-start) | copy-done | bytes 196632
  6.0 2.5 %collective-permute-start.3 = (bf16[784,128]{1,0:T(8,128)(2,1)S(1)}, bf16[784,128]{1,0:T(8,128)(2,1)S(1)}, u32[]{:S(2)}, u32[]{:S(2)}) collective-permute-start(bf16[784,128]{1,0:T(8,128)(2,1)S(1)} %pack.1), channel_id=1, source_target_pairs={{0,6},{1,7},{2,4},{3,5},{4,2},{5,3},{6,0},{7,1},{8,14},{9,15},{10,... | collective-permute-start | bytes 602120 | tf_op jit(solution)/shard_map/ppermute | solution.py:21
  8.6 0.1 pad_add_fusion.place
  8.7 2.0 %collective-permute-done.1.refs_2_ = bf16[3,256,128]{2,1,0:T(8,128)(2,1)S(1)} collective-permute-done((bf16[3,256,128]{2,1,0:T(8,128)(2,1)}, bf16[3,256,128]{2,1,0:T(8,128)(2,1)S(1)}, u32[]{:S(2)}, u32[]{:S(2)}) %collective-permute-start.1) | collective-permute-done | bytes 196640 | tf_op jit(solution)/shard_map/ppermute | solution.py:21
  10.7 3.4 %collective-permute-start.2 = (bf16[3,256,128]{2,1,0:T(8,128)(2,1)S(1)}, bf16[3,256,128]{2,1,0:T(8,128)(2,1)S(1)}, u32[]{:S(2)}, u32[]{:S(2)}) collective-permute-start(bf16[3,256,128]{2,1,0:T(8,128)(2,1)S(1)} %collective-permute-done.1.refs_2_), channel_id=1, source_target_pairs={{0,8},{8,0},{16,24},{24,16},{1,9},{9,1},{17,25},{25,17},{2,10},{10... | collective-permute-start | bytes 589832 | tf_op jit(solution)/shard_map/ppermute | solution.py:21
  14.2 0.1 pad_add_fusion.3.place
  14.2 2.5 %collective-permute-start.5 = (bf16[3,256,128]{2,1,0:T(8,128)(2,1)S(1)}, bf16[3,256,128]{2,1,0:T(8,128)(2,1)S(1)}, u32[]{:S(2)}, u32[]{:S(2)}) collective-permute-start(bf16[3,256,128]{2,1,0:T(8,128)(2,1)S(1)} %collective-permute-done.1.refs_2_), channel_id=1, source_target_pairs={{0,6},{1,7},{2,4},{3,5},{4,2},{5,3},{6,0},{7,1},{8,14},{9,15},{10,... | collective-permute-start | bytes 589832 | tf_op jit(solution)/shard_map/ppermute | solution.py:21
  16.7 0.8 %collective-permute-start.4 = (bf16[3,256,128]{2,1,0:T(8,128)(2,1)S(1)}, bf16[3,256,128]{2,1,0:T(8,128)(2,1)S(1)}, u32[]{:S(2)}, u32[]{:S(2)}) collective-permute-start(bf16[3,256,128]{2,1,0:T(8,128)(2,1)S(1)} %bitcast.14), channel_id=1, source_target_pairs={{0,6},{1,7},{2,4},{3,5},{4,2},{5,3},{6,0},{7,1},{8,14},{9,15},{10,... | collective-permute-start | bytes 589832 | tf_op jit(solution)/shard_map/ppermute | solution.py:21
  17.5 0.2 turn_shards.1.refs_5_
  17.8 1.3 %collective-permute-done.2.refs_6_ = bf16[3,256,128]{2,1,0:T(8,128)(2,1)S(1)} collective-permute-done((bf16[3,256,128]{2,1,0:T(8,128)(2,1)S(1)}, bf16[3,256,128]{2,1,0:T(8,128)(2,1)S(1)}, u32[]{:S(2)}, u32[]{:S(2)}) %collective-permute-start.2) | collective-permute-done | bytes 196640 | tf_op jit(solution)/shard_map/ppermute | solution.py:21
  19.0 4.1 %sensitivities.3.own_send = bf16[128,2048]{1,0:T(8,128)(2,1)S(1)} custom-call(s32[3]{0:T(128)S(1)} %pad_add_fusion.1.place, s32[4,4096]{1,0:T(4,128)S(1)} %bitcast.20, s32[4,4096]{1,0:T(4,128)S(1)} %bitcast.21, f32[1,4096]{1,0:T(1,128)S(1)} %bitcast.26, f32[1,4096]{1,0:T(1,128)S(1)} %bitcast.27, f32[1,128]{1,0:T(1,128)S(1)} %bitcast.18, ...), custom_call_target="tpu_custom_call" | custom-call | flops 3221225472 | bytes 1 | tf_op jit(solution)/shard_map/sensitivities/pallas_call | solution.py:127
  23.2 1.4 %collective-permute-start.8 = (bf16[128,2048]{1,0:T(8,128)(2,1)S(1)}, bf16[128,2048]{1,0:T(8,128)(2,1)S(1)}, u32[]{:S(2)}, u32[]{:S(2)}) collective-permute-start(bf16[128,2048]{1,0:T(8,128)(2,1)S(1)} %sensitivities.3.own_send), channel_id=1, source_target_pairs={{0,4},{1,5},{2,6},{3,7},{4,0},{5,1},{6,2},{7,3},{8,12},{9,13},{10,... | collective-permute-start | bytes 1572872 | tf_op jit(solution)/shard_map/ppermute | solution.py:21
  24.6 1.4 %collective-permute-start.7 = (bf16[128,2048]{1,0:T(8,128)(2,1)S(1)}, bf16[128,2048]{1,0:T(8,128)(2,1)S(1)}, u32[]{:S(2)}, u32[]{:S(2)}) collective-permute-start(bf16[128,2048]{1,0:T(8,128)(2,1)S(1)} %sensitivities.3.own_send), channel_id=1, source_target_pairs={{0,2},{1,3},{2,0},{3,1},{4,6},{5,7},{6,4},{7,5},{8,10},{9,11},{10,... | collective-permute-start | bytes 1572872 | tf_op jit(solution)/shard_map/ppermute | solution.py:21
  26.0 1.7 %collective-permute-start.10 = (bf16[3,256,128]{2,1,0:T(8,128)(2,1)S(1)}, bf16[3,256,128]{2,1,0:T(8,128)(2,1)S(1)}, u32[]{:S(2)}, u32[]{:S(2)}) collective-permute-start(bf16[3,256,128]{2,1,0:T(8,128)(2,1)S(1)} %collective-permute-done.5.refs_8_), channel_id=1, source_target_pairs={{0,8},{8,0},{16,24},{24,16},{1,9},{9,1},{17,25},{25,17},{2,10},{10... | collective-permute-start | bytes 589832 | tf_op jit(solution)/shard_map/ppermute | solution.py:21
  27.7 4.1 %sensitivities.4.own_keep = bf16[128,2048]{1,0:T(8,128)(2,1)S(1)} custom-call(s32[3]{0:T(128)S(1)} %pad_add_fusion.2.place, s32[4,4096]{1,0:T(4,128)S(1)} %bitcast.22, s32[4,4096]{1,0:T(4,128)S(1)} %bitcast.23, f32[1,4096]{1,0:T(1,128)S(1)} %bitcast.28, f32[1,4096]{1,0:T(1,128)S(1)} %bitcast.29, f32[1,128]{1,0:T(1,128)S(1)} %bitcast.19, ...), custom_call_target="tpu_custom_call" | custom-call | flops 3221225472 | bytes 1 | tf_op jit(solution)/shard_map/sensitivities/pallas_call | solution.py:127
  31.9 0.9 %collective-permute-done.10.refs_7_ = bf16[3,256,128]{2,1,0:T(8,128)(2,1)S(1)} collective-permute-done((bf16[3,256,128]{2,1,0:T(8,128)(2,1)S(1)}, bf16[3,256,128]{2,1,0:T(8,128)(2,1)S(1)}, u32[]{:S(2)}, u32[]{:S(2)}) %collective-permute-start.10) | collective-permute-done | bytes 196640 | tf_op jit(solution)/shard_map/ppermute | solution.py:21
  32.7 4.1 %sensitivities.5.refs_0_ = bf16[128,2048]{1,0:T(8,128)(2,1)S(1)} custom-call(s32[3]{0:T(128)S(1)} %pad_add_fusion.3.place, s32[4,4096]{1,0:T(4,128)S(1)} %bitcast.24, s32[4,4096]{1,0:T(4,128)S(1)} %bitcast.25, f32[1,4096]{1,0:T(1,128)S(1)} %bitcast.30, f32[1,4096]{1,0:T(1,128)S(1)} %bitcast.31, bf16[16,128]{1,0:T(8,128)(2,1)S(1)} %slice.14.refs_4_, ...), custom_call_target="tpu_custom_call" | custom-call | flops 12884901888 | bytes 1 | tf_op jit(solution)/shard_map/sensitivities/pallas_call | solution.py:127
  36.8 1.1 %early_blocks.1 = (f32[1,128,128]{2,1,0:T(8,128)S(1)}, bf16[1,128,128]{2,1,0:T(8,128)(2,1)S(1)}, bf16[256,128]{1,0:T(8,128)(2,1)S(1)}) custom-call(s32[3]{0:T(128)S(1)} %pad_add_fusion.place, bf16[128,2048]{1,0:T(8,128)(2,1)S(1)} %sensitivities.3.own_send, bf16[128,2048]{1,0:T(8,128)(2,1)S(1)} %sensitivities.4.own_keep, ...), custom_call_target="tpu_custom_call" | custom-call | flops 1 | bytes 1 | tf_op jit(solution)/shard_map/early_blocks/pallas_call | solution.py:234
  37.9 0.8 %collective-permute-start.12 = (bf16[256,128]{1,0:T(8,128)(2,1)S(1)}, bf16[256,128]{1,0:T(8,128)(2,1)S(1)}, u32[]{:S(2)}, u32[]{:S(2)}) collective-permute-start(bf16[256,128]{1,0:T(8,128)(2,1)S(1)} %get-tuple-element.38), channel_id=1, source_target_pairs={{0,6},{1,7},{2,4},{3,5},{4,2},{5,3},{6,0},{7,1},{8,14},{9,15},{10,... | collective-permute-start | bytes 196616 | tf_op jit(solution)/shard_map/ppermute | solution.py:21
  38.7 1.3 %late_blocks.1 = (f32[2,128,128]{2,1,0:T(8,128)S(1)}, bf16[2,128,128]{2,1,0:T(8,128)(2,1)S(1)}, bf16[256,128]{1,0:T(8,128)(2,1)S(1)}, bf16[256,128]{1,0:T(8,128)(2,1)S(1)}) custom-call(s32[3]{0:T(128)S(1)} %pad_add_fusion.place, bf16[128,2048]{1,0:T(8,128)(2,1)S(1)} %sensitivities.4.own_keep, bf16[128,2048]{1,0:T(8,128)(2,1)S(1)} %collective-permute-done.6.other_keep, ...), custom_call_target="tpu_custom_call" | custom-call | flops 1 | bytes 1 | tf_op jit(solution)/shard_map/late_blocks/pallas_call | solution.py:234
  40.1 1.4 %collective-permute-start.14 = (bf16[256,128]{1,0:T(8,128)(2,1)S(1)}, bf16[256,128]{1,0:T(8,128)(2,1)S(1)}, u32[]{:S(2)}, u32[]{:S(2)}) collective-permute-start(bf16[256,128]{1,0:T(8,128)(2,1)S(1)} %get-tuple-element.41), channel_id=1, source_target_pairs={{0,2},{1,3},{2,0},{3,1},{4,6},{5,7},{6,4},{7,5},{8,10},{9,11},{10,... | collective-permute-start | bytes 196616 | tf_op jit(solution)/shard_map/ppermute | solution.py:21
  41.5 1.4 %collective-permute-start.15 = (bf16[256,128]{1,0:T(8,128)(2,1)S(1)}, bf16[256,128]{1,0:T(8,128)(2,1)S(1)}, u32[]{:S(2)}, u32[]{:S(2)}) collective-permute-start(bf16[256,128]{1,0:T(8,128)(2,1)S(1)} %get-tuple-element.42), channel_id=1, source_target_pairs={{0,4},{1,5},{2,6},{3,7},{4,0},{5,1},{6,2},{7,3},{8,12},{9,13},{10,... | collective-permute-start | bytes 196616 | tf_op jit(solution)/shard_map/ppermute | solution.py:21
  42.9 1.2 %own_block.1 = f32[256,128]{1,0:T(8,128)S(1)} custom-call(s32[3]{0:T(128)S(1)} %pad_add_fusion.place, bf16[128,2048]{1,0:T(8,128)(2,1)S(1)} %sensitivities.3.own_send, bf16[128,2048]{1,0:T(8,128)(2,1)S(1)} %sensitivities.4.own_keep, bf16[128,2048]{1,0:T(8,128)(2,1)S(1)} %collective-permute-done.9.other_send, ...), custom_call_target="tpu_custom_call" | custom-call | flops 1 | bytes 1 | tf_op jit(solution)/shard_map/own_block/pallas_call | solution.py:234
  44.2 0.4 collective-permute-done.14.refs_5_
  44.6 1.2 %collective-permute-done.15.refs_6_ = bf16[256,128]{1,0:T(8,128)(2,1)S(1)} collective-permute-done((bf16[256,128]{1,0:T(8,128)(2,1)S(1)}, bf16[256,128]{1,0:T(8,128)(2,1)S(1)}, u32[]{:S(2)}, u32[]{:S(2)}) %collective-permute-start.15) | collective-permute-done | bytes 65568 | tf_op jit(solution)/shard_map/ppermute | solution.py:21
  45.8 0.7 %combine.1 = (f32[256,128]{1,0:T(8,128)S(1)}, bf16[272,128]{1,0:T(8,128)(2,1)S(1)}, bf16[272,128]{1,0:T(8,128)(2,1)S(1)}, bf16[272,128]{1,0:T(8,128)(2,1)S(1)}) custom-call(s32[3]{0:T(128)S(1)} %pad_add_fusion.place, f32[256,128]{1,0:T(8,128)S(1)} %own_block.1, f32[1,128,128]{2,1,0:T(8,128)S(1)} %get-tuple-element.36.refs_0_, ...), custom_call_target="tpu_custom_call" | custom-call | flops 1 | bytes 1 | tf_op jit(solution)/shard_map/combine/pallas_call | solution.py:234
  46.4 3.5 %collective-permute-start.16 = (bf16[272,128]{1,0:T(8,128)(2,1)S(1)}, bf16[272,128]{1,0:T(8,128)(2,1)S(1)}, u32[]{:S(2)}, u32[]{:S(2)}) collective-permute-start(bf16[272,128]{1,0:T(8,128)(2,1)S(1)} %get-tuple-element.44), channel_id=1, source_target_pairs={{0,24},{8,16},{16,8},{24,0},{1,25},{9,17},{17,9},{25,1},{2,26},{10... | collective-permute-start | bytes 208904 | tf_op jit(solution)/shard_map/ppermute | solution.py:21
  49.9 0.9 %collective-permute-start.18 = (bf16[272,128]{1,0:T(8,128)(2,1)S(1)}, bf16[272,128]{1,0:T(8,128)(2,1)S(1)}, u32[]{:S(2)}, u32[]{:S(2)}) collective-permute-start(bf16[272,128]{1,0:T(8,128)(2,1)S(1)} %get-tuple-element.46), channel_id=1, source_target_pairs={{0,8},{8,0},{16,24},{24,16},{1,9},{9,1},{17,25},{25,17},{2,10},{10... | collective-permute-start | bytes 208904 | tf_op jit(solution)/shard_map/ppermute | solution.py:21
  50.9 1.8 %collective-permute-done.16.refs_0_ = bf16[272,128]{1,0:T(8,128)(2,1)S(1)} collective-permute-done((bf16[272,128]{1,0:T(8,128)(2,1)S(1)}, bf16[272,128]{1,0:T(8,128)(2,1)S(1)}, u32[]{:S(2)}, u32[]{:S(2)}) %collective-permute-start.16) | collective-permute-done | bytes 69664 | tf_op jit(solution)/shard_map/ppermute | solution.py:21
  52.7 2.8 %collective-permute-done.17.refs_1_ = bf16[272,128]{1,0:T(8,128)(2,1)S(1)} collective-permute-done((bf16[272,128]{1,0:T(8,128)(2,1)S(1)}, bf16[272,128]{1,0:T(8,128)(2,1)S(1)}, u32[]{:S(2)}, u32[]{:S(2)}) %collective-permute-start.17) | collective-permute-done | bytes 69664 | tf_op jit(solution)/shard_map/ppermute | solution.py:21
  55.5 1.2 %finish.1 = f32[256,128]{1,0:T(8,128)} custom-call(s32[3]{0:T(128)S(1)} %pad_add_fusion.place, f32[256,128]{1,0:T(8,128)S(1)} %get-tuple-element.43.own, bf16[272,128]{1,0:T(8,128)(2,1)S(1)} %collective-permute-done.16.refs_0_, bf16[272,128]{1,0:T(8,128)(2,1)S(1)} %collective-permute-done.17.refs_1_, bf16[272,128]{1,0:T(8,128)(2,1)S(1)} %collective-permute-done.18.refs_2_), custom_call_target="tpu_custom_call" | custom-call | flops 1 | bytes 1 | tf_op jit(solution)/shard_map/finish/pallas_call | solution.py:234
  (33 shorter events, 0.5 us)
Async XLA Ops:
  0.0 5.1 %copy-start.2 = (f32[128]{0:T(128)S(1)}, f32[128]{0:T(128)}, u32[]{:S(2)}) copy-start(f32[128]{0:T(128)} %param.6) | copy-start | bytes 1540
  0.0 10.7 %collective-permute-start.1 = (bf16[3,256,128]{2,1,0:T(8,128)(2,1)}, bf16[3,256,128]{2,1,0:T(8,128)(2,1)S(1)}, u32[]{:S(2)}, u32[]{:S(2)}) collective-permute-start(bf16[3,256,128]{2,1,0:T(8,128)(2,1)} %refs_0_.1), channel_id=1, source_target_pairs={{0,24},{8,16},{16,8},{24,0},{1,25},{9,17},{17,9},{25,1},{2,26},{10... | collective-permute-start | bytes 589832 | tf_op jit(solution)/shard_map/ppermute | solution.py:21
  5.1 1.0 %copy-start = (bf16[3,256,128]{2,1,0:T(8,128)(2,1)S(1)}, bf16[3,256,128]{2,1,0:T(8,128)(2,1)}, u32[]{:S(2)}) copy-start(bf16[3,256,128]{2,1,0:T(8,128)(2,1)} %refs_0_.1) | copy-start | bytes 589828
  6.0 11.7 %collective-permute-start.3 = (bf16[784,128]{1,0:T(8,128)(2,1)S(1)}, bf16[784,128]{1,0:T(8,128)(2,1)S(1)}, u32[]{:S(2)}, u32[]{:S(2)}) collective-permute-start(bf16[784,128]{1,0:T(8,128)(2,1)S(1)} %pack.1), channel_id=1, source_target_pairs={{0,6},{1,7},{2,4},{3,5},{4,2},{5,3},{6,0},{7,1},{8,14},{9,15},{10,... | collective-permute-start | bytes 602120 | tf_op jit(solution)/shard_map/ppermute | solution.py:21
  8.5 8.2 %collective-permute-start = (bf16[784,128]{1,0:T(8,128)(2,1)S(1)}, bf16[784,128]{1,0:T(8,128)(2,1)S(1)}, u32[]{:S(2)}, u32[]{:S(2)}) collective-permute-start(bf16[784,128]{1,0:T(8,128)(2,1)S(1)} %pack.1), channel_id=1, source_target_pairs={{0,8},{8,0},{16,24},{24,16},{1,9},{9,1},{17,25},{25,17},{2,10},{10... | collective-permute-start | bytes 602120 | tf_op jit(solution)/shard_map/ppermute | solution.py:21
  10.7 8.4 %collective-permute-start.2 = (bf16[3,256,128]{2,1,0:T(8,128)(2,1)S(1)}, bf16[3,256,128]{2,1,0:T(8,128)(2,1)S(1)}, u32[]{:S(2)}, u32[]{:S(2)}) collective-permute-start(bf16[3,256,128]{2,1,0:T(8,128)(2,1)S(1)} %collective-permute-done.1.refs_2_), channel_id=1, source_target_pairs={{0,8},{8,0},{16,24},{24,16},{1,9},{9,1},{17,25},{25,17},{2,10},{10... | collective-permute-start | bytes 589832 | tf_op jit(solution)/shard_map/ppermute | solution.py:21
  14.2 3.3 %copy-start.1 = (bf16[3,256,128]{2,1,0:T(8,128)(2,1)S(1)}, bf16[3,256,128]{2,1,0:T(8,128)(2,1)}, u32[]{:S(2)}) copy-start(bf16[3,256,128]{2,1,0:T(8,128)(2,1)} %refs_0_.1) | copy-start | bytes 589828
  14.2 11.8 %collective-permute-start.5 = (bf16[3,256,128]{2,1,0:T(8,128)(2,1)S(1)}, bf16[3,256,128]{2,1,0:T(8,128)(2,1)S(1)}, u32[]{:S(2)}, u32[]{:S(2)}) collective-permute-start(bf16[3,256,128]{2,1,0:T(8,128)(2,1)S(1)} %collective-permute-done.1.refs_2_), channel_id=1, source_target_pairs={{0,6},{1,7},{2,4},{3,5},{4,2},{5,3},{6,0},{7,1},{8,14},{9,15},{10,... | collective-permute-start | bytes 589832 | tf_op jit(solution)/shard_map/ppermute | solution.py:21
  16.7 9.3 %collective-permute-start.4 = (bf16[3,256,128]{2,1,0:T(8,128)(2,1)S(1)}, bf16[3,256,128]{2,1,0:T(8,128)(2,1)S(1)}, u32[]{:S(2)}, u32[]{:S(2)}) collective-permute-start(bf16[3,256,128]{2,1,0:T(8,128)(2,1)S(1)} %bitcast.14), channel_id=1, source_target_pairs={{0,6},{1,7},{2,4},{3,5},{4,2},{5,3},{6,0},{7,1},{8,14},{9,15},{10,... | collective-permute-start | bytes 589832 | tf_op jit(solution)/shard_map/ppermute | solution.py:21
  17.7 1.3 %copy-start.3 = (s32[4096,4]{0,1:T(4,128)S(1)}, s32[4096,4]{0,1:T(4,128)}, u32[]{:S(2)}) copy-start(s32[4096,4]{0,1:T(4,128)} %param.5) | copy-start | bytes 196612
  17.7 1.3 %copy-start.4 = (f32[4096]{0:T(1024)S(1)}, f32[4096]{0:T(1024)}, u32[]{:S(2)}) copy-start(f32[4096]{0:T(1024)} %param.7) | copy-start | bytes 49156
  23.1 13.7 %collective-permute-start.9 = (bf16[128,2048]{1,0:T(8,128)(2,1)S(1)}, bf16[128,2048]{1,0:T(8,128)(2,1)S(1)}, u32[]{:S(2)}, u32[]{:S(2)}) collective-permute-start(bf16[128,2048]{1,0:T(8,128)(2,1)S(1)} %sensitivities.3.own_send), channel_id=1, source_target_pairs={{0,1},{1,0},{2,3},{3,2},{4,5},{5,4},{6,7},{7,6},{8,9},{9,8},{10,11... | collective-permute-start | bytes 1572872 | tf_op jit(solution)/shard_map/ppermute | solution.py:21
  23.2 15.5 %collective-permute-start.8 = (bf16[128,2048]{1,0:T(8,128)(2,1)S(1)}, bf16[128,2048]{1,0:T(8,128)(2,1)S(1)}, u32[]{:S(2)}, u32[]{:S(2)}) collective-permute-start(bf16[128,2048]{1,0:T(8,128)(2,1)S(1)} %sensitivities.3.own_send), channel_id=1, source_target_pairs={{0,4},{1,5},{2,6},{3,7},{4,0},{5,1},{6,2},{7,3},{8,12},{9,13},{10,... | collective-permute-start | bytes 1572872 | tf_op jit(solution)/shard_map/ppermute | solution.py:21
  24.6 14.1 %collective-permute-start.7 = (bf16[128,2048]{1,0:T(8,128)(2,1)S(1)}, bf16[128,2048]{1,0:T(8,128)(2,1)S(1)}, u32[]{:S(2)}, u32[]{:S(2)}) collective-permute-start(bf16[128,2048]{1,0:T(8,128)(2,1)S(1)} %sensitivities.3.own_send), channel_id=1, source_target_pairs={{0,2},{1,3},{2,0},{3,1},{4,6},{5,7},{6,4},{7,5},{8,10},{9,11},{10,... | collective-permute-start | bytes 1572872 | tf_op jit(solution)/shard_map/ppermute | solution.py:21
  26.0 6.7 %collective-permute-start.10 = (bf16[3,256,128]{2,1,0:T(8,128)(2,1)S(1)}, bf16[3,256,128]{2,1,0:T(8,128)(2,1)S(1)}, u32[]{:S(2)}, u32[]{:S(2)}) collective-permute-start(bf16[3,256,128]{2,1,0:T(8,128)(2,1)S(1)} %collective-permute-done.5.refs_8_), channel_id=1, source_target_pairs={{0,8},{8,0},{16,24},{24,16},{1,9},{9,1},{17,25},{25,17},{2,10},{10... | collective-permute-start | bytes 589832 | tf_op jit(solution)/shard_map/ppermute | solution.py:21
  31.8 5.0 %collective-permute-start.6 = (bf16[128,2048]{1,0:T(8,128)(2,1)S(1)}, bf16[128,2048]{1,0:T(8,128)(2,1)S(1)}, u32[]{:S(2)}, u32[]{:S(2)}) collective-permute-start(bf16[128,2048]{1,0:T(8,128)(2,1)S(1)} %sensitivities.4.own_keep), channel_id=1, source_target_pairs={{0,1},{1,0},{2,3},{3,2},{4,5},{5,4},{6,7},{7,6},{8,9},{9,8},{10,11... | collective-permute-start | bytes 1572872 | tf_op jit(solution)/shard_map/ppermute | solution.py:21
  37.9 6.3 %collective-permute-start.12 = (bf16[256,128]{1,0:T(8,128)(2,1)S(1)}, bf16[256,128]{1,0:T(8,128)(2,1)S(1)}, u32[]{:S(2)}, u32[]{:S(2)}) collective-permute-start(bf16[256,128]{1,0:T(8,128)(2,1)S(1)} %get-tuple-element.38), channel_id=1, source_target_pairs={{0,6},{1,7},{2,4},{3,5},{4,2},{5,3},{6,0},{7,1},{8,14},{9,15},{10,... | collective-permute-start | bytes 196616 | tf_op jit(solution)/shard_map/ppermute | solution.py:21
  40.0 4.2 %collective-permute-start.13 = (bf16[2,128,128]{2,1,0:T(8,128)(2,1)S(1)}, bf16[2,128,128]{2,1,0:T(8,128)(2,1)S(1)}, u32[]{:S(2)}, u32[]{:S(2)}) collective-permute-start(bf16[2,128,128]{2,1,0:T(8,128)(2,1)S(1)} %get-tuple-element.40), channel_id=1, source_target_pairs={{0,1},{1,0},{2,3},{3,2},{4,5},{5,4},{6,7},{7,6},{8,9},{9,8},{10,11... | collective-permute-start | bytes 196616 | tf_op jit(solution)/shard_map/ppermute | solution.py:21
  40.1 4.5 %collective-permute-start.14 = (bf16[256,128]{1,0:T(8,128)(2,1)S(1)}, bf16[256,128]{1,0:T(8,128)(2,1)S(1)}, u32[]{:S(2)}, u32[]{:S(2)}) collective-permute-start(bf16[256,128]{1,0:T(8,128)(2,1)S(1)} %get-tuple-element.41), channel_id=1, source_target_pairs={{0,2},{1,3},{2,0},{3,1},{4,6},{5,7},{6,4},{7,5},{8,10},{9,11},{10,... | collective-permute-start | bytes 196616 | tf_op jit(solution)/shard_map/ppermute | solution.py:21
  41.5 4.3 %collective-permute-start.15 = (bf16[256,128]{1,0:T(8,128)(2,1)S(1)}, bf16[256,128]{1,0:T(8,128)(2,1)S(1)}, u32[]{:S(2)}, u32[]{:S(2)}) collective-permute-start(bf16[256,128]{1,0:T(8,128)(2,1)S(1)} %get-tuple-element.42), channel_id=1, source_target_pairs={{0,4},{1,5},{2,6},{3,7},{4,0},{5,1},{6,2},{7,3},{8,12},{9,13},{10,... | collective-permute-start | bytes 196616 | tf_op jit(solution)/shard_map/ppermute | solution.py:21
  42.9 1.3 %collective-permute-start.11 = (bf16[1,128,128]{2,1,0:T(8,128)(2,1)S(1)}, bf16[1,128,128]{2,1,0:T(8,128)(2,1)S(1)}, u32[]{:S(2)}, u32[]{:S(2)}) collective-permute-start(bf16[1,128,128]{2,1,0:T(8,128)(2,1)S(1)} %get-tuple-element.37), channel_id=1, source_target_pairs={{0,1},{1,0},{2,3},{3,2},{4,5},{5,4},{6,7},{7,6},{8,9},{9,8},{10,11... | collective-permute-start | bytes 98312 | tf_op jit(solution)/shard_map/ppermute | solution.py:21
  46.4 6.3 %collective-permute-start.16 = (bf16[272,128]{1,0:T(8,128)(2,1)S(1)}, bf16[272,128]{1,0:T(8,128)(2,1)S(1)}, u32[]{:S(2)}, u32[]{:S(2)}) collective-permute-start(bf16[272,128]{1,0:T(8,128)(2,1)S(1)} %get-tuple-element.44), channel_id=1, source_target_pairs={{0,24},{8,16},{16,8},{24,0},{1,25},{9,17},{17,9},{25,1},{2,26},{10... | collective-permute-start | bytes 208904 | tf_op jit(solution)/shard_map/ppermute | solution.py:21
  49.9 5.5 %collective-permute-start.17 = (bf16[272,128]{1,0:T(8,128)(2,1)S(1)}, bf16[272,128]{1,0:T(8,128)(2,1)S(1)}, u32[]{:S(2)}, u32[]{:S(2)}) collective-permute-start(bf16[272,128]{1,0:T(8,128)(2,1)S(1)} %get-tuple-element.45), channel_id=1, source_target_pairs={{0,16},{8,24},{16,0},{24,8},{1,17},{9,25},{17,1},{25,9},{2,18},{10... | collective-permute-start | bytes 208904 | tf_op jit(solution)/shard_map/ppermute | solution.py:21
  49.9 5.5 %collective-permute-start.18 = (bf16[272,128]{1,0:T(8,128)(2,1)S(1)}, bf16[272,128]{1,0:T(8,128)(2,1)S(1)}, u32[]{:S(2)}, u32[]{:S(2)}) collective-permute-start(bf16[272,128]{1,0:T(8,128)(2,1)S(1)} %get-tuple-element.46), channel_id=1, source_target_pairs={{0,8},{8,0},{16,24},{24,16},{1,9},{9,1},{17,25},{25,17},{2,10},{10... | collective-permute-start | bytes 208904 | tf_op jit(solution)/shard_map/ppermute | solution.py:21

commit v5 on v4

v5 whole, which is shorter than its diff:
```python
import functools

import jax
import jax.numpy as jnp
from jax import lax
from jax.experimental import pallas as pl
from jax.experimental.pallas import tpu as pltpu
from jax.sharding import PartitionSpec as P

F32, BF16, I32 = jnp.float32, jnp.bfloat16, jnp.int32
WEIGH = 4
TILES = 4
LIMIT = 24 * 1024 * 1024


def params():
    return pltpu.CompilerParams(vmem_limit_bytes=LIMIT)


def hop(x, axis, size, mask):
    return lax.ppermute(x, axis, [(i, i ^ mask) for i in range(size)])


def odd(d):
    return bin(d).count("1") % 2 == 1


def position():
    here = lax.axis_index("cell")
    return lax.axis_index("elec"), jnp.right_shift(here, 1), jnp.bitwise_and(here, 1)


def bit_of(number, at):
    return jnp.bitwise_and(jnp.right_shift(number, at), 1)


def tiles_of(which, bits):
    _, chip, _ = position()
    keep = functools.reduce(jnp.bitwise_xor, [bit_of(chip, b) for b in range(bits)])
    send = 1 - keep
    if which == "send":
        return 2 * send, 2 * send + 1
    if which == "keep":
        return 2 * keep, 2 * keep + 1
    bit = bit_of(chip, low_bit(which))
    return 2 * send + bit, 2 * keep + bit


def low_bit(d):
    return (d & -d).bit_length() - 1


def difference_map(places, at, total):
    labels = lax.broadcasted_iota(jnp.int16, (total, places.shape[1]), 0)
    plus, minus = places[at : at + 1, :] == labels, places[at + 1 : at + 2, :] == labels
    one = jnp.ones((), BF16)
    return jnp.where(plus, one, jnp.where(minus, -one, jnp.zeros((), BF16)))


def turn(shards, turned, start=0):
    _, depth, cells = shards[0].shape
    for at, shard in enumerate(shards, start):
        for k in range(3):
            turned[k * cells : (k + 1) * cells, at * depth : (at + 1) * depth] = shard[k].T


def turn_kernel(*refs):
    turn(refs[:-1], refs[-1])


def turn_shards(shards):
    _, depth, cells = shards[0].shape
    return pl.pallas_call(
        turn_kernel,
        out_shape=jax.ShapeDtypeStruct((3 * cells, len(shards) * depth), BF16),
        compiler_params=params(),
        cost_estimate=pl.CostEstimate(flops=1000, bytes_accessed=1000, transcendentals=0),
        name="turn_shards",
    )(*shards)


def pack_kernel(shard, volume, out):
    parts, depth, cells = shard.shape
    for k in range(parts):
        out[k * depth : (k + 1) * depth, :] = shard[k]
    rest = volume[...]
    rows = []
    for _ in range(3):
        rows.append(rest.astype(BF16).astype(F32))
        rest = rest - rows[-1]
    tail = jnp.concatenate(rows + [jnp.zeros((13, cells), F32)], axis=0)
    out[parts * depth :, :] = tail.astype(BF16)


def pack(shard, volume):
    parts, depth, cells = shard.shape
    return pl.pallas_call(
        pack_kernel,
        out_shape=jax.ShapeDtypeStruct((parts * depth + 16, cells), BF16),
        compiler_params=params(),
        cost_estimate=pl.CostEstimate(flops=1000, bytes_accessed=1000, transcendentals=0),
        name="pack",
    )(shard, volume.reshape(1, cells))


def sensitivity_kernel(offsets, ready, which, bits, quads, weight, volume, *refs):
    shards, out, turned = refs[1 if ready else 0 : -2], refs[-2], refs[-1]
    cells, width = out.shape[0], quads.shape[1] // TILES
    depth = turned.shape[1] // len(offsets)
    if ready:
        turned[:, : ready * depth] = refs[0][...]
    turn(shards, turned, ready)
    terms = volume[...].astype(F32)
    column = jnp.sum(jnp.broadcast_to(terms[:, None, :], (terms.shape[0], 8, cells)), axis=0).T[:, :1]
    group, _, _ = position()
    for at, tile in enumerate(tiles_of(which, bits)):
        lanes = pl.ds(pl.multiple_of(tile * width, width), width)
        rows = quads[:, lanes]
        owner = rows // depth
        slot = jnp.bitwise_xor(owner, group)
        if offsets != tuple(range(len(offsets))):
            slot = functools.reduce(jnp.add, [jnp.where(slot == k, n, 0) for n, k in enumerate(offsets)])
        places = (slot * depth + (rows - owner * depth)).astype(jnp.int16)
        source = jnp.dot(turned[...], difference_map(places, 0, turned.shape[1]), preferred_element_type=F32)
        receiver = jnp.dot(turned[...], difference_map(places, 2, turned.shape[1]), preferred_element_type=F32)
        product = source * receiver
        dots = product[:cells] + product[cells : 2 * cells] + product[2 * cells :]
        out[:, at * width : (at + 1) * width] = (weight[:, lanes] * -(column * dots)).astype(BF16)


def sensitivities(which, bits, quads, weight, volume, shards, turned=None, ready=(), weigh=1):
    offsets = tuple(ready) + tuple(sorted(shards))
    held = [shards[k] for k in offsets[len(ready) :]]
    _, depth, cells = held[0].shape
    count, width = 2, quads.shape[1] // TILES
    flops = weigh * 4 * count * width * len(offsets) * depth * 3 * cells
    return whole_call(
        functools.partial(sensitivity_kernel, offsets, len(ready), which, bits),
        "sensitivities",
        jax.ShapeDtypeStruct((cells, count * width), BF16),
        [pltpu.VMEM((3 * cells, len(offsets) * depth), BF16)],
        quads, weight, volume, *([turned] if ready else []), *held,
        flops=flops,
    )


def same_columns(left, right):
    return lax.dot_general(left, right, (((1,), (1,)), ((), ())), preferred_element_type=F32)


def rows_of(core, cells):
    return pl.ds(pl.multiple_of(core * cells, cells), cells)


def early_kernel(evens, own_send, own_keep, other_send, other_keep, *refs):
    count, (_, chip, core) = len(evens), position()
    recomputed, mine, swap = refs[:count], *refs[count : count + 2]
    mirrors, pair = refs[count + 2 : -1], refs[-1]
    cells = own_send.shape[0]
    here, there = rows_of(core, cells), rows_of(1 - core, cells)
    sides = ((0, own_send, other_send), (1, own_keep, other_keep))
    for at, d in enumerate(evens):
        part = own_send.shape[1] // 2
        for bit in range(2):

            @pl.when(bit_of(chip, low_bit(d)) == bit)
            def _():
                lanes = slice(bit * part, (bit + 1) * part)
                columns = [jnp.concatenate([own[:, lanes], other[:, lanes]], axis=0) for _, own, other in sides]
                blocks = same_columns(recomputed[at][...], jnp.concatenate(columns, axis=1))
                pair[0], pair[1] = jnp.split(blocks, 2, axis=1)

        mine[at] = pair[0]
        swap[at] = pair[1].astype(BF16)
        mirrors[at][here, :] = pair[0].T.astype(BF16)
        mirrors[at][there, :] = pair[1].T.astype(BF16)


def own_kernel(own_send, own_keep, other_send, other_keep, out):
    cells = own_send.shape[0]
    sides = ((own_send[...], other_send[...]), (own_keep[...], other_keep[...]))
    _, _, core = position()
    both = functools.reduce(jnp.add, [same_columns(own, jnp.concatenate([own, other], axis=0)) for own, other in sides])
    out[rows_of(core, cells), :] = both[:, :cells]
    out[rows_of(1 - core, cells), :] = both[:, cells:].T


def late_kernel(odds, own_keep, other_keep, *refs):
    count, (_, _, core) = len(odds), position()
    received, mine, swap, mirrors = refs[:count], refs[count], refs[count + 1], refs[count + 2 :]
    cells = own_keep.shape[0]
    here, there = rows_of(core, cells), rows_of(1 - core, cells)
    rows = jnp.concatenate([r[...] for r in received], axis=0)
    blocks = same_columns(rows, jnp.concatenate([own_keep[...], other_keep[...]], axis=0))
    for at in range(count):
        block, across = jnp.split(blocks[at * cells : (at + 1) * cells], 2, axis=1)
        mine[at] = block
        swap[at] = across.astype(BF16)
        mirrors[at][here, :] = block.astype(BF16).T
        mirrors[at][there, :] = across.astype(BF16).T


def diagonal(cells):
    return lax.broadcasted_iota(I32, (cells, cells), 0) == lax.broadcasted_iota(I32, (cells, cells), 1)


def combine_kernel(evens, odds, own_block, *refs):
    (mine_group, chip, core), every = position(), refs[-1]
    cells = own_block.shape[1]
    here, there = rows_of(core, cells), rows_of(1 - core, cells)
    every[0] = own_block[...]
    at = 0
    for group in (evens, odds):
        mine, swapped, mirrored = refs[at], refs[at + 1], refs[at + 2 : at + 2 + len(group)]
        at += 2 + len(group)
        for i, d in enumerate(group):
            every[d, here, :] = mine[i] + mirrored[i][here, :].astype(F32)
            every[d, there, :] = swapped[i].astype(F32) + mirrored[i][there, :].astype(F32)
    out_own, outs = refs[at], refs[at + 1 : -1]
    first = jnp.bitwise_xor(mine_group, chip)
    out_own[...] = every[first]
    for k, out in enumerate(outs, 1):
        d = jnp.bitwise_xor(first, k)
        out[: 2 * cells, :] = every[d].astype(BF16)
        square = every[d, here, :]
        lost = jnp.where(diagonal(cells), square - square.astype(BF16).astype(F32), 0.0)
        out[2 * cells :, :] = jnp.broadcast_to(jnp.sum(lost, axis=0, keepdims=True), (16, cells)).astype(BF16)


def final_kernel(amount, own, *refs):
    received, out = refs[:-1], refs[-1]
    cells = own.shape[1]
    total = own[...]
    for part in received:
        total = total + part[: 2 * cells, :].astype(F32)
    out[...] = total / amount
    lost = functools.reduce(jnp.add, [part[2 * cells : 2 * cells + 1, :].astype(F32) for part in received])
    here = rows_of(position()[2], cells)
    out[here, :] += jnp.where(diagonal(cells), lost / amount, 0.0)


def whole_call(kernel, name, shapes, scratch, *arrays, flops=1000):
    vmem = pl.BlockSpec(memory_space=pltpu.VMEM)
    many = isinstance(shapes, list)
    return pl.pallas_call(
        kernel,
        in_specs=[vmem] * len(arrays),
        out_specs=[vmem] * len(shapes) if many else vmem,
        out_shape=shapes,
        scratch_shapes=scratch,
        compiler_params=params(),
        cost_estimate=pl.CostEstimate(flops=flops, bytes_accessed=1, transcendentals=0),
        name=name,
    )(*arrays)


def per_device(grads, quads, volume, weight):
    groups, devices = lax.axis_size("elec"), lax.axis_size("cell")
    chips = devices // 2
    cells, measured = grads.shape[2], quads.shape[0]
    half, far = groups // 2, groups - 1
    odds = [d for d in range(1, chips) if odd(d)]
    evens = [d for d in range(1, chips) if not odd(d)]
    packed = pack(grads, volume)
    shape = grads.shape
    gradients = lambda x: x[: 3 * shape[1], :].reshape(shape)
    shards = {0: grads, far: hop(grads, "elec", groups, far)}
    for j in range(1, half):
        shards[j] = gradients(hop(packed, "elec", groups, j))
    for j in range(1, half):
        shards[far ^ j] = hop(shards[far], "elec", groups, j)

    bits = max(1, (chips - 1).bit_length())
    columns, weights = quads.T, weight.reshape(1, measured)
    volumes = volume.reshape(1, cells)
    relayed = {far ^ j: shards[far ^ j] for j in range(1, half)}
    direct = {k: shards[k] for k in shards if k not in relayed}
    ready = tuple(sorted(direct))
    turned = turn_shards([direct[k] for k in ready])

    across, volumes_across = {}, {}
    for d in evens:
        near = hop(packed, "cell", devices, 2 * d)
        near, volumes_across[d] = gradients(near), near[3 * shape[1] :, :]
        across[d] = {0: near}
        for k in [far, *range(1, half)]:
            across[d][k] = hop(shards[k], "cell", devices, 2 * d)

    form = functools.partial(sensitivities, bits=bits)
    own_send = form("send", quads=columns, weight=weights, volume=volumes, shards=relayed, turned=turned, ready=ready)
    received = [hop(own_send, "cell", devices, 2 * d) for d in odds]
    other_send = hop(own_send, "cell", devices, 1)
    columns, own_send, across = lax.optimization_barrier((columns, own_send, across))
    for d in evens:
        for j in range(1, half):
            across[d][far ^ j] = hop(across[d][far], "elec", groups, j)
    own_keep = form("keep", quads=columns, weight=weights, volume=volumes, shards=relayed, turned=turned, ready=ready)
    other_keep = hop(own_keep, "cell", devices, 1)
    recomputed = []
    for d in evens:
        recomputed.append(
            form(d, quads=columns, weight=weights, volume=volumes_across[d], shards=across[d], weigh=WEIGH)
        )

    whole, small = (2 * cells, cells), (cells, cells)
    outputs = lambda group: [
        jax.ShapeDtypeStruct((len(group), *small), F32),
        jax.ShapeDtypeStruct((len(group), *small), BF16),
    ] + [jax.ShapeDtypeStruct(whole, BF16)] * len(group)
    early = whole_call(
        functools.partial(early_kernel, evens),
        "early_blocks",
        outputs(evens),
        [pltpu.VMEM((2, *small), F32)],
        own_send, own_keep, other_send, other_keep, *recomputed,
    )
    late = whole_call(functools.partial(late_kernel, odds), "late_blocks", outputs(odds), [], own_keep, other_keep, *received)

    own_keep, late = lax.optimization_barrier((own_keep, late))
    own_block = whole_call(
        own_kernel, "own_block", jax.ShapeDtypeStruct(whole, F32), [], own_send, own_keep, other_send, other_keep
    )

    def exchange(group, mine, swap, *mirrors):
        moved = [hop(m, "cell", devices, 2 * d) for d, m in zip(group, mirrors)]
        return [mine, hop(swap, "cell", devices, 1)] + moved

    parts = whole_call(
        functools.partial(combine_kernel, evens, odds),
        "combine",
        [jax.ShapeDtypeStruct(whole, F32)] + [jax.ShapeDtypeStruct((2 * cells + 16, cells), BF16)] * (groups - 1),
        [pltpu.VMEM((chips, *whole), F32)],
        own_block, *exchange(evens, *early), *exchange(odds, *late),
    )
    arrived = [hop(parts[k], "elec", groups, k) for k in sorted(range(1, groups), key=lambda k: (k < half, k))]
    return whole_call(
        functools.partial(final_kernel, float(measured * groups)),
        "finish",
        jax.ShapeDtypeStruct(whole, F32),
        [],
        parts[0], *arrived,
    )


def solution(mesh):
    placed = (P(None, "elec", "cell"), P("elec", None), P("cell"), P("elec"))
    return jax.shard_map(
        per_device, mesh=mesh, in_specs=placed, out_specs=P("elec", "cell"), check_vma=False
    )
```

time: 56.9 us -> 54.9 us (0.965)
  Pallas kernels: 18 us -> 13.7 us
  waiting for transfers between devices: 10.2 us -> 13.7 us
  starting transfers between devices: 27 us -> 26.3 us
    pallas_call x8, Pallas kernels: 17.7 us -> 13.4 us  [whole_call(): pl.pallas_call(kernel, in_specs=[vmem] * len(arrays), out_specs=[vmem] *...]
    ppermute x19, waiting for transfers between devices: 10.2 us -> 13.7 us  [hop(): return lax.ppermute(x, axis, [(i, i ^ mask) for i in range(size)])]
    ppermute x19, starting transfers between devices: 27 us -> 26.3 us  [hop(): return lax.ppermute(x, axis, [(i, i ^ mask) for i in range(size)])]
  transfers between devices with their start and end apart: 19 -> 19, of which waited for: 7 -> 9; matrix products, arithmetic and copies ran while one was open for 1% -> 0% of each run, Pallas kernels for 28% -> 23%
where the time goes in v5:
time: 54.9 us; the launch traced here: 54.8 us
  starting transfers between devices  26.3 us (48%)
  Pallas kernels  13.7 us (25%)
  waiting for transfers between devices  13.7 us (25%)
  local copies, waits for them, and re-layouts  1 us (2%)
    ppermute x19, starting transfers between devices, hop(): return lax.ppermute(x, axis, [(i, i ^ mask) for i in range(size)])  26.3 us
    ppermute x19, waiting for transfers between devices, hop(): return lax.ppermute(x, axis, [(i, i ^ mask) for i in range(size)])  13.7 us
    pallas_call x8, Pallas kernels, whole_call(): pl.pallas_call(kernel, in_specs=[vmem] * len(arrays), out_specs=[vmem] *...  13.4 us
  transfers between devices with their start and end apart: 19, of which 9 were waited for; matrix products, arithmetic and copies ran while one was open for 0% of the time, Pallas kernels for 23%

profile of v5, /device:TPU:0, one launch (start us, length us, event | category | flops | bytes accessed | tf_op | source)
XLA Modules:
  0.0 54.8 jit_solution(5728083673401481583)
XLA Ops:
  0.0 5.0 %collective-permute-start.1 = (bf16[3,256,128]{2,1,0:T(8,128)(2,1)}, bf16[3,256,128]{2,1,0:T(8,128)(2,1)S(1)}, u32[]{:S(2)}, u32[]{:S(2)}) collective-permute-start(bf16[3,256,128]{2,1,0:T(8,128)(2,1)} %refs_0_.1), channel_id=1, source_target_pairs={{0,24},{8,16},{16,8},{24,0},{1,25},{9,17},{17,9},{25,1},{2,26},{10... | collective-permute-start | bytes 589832 | tf_op jit(solution)/shard_map/ppermute | solution.py:21
  5.1 1.0 %copy-done = bf16[3,256,128]{2,1,0:T(8,128)(2,1)S(1)} copy-done((bf16[3,256,128]{2,1,0:T(8,128)(2,1)S(1)}, bf16[3,256,128]{2,1,0:T(8,128)(2,1)}, u32[]{:S(2)}) %copy-start) | copy-done | bytes 196632
  6.1 2.5 %collective-permute-start.3 = (bf16[784,128]{1,0:T(8,128)(2,1)S(1)}, bf16[784,128]{1,0:T(8,128)(2,1)S(1)}, u32[]{:S(2)}, u32[]{:S(2)}) collective-permute-start(bf16[784,128]{1,0:T(8,128)(2,1)S(1)} %pack.1), channel_id=1, source_target_pairs={{0,6},{1,7},{2,4},{3,5},{4,2},{5,3},{6,0},{7,1},{8,14},{9,15},{10,... | collective-permute-start | bytes 602120 | tf_op jit(solution)/shard_map/ppermute | solution.py:21
  8.6 2.4 %collective-permute-done.1.refs_2_ = bf16[3,256,128]{2,1,0:T(8,128)(2,1)S(1)} collective-permute-done((bf16[3,256,128]{2,1,0:T(8,128)(2,1)}, bf16[3,256,128]{2,1,0:T(8,128)(2,1)S(1)}, u32[]{:S(2)}, u32[]{:S(2)}) %collective-permute-start.1) | collective-permute-done | bytes 196640 | tf_op jit(solution)/shard_map/ppermute | solution.py:21
  11.0 3.1 %collective-permute-start.2 = (bf16[3,256,128]{2,1,0:T(8,128)(2,1)S(1)}, bf16[3,256,128]{2,1,0:T(8,128)(2,1)S(1)}, u32[]{:S(2)}, u32[]{:S(2)}) collective-permute-start(bf16[3,256,128]{2,1,0:T(8,128)(2,1)S(1)} %collective-permute-done.1.refs_2_), channel_id=1, source_target_pairs={{0,8},{8,0},{16,24},{24,16},{1,9},{9,1},{17,25},{25,17},{2,10},{10... | collective-permute-start | bytes 589832 | tf_op jit(solution)/shard_map/ppermute | solution.py:21
  14.1 2.4 %collective-permute-start.5 = (bf16[3,256,128]{2,1,0:T(8,128)(2,1)S(1)}, bf16[3,256,128]{2,1,0:T(8,128)(2,1)S(1)}, u32[]{:S(2)}, u32[]{:S(2)}) collective-permute-start(bf16[3,256,128]{2,1,0:T(8,128)(2,1)S(1)} %collective-permute-done.1.refs_2_), channel_id=1, source_target_pairs={{0,6},{1,7},{2,4},{3,5},{4,2},{5,3},{6,0},{7,1},{8,14},{9,15},{10,... | collective-permute-start | bytes 589832 | tf_op jit(solution)/shard_map/ppermute | solution.py:21
  16.6 0.7 %collective-permute-start.4 = (bf16[3,256,128]{2,1,0:T(8,128)(2,1)S(1)}, bf16[3,256,128]{2,1,0:T(8,128)(2,1)S(1)}, u32[]{:S(2)}, u32[]{:S(2)}) collective-permute-start(bf16[3,256,128]{2,1,0:T(8,128)(2,1)S(1)} %bitcast.5), channel_id=1, source_target_pairs={{0,6},{1,7},{2,4},{3,5},{4,2},{5,3},{6,0},{7,1},{8,14},{9,15},{10,... | collective-permute-start | bytes 589832 | tf_op jit(solution)/shard_map/ppermute | solution.py:21
  17.3 0.2 turn_shards.1.refs_0_
  17.6 1.2 %collective-permute-done.2.refs_1_ = bf16[3,256,128]{2,1,0:T(8,128)(2,1)S(1)} collective-permute-done((bf16[3,256,128]{2,1,0:T(8,128)(2,1)S(1)}, bf16[3,256,128]{2,1,0:T(8,128)(2,1)S(1)}, u32[]{:S(2)}, u32[]{:S(2)}) %collective-permute-start.2) | collective-permute-done | bytes 196640 | tf_op jit(solution)/shard_map/ppermute | solution.py:21
  18.8 3.5 %sensitivities.3.own_send = bf16[128,2048]{1,0:T(8,128)(2,1)S(1)} custom-call(s32[4,4096]{1,0:T(4,128)S(1)} %bitcast.11, f32[1,4096]{1,0:T(1,128)S(1)} %bitcast.14, f32[1,128]{1,0:T(1,128)S(1)} %bitcast.9, bf16[384,768]{1,0:T(8,128)(2,1)S(1)} %turn_shards.1.refs_0_, bf16[3,256,128]{2,1,0:T(8,128)(2,1)S(1)} %collective-permute-done.2.refs_1_), custom_call_target="tpu_custom_call" | custom-call | flops 3221225472 | bytes 1 | tf_op jit(solution)/shard_map/sensitivities/pallas_call | solution.py:245
  22.4 1.6 %collective-permute-start.8 = (bf16[128,2048]{1,0:T(8,128)(2,1)S(1)}, bf16[128,2048]{1,0:T(8,128)(2,1)S(1)}, u32[]{:S(2)}, u32[]{:S(2)}) collective-permute-start(bf16[128,2048]{1,0:T(8,128)(2,1)S(1)} %sensitivities.3.own_send), channel_id=1, source_target_pairs={{0,4},{1,5},{2,6},{3,7},{4,0},{5,1},{6,2},{7,3},{8,12},{9,13},{10,... | collective-permute-start | bytes 1572872 | tf_op jit(solution)/shard_map/ppermute | solution.py:21
  24.0 1.5 %collective-permute-start.7 = (bf16[128,2048]{1,0:T(8,128)(2,1)S(1)}, bf16[128,2048]{1,0:T(8,128)(2,1)S(1)}, u32[]{:S(2)}, u32[]{:S(2)}) collective-permute-start(bf16[128,2048]{1,0:T(8,128)(2,1)S(1)} %sensitivities.3.own_send), channel_id=1, source_target_pairs={{0,2},{1,3},{2,0},{3,1},{4,6},{5,7},{6,4},{7,5},{8,10},{9,11},{10,... | collective-permute-start | bytes 1572872 | tf_op jit(solution)/shard_map/ppermute | solution.py:21
  25.5 1.7 %collective-permute-start.10 = (bf16[3,256,128]{2,1,0:T(8,128)(2,1)S(1)}, bf16[3,256,128]{2,1,0:T(8,128)(2,1)S(1)}, u32[]{:S(2)}, u32[]{:S(2)}) collective-permute-start(bf16[3,256,128]{2,1,0:T(8,128)(2,1)S(1)} %collective-permute-done.5.refs_3_), channel_id=1, source_target_pairs={{0,8},{8,0},{16,24},{24,16},{1,9},{9,1},{17,25},{25,17},{2,10},{10... | collective-permute-start | bytes 589832 | tf_op jit(solution)/shard_map/ppermute | solution.py:21
  27.2 3.5 %sensitivities.4.own_keep = bf16[128,2048]{1,0:T(8,128)(2,1)S(1)} custom-call(s32[4,4096]{1,0:T(4,128)S(1)} %bitcast.12, f32[1,4096]{1,0:T(1,128)S(1)} %bitcast.15, f32[1,128]{1,0:T(1,128)S(1)} %bitcast.10, bf16[384,768]{1,0:T(8,128)(2,1)S(1)} %turn_shards.1.refs_0_, bf16[3,256,128]{2,1,0:T(8,128)(2,1)S(1)} %collective-permute-done.2.refs_1_), custom_call_target="tpu_custom_call" | custom-call | flops 3221225472 | bytes 1 | tf_op jit(solution)/shard_map/sensitivities/pallas_call | solution.py:245
  30.8 1.4 %collective-permute-done.10.refs_2_ = bf16[3,256,128]{2,1,0:T(8,128)(2,1)S(1)} collective-permute-done((bf16[3,256,128]{2,1,0:T(8,128)(2,1)S(1)}, bf16[3,256,128]{2,1,0:T(8,128)(2,1)S(1)}, u32[]{:S(2)}, u32[]{:S(2)}) %collective-permute-start.10) | collective-permute-done | bytes 196640 | tf_op jit(solution)/shard_map/ppermute | solution.py:21
  32.2 3.5 %sensitivities.5.refs_0_ = bf16[128,2048]{1,0:T(8,128)(2,1)S(1)} custom-call(s32[4,4096]{1,0:T(4,128)S(1)} %bitcast.13, f32[1,4096]{1,0:T(1,128)S(1)} %bitcast.16, bf16[16,128]{1,0:T(8,128)(2,1)S(1)} %slice.14.volume, bf16[3,256,128]{2,1,0:T(8,128)(2,1)S(1)} %bitcast.7, bf16[3,256,128]{2,1,0:T(8,128)(2,1)S(1)} %collective-permute-done.4.refs_1_, ...), custom_call_target="tpu_custom_call" | custom-call | flops 12884901888 | bytes 1 | tf_op jit(solution)/shard_map/sensitivities/pallas_call | solution.py:245
  35.7 0.6 %early_blocks.1 = (f32[1,128,128]{2,1,0:T(8,128)S(1)}, bf16[1,128,128]{2,1,0:T(8,128)(2,1)S(1)}, bf16[256,128]{1,0:T(8,128)(2,1)S(1)}) custom-call(bf16[128,2048]{1,0:T(8,128)(2,1)S(1)} %sensitivities.3.own_send, bf16[128,2048]{1,0:T(8,128)(2,1)S(1)} %sensitivities.4.own_keep, bf16[128,2048]{1,0:T(8,128)(2,1)S(1)} %collective-permute-done.9.other_send, ...), custom_call_target="tpu_custom_call" | custom-call | flops 1000 | bytes 1 | tf_op jit(solution)/shard_map/early_blocks/pallas_call | solution.py:245
  36.3 0.9 %collective-permute-start.12 = (bf16[256,128]{1,0:T(8,128)(2,1)S(1)}, bf16[256,128]{1,0:T(8,128)(2,1)S(1)}, u32[]{:S(2)}, u32[]{:S(2)}) collective-permute-start(bf16[256,128]{1,0:T(8,128)(2,1)S(1)} %get-tuple-element.38), channel_id=1, source_target_pairs={{0,6},{1,7},{2,4},{3,5},{4,2},{5,3},{6,0},{7,1},{8,14},{9,15},{10,... | collective-permute-start | bytes 196616 | tf_op jit(solution)/shard_map/ppermute | solution.py:21
  37.2 0.7 %collective-permute-done.7.refs_0_ = bf16[128,2048]{1,0:T(8,128)(2,1)S(1)} collective-permute-done((bf16[128,2048]{1,0:T(8,128)(2,1)S(1)}, bf16[128,2048]{1,0:T(8,128)(2,1)S(1)}, u32[]{:S(2)}, u32[]{:S(2)}) %collective-permute-start.7) | collective-permute-done | bytes 524320 | tf_op jit(solution)/shard_map/ppermute | solution.py:21
  38.0 0.5 late_blocks.1
  38.6 2.3 %collective-permute-start.14 = (bf16[256,128]{1,0:T(8,128)(2,1)S(1)}, bf16[256,128]{1,0:T(8,128)(2,1)S(1)}, u32[]{:S(2)}, u32[]{:S(2)}) collective-permute-start(bf16[256,128]{1,0:T(8,128)(2,1)S(1)} %get-tuple-element.41), channel_id=1, source_target_pairs={{0,2},{1,3},{2,0},{3,1},{4,6},{5,7},{6,4},{7,5},{8,10},{9,11},{10,... | collective-permute-start | bytes 196616 | tf_op jit(solution)/shard_map/ppermute | solution.py:21
  40.9 0.2 collective-permute-start.11
  41.0 0.9 %own_block.1 = f32[256,128]{1,0:T(8,128)S(1)} custom-call(bf16[128,2048]{1,0:T(8,128)(2,1)S(1)} %sensitivities.3.own_send, bf16[128,2048]{1,0:T(8,128)(2,1)S(1)} %sensitivities.4.own_keep, bf16[128,2048]{1,0:T(8,128)(2,1)S(1)} %collective-permute-done.9.other_send, bf16[128,2048]{1,0:T(8,128)(2,1)S(1)} %collective-permute-done.6.other_keep), custom_call_target="tpu_custom_call" | custom-call | flops 1000 | bytes 1 | tf_op jit(solution)/shard_map/own_block/pallas_call | solution.py:245
  41.9 0.2 collective-permute-done.11.refs_1_
  42.1 1.5 %collective-permute-done.14.refs_5_ = bf16[256,128]{1,0:T(8,128)(2,1)S(1)} collective-permute-done((bf16[256,128]{1,0:T(8,128)(2,1)S(1)}, bf16[256,128]{1,0:T(8,128)(2,1)S(1)}, u32[]{:S(2)}, u32[]{:S(2)}) %collective-permute-start.14) | collective-permute-done | bytes 65568 | tf_op jit(solution)/shard_map/ppermute | solution.py:21
  43.6 1.6 %collective-permute-done.15.refs_6_ = bf16[256,128]{1,0:T(8,128)(2,1)S(1)} collective-permute-done((bf16[256,128]{1,0:T(8,128)(2,1)S(1)}, bf16[256,128]{1,0:T(8,128)(2,1)S(1)}, u32[]{:S(2)}, u32[]{:S(2)}) %collective-permute-start.15) | collective-permute-done | bytes 65568 | tf_op jit(solution)/shard_map/ppermute | solution.py:21
  45.1 0.1 combine.1
  45.2 1.8 %collective-permute-start.16 = (bf16[272,128]{1,0:T(8,128)(2,1)S(1)}, bf16[272,128]{1,0:T(8,128)(2,1)S(1)}, u32[]{:S(2)}, u32[]{:S(2)}) collective-permute-start(bf16[272,128]{1,0:T(8,128)(2,1)S(1)} %get-tuple-element.44), channel_id=1, source_target_pairs={{0,16},{8,24},{16,0},{24,8},{1,17},{9,25},{17,1},{25,9},{2,18},{10... | collective-permute-start | bytes 208904 | tf_op jit(solution)/shard_map/ppermute | solution.py:21
  47.1 2.3 %collective-permute-start.17 = (bf16[272,128]{1,0:T(8,128)(2,1)S(1)}, bf16[272,128]{1,0:T(8,128)(2,1)S(1)}, u32[]{:S(2)}, u32[]{:S(2)}) collective-permute-start(bf16[272,128]{1,0:T(8,128)(2,1)S(1)} %get-tuple-element.45), channel_id=1, source_target_pairs={{0,24},{8,16},{16,8},{24,0},{1,25},{9,17},{17,9},{25,1},{2,26},{10... | collective-permute-start | bytes 208904 | tf_op jit(solution)/shard_map/ppermute | solution.py:21
  49.4 4.1 %collective-permute-done.16.refs_0_ = bf16[272,128]{1,0:T(8,128)(2,1)S(1)} collective-permute-done((bf16[272,128]{1,0:T(8,128)(2,1)S(1)}, bf16[272,128]{1,0:T(8,128)(2,1)S(1)}, u32[]{:S(2)}, u32[]{:S(2)}) %collective-permute-start.16) | collective-permute-done | bytes 69664 | tf_op jit(solution)/shard_map/ppermute | solution.py:21
  53.5 0.6 %collective-permute-done.18.refs_2_ = bf16[272,128]{1,0:T(8,128)(2,1)S(1)} collective-permute-done((bf16[272,128]{1,0:T(8,128)(2,1)S(1)}, bf16[272,128]{1,0:T(8,128)(2,1)S(1)}, u32[]{:S(2)}, u32[]{:S(2)}) %collective-permute-start.18) | collective-permute-done | bytes 69664 | tf_op jit(solution)/shard_map/ppermute | solution.py:21
  54.1 0.7 %finish.1 = f32[256,128]{1,0:T(8,128)} custom-call(f32[256,128]{1,0:T(8,128)S(1)} %get-tuple-element.43.own, bf16[272,128]{1,0:T(8,128)(2,1)S(1)} %collective-permute-done.16.refs_0_, bf16[272,128]{1,0:T(8,128)(2,1)S(1)} %collective-permute-done.17.refs_1_, bf16[272,128]{1,0:T(8,128)(2,1)S(1)} %collective-permute-done.18.refs_2_), custom_call_target="tpu_custom_call" | custom-call | flops 1000 | bytes 1 | tf_op jit(solution)/shard_map/finish/pallas_call | solution.py:245
  (27 shorter events, 0.4 us)
Async XLA Ops:
  0.0 5.1 %copy-start.1 = (f32[128]{0:T(128)S(1)}, f32[128]{0:T(128)}, u32[]{:S(2)}) copy-start(f32[128]{0:T(128)} %param.6) | copy-start | bytes 1540
  0.0 11.0 %collective-permute-start.1 = (bf16[3,256,128]{2,1,0:T(8,128)(2,1)}, bf16[3,256,128]{2,1,0:T(8,128)(2,1)S(1)}, u32[]{:S(2)}, u32[]{:S(2)}) collective-permute-start(bf16[3,256,128]{2,1,0:T(8,128)(2,1)} %refs_0_.1), channel_id=1, source_target_pairs={{0,24},{8,16},{16,8},{24,0},{1,25},{9,17},{17,9},{25,1},{2,26},{10... | collective-permute-start | bytes 589832 | tf_op jit(solution)/shard_map/ppermute | solution.py:21
  5.1 1.0 %copy-start = (bf16[3,256,128]{2,1,0:T(8,128)(2,1)S(1)}, bf16[3,256,128]{2,1,0:T(8,128)(2,1)}, u32[]{:S(2)}) copy-start(bf16[3,256,128]{2,1,0:T(8,128)(2,1)} %refs_0_.1) | copy-start | bytes 589828
  6.0 10.5 %collective-permute-start = (bf16[784,128]{1,0:T(8,128)(2,1)S(1)}, bf16[784,128]{1,0:T(8,128)(2,1)S(1)}, u32[]{:S(2)}, u32[]{:S(2)}) collective-permute-start(bf16[784,128]{1,0:T(8,128)(2,1)S(1)} %pack.1), channel_id=1, source_target_pairs={{0,8},{8,0},{16,24},{24,16},{1,9},{9,1},{17,25},{25,17},{2,10},{10... | collective-permute-start | bytes 602120 | tf_op jit(solution)/shard_map/ppermute | solution.py:21
  6.1 11.4 %collective-permute-start.3 = (bf16[784,128]{1,0:T(8,128)(2,1)S(1)}, bf16[784,128]{1,0:T(8,128)(2,1)S(1)}, u32[]{:S(2)}, u32[]{:S(2)}) collective-permute-start(bf16[784,128]{1,0:T(8,128)(2,1)S(1)} %pack.1), channel_id=1, source_target_pairs={{0,6},{1,7},{2,4},{3,5},{4,2},{5,3},{6,0},{7,1},{8,14},{9,15},{10,... | collective-permute-start | bytes 602120 | tf_op jit(solution)/shard_map/ppermute | solution.py:21
  11.0 7.7 %collective-permute-start.2 = (bf16[3,256,128]{2,1,0:T(8,128)(2,1)S(1)}, bf16[3,256,128]{2,1,0:T(8,128)(2,1)S(1)}, u32[]{:S(2)}, u32[]{:S(2)}) collective-permute-start(bf16[3,256,128]{2,1,0:T(8,128)(2,1)S(1)} %collective-permute-done.1.refs_2_), channel_id=1, source_target_pairs={{0,8},{8,0},{16,24},{24,16},{1,9},{9,1},{17,25},{25,17},{2,10},{10... | collective-permute-start | bytes 589832 | tf_op jit(solution)/shard_map/ppermute | solution.py:21
  14.1 11.4 %collective-permute-start.5 = (bf16[3,256,128]{2,1,0:T(8,128)(2,1)S(1)}, bf16[3,256,128]{2,1,0:T(8,128)(2,1)S(1)}, u32[]{:S(2)}, u32[]{:S(2)}) collective-permute-start(bf16[3,256,128]{2,1,0:T(8,128)(2,1)S(1)} %collective-permute-done.1.refs_2_), channel_id=1, source_target_pairs={{0,6},{1,7},{2,4},{3,5},{4,2},{5,3},{6,0},{7,1},{8,14},{9,15},{10,... | collective-permute-start | bytes 589832 | tf_op jit(solution)/shard_map/ppermute | solution.py:21
  16.6 8.9 %collective-permute-start.4 = (bf16[3,256,128]{2,1,0:T(8,128)(2,1)S(1)}, bf16[3,256,128]{2,1,0:T(8,128)(2,1)S(1)}, u32[]{:S(2)}, u32[]{:S(2)}) collective-permute-start(bf16[3,256,128]{2,1,0:T(8,128)(2,1)S(1)} %bitcast.5), channel_id=1, source_target_pairs={{0,6},{1,7},{2,4},{3,5},{4,2},{5,3},{6,0},{7,1},{8,14},{9,15},{10,... | collective-permute-start | bytes 589832 | tf_op jit(solution)/shard_map/ppermute | solution.py:21
  17.5 1.3 %copy-start.2 = (s32[4096,4]{0,1:T(4,128)S(1)}, s32[4096,4]{0,1:T(4,128)}, u32[]{:S(2)}) copy-start(s32[4096,4]{0,1:T(4,128)} %param.5) | copy-start | bytes 196612
  17.5 1.3 %copy-start.3 = (f32[4096]{0:T(1024)S(1)}, f32[4096]{0:T(1024)}, u32[]{:S(2)}) copy-start(f32[4096]{0:T(1024)} %param.7) | copy-start | bytes 49156
  22.3 13.4 %collective-permute-start.9 = (bf16[128,2048]{1,0:T(8,128)(2,1)S(1)}, bf16[128,2048]{1,0:T(8,128)(2,1)S(1)}, u32[]{:S(2)}, u32[]{:S(2)}) collective-permute-start(bf16[128,2048]{1,0:T(8,128)(2,1)S(1)} %sensitivities.3.own_send), channel_id=1, source_target_pairs={{0,1},{1,0},{2,3},{3,2},{4,5},{5,4},{6,7},{7,6},{8,9},{9,8},{10,11... | collective-permute-start | bytes 1572872 | tf_op jit(solution)/shard_map/ppermute | solution.py:21
  22.4 14.8 %collective-permute-start.8 = (bf16[128,2048]{1,0:T(8,128)(2,1)S(1)}, bf16[128,2048]{1,0:T(8,128)(2,1)S(1)}, u32[]{:S(2)}, u32[]{:S(2)}) collective-permute-start(bf16[128,2048]{1,0:T(8,128)(2,1)S(1)} %sensitivities.3.own_send), channel_id=1, source_target_pairs={{0,4},{1,5},{2,6},{3,7},{4,0},{5,1},{6,2},{7,3},{8,12},{9,13},{10,... | collective-permute-start | bytes 1572872 | tf_op jit(solution)/shard_map/ppermute | solution.py:21
  24.0 14.0 %collective-permute-start.7 = (bf16[128,2048]{1,0:T(8,128)(2,1)S(1)}, bf16[128,2048]{1,0:T(8,128)(2,1)S(1)}, u32[]{:S(2)}, u32[]{:S(2)}) collective-permute-start(bf16[128,2048]{1,0:T(8,128)(2,1)S(1)} %sensitivities.3.own_send), channel_id=1, source_target_pairs={{0,2},{1,3},{2,0},{3,1},{4,6},{5,7},{6,4},{7,5},{8,10},{9,11},{10,... | collective-permute-start | bytes 1572872 | tf_op jit(solution)/shard_map/ppermute | solution.py:21
  25.5 6.7 %collective-permute-start.10 = (bf16[3,256,128]{2,1,0:T(8,128)(2,1)S(1)}, bf16[3,256,128]{2,1,0:T(8,128)(2,1)S(1)}, u32[]{:S(2)}, u32[]{:S(2)}) collective-permute-start(bf16[3,256,128]{2,1,0:T(8,128)(2,1)S(1)} %collective-permute-done.5.refs_3_), channel_id=1, source_target_pairs={{0,8},{8,0},{16,24},{24,16},{1,9},{9,1},{17,25},{25,17},{2,10},{10... | collective-permute-start | bytes 589832 | tf_op jit(solution)/shard_map/ppermute | solution.py:21
  30.7 5.0 %collective-permute-start.6 = (bf16[128,2048]{1,0:T(8,128)(2,1)S(1)}, bf16[128,2048]{1,0:T(8,128)(2,1)S(1)}, u32[]{:S(2)}, u32[]{:S(2)}) collective-permute-start(bf16[128,2048]{1,0:T(8,128)(2,1)S(1)} %sensitivities.4.own_keep), channel_id=1, source_target_pairs={{0,1},{1,0},{2,3},{3,2},{4,5},{5,4},{6,7},{7,6},{8,9},{9,8},{10,11... | collective-permute-start | bytes 1572872 | tf_op jit(solution)/shard_map/ppermute | solution.py:21
  36.3 5.7 %collective-permute-start.12 = (bf16[256,128]{1,0:T(8,128)(2,1)S(1)}, bf16[256,128]{1,0:T(8,128)(2,1)S(1)}, u32[]{:S(2)}, u32[]{:S(2)}) collective-permute-start(bf16[256,128]{1,0:T(8,128)(2,1)S(1)} %get-tuple-element.38), channel_id=1, source_target_pairs={{0,6},{1,7},{2,4},{3,5},{4,2},{5,3},{6,0},{7,1},{8,14},{9,15},{10,... | collective-permute-start | bytes 196616 | tf_op jit(solution)/shard_map/ppermute | solution.py:21
  38.5 3.6 %collective-permute-start.13 = (bf16[2,128,128]{2,1,0:T(8,128)(2,1)S(1)}, bf16[2,128,128]{2,1,0:T(8,128)(2,1)S(1)}, u32[]{:S(2)}, u32[]{:S(2)}) collective-permute-start(bf16[2,128,128]{2,1,0:T(8,128)(2,1)S(1)} %get-tuple-element.40), channel_id=1, source_target_pairs={{0,1},{1,0},{2,3},{3,2},{4,5},{5,4},{6,7},{7,6},{8,9},{9,8},{10,11... | collective-permute-start | bytes 196616 | tf_op jit(solution)/shard_map/ppermute | solution.py:21
  38.6 4.9 %collective-permute-start.14 = (bf16[256,128]{1,0:T(8,128)(2,1)S(1)}, bf16[256,128]{1,0:T(8,128)(2,1)S(1)}, u32[]{:S(2)}, u32[]{:S(2)}) collective-permute-start(bf16[256,128]{1,0:T(8,128)(2,1)S(1)} %get-tuple-element.41), channel_id=1, source_target_pairs={{0,2},{1,3},{2,0},{3,1},{4,6},{5,7},{6,4},{7,5},{8,10},{9,11},{10,... | collective-permute-start | bytes 196616 | tf_op jit(solution)/shard_map/ppermute | solution.py:21
  40.9 4.3 %collective-permute-start.15 = (bf16[256,128]{1,0:T(8,128)(2,1)S(1)}, bf16[256,128]{1,0:T(8,128)(2,1)S(1)}, u32[]{:S(2)}, u32[]{:S(2)}) collective-permute-start(bf16[256,128]{1,0:T(8,128)(2,1)S(1)} %get-tuple-element.42), channel_id=1, source_target_pairs={{0,4},{1,5},{2,6},{3,7},{4,0},{5,1},{6,2},{7,3},{8,12},{9,13},{10,... | collective-permute-start | bytes 196616 | tf_op jit(solution)/shard_map/ppermute | solution.py:21
  40.9 1.2 %collective-permute-start.11 = (bf16[1,128,128]{2,1,0:T(8,128)(2,1)S(1)}, bf16[1,128,128]{2,1,0:T(8,128)(2,1)S(1)}, u32[]{:S(2)}, u32[]{:S(2)}) collective-permute-start(bf16[1,128,128]{2,1,0:T(8,128)(2,1)S(1)} %get-tuple-element.37), channel_id=1, source_target_pairs={{0,1},{1,0},{2,3},{3,2},{4,5},{5,4},{6,7},{7,6},{8,9},{9,8},{10,11... | collective-permute-start | bytes 98312 | tf_op jit(solution)/shard_map/ppermute | solution.py:21
  45.2 8.2 %collective-permute-start.16 = (bf16[272,128]{1,0:T(8,128)(2,1)S(1)}, bf16[272,128]{1,0:T(8,128)(2,1)S(1)}, u32[]{:S(2)}, u32[]{:S(2)}) collective-permute-start(bf16[272,128]{1,0:T(8,128)(2,1)S(1)} %get-tuple-element.44), channel_id=1, source_target_pairs={{0,16},{8,24},{16,0},{24,8},{1,17},{9,25},{17,1},{25,9},{2,18},{10... | collective-permute-start | bytes 208904 | tf_op jit(solution)/shard_map/ppermute | solution.py:21
  47.1 6.4 %collective-permute-start.17 = (bf16[272,128]{1,0:T(8,128)(2,1)S(1)}, bf16[272,128]{1,0:T(8,128)(2,1)S(1)}, u32[]{:S(2)}, u32[]{:S(2)}) collective-permute-start(bf16[272,128]{1,0:T(8,128)(2,1)S(1)} %get-tuple-element.45), channel_id=1, source_target_pairs={{0,24},{8,16},{16,8},{24,0},{1,25},{9,17},{17,9},{25,1},{2,26},{10... | collective-permute-start | bytes 208904 | tf_op jit(solution)/shard_map/ppermute | solution.py:21
  49.4 4.7 %collective-permute-start.18 = (bf16[272,128]{1,0:T(8,128)(2,1)S(1)}, bf16[272,128]{1,0:T(8,128)(2,1)S(1)}, u32[]{:S(2)}, u32[]{:S(2)}) collective-permute-start(bf16[272,128]{1,0:T(8,128)(2,1)S(1)} %get-tuple-element.46), channel_id=1, source_target_pairs={{0,8},{8,0},{16,24},{24,16},{1,9},{9,1},{17,25},{25,17},{2,10},{10... | collective-permute-start | bytes 208904 | tf_op jit(solution)/shard_map/ppermute | solution.py:21

commit v6 on v5

--- a/solution.py
+++ b/solution.py
@@ -79,8 +79,9 @@
     )(*shards)
 
 
-def pack_kernel(shard, volume, out):
+def pack_kernel(shard, volume, quads, out, kept):
     parts, depth, cells = shard.shape
+    kept[...] = quads[...]
     for k in range(parts):
         out[k * depth : (k + 1) * depth, :] = shard[k]
     rest = volume[...]
@@ -92,19 +93,45 @@
     out[parts * depth :, :] = tail.astype(BF16)
 
 
-def pack(shard, volume):
+def pack(shard, volume, quads):
     parts, depth, cells = shard.shape
     return pl.pallas_call(
         pack_kernel,
-        out_shape=jax.ShapeDtypeStruct((parts * depth + 16, cells), BF16),
+        out_shape=[jax.ShapeDtypeStruct((parts * depth + 16, cells), BF16), jax.ShapeDtypeStruct(quads.shape, I32)],
         compiler_params=params(),
         cost_estimate=pl.CostEstimate(flops=1000, bytes_accessed=1000, transcendentals=0),
         name="pack",
-    )(shard, volume.reshape(1, cells))
-
-
-def sensitivity_kernel(offsets, ready, which, bits, quads, weight, volume, *refs):
-    shards, out, turned = refs[1 if ready else 0 : -2], refs[-2], refs[-1]
+    )(shard, volume.reshape(1, cells), quads)
+
+
+def products(offsets, rows, turned, depth):
+    group, _, _ = position()
+    total = len(offsets) * depth
+    owner = rows // depth
+    slot = jnp.bitwise_xor(owner, group)
+    if offsets != tuple(range(len(offsets))):
+        slot = functools.reduce(jnp.add, [jnp.where(slot == k, n + 1, 0) for n, k in enumerate(offsets)]) - 1
+    places = (slot * depth + (rows - owner * depth)).astype(jnp.int16)
+    return [
+        jnp.dot(turned[:, :total], difference_map(places, at, total), preferred_element_type=F32) for at in (0, 2)
+    ]
+
+
+def tile_lanes(quads, tile):
+    width = quads.shape[1] // TILES
+    return pl.ds(pl.multiple_of(tile * width, width), width)
+
+
+def partial_kernel(offsets, which, bits, quads, turned, out):
+    width = quads.shape[1] // TILES
+    for at, tile in enumerate(tiles_of(which, bits)):
+        source, receiver = products(offsets, quads[:, tile_lanes(quads, tile)], turned, turned.shape[1] // len(offsets))
+        out[0, :, at * width : (at + 1) * width] = source
+        out[1, :, at * width : (at + 1) * width] = receiver
+
+
+def sensitivity_kernel(offsets, ready, begun, which, bits, quads, weight, volume, *refs):
+    shards, out, turned = refs[1 if ready or begun else 0 : -2], refs[-2], refs[-1]
     cells, width = out.shape[0], quads.shape[1] // TILES
     depth = turned.shape[1] // len(offsets)
     if ready:
@@ -112,35 +139,44 @@
     turn(shards, turned, ready)
     terms = volume[...].astype(F32)
     column = jnp.sum(jnp.broadcast_to(terms[:, None, :], (terms.shape[0], 8, cells)), axis=0).T[:, :1]
-    group, _, _ = position()
     for at, tile in enumerate(tiles_of(which, bits)):
-        lanes = pl.ds(pl.multiple_of(tile * width, width), width)
-        rows = quads[:, lanes]
-        owner = rows // depth
-        slot = jnp.bitwise_xor(owner, group)
-        if offsets != tuple(range(len(offsets))):
-            slot = functools.reduce(jnp.add, [jnp.where(slot == k, n, 0) for n, k in enumerate(offsets)])
-        places = (slot * depth + (rows - owner * depth)).astype(jnp.int16)
-        source = jnp.dot(turned[...], difference_map(places, 0, turned.shape[1]), preferred_element_type=F32)
-        receiver = jnp.dot(turned[...], difference_map(places, 2, turned.shape[1]), preferred_element_type=F32)
+        lanes = tile_lanes(quads, tile)
+        source, receiver = products(offsets, quads[:, lanes], turned, depth)
+        if begun:
+            own = slice(at * width, (at + 1) * width)
+            source, receiver = refs[0][0, :, own] + source, refs[0][1, :, own] + receiver
         product = source * receiver
         dots = product[:cells] + product[cells : 2 * cells] + product[2 * cells :]
         out[:, at * width : (at + 1) * width] = (weight[:, lanes] * -(column * dots)).astype(BF16)
 
 
-def sensitivities(which, bits, quads, weight, volume, shards, turned=None, ready=(), weigh=1):
+def sensitivities(which, bits, quads, weight, volume, shards, turned=None, ready=(), begun=None, weigh=1):
     offsets = tuple(ready) + tuple(sorted(shards))
     held = [shards[k] for k in offsets[len(ready) :]]
     _, depth, cells = held[0].shape
     count, width = 2, quads.shape[1] // TILES
+    first = [] if begun is None else [pltpu.with_memory_space_constraint(begun, pltpu.VMEM)]
     flops = weigh * 4 * count * width * len(offsets) * depth * 3 * cells
     return whole_call(
-        functools.partial(sensitivity_kernel, offsets, len(ready), which, bits),
+        functools.partial(sensitivity_kernel, offsets, len(ready), begun is not None, which, bits),
         "sensitivities",
         jax.ShapeDtypeStruct((cells, count * width), BF16),
         [pltpu.VMEM((3 * cells, len(offsets) * depth), BF16)],
-        quads, weight, volume, *([turned] if ready else []), *held,
+        quads, weight, volume, *([turned] if ready else []), *first, *held,
         flops=flops,
+    )
+
+
+def partial_products(which, bits, quads, turned, offsets):
+    rows, total = turned.shape
+    count = quads.shape[1] * 2 // TILES
+    return whole_call(
+        functools.partial(partial_kernel, offsets, which, bits),
+        "partial_products",
+        pltpu.VMEM((2, rows, count), F32),
+        [],
+        quads, turned,
+        flops=1000,
     )
 
 
@@ -261,17 +297,17 @@
     half, far = groups // 2, groups - 1
     odds = [d for d in range(1, chips) if odd(d)]
     evens = [d for d in range(1, chips) if not odd(d)]
-    packed = pack(grads, volume)
+    packed, columns = pack(grads, volume, quads.T)
     shape = grads.shape
     gradients = lambda x: x[: 3 * shape[1], :].reshape(shape)
-    shards = {0: grads, far: hop(grads, "elec", groups, far)}
+    shards = {0: gradients(packed), far: hop(grads, "elec", groups, far)}
     for j in range(1, half):
-        shards[j] = gradients(hop(packed, "elec", groups, j))
+        shards[j] = hop(grads, "elec", groups, j)
     for j in range(1, half):
         shards[far ^ j] = hop(shards[far], "elec", groups, j)
 
     bits = max(1, (chips - 1).bit_length())
-    columns, weights = quads.T, weight.reshape(1, measured)
+    weights = weight.reshape(1, measured)
     volumes = volume.reshape(1, cells)
     relayed = {far ^ j: shards[far ^ j] for j in range(1, half)}
     direct = {k: shards[k] for k in shards if k not in relayed}
@@ -287,7 +323,8 @@
             across[d][k] = hop(shards[k], "cell", devices, 2 * d)
 
     form = functools.partial(sensitivities, bits=bits)
-    own_send = form("send", quads=columns, weight=weights, volume=volumes, shards=relayed, turned=turned, ready=ready)
+    begun = partial_products("send", bits, columns, turned, ready)
+    own_send = form("send", quads=columns, weight=weights, volume=volumes, shards=relayed, begun=begun)
     received = [hop(own_send, "cell", devices, 2 * d) for d in odds]
     other_send = hop(own_send, "cell", devices, 1)
     columns, own_send, across = lax.optimization_barrier((columns, own_send, across))

time: 54.9 us -> 53.3 us (0.971)
  waiting for transfers between devices: 13.7 us -> 11.6 us
  starting transfers between devices: 26.3 us -> 24.3 us
  local copies, waits for them, and re-layouts: 1 us -> 2.52 us
  Pallas kernels: 13.7 us -> 14.5 us
    ppermute x19, waiting for transfers between devices: 13.7 us -> 11.6 us  [hop(): return lax.ppermute(x, axis, [(i, i ^ mask) for i in range(size)])]
    ppermute x19, starting transfers between devices: 26.3 us -> 24.3 us  [hop(): return lax.ppermute(x, axis, [(i, i ^ mask) for i in range(size)])]
    unnamed x8 -> x10, local copies, waits for them, and re-layouts: 0.97 us -> 2.49 us
    pallas_call x8 -> x9, Pallas kernels: 13.4 us -> 14.3 us  [whole_call(): pl.pallas_call(kernel, in_specs=[vmem] * len(arrays), out_specs=[vmem] *...]
  transfers between devices with their start and end apart: 19 -> 19, of which waited for: 9 -> 9; matrix products, arithmetic and copies ran while one was open for 0% -> 0% of each run, Pallas kernels for 23% -> 26%
where the time goes in v6:
time: 53.3 us; the launch traced here: 53.1 us
  starting transfers between devices  24.3 us (46%)
  Pallas kernels  14.5 us (27%)
  waiting for transfers between devices  11.6 us (22%)
  local copies, waits for them, and re-layouts  2.52 us (5%)
    ppermute x19, starting transfers between devices, hop(): return lax.ppermute(x, axis, [(i, i ^ mask) for i in range(size)])  24.3 us
    pallas_call x9, Pallas kernels, whole_call(): pl.pallas_call(kernel, in_specs=[vmem] * len(arrays), out_specs=[vmem] *...  14.3 us
    ppermute x19, waiting for transfers between devices, hop(): return lax.ppermute(x, axis, [(i, i ^ mask) for i in range(size)])  11.6 us
    unnamed x10, local copies, waits for them, and re-layouts  2.49 us
  transfers between devices with their start and end apart: 19, of which 9 were waited for; matrix products, arithmetic and copies ran while one was open for 0% of the time, Pallas kernels for 26%

profile of v6, /device:TPU:0, one launch (start us, length us, event | category | flops | bytes accessed | tf_op | source)
XLA Modules:
  0.0 53.1 jit_solution(16804171011174949974)
XLA Ops:
  0.0 5.0 %collective-permute-start.1 = (bf16[3,256,128]{2,1,0:T(8,128)(2,1)}, bf16[3,256,128]{2,1,0:T(8,128)(2,1)S(1)}, u32[]{:S(2)}, u32[]{:S(2)}) collective-permute-start(bf16[3,256,128]{2,1,0:T(8,128)(2,1)} %shard.1), channel_id=1, source_target_pairs={{0,24},{8,16},{16,8},{24,0},{1,25},{9,17},{17,9},{25,1},{2,26},{10... | collective-permute-start | bytes 589832 | tf_op jit(solution)/shard_map/ppermute | solution.py:21
  5.1 1.0 %copy-done = bf16[3,256,128]{2,1,0:T(8,128)(2,1)S(1)} copy-done((bf16[3,256,128]{2,1,0:T(8,128)(2,1)S(1)}, bf16[3,256,128]{2,1,0:T(8,128)(2,1)}, u32[]{:S(2)}) %copy-start) | copy-done | bytes 196632
  6.1 0.8 %copy-done.1 = s32[4096,4]{0,1:T(4,128)S(1)} copy-done((s32[4096,4]{0,1:T(4,128)S(1)}, s32[4096,4]{0,1:T(4,128)}, u32[]{:S(2)}) %copy-start.1) | copy-done | bytes 65560
  6.9 0.7 %copy-done.3 = f32[128]{0:T(128)S(1)} copy-done((f32[128]{0:T(128)S(1)}, f32[128]{0:T(128)}, u32[]{:S(2)}) %copy-start.3) | copy-done | bytes 536
  7.6 2.5 %collective-permute-start.3 = (bf16[784,128]{1,0:T(8,128)(2,1)S(1)}, bf16[784,128]{1,0:T(8,128)(2,1)S(1)}, u32[]{:S(2)}, u32[]{:S(2)}) collective-permute-start(bf16[784,128]{1,0:T(8,128)(2,1)S(1)} %get-tuple-element.29), channel_id=1, source_target_pairs={{0,6},{1,7},{2,4},{3,5},{4,2},{5,3},{6,0},{7,1},{8,14},{9,15},{10,... | collective-permute-start | bytes 602120 | tf_op jit(solution)/shard_map/ppermute | solution.py:21
  10.1 1.0 %collective-permute-done.1.refs_2_ = bf16[3,256,128]{2,1,0:T(8,128)(2,1)S(1)} collective-permute-done((bf16[3,256,128]{2,1,0:T(8,128)(2,1)}, bf16[3,256,128]{2,1,0:T(8,128)(2,1)S(1)}, u32[]{:S(2)}, u32[]{:S(2)}) %collective-permute-start.1) | collective-permute-done | bytes 196640 | tf_op jit(solution)/shard_map/ppermute | solution.py:21
  11.0 3.1 %collective-permute-start.2 = (bf16[3,256,128]{2,1,0:T(8,128)(2,1)S(1)}, bf16[3,256,128]{2,1,0:T(8,128)(2,1)S(1)}, u32[]{:S(2)}, u32[]{:S(2)}) collective-permute-start(bf16[3,256,128]{2,1,0:T(8,128)(2,1)S(1)} %collective-permute-done.1.refs_2_), channel_id=1, source_target_pairs={{0,8},{8,0},{16,24},{24,16},{1,9},{9,1},{17,25},{25,17},{2,10},{10... | collective-permute-start | bytes 589832 | tf_op jit(solution)/shard_map/ppermute | solution.py:21
  14.1 2.4 %collective-permute-start.5 = (bf16[3,256,128]{2,1,0:T(8,128)(2,1)S(1)}, bf16[3,256,128]{2,1,0:T(8,128)(2,1)S(1)}, u32[]{:S(2)}, u32[]{:S(2)}) collective-permute-start(bf16[3,256,128]{2,1,0:T(8,128)(2,1)S(1)} %collective-permute-done.1.refs_2_), channel_id=1, source_target_pairs={{0,6},{1,7},{2,4},{3,5},{4,2},{5,3},{6,0},{7,1},{8,14},{9,15},{10,... | collective-permute-start | bytes 589832 | tf_op jit(solution)/shard_map/ppermute | solution.py:21
  16.5 0.5 collective-permute-start.4
  17.2 2.6 %partial_products.1.refs_0_ = f32[2,384,2048]{2,1,0:T(8,128)S(1)} custom-call(s32[4,4096]{1,0:T(4,128)S(1)} %get-tuple-element.31.quads, bf16[384,768]{1,0:T(8,128)(2,1)S(1)} %turn_shards.1.turned.refs_0_), custom_call_target="tpu_custom_call" | custom-call | flops 1000 | bytes 1 | tf_op jit(solution)/shard_map/partial_products/pallas_call | solution.py:281
  20.0 1.7 %sensitivities.3.own_send = bf16[128,2048]{1,0:T(8,128)(2,1)S(1)} custom-call(s32[4,4096]{1,0:T(4,128)S(1)} %get-tuple-element.31.quads, f32[1,4096]{1,0:T(1,128)S(1)} %bitcast.8, f32[1,128]{1,0:T(1,128)S(1)} %bitcast.12, f32[2,384,2048]{2,1,0:T(8,128)S(1)} %partial_products.1.refs_0_, bf16[3,256,128]{2,1,0:T(8,128)(2,1)S(1)} %collective-permute-done.2.refs_1_), custom_call_target="tpu_custom_call" | custom-call | flops 805306368 | bytes 1 | tf_op jit(solution)/shard_map/sensitivities/pallas_call | solution.py:281
  21.7 1.6 %collective-permute-start.8 = (bf16[128,2048]{1,0:T(8,128)(2,1)S(1)}, bf16[128,2048]{1,0:T(8,128)(2,1)S(1)}, u32[]{:S(2)}, u32[]{:S(2)}) collective-permute-start(bf16[128,2048]{1,0:T(8,128)(2,1)S(1)} %sensitivities.3.own_send), channel_id=1, source_target_pairs={{0,4},{1,5},{2,6},{3,7},{4,0},{5,1},{6,2},{7,3},{8,12},{9,13},{10,... | collective-permute-start | bytes 1572872 | tf_op jit(solution)/shard_map/ppermute | solution.py:21
  23.3 1.5 %collective-permute-start.7 = (bf16[128,2048]{1,0:T(8,128)(2,1)S(1)}, bf16[128,2048]{1,0:T(8,128)(2,1)S(1)}, u32[]{:S(2)}, u32[]{:S(2)}) collective-permute-start(bf16[128,2048]{1,0:T(8,128)(2,1)S(1)} %sensitivities.3.own_send), channel_id=1, source_target_pairs={{0,2},{1,3},{2,0},{3,1},{4,6},{5,7},{6,4},{7,5},{8,10},{9,11},{10,... | collective-permute-start | bytes 1572872 | tf_op jit(solution)/shard_map/ppermute | solution.py:21
  24.9 0.4 collective-permute-start.10
  25.2 3.6 %sensitivities.4.own_keep = bf16[128,2048]{1,0:T(8,128)(2,1)S(1)} custom-call(s32[4,4096]{1,0:T(4,128)S(1)} %get-tuple-element.31.quads, f32[1,4096]{1,0:T(1,128)S(1)} %bitcast.9, f32[1,128]{1,0:T(1,128)S(1)} %bitcast.13, bf16[384,768]{1,0:T(8,128)(2,1)S(1)} %turn_shards.1.turned.refs_0_, bf16[3,256,128]{2,1,0:T(8,128)(2,1)S(1)} %collective-permute-done.2.refs_1_), custom_call_target="tpu_custom_call" | custom-call | flops 3221225472 | bytes 1 | tf_op jit(solution)/shard_map/sensitivities/pallas_call | solution.py:281
  28.9 2.6 %collective-permute-done.10.refs_2_ = bf16[3,256,128]{2,1,0:T(8,128)(2,1)S(1)} collective-permute-done((bf16[3,256,128]{2,1,0:T(8,128)(2,1)S(1)}, bf16[3,256,128]{2,1,0:T(8,128)(2,1)S(1)}, u32[]{:S(2)}, u32[]{:S(2)}) %collective-permute-start.10) | collective-permute-done | bytes 196640 | tf_op jit(solution)/shard_map/ppermute | solution.py:21
  31.5 3.5 %sensitivities.5.refs_0_ = bf16[128,2048]{1,0:T(8,128)(2,1)S(1)} custom-call(s32[4,4096]{1,0:T(4,128)S(1)} %get-tuple-element.31.quads, f32[1,4096]{1,0:T(1,128)S(1)} %bitcast.10, bf16[16,128]{1,0:T(8,128)(2,1)S(1)} %slice.13.volume, bf16[3,256,128]{2,1,0:T(8,128)(2,1)S(1)} %bitcast.6, bf16[3,256,128]{2,1,0:T(8,128)(2,1)S(1)} %collective-permute-done.4.refs_1_, ...), custom_call_target="tpu_custom_call" | custom-call | flops 12884901888 | bytes 1 | tf_op jit(solution)/shard_map/sensitivities/pallas_call | solution.py:281
  35.1 0.6 %early_blocks.1 = (f32[1,128,128]{2,1,0:T(8,128)S(1)}, bf16[1,128,128]{2,1,0:T(8,128)(2,1)S(1)}, bf16[256,128]{1,0:T(8,128)(2,1)S(1)}) custom-call(bf16[128,2048]{1,0:T(8,128)(2,1)S(1)} %sensitivities.3.own_send, bf16[128,2048]{1,0:T(8,128)(2,1)S(1)} %sensitivities.4.own_keep, bf16[128,2048]{1,0:T(8,128)(2,1)S(1)} %collective-permute-done.9.other_send, ...), custom_call_target="tpu_custom_call" | custom-call | flops 1000 | bytes 1 | tf_op jit(solution)/shard_map/early_blocks/pallas_call | solution.py:281
  35.7 1.5 %collective-permute-start.12 = (bf16[256,128]{1,0:T(8,128)(2,1)S(1)}, bf16[256,128]{1,0:T(8,128)(2,1)S(1)}, u32[]{:S(2)}, u32[]{:S(2)}) collective-permute-start(bf16[256,128]{1,0:T(8,128)(2,1)S(1)} %get-tuple-element.42), channel_id=1, source_target_pairs={{0,6},{1,7},{2,4},{3,5},{4,2},{5,3},{6,0},{7,1},{8,14},{9,15},{10,... | collective-permute-start | bytes 196616 | tf_op jit(solution)/shard_map/ppermute | solution.py:21
  37.5 0.5 %late_blocks.1 = (f32[2,128,128]{2,1,0:T(8,128)S(1)}, bf16[2,128,128]{2,1,0:T(8,128)(2,1)S(1)}, bf16[256,128]{1,0:T(8,128)(2,1)S(1)}, bf16[256,128]{1,0:T(8,128)(2,1)S(1)}) custom-call(bf16[128,2048]{1,0:T(8,128)(2,1)S(1)} %sensitivities.4.own_keep, bf16[128,2048]{1,0:T(8,128)(2,1)S(1)} %collective-permute-done.6.other_keep, ...), custom_call_target="tpu_custom_call" | custom-call | flops 1000 | bytes 1 | tf_op jit(solution)/shard_map/late_blocks/pallas_call | solution.py:281
  38.1 1.6 %collective-permute-start.14 = (bf16[256,128]{1,0:T(8,128)(2,1)S(1)}, bf16[256,128]{1,0:T(8,128)(2,1)S(1)}, u32[]{:S(2)}, u32[]{:S(2)}) collective-permute-start(bf16[256,128]{1,0:T(8,128)(2,1)S(1)} %get-tuple-element.45), channel_id=1, source_target_pairs={{0,2},{1,3},{2,0},{3,1},{4,6},{5,7},{6,4},{7,5},{8,10},{9,11},{10,... | collective-permute-start | bytes 196616 | tf_op jit(solution)/shard_map/ppermute | solution.py:21
  39.6 0.5 collective-permute-start.15
  40.1 0.9 %own_block.1 = f32[256,128]{1,0:T(8,128)S(1)} custom-call(bf16[128,2048]{1,0:T(8,128)(2,1)S(1)} %sensitivities.3.own_send, bf16[128,2048]{1,0:T(8,128)(2,1)S(1)} %sensitivities.4.own_keep, bf16[128,2048]{1,0:T(8,128)(2,1)S(1)} %collective-permute-done.9.other_send, bf16[128,2048]{1,0:T(8,128)(2,1)S(1)} %collective-permute-done.6.other_keep), custom_call_target="tpu_custom_call" | custom-call | flops 1000 | bytes 1 | tf_op jit(solution)/shard_map/own_block/pallas_call | solution.py:281
  41.0 0.3 collective-permute-done.11.refs_1_
  41.3 1.2 %collective-permute-done.14.refs_5_ = bf16[256,128]{1,0:T(8,128)(2,1)S(1)} collective-permute-done((bf16[256,128]{1,0:T(8,128)(2,1)S(1)}, bf16[256,128]{1,0:T(8,128)(2,1)S(1)}, u32[]{:S(2)}, u32[]{:S(2)}) %collective-permute-start.14) | collective-permute-done | bytes 65568 | tf_op jit(solution)/shard_map/ppermute | solution.py:21
  42.6 1.3 %collective-permute-done.15.refs_6_ = bf16[256,128]{1,0:T(8,128)(2,1)S(1)} collective-permute-done((bf16[256,128]{1,0:T(8,128)(2,1)S(1)}, bf16[256,128]{1,0:T(8,128)(2,1)S(1)}, u32[]{:S(2)}, u32[]{:S(2)}) %collective-permute-start.15) | collective-permute-done | bytes 65568 | tf_op jit(solution)/shard_map/ppermute | solution.py:21
  44.0 1.3 %collective-permute-start.16 = (bf16[272,128]{1,0:T(8,128)(2,1)S(1)}, bf16[272,128]{1,0:T(8,128)(2,1)S(1)}, u32[]{:S(2)}, u32[]{:S(2)}) collective-permute-start(bf16[272,128]{1,0:T(8,128)(2,1)S(1)} %get-tuple-element.48), channel_id=1, source_target_pairs={{0,16},{8,24},{16,0},{24,8},{1,17},{9,25},{17,1},{25,9},{2,18},{10... | collective-permute-start | bytes 208904 | tf_op jit(solution)/shard_map/ppermute | solution.py:21
  45.3 1.6 %collective-permute-start.17 = (bf16[272,128]{1,0:T(8,128)(2,1)S(1)}, bf16[272,128]{1,0:T(8,128)(2,1)S(1)}, u32[]{:S(2)}, u32[]{:S(2)}) collective-permute-start(bf16[272,128]{1,0:T(8,128)(2,1)S(1)} %get-tuple-element.49), channel_id=1, source_target_pairs={{0,24},{8,16},{16,8},{24,0},{1,25},{9,17},{17,9},{25,1},{2,26},{10... | collective-permute-start | bytes 208904 | tf_op jit(solution)/shard_map/ppermute | solution.py:21
  46.8 0.7 %collective-permute-start.18 = (bf16[272,128]{1,0:T(8,128)(2,1)S(1)}, bf16[272,128]{1,0:T(8,128)(2,1)S(1)}, u32[]{:S(2)}, u32[]{:S(2)}) collective-permute-start(bf16[272,128]{1,0:T(8,128)(2,1)S(1)} %get-tuple-element.50), channel_id=1, source_target_pairs={{0,8},{8,0},{16,24},{24,16},{1,9},{9,1},{17,25},{25,17},{2,10},{10... | collective-permute-start | bytes 208904 | tf_op jit(solution)/shard_map/ppermute | solution.py:21
  47.6 4.3 %collective-permute-done.16.refs_0_ = bf16[272,128]{1,0:T(8,128)(2,1)S(1)} collective-permute-done((bf16[272,128]{1,0:T(8,128)(2,1)S(1)}, bf16[272,128]{1,0:T(8,128)(2,1)S(1)}, u32[]{:S(2)}, u32[]{:S(2)}) %collective-permute-start.16) | collective-permute-done | bytes 69664 | tf_op jit(solution)/shard_map/ppermute | solution.py:21
  51.9 0.5 collective-permute-done.18.refs_2_
  52.4 0.7 %finish.1 = f32[256,128]{1,0:T(8,128)} custom-call(f32[256,128]{1,0:T(8,128)S(1)} %get-tuple-element.47.own, bf16[272,128]{1,0:T(8,128)(2,1)S(1)} %collective-permute-done.16.refs_0_, bf16[272,128]{1,0:T(8,128)(2,1)S(1)} %collective-permute-done.17.refs_1_, bf16[272,128]{1,0:T(8,128)(2,1)S(1)} %collective-permute-done.18.refs_2_), custom_call_target="tpu_custom_call" | custom-call | flops 1000 | bytes 1 | tf_op jit(solution)/shard_map/finish/pallas_call | solution.py:281
  (30 shorter events, 0.9 us)
Async XLA Ops:
  0.0 20.0 %copy-start.4 = (f32[128]{0:T(128)S(1)}, f32[128]{0:T(128)}, u32[]{:S(2)}) copy-start(f32[128]{0:T(128)} %param.6) | copy-start | bytes 1540
  0.0 11.0 %collective-permute-start.1 = (bf16[3,256,128]{2,1,0:T(8,128)(2,1)}, bf16[3,256,128]{2,1,0:T(8,128)(2,1)S(1)}, u32[]{:S(2)}, u32[]{:S(2)}) collective-permute-start(bf16[3,256,128]{2,1,0:T(8,128)(2,1)} %shard.1), channel_id=1, source_target_pairs={{0,24},{8,16},{16,8},{24,0},{1,25},{9,17},{17,9},{25,1},{2,26},{10... | collective-permute-start | bytes 589832 | tf_op jit(solution)/shard_map/ppermute | solution.py:21
  5.1 11.5 %collective-permute-start = (bf16[3,256,128]{2,1,0:T(8,128)(2,1)}, bf16[3,256,128]{2,1,0:T(8,128)(2,1)S(1)}, u32[]{:S(2)}, u32[]{:S(2)}) collective-permute-start(bf16[3,256,128]{2,1,0:T(8,128)(2,1)} %shard.1), channel_id=1, source_target_pairs={{0,8},{8,0},{16,24},{24,16},{1,9},{9,1},{17,25},{25,17},{2,10},{10... | collective-permute-start | bytes 589832 | tf_op jit(solution)/shard_map/ppermute | solution.py:21
  5.1 1.0 %copy-start = (bf16[3,256,128]{2,1,0:T(8,128)(2,1)S(1)}, bf16[3,256,128]{2,1,0:T(8,128)(2,1)}, u32[]{:S(2)}) copy-start(bf16[3,256,128]{2,1,0:T(8,128)(2,1)} %shard.1) | copy-start | bytes 589828
  6.0 0.8 %copy-start.1 = (s32[4096,4]{0,1:T(4,128)S(1)}, s32[4096,4]{0,1:T(4,128)}, u32[]{:S(2)}) copy-start(s32[4096,4]{0,1:T(4,128)} %param.5) | copy-start | bytes 196612
  6.9 0.7 %copy-start.3 = (f32[128]{0:T(128)S(1)}, f32[128]{0:T(128)}, u32[]{:S(2)}) copy-start(f32[128]{0:T(128)} %param.6) | copy-start | bytes 1540
  7.5 12.4 %copy-start.2 = (f32[4096]{0:T(1024)S(1)}, f32[4096]{0:T(1024)}, u32[]{:S(2)}) copy-start(f32[4096]{0:T(1024)} %param.7) | copy-start | bytes 49156
  7.6 12.3 %collective-permute-start.3 = (bf16[784,128]{1,0:T(8,128)(2,1)S(1)}, bf16[784,128]{1,0:T(8,128)(2,1)S(1)}, u32[]{:S(2)}, u32[]{:S(2)}) collective-permute-start(bf16[784,128]{1,0:T(8,128)(2,1)S(1)} %get-tuple-element.29), channel_id=1, source_target_pairs={{0,6},{1,7},{2,4},{3,5},{4,2},{5,3},{6,0},{7,1},{8,14},{9,15},{10,... | collective-permute-start | bytes 602120 | tf_op jit(solution)/shard_map/ppermute | solution.py:21
  11.0 8.9 %collective-permute-start.2 = (bf16[3,256,128]{2,1,0:T(8,128)(2,1)S(1)}, bf16[3,256,128]{2,1,0:T(8,128)(2,1)S(1)}, u32[]{:S(2)}, u32[]{:S(2)}) collective-permute-start(bf16[3,256,128]{2,1,0:T(8,128)(2,1)S(1)} %collective-permute-done.1.refs_2_), channel_id=1, source_target_pairs={{0,8},{8,0},{16,24},{24,16},{1,9},{9,1},{17,25},{25,17},{2,10},{10... | collective-permute-start | bytes 589832 | tf_op jit(solution)/shard_map/ppermute | solution.py:21
  14.1 10.7 %collective-permute-start.5 = (bf16[3,256,128]{2,1,0:T(8,128)(2,1)S(1)}, bf16[3,256,128]{2,1,0:T(8,128)(2,1)S(1)}, u32[]{:S(2)}, u32[]{:S(2)}) collective-permute-start(bf16[3,256,128]{2,1,0:T(8,128)(2,1)S(1)} %collective-permute-done.1.refs_2_), channel_id=1, source_target_pairs={{0,6},{1,7},{2,4},{3,5},{4,2},{5,3},{6,0},{7,1},{8,14},{9,15},{10,... | collective-permute-start | bytes 589832 | tf_op jit(solution)/shard_map/ppermute | solution.py:21
  16.5 8.3 %collective-permute-start.4 = (bf16[3,256,128]{2,1,0:T(8,128)(2,1)S(1)}, bf16[3,256,128]{2,1,0:T(8,128)(2,1)S(1)}, u32[]{:S(2)}, u32[]{:S(2)}) collective-permute-start(bf16[3,256,128]{2,1,0:T(8,128)(2,1)S(1)} %collective-permute-done.refs_1_), channel_id=1, source_target_pairs={{0,6},{1,7},{2,4},{3,5},{4,2},{5,3},{6,0},{7,1},{8,14},{9,15},{10,... | collective-permute-start | bytes 589832 | tf_op jit(solution)/shard_map/ppermute | solution.py:21
  21.7 13.4 %collective-permute-start.9 = (bf16[128,2048]{1,0:T(8,128)(2,1)S(1)}, bf16[128,2048]{1,0:T(8,128)(2,1)S(1)}, u32[]{:S(2)}, u32[]{:S(2)}) collective-permute-start(bf16[128,2048]{1,0:T(8,128)(2,1)S(1)} %sensitivities.3.own_send), channel_id=1, source_target_pairs={{0,1},{1,0},{2,3},{3,2},{4,5},{5,4},{6,7},{7,6},{8,9},{9,8},{10,11... | collective-permute-start | bytes 1572872 | tf_op jit(solution)/shard_map/ppermute | solution.py:21
  21.7 15.5 %collective-permute-start.8 = (bf16[128,2048]{1,0:T(8,128)(2,1)S(1)}, bf16[128,2048]{1,0:T(8,128)(2,1)S(1)}, u32[]{:S(2)}, u32[]{:S(2)}) collective-permute-start(bf16[128,2048]{1,0:T(8,128)(2,1)S(1)} %sensitivities.3.own_send), channel_id=1, source_target_pairs={{0,4},{1,5},{2,6},{3,7},{4,0},{5,1},{6,2},{7,3},{8,12},{9,13},{10,... | collective-permute-start | bytes 1572872 | tf_op jit(solution)/shard_map/ppermute | solution.py:21
  23.3 14.1 %collective-permute-start.7 = (bf16[128,2048]{1,0:T(8,128)(2,1)S(1)}, bf16[128,2048]{1,0:T(8,128)(2,1)S(1)}, u32[]{:S(2)}, u32[]{:S(2)}) collective-permute-start(bf16[128,2048]{1,0:T(8,128)(2,1)S(1)} %sensitivities.3.own_send), channel_id=1, source_target_pairs={{0,2},{1,3},{2,0},{3,1},{4,6},{5,7},{6,4},{7,5},{8,10},{9,11},{10,... | collective-permute-start | bytes 1572872 | tf_op jit(solution)/shard_map/ppermute | solution.py:21
  24.9 6.6 %collective-permute-start.10 = (bf16[3,256,128]{2,1,0:T(8,128)(2,1)S(1)}, bf16[3,256,128]{2,1,0:T(8,128)(2,1)S(1)}, u32[]{:S(2)}, u32[]{:S(2)}) collective-permute-start(bf16[3,256,128]{2,1,0:T(8,128)(2,1)S(1)} %collective-permute-done.5.refs_3_), channel_id=1, source_target_pairs={{0,8},{8,0},{16,24},{24,16},{1,9},{9,1},{17,25},{25,17},{2,10},{10... | collective-permute-start | bytes 589832 | tf_op jit(solution)/shard_map/ppermute | solution.py:21
  28.8 6.3 %collective-permute-start.6 = (bf16[128,2048]{1,0:T(8,128)(2,1)S(1)}, bf16[128,2048]{1,0:T(8,128)(2,1)S(1)}, u32[]{:S(2)}, u32[]{:S(2)}) collective-permute-start(bf16[128,2048]{1,0:T(8,128)(2,1)S(1)} %sensitivities.4.own_keep), channel_id=1, source_target_pairs={{0,1},{1,0},{2,3},{3,2},{4,5},{5,4},{6,7},{7,6},{8,9},{9,8},{10,11... | collective-permute-start | bytes 1572872 | tf_op jit(solution)/shard_map/ppermute | solution.py:21
  35.7 5.7 %collective-permute-start.12 = (bf16[256,128]{1,0:T(8,128)(2,1)S(1)}, bf16[256,128]{1,0:T(8,128)(2,1)S(1)}, u32[]{:S(2)}, u32[]{:S(2)}) collective-permute-start(bf16[256,128]{1,0:T(8,128)(2,1)S(1)} %get-tuple-element.42), channel_id=1, source_target_pairs={{0,6},{1,7},{2,4},{3,5},{4,2},{5,3},{6,0},{7,1},{8,14},{9,15},{10,... | collective-permute-start | bytes 196616 | tf_op jit(solution)/shard_map/ppermute | solution.py:21
  38.0 3.3 %collective-permute-start.13 = (bf16[2,128,128]{2,1,0:T(8,128)(2,1)S(1)}, bf16[2,128,128]{2,1,0:T(8,128)(2,1)S(1)}, u32[]{:S(2)}, u32[]{:S(2)}) collective-permute-start(bf16[2,128,128]{2,1,0:T(8,128)(2,1)S(1)} %get-tuple-element.44), channel_id=1, source_target_pairs={{0,1},{1,0},{2,3},{3,2},{4,5},{5,4},{6,7},{7,6},{8,9},{9,8},{10,11... | collective-permute-start | bytes 196616 | tf_op jit(solution)/shard_map/ppermute | solution.py:21
  38.1 4.5 %collective-permute-start.14 = (bf16[256,128]{1,0:T(8,128)(2,1)S(1)}, bf16[256,128]{1,0:T(8,128)(2,1)S(1)}, u32[]{:S(2)}, u32[]{:S(2)}) collective-permute-start(bf16[256,128]{1,0:T(8,128)(2,1)S(1)} %get-tuple-element.45), channel_id=1, source_target_pairs={{0,2},{1,3},{2,0},{3,1},{4,6},{5,7},{6,4},{7,5},{8,10},{9,11},{10,... | collective-permute-start | bytes 196616 | tf_op jit(solution)/shard_map/ppermute | solution.py:21
  39.6 4.3 %collective-permute-start.15 = (bf16[256,128]{1,0:T(8,128)(2,1)S(1)}, bf16[256,128]{1,0:T(8,128)(2,1)S(1)}, u32[]{:S(2)}, u32[]{:S(2)}) collective-permute-start(bf16[256,128]{1,0:T(8,128)(2,1)S(1)} %get-tuple-element.46), channel_id=1, source_target_pairs={{0,4},{1,5},{2,6},{3,7},{4,0},{5,1},{6,2},{7,3},{8,12},{9,13},{10,... | collective-permute-start | bytes 196616 | tf_op jit(solution)/shard_map/ppermute | solution.py:21
  40.1 1.2 %collective-permute-start.11 = (bf16[1,128,128]{2,1,0:T(8,128)(2,1)S(1)}, bf16[1,128,128]{2,1,0:T(8,128)(2,1)S(1)}, u32[]{:S(2)}, u32[]{:S(2)}) collective-permute-start(bf16[1,128,128]{2,1,0:T(8,128)(2,1)S(1)} %get-tuple-element.41), channel_id=1, source_target_pairs={{0,1},{1,0},{2,3},{3,2},{4,5},{5,4},{6,7},{7,6},{8,9},{9,8},{10,11... | collective-permute-start | bytes 98312 | tf_op jit(solution)/shard_map/ppermute | solution.py:21
  44.0 7.9 %collective-permute-start.16 = (bf16[272,128]{1,0:T(8,128)(2,1)S(1)}, bf16[272,128]{1,0:T(8,128)(2,1)S(1)}, u32[]{:S(2)}, u32[]{:S(2)}) collective-permute-start(bf16[272,128]{1,0:T(8,128)(2,1)S(1)} %get-tuple-element.48), channel_id=1, source_target_pairs={{0,16},{8,24},{16,0},{24,8},{1,17},{9,25},{17,1},{25,9},{2,18},{10... | collective-permute-start | bytes 208904 | tf_op jit(solution)/shard_map/ppermute | solution.py:21
  45.3 6.6 %collective-permute-start.17 = (bf16[272,128]{1,0:T(8,128)(2,1)S(1)}, bf16[272,128]{1,0:T(8,128)(2,1)S(1)}, u32[]{:S(2)}, u32[]{:S(2)}) collective-permute-start(bf16[272,128]{1,0:T(8,128)(2,1)S(1)} %get-tuple-element.49), channel_id=1, source_target_pairs={{0,24},{8,16},{16,8},{24,0},{1,25},{9,17},{17,9},{25,1},{2,26},{10... | collective-permute-start | bytes 208904 | tf_op jit(solution)/shard_map/ppermute | solution.py:21
  46.8 5.5 %collective-permute-start.18 = (bf16[272,128]{1,0:T(8,128)(2,1)S(1)}, bf16[272,128]{1,0:T(8,128)(2,1)S(1)}, u32[]{:S(2)}, u32[]{:S(2)}) collective-permute-start(bf16[272,128]{1,0:T(8,128)(2,1)S(1)} %get-tuple-element.50), channel_id=1, source_target_pairs={{0,8},{8,0},{16,24},{24,16},{1,9},{9,1},{17,25},{25,17},{2,10},{10... | collective-permute-start | bytes 208904 | tf_op jit(solution)/shard_map/ppermute | solution.py:21

commit v7 on v6

--- a/solution.py
+++ b/solution.py
@@ -79,29 +79,36 @@
     )(*shards)
 
 
-def pack_kernel(shard, volume, quads, out, kept):
+def pack_kernel(shard, volume, quads, out, kept, rest, sems):
     parts, depth, cells = shard.shape
-    kept[...] = quads[...]
-    for k in range(parts):
-        out[k * depth : (k + 1) * depth, :] = shard[k]
-    rest = volume[...]
+    pairs = [(shard.at[k], out.at[pl.ds(k * depth, depth)]) for k in range(parts)] + [(volume, rest), (quads, kept)]
+    copies = [pltpu.make_async_copy(source, target, sems.at[n]) for n, (source, target) in enumerate(pairs)]
+    for copy in copies:
+        copy.start()
+    for copy in copies:
+        copy.wait()
+    value = rest[...]
     rows = []
     for _ in range(3):
-        rows.append(rest.astype(BF16).astype(F32))
-        rest = rest - rows[-1]
+        rows.append(value.astype(BF16).astype(F32))
+        value = value - rows[-1]
     tail = jnp.concatenate(rows + [jnp.zeros((13, cells), F32)], axis=0)
     out[parts * depth :, :] = tail.astype(BF16)
 
 
 def pack(shard, volume, quads):
     parts, depth, cells = shard.shape
+    volume = volume.reshape(1, cells)
     return pl.pallas_call(
         pack_kernel,
+        in_specs=[pl.BlockSpec(memory_space=pl.ANY)] * 3,
+        out_specs=[pl.BlockSpec(memory_space=pltpu.VMEM)] * 2,
         out_shape=[jax.ShapeDtypeStruct((parts * depth + 16, cells), BF16), jax.ShapeDtypeStruct(quads.shape, I32)],
+        scratch_shapes=[pltpu.VMEM(volume.shape, F32), pltpu.SemaphoreType.DMA((parts + 2,))],
         compiler_params=params(),
         cost_estimate=pl.CostEstimate(flops=1000, bytes_accessed=1000, transcendentals=0),
         name="pack",
-    )(shard, volume.reshape(1, cells), quads)
+    )(*[pltpu.with_memory_space_constraint(x, pltpu.HBM) for x in (shard, volume, quads)])
 
 
 def products(offsets, rows, turned, depth):
@@ -270,7 +277,7 @@
     for part in received:
         total = total + part[: 2 * cells, :].astype(F32)
     out[...] = total / amount
-    lost = functools.reduce(jnp.add, [part[2 * cells : 2 * cells + 1, :].astype(F32) for part in received])
+    lost = functools.reduce(jnp.add, [part[2 * cells :, :].astype(F32)[:1] for part in received])
     here = rows_of(position()[2], cells)
     out[here, :] += jnp.where(diagonal(cells), lost / amount, 0.0)
 
@@ -327,7 +334,9 @@
     own_send = form("send", quads=columns, weight=weights, volume=volumes, shards=relayed, begun=begun)
     received = [hop(own_send, "cell", devices, 2 * d) for d in odds]
     other_send = hop(own_send, "cell", devices, 1)
-    columns, own_send, across = lax.optimization_barrier((columns, own_send, across))
+    first = {d: {k: across[d][k] for k in (0, far)} for d in evens}
+    columns, own_send, first = lax.optimization_barrier((columns, own_send, first))
+    across = {d: {**across[d], **first[d]} for d in evens}
     for d in evens:
         for j in range(1, half):
             across[d][far ^ j] = hop(across[d][far], "elec", groups, j)

time: 53.3 us -> 53.2 us (level)
  local copies, waits for them, and re-layouts: 2.52 us -> 0.04 us
  waiting for transfers between devices: 11.6 us -> 13.3 us
  Pallas kernels: 14.5 us -> 15.5 us
    unnamed x10 -> x4, local copies, waits for them, and re-layouts: 2.49 us -> 0.01 us
    ppermute x19, waiting for transfers between devices: 11.6 us -> 13.3 us  [hop(): return lax.ppermute(x, axis, [(i, i ^ mask) for i in range(size)])]
    pallas_call x1, Pallas kernels: 0.03 us -> 1 us  [pack(): pl.pallas_call(pack_kernel, in_specs=[pl.BlockSpec(memory_space=pl.ANY)]...]
  transfers between devices with their start and end apart: 19 -> 19, of which waited for: 9 -> 9; matrix products, arithmetic and copies ran while one was open for 0% -> 0% of each run, Pallas kernels for 26% -> 28%
where the time goes in v7:
time: 53.2 us; the launch traced here: 53 us
  starting transfers between devices  24.1 us (45%)
  Pallas kernels  15.5 us (29%)
  waiting for transfers between devices  13.3 us (25%)
    ppermute x19, starting transfers between devices, hop(): return lax.ppermute(x, axis, [(i, i ^ mask) for i in range(size)])  24.1 us
    pallas_call x9, Pallas kernels, whole_call(): pl.pallas_call(kernel, in_specs=[vmem] * len(arrays), out_specs=[vmem] *...  14.3 us
    ppermute x19, waiting for transfers between devices, hop(): return lax.ppermute(x, axis, [(i, i ^ mask) for i in range(size)])  13.3 us
  transfers between devices with their start and end apart: 19, of which 9 were waited for; matrix products, arithmetic and copies ran while one was open for 0% of the time, Pallas kernels for 28%

profile of v7, /device:TPU:0, one launch (start us, length us, event | category | flops | bytes accessed | tf_op | source)
XLA Modules:
  0.0 53.0 jit_solution(11787958480038793287)
XLA Ops:
  0.0 5.0 %collective-permute-start.1 = (bf16[3,256,128]{2,1,0:T(8,128)(2,1)}, bf16[3,256,128]{2,1,0:T(8,128)(2,1)S(1)}, u32[]{:S(2)}, u32[]{:S(2)}) collective-permute-start(bf16[3,256,128]{2,1,0:T(8,128)(2,1)} %shard.1), channel_id=1, source_target_pairs={{0,24},{8,16},{16,8},{24,0},{1,25},{9,17},{17,9},{25,1},{2,26},{10... | collective-permute-start | bytes 589832 | tf_op jit(solution)/shard_map/ppermute | solution.py:21
  5.1 1.0 %pack.1 = (bf16[784,128]{1,0:T(8,128)(2,1)S(1)}, s32[4,4096]{1,0:T(4,128)S(1)}) custom-call(bf16[3,256,128]{2,1,0:T(8,128)(2,1)} %shard.1, f32[1,128]{1,0:T(1,128)} %bitcast.10, s32[4,4096]{1,0:T(4,128)} %bitcast.13), custom_call_target="tpu_custom_call" | custom-call | flops 1000 | bytes 1000 | tf_op jit(solution)/shard_map/pack/pallas_call | solution.py:102
  6.1 2.5 %collective-permute-start.3 = (bf16[784,128]{1,0:T(8,128)(2,1)S(1)}, bf16[784,128]{1,0:T(8,128)(2,1)S(1)}, u32[]{:S(2)}, u32[]{:S(2)}) collective-permute-start(bf16[784,128]{1,0:T(8,128)(2,1)S(1)} %get-tuple-element.28), channel_id=1, source_target_pairs={{0,6},{1,7},{2,4},{3,5},{4,2},{5,3},{6,0},{7,1},{8,14},{9,15},{10,... | collective-permute-start | bytes 602120 | tf_op jit(solution)/shard_map/ppermute | solution.py:21
  8.6 2.3 %collective-permute-done.1.refs_2_ = bf16[3,256,128]{2,1,0:T(8,128)(2,1)S(1)} collective-permute-done((bf16[3,256,128]{2,1,0:T(8,128)(2,1)}, bf16[3,256,128]{2,1,0:T(8,128)(2,1)S(1)}, u32[]{:S(2)}, u32[]{:S(2)}) %collective-permute-start.1) | collective-permute-done | bytes 196640 | tf_op jit(solution)/shard_map/ppermute | solution.py:21
  10.8 3.3 %collective-permute-start.2 = (bf16[3,256,128]{2,1,0:T(8,128)(2,1)S(1)}, bf16[3,256,128]{2,1,0:T(8,128)(2,1)S(1)}, u32[]{:S(2)}, u32[]{:S(2)}) collective-permute-start(bf16[3,256,128]{2,1,0:T(8,128)(2,1)S(1)} %collective-permute-done.1.refs_2_), channel_id=1, source_target_pairs={{0,8},{8,0},{16,24},{24,16},{1,9},{9,1},{17,25},{25,17},{2,10},{10... | collective-permute-start | bytes 589832 | tf_op jit(solution)/shard_map/ppermute | solution.py:21
  14.1 2.4 %collective-permute-start.4 = (bf16[3,256,128]{2,1,0:T(8,128)(2,1)S(1)}, bf16[3,256,128]{2,1,0:T(8,128)(2,1)S(1)}, u32[]{:S(2)}, u32[]{:S(2)}) collective-permute-start(bf16[3,256,128]{2,1,0:T(8,128)(2,1)S(1)} %collective-permute-done.1.refs_2_), channel_id=1, source_target_pairs={{0,6},{1,7},{2,4},{3,5},{4,2},{5,3},{6,0},{7,1},{8,14},{9,15},{10,... | collective-permute-start | bytes 589832 | tf_op jit(solution)/shard_map/ppermute | solution.py:21
  16.6 0.2 turn_shards.1.turned.refs_0_
  16.8 2.6 %partial_products.1.refs_0_ = f32[2,384,2048]{2,1,0:T(8,128)S(1)} custom-call(s32[4,4096]{1,0:T(4,128)S(1)} %get-tuple-element.30.quads, bf16[384,768]{1,0:T(8,128)(2,1)S(1)} %turn_shards.1.turned.refs_0_), custom_call_target="tpu_custom_call" | custom-call | flops 1000 | bytes 1 | tf_op jit(solution)/shard_map/partial_products/pallas_call | solution.py:288
  19.4 0.7 %collective-permute-start.9 = (bf16[3,256,128]{2,1,0:T(8,128)(2,1)S(1)}, bf16[3,256,128]{2,1,0:T(8,128)(2,1)S(1)}, u32[]{:S(2)}, u32[]{:S(2)}) collective-permute-start(bf16[3,256,128]{2,1,0:T(8,128)(2,1)S(1)} %collective-permute-done.refs_1_), channel_id=1, source_target_pairs={{0,6},{1,7},{2,4},{3,5},{4,2},{5,3},{6,0},{7,1},{8,14},{9,15},{10,... | collective-permute-start | bytes 589832 | tf_op jit(solution)/shard_map/ppermute | solution.py:21
  20.2 1.7 %sensitivities.3.own_send = bf16[128,2048]{1,0:T(8,128)(2,1)S(1)} custom-call(s32[4,4096]{1,0:T(4,128)S(1)} %get-tuple-element.30.quads, f32[1,4096]{1,0:T(1,128)S(1)} %bitcast.7, f32[1,128]{1,0:T(1,128)S(1)} %bitcast.11, f32[2,384,2048]{2,1,0:T(8,128)S(1)} %partial_products.1.refs_0_, bf16[3,256,128]{2,1,0:T(8,128)(2,1)S(1)} %collective-permute-done.2.refs_1_), custom_call_target="tpu_custom_call" | custom-call | flops 805306368 | bytes 1 | tf_op jit(solution)/shard_map/sensitivities/pallas_call | solution.py:288
  22.0 1.4 %collective-permute-start.7 = (bf16[128,2048]{1,0:T(8,128)(2,1)S(1)}, bf16[128,2048]{1,0:T(8,128)(2,1)S(1)}, u32[]{:S(2)}, u32[]{:S(2)}) collective-permute-start(bf16[128,2048]{1,0:T(8,128)(2,1)S(1)} %sensitivities.3.own_send), channel_id=1, source_target_pairs={{0,4},{1,5},{2,6},{3,7},{4,0},{5,1},{6,2},{7,3},{8,12},{9,13},{10,... | collective-permute-start | bytes 1572872 | tf_op jit(solution)/shard_map/ppermute | solution.py:21
  23.4 1.5 %collective-permute-start.6 = (bf16[128,2048]{1,0:T(8,128)(2,1)S(1)}, bf16[128,2048]{1,0:T(8,128)(2,1)S(1)}, u32[]{:S(2)}, u32[]{:S(2)}) collective-permute-start(bf16[128,2048]{1,0:T(8,128)(2,1)S(1)} %sensitivities.3.own_send), channel_id=1, source_target_pairs={{0,2},{1,3},{2,0},{3,1},{4,6},{5,7},{6,4},{7,5},{8,10},{9,11},{10,... | collective-permute-start | bytes 1572872 | tf_op jit(solution)/shard_map/ppermute | solution.py:21
  24.9 0.4 collective-permute-start.10
  25.2 3.6 %sensitivities.4.own_keep = bf16[128,2048]{1,0:T(8,128)(2,1)S(1)} custom-call(s32[4,4096]{1,0:T(4,128)S(1)} %get-tuple-element.30.quads, f32[1,4096]{1,0:T(1,128)S(1)} %bitcast.8, f32[1,128]{1,0:T(1,128)S(1)} %bitcast.12, bf16[384,768]{1,0:T(8,128)(2,1)S(1)} %turn_shards.1.turned.refs_0_, bf16[3,256,128]{2,1,0:T(8,128)(2,1)S(1)} %collective-permute-done.2.refs_1_), custom_call_target="tpu_custom_call" | custom-call | flops 3221225472 | bytes 1 | tf_op jit(solution)/shard_map/sensitivities/pallas_call | solution.py:288
  28.9 2.7 %collective-permute-done.10.refs_2_ = bf16[3,256,128]{2,1,0:T(8,128)(2,1)S(1)} collective-permute-done((bf16[3,256,128]{2,1,0:T(8,128)(2,1)S(1)}, bf16[3,256,128]{2,1,0:T(8,128)(2,1)S(1)}, u32[]{:S(2)}, u32[]{:S(2)}) %collective-permute-start.10) | collective-permute-done | bytes 196640 | tf_op jit(solution)/shard_map/ppermute | solution.py:21
  31.6 3.5 %sensitivities.5.refs_0_ = bf16[128,2048]{1,0:T(8,128)(2,1)S(1)} custom-call(s32[4,4096]{1,0:T(4,128)S(1)} %get-tuple-element.30.quads, f32[1,4096]{1,0:T(1,128)S(1)} %bitcast.9, bf16[16,128]{1,0:T(8,128)(2,1)S(1)} %slice.13.volume, bf16[3,256,128]{2,1,0:T(8,128)(2,1)S(1)} %bitcast.6, bf16[3,256,128]{2,1,0:T(8,128)(2,1)S(1)} %collective-permute-done.9.refs_1_, ...), custom_call_target="tpu_custom_call" | custom-call | flops 12884901888 | bytes 1 | tf_op jit(solution)/shard_map/sensitivities/pallas_call | solution.py:288
  35.1 0.6 %early_blocks.1 = (f32[1,128,128]{2,1,0:T(8,128)S(1)}, bf16[1,128,128]{2,1,0:T(8,128)(2,1)S(1)}, bf16[256,128]{1,0:T(8,128)(2,1)S(1)}) custom-call(bf16[128,2048]{1,0:T(8,128)(2,1)S(1)} %sensitivities.3.own_send, bf16[128,2048]{1,0:T(8,128)(2,1)S(1)} %sensitivities.4.own_keep, bf16[128,2048]{1,0:T(8,128)(2,1)S(1)} %collective-permute-done.8.other_send, ...), custom_call_target="tpu_custom_call" | custom-call | flops 1000 | bytes 1 | tf_op jit(solution)/shard_map/early_blocks/pallas_call | solution.py:288
  35.7 0.7 %collective-permute-start.12 = (bf16[256,128]{1,0:T(8,128)(2,1)S(1)}, bf16[256,128]{1,0:T(8,128)(2,1)S(1)}, u32[]{:S(2)}, u32[]{:S(2)}) collective-permute-start(bf16[256,128]{1,0:T(8,128)(2,1)S(1)} %get-tuple-element.40), channel_id=1, source_target_pairs={{0,6},{1,7},{2,4},{3,5},{4,2},{5,3},{6,0},{7,1},{8,14},{9,15},{10,... | collective-permute-start | bytes 196616 | tf_op jit(solution)/shard_map/ppermute | solution.py:21
  36.5 0.8 %collective-permute-done.7.refs_1_ = bf16[128,2048]{1,0:T(8,128)(2,1)S(1)} collective-permute-done((bf16[128,2048]{1,0:T(8,128)(2,1)S(1)}, bf16[128,2048]{1,0:T(8,128)(2,1)S(1)}, u32[]{:S(2)}, u32[]{:S(2)}) %collective-permute-start.7) | collective-permute-done | bytes 524320 | tf_op jit(solution)/shard_map/ppermute | solution.py:21
  37.4 0.5 %late_blocks.1 = (f32[2,128,128]{2,1,0:T(8,128)S(1)}, bf16[2,128,128]{2,1,0:T(8,128)(2,1)S(1)}, bf16[256,128]{1,0:T(8,128)(2,1)S(1)}, bf16[256,128]{1,0:T(8,128)(2,1)S(1)}) custom-call(bf16[128,2048]{1,0:T(8,128)(2,1)S(1)} %sensitivities.4.own_keep, bf16[128,2048]{1,0:T(8,128)(2,1)S(1)} %collective-permute-done.5.other_keep, ...), custom_call_target="tpu_custom_call" | custom-call | flops 1000 | bytes 1 | tf_op jit(solution)/shard_map/late_blocks/pallas_call | solution.py:288
  38.0 2.2 %collective-permute-start.14 = (bf16[256,128]{1,0:T(8,128)(2,1)S(1)}, bf16[256,128]{1,0:T(8,128)(2,1)S(1)}, u32[]{:S(2)}, u32[]{:S(2)}) collective-permute-start(bf16[256,128]{1,0:T(8,128)(2,1)S(1)} %get-tuple-element.43), channel_id=1, source_target_pairs={{0,2},{1,3},{2,0},{3,1},{4,6},{5,7},{6,4},{7,5},{8,10},{9,11},{10,... | collective-permute-start | bytes 196616 | tf_op jit(solution)/shard_map/ppermute | solution.py:21
  40.2 0.2 collective-permute-start.11
  40.3 0.9 %own_block.1 = f32[256,128]{1,0:T(8,128)S(1)} custom-call(bf16[128,2048]{1,0:T(8,128)(2,1)S(1)} %sensitivities.3.own_send, bf16[128,2048]{1,0:T(8,128)(2,1)S(1)} %sensitivities.4.own_keep, bf16[128,2048]{1,0:T(8,128)(2,1)S(1)} %collective-permute-done.8.other_send, bf16[128,2048]{1,0:T(8,128)(2,1)S(1)} %collective-permute-done.5.other_keep), custom_call_target="tpu_custom_call" | custom-call | flops 1000 | bytes 1 | tf_op jit(solution)/shard_map/own_block/pallas_call | solution.py:288
  41.2 0.2 collective-permute-done.11.refs_1_
  41.4 1.5 %collective-permute-done.14.refs_5_ = bf16[256,128]{1,0:T(8,128)(2,1)S(1)} collective-permute-done((bf16[256,128]{1,0:T(8,128)(2,1)S(1)}, bf16[256,128]{1,0:T(8,128)(2,1)S(1)}, u32[]{:S(2)}, u32[]{:S(2)}) %collective-permute-start.14) | collective-permute-done | bytes 65568 | tf_op jit(solution)/shard_map/ppermute | solution.py:21
  42.9 1.6 %collective-permute-done.15.refs_6_ = bf16[256,128]{1,0:T(8,128)(2,1)S(1)} collective-permute-done((bf16[256,128]{1,0:T(8,128)(2,1)S(1)}, bf16[256,128]{1,0:T(8,128)(2,1)S(1)}, u32[]{:S(2)}, u32[]{:S(2)}) %collective-permute-start.15) | collective-permute-done | bytes 65568 | tf_op jit(solution)/shard_map/ppermute | solution.py:21
  44.6 0.8 %collective-permute-start.16 = (bf16[272,128]{1,0:T(8,128)(2,1)S(1)}, bf16[272,128]{1,0:T(8,128)(2,1)S(1)}, u32[]{:S(2)}, u32[]{:S(2)}) collective-permute-start(bf16[272,128]{1,0:T(8,128)(2,1)S(1)} %get-tuple-element.46), channel_id=1, source_target_pairs={{0,16},{8,24},{16,0},{24,8},{1,17},{9,25},{17,1},{25,9},{2,18},{10... | collective-permute-start | bytes 208904 | tf_op jit(solution)/shard_map/ppermute | solution.py:21
  45.3 1.4 %collective-permute-start.17 = (bf16[272,128]{1,0:T(8,128)(2,1)S(1)}, bf16[272,128]{1,0:T(8,128)(2,1)S(1)}, u32[]{:S(2)}, u32[]{:S(2)}) collective-permute-start(bf16[272,128]{1,0:T(8,128)(2,1)S(1)} %get-tuple-element.47), channel_id=1, source_target_pairs={{0,24},{8,16},{16,8},{24,0},{1,25},{9,17},{17,9},{25,1},{2,26},{10... | collective-permute-start | bytes 208904 | tf_op jit(solution)/shard_map/ppermute | solution.py:21
  46.7 1.4 %collective-permute-start.18 = (bf16[272,128]{1,0:T(8,128)(2,1)S(1)}, bf16[272,128]{1,0:T(8,128)(2,1)S(1)}, u32[]{:S(2)}, u32[]{:S(2)}) collective-permute-start(bf16[272,128]{1,0:T(8,128)(2,1)S(1)} %get-tuple-element.48), channel_id=1, source_target_pairs={{0,8},{8,0},{16,24},{24,16},{1,9},{9,1},{17,25},{25,17},{2,10},{10... | collective-permute-start | bytes 208904 | tf_op jit(solution)/shard_map/ppermute | solution.py:21
  48.1 3.8 %collective-permute-done.16.refs_0_ = bf16[272,128]{1,0:T(8,128)(2,1)S(1)} collective-permute-done((bf16[272,128]{1,0:T(8,128)(2,1)S(1)}, bf16[272,128]{1,0:T(8,128)(2,1)S(1)}, u32[]{:S(2)}, u32[]{:S(2)}) %collective-permute-start.16) | collective-permute-done | bytes 69664 | tf_op jit(solution)/shard_map/ppermute | solution.py:21
  51.9 0.4 collective-permute-done.18.refs_2_
  52.3 0.7 %finish.1 = f32[256,128]{1,0:T(8,128)} custom-call(f32[256,128]{1,0:T(8,128)S(1)} %get-tuple-element.45.own, bf16[272,128]{1,0:T(8,128)(2,1)S(1)} %collective-permute-done.16.refs_0_, bf16[272,128]{1,0:T(8,128)(2,1)S(1)} %collective-permute-done.17.refs_1_, bf16[272,128]{1,0:T(8,128)(2,1)S(1)} %collective-permute-done.18.refs_2_), custom_call_target="tpu_custom_call" | custom-call | flops 1000 | bytes 1 | tf_op jit(solution)/shard_map/finish/pallas_call | solution.py:288
  (24 shorter events, 0.5 us)
Async XLA Ops:
  0.0 20.2 %copy-start.1 = (f32[128]{0:T(128)S(1)}, f32[128]{0:T(128)}, u32[]{:S(2)}) copy-start(f32[128]{0:T(128)} %param.6) | copy-start | bytes 1540
  0.0 20.2 %copy-start = (f32[4096]{0:T(1024)S(1)}, f32[4096]{0:T(1024)}, u32[]{:S(2)}) copy-start(f32[4096]{0:T(1024)} %param.7) | copy-start | bytes 49156
  0.0 10.8 %collective-permute-start.1 = (bf16[3,256,128]{2,1,0:T(8,128)(2,1)}, bf16[3,256,128]{2,1,0:T(8,128)(2,1)S(1)}, u32[]{:S(2)}, u32[]{:S(2)}) collective-permute-start(bf16[3,256,128]{2,1,0:T(8,128)(2,1)} %shard.1), channel_id=1, source_target_pairs={{0,24},{8,16},{16,8},{24,0},{1,25},{9,17},{17,9},{25,1},{2,26},{10... | collective-permute-start | bytes 589832 | tf_op jit(solution)/shard_map/ppermute | solution.py:21
  6.1 14.1 %collective-permute-start.3 = (bf16[784,128]{1,0:T(8,128)(2,1)S(1)}, bf16[784,128]{1,0:T(8,128)(2,1)S(1)}, u32[]{:S(2)}, u32[]{:S(2)}) collective-permute-start(bf16[784,128]{1,0:T(8,128)(2,1)S(1)} %get-tuple-element.28), channel_id=1, source_target_pairs={{0,6},{1,7},{2,4},{3,5},{4,2},{5,3},{6,0},{7,1},{8,14},{9,15},{10,... | collective-permute-start | bytes 602120 | tf_op jit(solution)/shard_map/ppermute | solution.py:21
  8.6 8.0 %collective-permute-start = (bf16[3,256,128]{2,1,0:T(8,128)(2,1)}, bf16[3,256,128]{2,1,0:T(8,128)(2,1)S(1)}, u32[]{:S(2)}, u32[]{:S(2)}) collective-permute-start(bf16[3,256,128]{2,1,0:T(8,128)(2,1)} %shard.1), channel_id=1, source_target_pairs={{0,8},{8,0},{16,24},{24,16},{1,9},{9,1},{17,25},{25,17},{2,10},{10... | collective-permute-start | bytes 589832 | tf_op jit(solution)/shard_map/ppermute | solution.py:21
  10.8 9.4 %collective-permute-start.2 = (bf16[3,256,128]{2,1,0:T(8,128)(2,1)S(1)}, bf16[3,256,128]{2,1,0:T(8,128)(2,1)S(1)}, u32[]{:S(2)}, u32[]{:S(2)}) collective-permute-start(bf16[3,256,128]{2,1,0:T(8,128)(2,1)S(1)} %collective-permute-done.1.refs_2_), channel_id=1, source_target_pairs={{0,8},{8,0},{16,24},{24,16},{1,9},{9,1},{17,25},{25,17},{2,10},{10... | collective-permute-start | bytes 589832 | tf_op jit(solution)/shard_map/ppermute | solution.py:21
  14.1 10.8 %collective-permute-start.4 = (bf16[3,256,128]{2,1,0:T(8,128)(2,1)S(1)}, bf16[3,256,128]{2,1,0:T(8,128)(2,1)S(1)}, u32[]{:S(2)}, u32[]{:S(2)}) collective-permute-start(bf16[3,256,128]{2,1,0:T(8,128)(2,1)S(1)} %collective-permute-done.1.refs_2_), channel_id=1, source_target_pairs={{0,6},{1,7},{2,4},{3,5},{4,2},{5,3},{6,0},{7,1},{8,14},{9,15},{10,... | collective-permute-start | bytes 589832 | tf_op jit(solution)/shard_map/ppermute | solution.py:21
  19.4 9.4 %collective-permute-start.9 = (bf16[3,256,128]{2,1,0:T(8,128)(2,1)S(1)}, bf16[3,256,128]{2,1,0:T(8,128)(2,1)S(1)}, u32[]{:S(2)}, u32[]{:S(2)}) collective-permute-start(bf16[3,256,128]{2,1,0:T(8,128)(2,1)S(1)} %collective-permute-done.refs_1_), channel_id=1, source_target_pairs={{0,6},{1,7},{2,4},{3,5},{4,2},{5,3},{6,0},{7,1},{8,14},{9,15},{10,... | collective-permute-start | bytes 589832 | tf_op jit(solution)/shard_map/ppermute | solution.py:21
  21.9 13.2 %collective-permute-start.8 = (bf16[128,2048]{1,0:T(8,128)(2,1)S(1)}, bf16[128,2048]{1,0:T(8,128)(2,1)S(1)}, u32[]{:S(2)}, u32[]{:S(2)}) collective-permute-start(bf16[128,2048]{1,0:T(8,128)(2,1)S(1)} %sensitivities.3.own_send), channel_id=1, source_target_pairs={{0,1},{1,0},{2,3},{3,2},{4,5},{5,4},{6,7},{7,6},{8,9},{9,8},{10,11... | collective-permute-start | bytes 1572872 | tf_op jit(solution)/shard_map/ppermute | solution.py:21
  22.0 15.3 %collective-permute-start.7 = (bf16[128,2048]{1,0:T(8,128)(2,1)S(1)}, bf16[128,2048]{1,0:T(8,128)(2,1)S(1)}, u32[]{:S(2)}, u32[]{:S(2)}) collective-permute-start(bf16[128,2048]{1,0:T(8,128)(2,1)S(1)} %sensitivities.3.own_send), channel_id=1, source_target_pairs={{0,4},{1,5},{2,6},{3,7},{4,0},{5,1},{6,2},{7,3},{8,12},{9,13},{10,... | collective-permute-start | bytes 1572872 | tf_op jit(solution)/shard_map/ppermute | solution.py:21
  23.4 14.0 %collective-permute-start.6 = (bf16[128,2048]{1,0:T(8,128)(2,1)S(1)}, bf16[128,2048]{1,0:T(8,128)(2,1)S(1)}, u32[]{:S(2)}, u32[]{:S(2)}) collective-permute-start(bf16[128,2048]{1,0:T(8,128)(2,1)S(1)} %sensitivities.3.own_send), channel_id=1, source_target_pairs={{0,2},{1,3},{2,0},{3,1},{4,6},{5,7},{6,4},{7,5},{8,10},{9,11},{10,... | collective-permute-start | bytes 1572872 | tf_op jit(solution)/shard_map/ppermute | solution.py:21
  24.9 6.7 %collective-permute-start.10 = (bf16[3,256,128]{2,1,0:T(8,128)(2,1)S(1)}, bf16[3,256,128]{2,1,0:T(8,128)(2,1)S(1)}, u32[]{:S(2)}, u32[]{:S(2)}) collective-permute-start(bf16[3,256,128]{2,1,0:T(8,128)(2,1)S(1)} %collective-permute-done.4.refs_3_), channel_id=1, source_target_pairs={{0,8},{8,0},{16,24},{24,16},{1,9},{9,1},{17,25},{25,17},{2,10},{10... | collective-permute-start | bytes 589832 | tf_op jit(solution)/shard_map/ppermute | solution.py:21
  28.8 6.3 %collective-permute-start.5 = (bf16[128,2048]{1,0:T(8,128)(2,1)S(1)}, bf16[128,2048]{1,0:T(8,128)(2,1)S(1)}, u32[]{:S(2)}, u32[]{:S(2)}) collective-permute-start(bf16[128,2048]{1,0:T(8,128)(2,1)S(1)} %sensitivities.4.own_keep), channel_id=1, source_target_pairs={{0,1},{1,0},{2,3},{3,2},{4,5},{5,4},{6,7},{7,6},{8,9},{9,8},{10,11... | collective-permute-start | bytes 1572872 | tf_op jit(solution)/shard_map/ppermute | solution.py:21
  35.7 5.6 %collective-permute-start.12 = (bf16[256,128]{1,0:T(8,128)(2,1)S(1)}, bf16[256,128]{1,0:T(8,128)(2,1)S(1)}, u32[]{:S(2)}, u32[]{:S(2)}) collective-permute-start(bf16[256,128]{1,0:T(8,128)(2,1)S(1)} %get-tuple-element.40), channel_id=1, source_target_pairs={{0,6},{1,7},{2,4},{3,5},{4,2},{5,3},{6,0},{7,1},{8,14},{9,15},{10,... | collective-permute-start | bytes 196616 | tf_op jit(solution)/shard_map/ppermute | solution.py:21
  37.9 3.5 %collective-permute-start.13 = (bf16[2,128,128]{2,1,0:T(8,128)(2,1)S(1)}, bf16[2,128,128]{2,1,0:T(8,128)(2,1)S(1)}, u32[]{:S(2)}, u32[]{:S(2)}) collective-permute-start(bf16[2,128,128]{2,1,0:T(8,128)(2,1)S(1)} %get-tuple-element.42), channel_id=1, source_target_pairs={{0,1},{1,0},{2,3},{3,2},{4,5},{5,4},{6,7},{7,6},{8,9},{9,8},{10,11... | collective-permute-start | bytes 196616 | tf_op jit(solution)/shard_map/ppermute | solution.py:21
  38.0 4.9 %collective-permute-start.14 = (bf16[256,128]{1,0:T(8,128)(2,1)S(1)}, bf16[256,128]{1,0:T(8,128)(2,1)S(1)}, u32[]{:S(2)}, u32[]{:S(2)}) collective-permute-start(bf16[256,128]{1,0:T(8,128)(2,1)S(1)} %get-tuple-element.43), channel_id=1, source_target_pairs={{0,2},{1,3},{2,0},{3,1},{4,6},{5,7},{6,4},{7,5},{8,10},{9,11},{10,... | collective-permute-start | bytes 196616 | tf_op jit(solution)/shard_map/ppermute | solution.py:21
  40.2 4.3 %collective-permute-start.15 = (bf16[256,128]{1,0:T(8,128)(2,1)S(1)}, bf16[256,128]{1,0:T(8,128)(2,1)S(1)}, u32[]{:S(2)}, u32[]{:S(2)}) collective-permute-start(bf16[256,128]{1,0:T(8,128)(2,1)S(1)} %get-tuple-element.44), channel_id=1, source_target_pairs={{0,4},{1,5},{2,6},{3,7},{4,0},{5,1},{6,2},{7,3},{8,12},{9,13},{10,... | collective-permute-start | bytes 196616 | tf_op jit(solution)/shard_map/ppermute | solution.py:21
  40.2 1.2 %collective-permute-start.11 = (bf16[1,128,128]{2,1,0:T(8,128)(2,1)S(1)}, bf16[1,128,128]{2,1,0:T(8,128)(2,1)S(1)}, u32[]{:S(2)}, u32[]{:S(2)}) collective-permute-start(bf16[1,128,128]{2,1,0:T(8,128)(2,1)S(1)} %get-tuple-element.39), channel_id=1, source_target_pairs={{0,1},{1,0},{2,3},{3,2},{4,5},{5,4},{6,7},{7,6},{8,9},{9,8},{10,11... | collective-permute-start | bytes 98312 | tf_op jit(solution)/shard_map/ppermute | solution.py:21
  44.6 7.3 %collective-permute-start.16 = (bf16[272,128]{1,0:T(8,128)(2,1)S(1)}, bf16[272,128]{1,0:T(8,128)(2,1)S(1)}, u32[]{:S(2)}, u32[]{:S(2)}) collective-permute-start(bf16[272,128]{1,0:T(8,128)(2,1)S(1)} %get-tuple-element.46), channel_id=1, source_target_pairs={{0,16},{8,24},{16,0},{24,8},{1,17},{9,25},{17,1},{25,9},{2,18},{10... | collective-permute-start | bytes 208904 | tf_op jit(solution)/shard_map/ppermute | solution.py:21
  45.3 6.6 %collective-permute-start.17 = (bf16[272,128]{1,0:T(8,128)(2,1)S(1)}, bf16[272,128]{1,0:T(8,128)(2,1)S(1)}, u32[]{:S(2)}, u32[]{:S(2)}) collective-permute-start(bf16[272,128]{1,0:T(8,128)(2,1)S(1)} %get-tuple-element.47), channel_id=1, source_target_pairs={{0,24},{8,16},{16,8},{24,0},{1,25},{9,17},{17,9},{25,1},{2,26},{10... | collective-permute-start | bytes 208904 | tf_op jit(solution)/shard_map/ppermute | solution.py:21
  46.7 5.6 %collective-permute-start.18 = (bf16[272,128]{1,0:T(8,128)(2,1)S(1)}, bf16[272,128]{1,0:T(8,128)(2,1)S(1)}, u32[]{:S(2)}, u32[]{:S(2)}) collective-permute-start(bf16[272,128]{1,0:T(8,128)(2,1)S(1)} %get-tuple-element.48), channel_id=1, source_target_pairs={{0,8},{8,0},{16,24},{24,16},{1,9},{9,1},{17,25},{25,17},{2,10},{10... | collective-permute-start | bytes 208904 | tf_op jit(solution)/shard_map/ppermute | solution.py:21

commit v8 on v7

--- a/solution.py
+++ b/solution.py
@@ -8,7 +8,7 @@
 from jax.sharding import PartitionSpec as P
 
 F32, BF16, I32 = jnp.float32, jnp.bfloat16, jnp.int32
-WEIGH = 4
+WEIGH = 16
 TILES = 4
 LIMIT = 24 * 1024 * 1024
 
@@ -344,8 +344,11 @@
     other_keep = hop(own_keep, "cell", devices, 1)
     recomputed = []
     for d in evens:
+        turned = turn_shards([across[d][k] for k in ready])
+        begun = partial_products(d, bits, columns, turned, ready)
+        rest = {k: across[d][k] for k in across[d] if k not in ready}
         recomputed.append(
-            form(d, quads=columns, weight=weights, volume=volumes_across[d], shards=across[d], weigh=WEIGH)
+            form(d, quads=columns, weight=weights, volume=volumes_across[d], shards=rest, begun=begun, weigh=WEIGH)
         )
 
     whole, small = (2 * cells, cells), (cells, cells)

time: 53.2 us -> 52.6 us (0.989)
  waiting for transfers between devices: 13.3 us -> 9.99 us
  starting transfers between devices: 24.1 us -> 25.8 us
  Pallas kernels: 15.5 us -> 16.4 us
    ppermute x19, waiting for transfers between devices: 13.3 us -> 9.99 us  [hop(): return lax.ppermute(x, axis, [(i, i ^ mask) for i in range(size)])]
    ppermute x19, starting transfers between devices: 24.1 us -> 25.8 us  [hop(): return lax.ppermute(x, axis, [(i, i ^ mask) for i in range(size)])]
    pallas_call x9 -> x10, Pallas kernels: 14.3 us -> 15 us  [whole_call(): pl.pallas_call(kernel, in_specs=[vmem] * len(arrays), out_specs=[vmem] *...]
  transfers between devices with their start and end apart: 19 -> 19, of which waited for: 9 -> 8; matrix products, arithmetic and copies ran while one was open for 0% -> 0% of each run, Pallas kernels for 28% -> 30%
where the time goes in v8:
time: 52.6 us; the launch traced here: 52.5 us
  starting transfers between devices  25.8 us (49%)
  Pallas kernels  16.4 us (31%)
  waiting for transfers between devices  9.99 us (19%)
    ppermute x19, starting transfers between devices, hop(): return lax.ppermute(x, axis, [(i, i ^ mask) for i in range(size)])  25.8 us
    pallas_call x10, Pallas kernels, whole_call(): pl.pallas_call(kernel, in_specs=[vmem] * len(arrays), out_specs=[vmem] *...  15 us
    ppermute x19, waiting for transfers between devices, hop(): return lax.ppermute(x, axis, [(i, i ^ mask) for i in range(size)])  9.99 us
  transfers between devices with their start and end apart: 19, of which 8 were waited for; matrix products, arithmetic and copies ran while one was open for 0% of the time, Pallas kernels for 30%

profile of v8, /device:TPU:0, one launch (start us, length us, event | category | flops | bytes accessed | tf_op | source)
XLA Modules:
  0.0 52.5 jit_solution(3761808146280497030)
XLA Ops:
  0.0 5.0 %collective-permute-start.1 = (bf16[3,256,128]{2,1,0:T(8,128)(2,1)}, bf16[3,256,128]{2,1,0:T(8,128)(2,1)S(1)}, u32[]{:S(2)}, u32[]{:S(2)}) collective-permute-start(bf16[3,256,128]{2,1,0:T(8,128)(2,1)} %shard.1), channel_id=1, source_target_pairs={{0,24},{8,16},{16,8},{24,0},{1,25},{9,17},{17,9},{25,1},{2,26},{10... | collective-permute-start | bytes 589832 | tf_op jit(solution)/shard_map/ppermute | solution.py:21
  5.1 1.0 %pack.1 = (bf16[784,128]{1,0:T(8,128)(2,1)S(1)}, s32[4,4096]{1,0:T(4,128)S(1)}) custom-call(bf16[3,256,128]{2,1,0:T(8,128)(2,1)} %shard.1, f32[1,128]{1,0:T(1,128)} %bitcast.10, s32[4,4096]{1,0:T(4,128)} %bitcast.13), custom_call_target="tpu_custom_call" | custom-call | flops 1000 | bytes 1000 | tf_op jit(solution)/shard_map/pack/pallas_call | solution.py:102
  6.1 2.5 %collective-permute-start.3 = (bf16[784,128]{1,0:T(8,128)(2,1)S(1)}, bf16[784,128]{1,0:T(8,128)(2,1)S(1)}, u32[]{:S(2)}, u32[]{:S(2)}) collective-permute-start(bf16[784,128]{1,0:T(8,128)(2,1)S(1)} %get-tuple-element.28), channel_id=1, source_target_pairs={{0,6},{1,7},{2,4},{3,5},{4,2},{5,3},{6,0},{7,1},{8,14},{9,15},{10,... | collective-permute-start | bytes 602120 | tf_op jit(solution)/shard_map/ppermute | solution.py:21
  8.6 2.5 %collective-permute-done.1.refs_2_ = bf16[3,256,128]{2,1,0:T(8,128)(2,1)S(1)} collective-permute-done((bf16[3,256,128]{2,1,0:T(8,128)(2,1)}, bf16[3,256,128]{2,1,0:T(8,128)(2,1)S(1)}, u32[]{:S(2)}, u32[]{:S(2)}) %collective-permute-start.1) | collective-permute-done | bytes 196640 | tf_op jit(solution)/shard_map/ppermute | solution.py:21
  11.0 3.1 %collective-permute-start.2 = (bf16[3,256,128]{2,1,0:T(8,128)(2,1)S(1)}, bf16[3,256,128]{2,1,0:T(8,128)(2,1)S(1)}, u32[]{:S(2)}, u32[]{:S(2)}) collective-permute-start(bf16[3,256,128]{2,1,0:T(8,128)(2,1)S(1)} %collective-permute-done.1.refs_2_), channel_id=1, source_target_pairs={{0,8},{8,0},{16,24},{24,16},{1,9},{9,1},{17,25},{25,17},{2,10},{10... | collective-permute-start | bytes 589832 | tf_op jit(solution)/shard_map/ppermute | solution.py:21
  14.1 2.4 %collective-permute-start.4 = (bf16[3,256,128]{2,1,0:T(8,128)(2,1)S(1)}, bf16[3,256,128]{2,1,0:T(8,128)(2,1)S(1)}, u32[]{:S(2)}, u32[]{:S(2)}) collective-permute-start(bf16[3,256,128]{2,1,0:T(8,128)(2,1)S(1)} %collective-permute-done.1.refs_2_), channel_id=1, source_target_pairs={{0,6},{1,7},{2,4},{3,5},{4,2},{5,3},{6,0},{7,1},{8,14},{9,15},{10,... | collective-permute-start | bytes 589832 | tf_op jit(solution)/shard_map/ppermute | solution.py:21
  16.5 0.5 collective-permute-start.9
  17.0 0.2 turn_shards.2.turned.refs_0_
  17.2 2.6 %partial_products.2.refs_0_ = f32[2,384,2048]{2,1,0:T(8,128)S(1)} custom-call(s32[4,4096]{1,0:T(4,128)S(1)} %get-tuple-element.30.quads, bf16[384,768]{1,0:T(8,128)(2,1)S(1)} %turn_shards.2.turned.refs_0_), custom_call_target="tpu_custom_call" | custom-call | flops 1000 | bytes 1 | tf_op jit(solution)/shard_map/partial_products/pallas_call | solution.py:288
  20.0 1.7 %sensitivities.3.own_send = bf16[128,2048]{1,0:T(8,128)(2,1)S(1)} custom-call(s32[4,4096]{1,0:T(4,128)S(1)} %get-tuple-element.30.quads, f32[1,4096]{1,0:T(1,128)S(1)} %bitcast.7, f32[1,128]{1,0:T(1,128)S(1)} %bitcast.11, f32[2,384,2048]{2,1,0:T(8,128)S(1)} %partial_products.2.refs_0_, bf16[3,256,128]{2,1,0:T(8,128)(2,1)S(1)} %collective-permute-done.2.refs_1_), custom_call_target="tpu_custom_call" | custom-call | flops 805306368 | bytes 1 | tf_op jit(solution)/shard_map/sensitivities/pallas_call | solution.py:288
  21.7 1.5 %collective-permute-start.6 = (bf16[128,2048]{1,0:T(8,128)(2,1)S(1)}, bf16[128,2048]{1,0:T(8,128)(2,1)S(1)}, u32[]{:S(2)}, u32[]{:S(2)}) collective-permute-start(bf16[128,2048]{1,0:T(8,128)(2,1)S(1)} %sensitivities.3.own_send), channel_id=1, source_target_pairs={{0,2},{1,3},{2,0},{3,1},{4,6},{5,7},{6,4},{7,5},{8,10},{9,11},{10,... | collective-permute-start | bytes 1572872 | tf_op jit(solution)/shard_map/ppermute | solution.py:21
  23.3 1.5 %collective-permute-start.7 = (bf16[128,2048]{1,0:T(8,128)(2,1)S(1)}, bf16[128,2048]{1,0:T(8,128)(2,1)S(1)}, u32[]{:S(2)}, u32[]{:S(2)}) collective-permute-start(bf16[128,2048]{1,0:T(8,128)(2,1)S(1)} %sensitivities.3.own_send), channel_id=1, source_target_pairs={{0,4},{1,5},{2,6},{3,7},{4,0},{5,1},{6,2},{7,3},{8,12},{9,13},{10,... | collective-permute-start | bytes 1572872 | tf_op jit(solution)/shard_map/ppermute | solution.py:21
  24.8 0.4 collective-permute-start.10
  25.4 2.6 %partial_products.3.refs_0_ = f32[2,384,2048]{2,1,0:T(8,128)S(1)} custom-call(s32[4,4096]{1,0:T(4,128)S(1)} %get-tuple-element.30.quads, bf16[384,768]{1,0:T(8,128)(2,1)S(1)} %turn_shards.3.turned), custom_call_target="tpu_custom_call" | custom-call | flops 1000 | bytes 1 | tf_op jit(solution)/shard_map/partial_products/pallas_call | solution.py:288
  28.1 3.5 %sensitivities.4.own_keep = bf16[128,2048]{1,0:T(8,128)(2,1)S(1)} custom-call(s32[4,4096]{1,0:T(4,128)S(1)} %get-tuple-element.30.quads, f32[1,4096]{1,0:T(1,128)S(1)} %bitcast.8, f32[1,128]{1,0:T(1,128)S(1)} %bitcast.12, bf16[384,768]{1,0:T(8,128)(2,1)S(1)} %turn_shards.2.turned.refs_0_, bf16[3,256,128]{2,1,0:T(8,128)(2,1)S(1)} %collective-permute-done.2.refs_1_), custom_call_target="tpu_custom_call" | custom-call | flops 3221225472 | bytes 1 | tf_op jit(solution)/shard_map/sensitivities/pallas_call | solution.py:288
  31.7 1.7 %sensitivities.5.refs_0_ = bf16[128,2048]{1,0:T(8,128)(2,1)S(1)} custom-call(s32[4,4096]{1,0:T(4,128)S(1)} %get-tuple-element.30.quads, f32[1,4096]{1,0:T(1,128)S(1)} %bitcast.9, bf16[16,128]{1,0:T(8,128)(2,1)S(1)} %slice.13.volume, f32[2,384,2048]{2,1,0:T(8,128)S(1)} %partial_products.3.refs_0_, bf16[3,256,128]{2,1,0:T(8,128)(2,1)S(1)} %collective-permute-done.10.refs_1_), custom_call_target="tpu_custom_call" | custom-call | flops 12884901888 | bytes 1 | tf_op jit(solution)/shard_map/sensitivities/pallas_call | solution.py:288
  33.4 0.2 collective-permute-done.5.other_keep
  33.6 0.6 %early_blocks.1 = (f32[1,128,128]{2,1,0:T(8,128)S(1)}, bf16[1,128,128]{2,1,0:T(8,128)(2,1)S(1)}, bf16[256,128]{1,0:T(8,128)(2,1)S(1)}) custom-call(bf16[128,2048]{1,0:T(8,128)(2,1)S(1)} %sensitivities.3.own_send, bf16[128,2048]{1,0:T(8,128)(2,1)S(1)} %sensitivities.4.own_keep, bf16[128,2048]{1,0:T(8,128)(2,1)S(1)} %collective-permute-done.8.other_send, ...), custom_call_target="tpu_custom_call" | custom-call | flops 1000 | bytes 1 | tf_op jit(solution)/shard_map/early_blocks/pallas_call | solution.py:288
  34.2 2.2 %collective-permute-start.12 = (bf16[256,128]{1,0:T(8,128)(2,1)S(1)}, bf16[256,128]{1,0:T(8,128)(2,1)S(1)}, u32[]{:S(2)}, u32[]{:S(2)}) collective-permute-start(bf16[256,128]{1,0:T(8,128)(2,1)S(1)} %get-tuple-element.40), channel_id=1, source_target_pairs={{0,6},{1,7},{2,4},{3,5},{4,2},{5,3},{6,0},{7,1},{8,14},{9,15},{10,... | collective-permute-start | bytes 196616 | tf_op jit(solution)/shard_map/ppermute | solution.py:21
  36.4 0.9 %collective-permute-done.7.refs_1_ = bf16[128,2048]{1,0:T(8,128)(2,1)S(1)} collective-permute-done((bf16[128,2048]{1,0:T(8,128)(2,1)S(1)}, bf16[128,2048]{1,0:T(8,128)(2,1)S(1)}, u32[]{:S(2)}, u32[]{:S(2)}) %collective-permute-start.7) | collective-permute-done | bytes 524320 | tf_op jit(solution)/shard_map/ppermute | solution.py:21
  37.3 0.5 %late_blocks.1 = (f32[2,128,128]{2,1,0:T(8,128)S(1)}, bf16[2,128,128]{2,1,0:T(8,128)(2,1)S(1)}, bf16[256,128]{1,0:T(8,128)(2,1)S(1)}, bf16[256,128]{1,0:T(8,128)(2,1)S(1)}) custom-call(bf16[128,2048]{1,0:T(8,128)(2,1)S(1)} %sensitivities.4.own_keep, bf16[128,2048]{1,0:T(8,128)(2,1)S(1)} %collective-permute-done.5.other_keep, ...), custom_call_target="tpu_custom_call" | custom-call | flops 1000 | bytes 1 | tf_op jit(solution)/shard_map/late_blocks/pallas_call | solution.py:288
  37.9 0.6 %collective-permute-start.14 = (bf16[256,128]{1,0:T(8,128)(2,1)S(1)}, bf16[256,128]{1,0:T(8,128)(2,1)S(1)}, u32[]{:S(2)}, u32[]{:S(2)}) collective-permute-start(bf16[256,128]{1,0:T(8,128)(2,1)S(1)} %get-tuple-element.43), channel_id=1, source_target_pairs={{0,2},{1,3},{2,0},{3,1},{4,6},{5,7},{6,4},{7,5},{8,10},{9,11},{10,... | collective-permute-start | bytes 196616 | tf_op jit(solution)/shard_map/ppermute | solution.py:21
  38.5 1.5 %collective-permute-start.15 = (bf16[256,128]{1,0:T(8,128)(2,1)S(1)}, bf16[256,128]{1,0:T(8,128)(2,1)S(1)}, u32[]{:S(2)}, u32[]{:S(2)}) collective-permute-start(bf16[256,128]{1,0:T(8,128)(2,1)S(1)} %get-tuple-element.44), channel_id=1, source_target_pairs={{0,4},{1,5},{2,6},{3,7},{4,0},{5,1},{6,2},{7,3},{8,12},{9,13},{10,... | collective-permute-start | bytes 196616 | tf_op jit(solution)/shard_map/ppermute | solution.py:21
  40.0 0.9 %own_block.1 = f32[256,128]{1,0:T(8,128)S(1)} custom-call(bf16[128,2048]{1,0:T(8,128)(2,1)S(1)} %sensitivities.3.own_send, bf16[128,2048]{1,0:T(8,128)(2,1)S(1)} %sensitivities.4.own_keep, bf16[128,2048]{1,0:T(8,128)(2,1)S(1)} %collective-permute-done.8.other_send, bf16[128,2048]{1,0:T(8,128)(2,1)S(1)} %collective-permute-done.5.other_keep), custom_call_target="tpu_custom_call" | custom-call | flops 1000 | bytes 1 | tf_op jit(solution)/shard_map/own_block/pallas_call | solution.py:288
  40.9 0.3 collective-permute-done.11.refs_1_
  41.2 1.2 %collective-permute-done.14.refs_5_ = bf16[256,128]{1,0:T(8,128)(2,1)S(1)} collective-permute-done((bf16[256,128]{1,0:T(8,128)(2,1)S(1)}, bf16[256,128]{1,0:T(8,128)(2,1)S(1)}, u32[]{:S(2)}, u32[]{:S(2)}) %collective-permute-start.14) | collective-permute-done | bytes 65568 | tf_op jit(solution)/shard_map/ppermute | solution.py:21
  42.4 0.4 collective-permute-done.15.refs_6_
  42.9 1.4 %collective-permute-start.16 = (bf16[272,128]{1,0:T(8,128)(2,1)S(1)}, bf16[272,128]{1,0:T(8,128)(2,1)S(1)}, u32[]{:S(2)}, u32[]{:S(2)}) collective-permute-start(bf16[272,128]{1,0:T(8,128)(2,1)S(1)} %get-tuple-element.46), channel_id=1, source_target_pairs={{0,16},{8,24},{16,0},{24,8},{1,17},{9,25},{17,1},{25,9},{2,18},{10... | collective-permute-start | bytes 208904 | tf_op jit(solution)/shard_map/ppermute | solution.py:21
  44.3 2.9 %collective-permute-start.17 = (bf16[272,128]{1,0:T(8,128)(2,1)S(1)}, bf16[272,128]{1,0:T(8,128)(2,1)S(1)}, u32[]{:S(2)}, u32[]{:S(2)}) collective-permute-start(bf16[272,128]{1,0:T(8,128)(2,1)S(1)} %get-tuple-element.47), channel_id=1, source_target_pairs={{0,24},{8,16},{16,8},{24,0},{1,25},{9,17},{17,9},{25,1},{2,26},{10... | collective-permute-start | bytes 208904 | tf_op jit(solution)/shard_map/ppermute | solution.py:21
  47.2 4.1 %collective-permute-done.16.refs_0_ = bf16[272,128]{1,0:T(8,128)(2,1)S(1)} collective-permute-done((bf16[272,128]{1,0:T(8,128)(2,1)S(1)}, bf16[272,128]{1,0:T(8,128)(2,1)S(1)}, u32[]{:S(2)}, u32[]{:S(2)}) %collective-permute-start.16) | collective-permute-done | bytes 69664 | tf_op jit(solution)/shard_map/ppermute | solution.py:21
  51.2 0.5 collective-permute-done.18.refs_2_
  51.7 0.7 %finish.1 = f32[256,128]{1,0:T(8,128)} custom-call(f32[256,128]{1,0:T(8,128)S(1)} %get-tuple-element.45.own, bf16[272,128]{1,0:T(8,128)(2,1)S(1)} %collective-permute-done.16.refs_0_, bf16[272,128]{1,0:T(8,128)(2,1)S(1)} %collective-permute-done.17.refs_1_, bf16[272,128]{1,0:T(8,128)(2,1)S(1)} %collective-permute-done.18.refs_2_), custom_call_target="tpu_custom_call" | custom-call | flops 1000 | bytes 1 | tf_op jit(solution)/shard_map/finish/pallas_call | solution.py:288
  (26 shorter events, 0.6 us)
Async XLA Ops:
  0.0 20.0 %copy-start.1 = (f32[128]{0:T(128)S(1)}, f32[128]{0:T(128)}, u32[]{:S(2)}) copy-start(f32[128]{0:T(128)} %param.6) | copy-start | bytes 1540
  0.0 20.0 %copy-start = (f32[4096]{0:T(1024)S(1)}, f32[4096]{0:T(1024)}, u32[]{:S(2)}) copy-start(f32[4096]{0:T(1024)} %param.7) | copy-start | bytes 49156
  0.0 11.0 %collective-permute-start.1 = (bf16[3,256,128]{2,1,0:T(8,128)(2,1)}, bf16[3,256,128]{2,1,0:T(8,128)(2,1)S(1)}, u32[]{:S(2)}, u32[]{:S(2)}) collective-permute-start(bf16[3,256,128]{2,1,0:T(8,128)(2,1)} %shard.1), channel_id=1, source_target_pairs={{0,24},{8,16},{16,8},{24,0},{1,25},{9,17},{17,9},{25,1},{2,26},{10... | collective-permute-start | bytes 589832 | tf_op jit(solution)/shard_map/ppermute | solution.py:21
  5.1 11.5 %collective-permute-start = (bf16[3,256,128]{2,1,0:T(8,128)(2,1)}, bf16[3,256,128]{2,1,0:T(8,128)(2,1)S(1)}, u32[]{:S(2)}, u32[]{:S(2)}) collective-permute-start(bf16[3,256,128]{2,1,0:T(8,128)(2,1)} %shard.1), channel_id=1, source_target_pairs={{0,8},{8,0},{16,24},{24,16},{1,9},{9,1},{17,25},{25,17},{2,10},{10... | collective-permute-start | bytes 589832 | tf_op jit(solution)/shard_map/ppermute | solution.py:21
  6.1 13.8 %collective-permute-start.3 = (bf16[784,128]{1,0:T(8,128)(2,1)S(1)}, bf16[784,128]{1,0:T(8,128)(2,1)S(1)}, u32[]{:S(2)}, u32[]{:S(2)}) collective-permute-start(bf16[784,128]{1,0:T(8,128)(2,1)S(1)} %get-tuple-element.28), channel_id=1, source_target_pairs={{0,6},{1,7},{2,4},{3,5},{4,2},{5,3},{6,0},{7,1},{8,14},{9,15},{10,... | collective-permute-start | bytes 602120 | tf_op jit(solution)/shard_map/ppermute | solution.py:21
  11.0 8.9 %collective-permute-start.2 = (bf16[3,256,128]{2,1,0:T(8,128)(2,1)S(1)}, bf16[3,256,128]{2,1,0:T(8,128)(2,1)S(1)}, u32[]{:S(2)}, u32[]{:S(2)}) collective-permute-start(bf16[3,256,128]{2,1,0:T(8,128)(2,1)S(1)} %collective-permute-done.1.refs_2_), channel_id=1, source_target_pairs={{0,8},{8,0},{16,24},{24,16},{1,9},{9,1},{17,25},{25,17},{2,10},{10... | collective-permute-start | bytes 589832 | tf_op jit(solution)/shard_map/ppermute | solution.py:21
  14.1 10.7 %collective-permute-start.4 = (bf16[3,256,128]{2,1,0:T(8,128)(2,1)S(1)}, bf16[3,256,128]{2,1,0:T(8,128)(2,1)S(1)}, u32[]{:S(2)}, u32[]{:S(2)}) collective-permute-start(bf16[3,256,128]{2,1,0:T(8,128)(2,1)S(1)} %collective-permute-done.1.refs_2_), channel_id=1, source_target_pairs={{0,6},{1,7},{2,4},{3,5},{4,2},{5,3},{6,0},{7,1},{8,14},{9,15},{10,... | collective-permute-start | bytes 589832 | tf_op jit(solution)/shard_map/ppermute | solution.py:21
  16.5 8.7 %collective-permute-start.9 = (bf16[3,256,128]{2,1,0:T(8,128)(2,1)S(1)}, bf16[3,256,128]{2,1,0:T(8,128)(2,1)S(1)}, u32[]{:S(2)}, u32[]{:S(2)}) collective-permute-start(bf16[3,256,128]{2,1,0:T(8,128)(2,1)S(1)} %collective-permute-done.refs_1_), channel_id=1, source_target_pairs={{0,6},{1,7},{2,4},{3,5},{4,2},{5,3},{6,0},{7,1},{8,14},{9,15},{10,... | collective-permute-start | bytes 589832 | tf_op jit(solution)/shard_map/ppermute | solution.py:21
  21.7 12.0 %collective-permute-start.8 = (bf16[128,2048]{1,0:T(8,128)(2,1)S(1)}, bf16[128,2048]{1,0:T(8,128)(2,1)S(1)}, u32[]{:S(2)}, u32[]{:S(2)}) collective-permute-start(bf16[128,2048]{1,0:T(8,128)(2,1)S(1)} %sensitivities.3.own_send), channel_id=1, source_target_pairs={{0,1},{1,0},{2,3},{3,2},{4,5},{5,4},{6,7},{7,6},{8,9},{9,8},{10,11... | collective-permute-start | bytes 1572872 | tf_op jit(solution)/shard_map/ppermute | solution.py:21
  21.7 14.7 %collective-permute-start.6 = (bf16[128,2048]{1,0:T(8,128)(2,1)S(1)}, bf16[128,2048]{1,0:T(8,128)(2,1)S(1)}, u32[]{:S(2)}, u32[]{:S(2)}) collective-permute-start(bf16[128,2048]{1,0:T(8,128)(2,1)S(1)} %sensitivities.3.own_send), channel_id=1, source_target_pairs={{0,2},{1,3},{2,0},{3,1},{4,6},{5,7},{6,4},{7,5},{8,10},{9,11},{10,... | collective-permute-start | bytes 1572872 | tf_op jit(solution)/shard_map/ppermute | solution.py:21
  23.3 14.0 %collective-permute-start.7 = (bf16[128,2048]{1,0:T(8,128)(2,1)S(1)}, bf16[128,2048]{1,0:T(8,128)(2,1)S(1)}, u32[]{:S(2)}, u32[]{:S(2)}) collective-permute-start(bf16[128,2048]{1,0:T(8,128)(2,1)S(1)} %sensitivities.3.own_send), channel_id=1, source_target_pairs={{0,4},{1,5},{2,6},{3,7},{4,0},{5,1},{6,2},{7,3},{8,12},{9,13},{10,... | collective-permute-start | bytes 1572872 | tf_op jit(solution)/shard_map/ppermute | solution.py:21
  24.8 6.9 %collective-permute-start.10 = (bf16[3,256,128]{2,1,0:T(8,128)(2,1)S(1)}, bf16[3,256,128]{2,1,0:T(8,128)(2,1)S(1)}, u32[]{:S(2)}, u32[]{:S(2)}) collective-permute-start(bf16[3,256,128]{2,1,0:T(8,128)(2,1)S(1)} %collective-permute-done.4.refs_2_), channel_id=1, source_target_pairs={{0,8},{8,0},{16,24},{24,16},{1,9},{9,1},{17,25},{25,17},{2,10},{10... | collective-permute-start | bytes 589832 | tf_op jit(solution)/shard_map/ppermute | solution.py:21
  31.6 2.0 %collective-permute-start.5 = (bf16[128,2048]{1,0:T(8,128)(2,1)S(1)}, bf16[128,2048]{1,0:T(8,128)(2,1)S(1)}, u32[]{:S(2)}, u32[]{:S(2)}) collective-permute-start(bf16[128,2048]{1,0:T(8,128)(2,1)S(1)} %sensitivities.4.own_keep), channel_id=1, source_target_pairs={{0,1},{1,0},{2,3},{3,2},{4,5},{5,4},{6,7},{7,6},{8,9},{9,8},{10,11... | collective-permute-start | bytes 1572872 | tf_op jit(solution)/shard_map/ppermute | solution.py:21
  34.2 7.0 %collective-permute-start.12 = (bf16[256,128]{1,0:T(8,128)(2,1)S(1)}, bf16[256,128]{1,0:T(8,128)(2,1)S(1)}, u32[]{:S(2)}, u32[]{:S(2)}) collective-permute-start(bf16[256,128]{1,0:T(8,128)(2,1)S(1)} %get-tuple-element.40), channel_id=1, source_target_pairs={{0,6},{1,7},{2,4},{3,5},{4,2},{5,3},{6,0},{7,1},{8,14},{9,15},{10,... | collective-permute-start | bytes 196616 | tf_op jit(solution)/shard_map/ppermute | solution.py:21
  37.8 3.4 %collective-permute-start.13 = (bf16[2,128,128]{2,1,0:T(8,128)(2,1)S(1)}, bf16[2,128,128]{2,1,0:T(8,128)(2,1)S(1)}, u32[]{:S(2)}, u32[]{:S(2)}) collective-permute-start(bf16[2,128,128]{2,1,0:T(8,128)(2,1)S(1)} %get-tuple-element.42), channel_id=1, source_target_pairs={{0,1},{1,0},{2,3},{3,2},{4,5},{5,4},{6,7},{7,6},{8,9},{9,8},{10,11... | collective-permute-start | bytes 196616 | tf_op jit(solution)/shard_map/ppermute | solution.py:21
  37.9 4.5 %collective-permute-start.14 = (bf16[256,128]{1,0:T(8,128)(2,1)S(1)}, bf16[256,128]{1,0:T(8,128)(2,1)S(1)}, u32[]{:S(2)}, u32[]{:S(2)}) collective-permute-start(bf16[256,128]{1,0:T(8,128)(2,1)S(1)} %get-tuple-element.43), channel_id=1, source_target_pairs={{0,2},{1,3},{2,0},{3,1},{4,6},{5,7},{6,4},{7,5},{8,10},{9,11},{10,... | collective-permute-start | bytes 196616 | tf_op jit(solution)/shard_map/ppermute | solution.py:21
  38.5 4.3 %collective-permute-start.15 = (bf16[256,128]{1,0:T(8,128)(2,1)S(1)}, bf16[256,128]{1,0:T(8,128)(2,1)S(1)}, u32[]{:S(2)}, u32[]{:S(2)}) collective-permute-start(bf16[256,128]{1,0:T(8,128)(2,1)S(1)} %get-tuple-element.44), channel_id=1, source_target_pairs={{0,4},{1,5},{2,6},{3,7},{4,0},{5,1},{6,2},{7,3},{8,12},{9,13},{10,... | collective-permute-start | bytes 196616 | tf_op jit(solution)/shard_map/ppermute | solution.py:21
  40.0 1.2 %collective-permute-start.11 = (bf16[1,128,128]{2,1,0:T(8,128)(2,1)S(1)}, bf16[1,128,128]{2,1,0:T(8,128)(2,1)S(1)}, u32[]{:S(2)}, u32[]{:S(2)}) collective-permute-start(bf16[1,128,128]{2,1,0:T(8,128)(2,1)S(1)} %get-tuple-element.39), channel_id=1, source_target_pairs={{0,1},{1,0},{2,3},{3,2},{4,5},{5,4},{6,7},{7,6},{8,9},{9,8},{10,11... | collective-permute-start | bytes 98312 | tf_op jit(solution)/shard_map/ppermute | solution.py:21
  42.9 8.3 %collective-permute-start.16 = (bf16[272,128]{1,0:T(8,128)(2,1)S(1)}, bf16[272,128]{1,0:T(8,128)(2,1)S(1)}, u32[]{:S(2)}, u32[]{:S(2)}) collective-permute-start(bf16[272,128]{1,0:T(8,128)(2,1)S(1)} %get-tuple-element.46), channel_id=1, source_target_pairs={{0,16},{8,24},{16,0},{24,8},{1,17},{9,25},{17,1},{25,9},{2,18},{10... | collective-permute-start | bytes 208904 | tf_op jit(solution)/shard_map/ppermute | solution.py:21
  44.3 6.9 %collective-permute-start.17 = (bf16[272,128]{1,0:T(8,128)(2,1)S(1)}, bf16[272,128]{1,0:T(8,128)(2,1)S(1)}, u32[]{:S(2)}, u32[]{:S(2)}) collective-permute-start(bf16[272,128]{1,0:T(8,128)(2,1)S(1)} %get-tuple-element.47), channel_id=1, source_target_pairs={{0,24},{8,16},{16,8},{24,0},{1,25},{9,17},{17,9},{25,1},{2,26},{10... | collective-permute-start | bytes 208904 | tf_op jit(solution)/shard_map/ppermute | solution.py:21
  47.2 4.6 %collective-permute-start.18 = (bf16[272,128]{1,0:T(8,128)(2,1)S(1)}, bf16[272,128]{1,0:T(8,128)(2,1)S(1)}, u32[]{:S(2)}, u32[]{:S(2)}) collective-permute-start(bf16[272,128]{1,0:T(8,128)(2,1)S(1)} %get-tuple-element.48), channel_id=1, source_target_pairs={{0,8},{8,0},{16,24},{24,16},{1,9},{9,1},{17,25},{25,17},{2,10},{10... | collective-permute-start | bytes 208904 | tf_op jit(solution)/shard_map/ppermute | solution.py:21

commit v9 on v8

--- a/solution.py
+++ b/solution.py
@@ -317,6 +317,7 @@
     weights = weight.reshape(1, measured)
     volumes = volume.reshape(1, cells)
     relayed = {far ^ j: shards[far ^ j] for j in range(1, half)}
+    relayed.update({j: shards[j] for j in range(1, half)})
     direct = {k: shards[k] for k in shards if k not in relayed}
     ready = tuple(sorted(direct))
     turned = turn_shards([direct[k] for k in ready])

time: 52.6 us -> 52.4 us (level)
  waiting for transfers between devices: 9.99 us -> 10.9 us
  starting transfers between devices: 25.8 us -> 25 us
    ppermute x19, waiting for transfers between devices: 9.99 us -> 10.9 us  [hop(): return lax.ppermute(x, axis, [(i, i ^ mask) for i in range(size)])]
    ppermute x19, starting transfers between devices: 25.8 us -> 25 us  [hop(): return lax.ppermute(x, axis, [(i, i ^ mask) for i in range(size)])]
  transfers between devices with their start and end apart: 19 -> 19, of which waited for: 8 -> 9; matrix products, arithmetic and copies ran while one was open for 0% -> 0% of each run, Pallas kernels for 30% -> 29%
where the time goes in v9:
time: 52.4 us; the launch traced here: 52.3 us
  starting transfers between devices  25 us (48%)
  Pallas kernels  16.1 us (31%)
  waiting for transfers between devices  10.9 us (21%)
    ppermute x19, starting transfers between devices, hop(): return lax.ppermute(x, axis, [(i, i ^ mask) for i in range(size)])  25 us
    pallas_call x10, Pallas kernels, whole_call(): pl.pallas_call(kernel, in_specs=[vmem] * len(arrays), out_specs=[vmem] *...  14.8 us
    ppermute x19, waiting for transfers between devices, hop(): return lax.ppermute(x, axis, [(i, i ^ mask) for i in range(size)])  10.9 us
  transfers between devices with their start and end apart: 19, of which 9 were waited for; matrix products, arithmetic and copies ran while one was open for 0% of the time, Pallas kernels for 29%

profile of v9, /device:TPU:0, one launch (start us, length us, event | category | flops | bytes accessed | tf_op | source)
XLA Modules:
  0.0 52.3 jit_solution(11744103443017790413)
XLA Ops:
  0.0 5.0 %collective-permute-start = (bf16[3,256,128]{2,1,0:T(8,128)(2,1)}, bf16[3,256,128]{2,1,0:T(8,128)(2,1)S(1)}, u32[]{:S(2)}, u32[]{:S(2)}) collective-permute-start(bf16[3,256,128]{2,1,0:T(8,128)(2,1)} %shard.1), channel_id=1, source_target_pairs={{0,24},{8,16},{16,8},{24,0},{1,25},{9,17},{17,9},{25,1},{2,26},{10... | collective-permute-start | bytes 589832 | tf_op jit(solution)/shard_map/ppermute | solution.py:21
  5.1 1.0 %pack.1 = (bf16[784,128]{1,0:T(8,128)(2,1)S(1)}, s32[4,4096]{1,0:T(4,128)S(1)}) custom-call(bf16[3,256,128]{2,1,0:T(8,128)(2,1)} %shard.1, f32[1,128]{1,0:T(1,128)} %bitcast.10, s32[4,4096]{1,0:T(4,128)} %bitcast.13), custom_call_target="tpu_custom_call" | custom-call | flops 1000 | bytes 1000 | tf_op jit(solution)/shard_map/pack/pallas_call | solution.py:102
  6.1 2.5 %collective-permute-start.3 = (bf16[784,128]{1,0:T(8,128)(2,1)S(1)}, bf16[784,128]{1,0:T(8,128)(2,1)S(1)}, u32[]{:S(2)}, u32[]{:S(2)}) collective-permute-start(bf16[784,128]{1,0:T(8,128)(2,1)S(1)} %get-tuple-element.28), channel_id=1, source_target_pairs={{0,6},{1,7},{2,4},{3,5},{4,2},{5,3},{6,0},{7,1},{8,14},{9,15},{10,... | collective-permute-start | bytes 602120 | tf_op jit(solution)/shard_map/ppermute | solution.py:21
  8.6 2.3 %collective-permute-done.refs_1_ = bf16[3,256,128]{2,1,0:T(8,128)(2,1)S(1)} collective-permute-done((bf16[3,256,128]{2,1,0:T(8,128)(2,1)}, bf16[3,256,128]{2,1,0:T(8,128)(2,1)S(1)}, u32[]{:S(2)}, u32[]{:S(2)}) %collective-permute-start) | collective-permute-done | bytes 196640 | tf_op jit(solution)/shard_map/ppermute | solution.py:21
  10.8 3.3 %collective-permute-start.2 = (bf16[3,256,128]{2,1,0:T(8,128)(2,1)S(1)}, bf16[3,256,128]{2,1,0:T(8,128)(2,1)S(1)}, u32[]{:S(2)}, u32[]{:S(2)}) collective-permute-start(bf16[3,256,128]{2,1,0:T(8,128)(2,1)S(1)} %collective-permute-done.refs_1_), channel_id=1, source_target_pairs={{0,8},{8,0},{16,24},{24,16},{1,9},{9,1},{17,25},{25,17},{2,10},{10... | collective-permute-start | bytes 589832 | tf_op jit(solution)/shard_map/ppermute | solution.py:21
  14.1 2.4 %collective-permute-start.4 = (bf16[3,256,128]{2,1,0:T(8,128)(2,1)S(1)}, bf16[3,256,128]{2,1,0:T(8,128)(2,1)S(1)}, u32[]{:S(2)}, u32[]{:S(2)}) collective-permute-start(bf16[3,256,128]{2,1,0:T(8,128)(2,1)S(1)} %collective-permute-done.refs_1_), channel_id=1, source_target_pairs={{0,6},{1,7},{2,4},{3,5},{4,2},{5,3},{6,0},{7,1},{8,14},{9,15},{10,... | collective-permute-start | bytes 589832 | tf_op jit(solution)/shard_map/ppermute | solution.py:21
  16.7 1.8 %partial_products.2.refs_0_ = f32[2,384,2048]{2,1,0:T(8,128)S(1)} custom-call(s32[4,4096]{1,0:T(4,128)S(1)} %get-tuple-element.30.quads, bf16[384,512]{1,0:T(8,128)(2,1)S(1)} %turn_shards.2.turned.refs_0_), custom_call_target="tpu_custom_call" | custom-call | flops 1000 | bytes 1 | tf_op jit(solution)/shard_map/partial_products/pallas_call | solution.py:288
  18.6 0.5 %collective-permute-start.9 = (bf16[3,256,128]{2,1,0:T(8,128)(2,1)S(1)}, bf16[3,256,128]{2,1,0:T(8,128)(2,1)S(1)}, u32[]{:S(2)}, u32[]{:S(2)}) collective-permute-start(bf16[3,256,128]{2,1,0:T(8,128)(2,1)S(1)} %collective-permute-done.1.refs_1_), channel_id=1, source_target_pairs={{0,6},{1,7},{2,4},{3,5},{4,2},{5,3},{6,0},{7,1},{8,14},{9,15},{10,... | collective-permute-start | bytes 589832 | tf_op jit(solution)/shard_map/ppermute | solution.py:21
  19.2 2.4 %sensitivities.3.own_send = bf16[128,2048]{1,0:T(8,128)(2,1)S(1)} custom-call(s32[4,4096]{1,0:T(4,128)S(1)} %get-tuple-element.30.quads, f32[1,4096]{1,0:T(1,128)S(1)} %bitcast.7, f32[1,128]{1,0:T(1,128)S(1)} %bitcast.11, f32[2,384,2048]{2,1,0:T(8,128)S(1)} %partial_products.2.refs_0_, bf16[3,256,128]{2,1,0:T(8,128)(2,1)S(1)} %collective-permute-done.1.refs_1_, ...), custom_call_target="tpu_custom_call" | custom-call | flops 1610612736 | bytes 1 | tf_op jit(solution)/shard_map/sensitivities/pallas_call | solution.py:288
  21.6 1.5 %collective-permute-start.6 = (bf16[128,2048]{1,0:T(8,128)(2,1)S(1)}, bf16[128,2048]{1,0:T(8,128)(2,1)S(1)}, u32[]{:S(2)}, u32[]{:S(2)}) collective-permute-start(bf16[128,2048]{1,0:T(8,128)(2,1)S(1)} %sensitivities.3.own_send), channel_id=1, source_target_pairs={{0,2},{1,3},{2,0},{3,1},{4,6},{5,7},{6,4},{7,5},{8,10},{9,11},{10,... | collective-permute-start | bytes 1572872 | tf_op jit(solution)/shard_map/ppermute | solution.py:21
  23.2 1.5 %collective-permute-start.7 = (bf16[128,2048]{1,0:T(8,128)(2,1)S(1)}, bf16[128,2048]{1,0:T(8,128)(2,1)S(1)}, u32[]{:S(2)}, u32[]{:S(2)}) collective-permute-start(bf16[128,2048]{1,0:T(8,128)(2,1)S(1)} %sensitivities.3.own_send), channel_id=1, source_target_pairs={{0,4},{1,5},{2,6},{3,7},{4,0},{5,1},{6,2},{7,3},{8,12},{9,13},{10,... | collective-permute-start | bytes 1572872 | tf_op jit(solution)/shard_map/ppermute | solution.py:21
  24.7 1.2 %collective-permute-start.10 = (bf16[3,256,128]{2,1,0:T(8,128)(2,1)S(1)}, bf16[3,256,128]{2,1,0:T(8,128)(2,1)S(1)}, u32[]{:S(2)}, u32[]{:S(2)}) collective-permute-start(bf16[3,256,128]{2,1,0:T(8,128)(2,1)S(1)} %collective-permute-done.4.refs_1_), channel_id=1, source_target_pairs={{0,8},{8,0},{16,24},{24,16},{1,9},{9,1},{17,25},{25,17},{2,10},{10... | collective-permute-start | bytes 589832 | tf_op jit(solution)/shard_map/ppermute | solution.py:21
  26.1 1.8 %partial_products.3.refs_0_ = f32[2,384,2048]{2,1,0:T(8,128)S(1)} custom-call(s32[4,4096]{1,0:T(4,128)S(1)} %get-tuple-element.30.quads, bf16[384,512]{1,0:T(8,128)(2,1)S(1)} %turn_shards.3.turned), custom_call_target="tpu_custom_call" | custom-call | flops 1000 | bytes 1 | tf_op jit(solution)/shard_map/partial_products/pallas_call | solution.py:288
  27.9 3.5 %sensitivities.4.own_keep = bf16[128,2048]{1,0:T(8,128)(2,1)S(1)} custom-call(s32[4,4096]{1,0:T(4,128)S(1)} %get-tuple-element.30.quads, f32[1,4096]{1,0:T(1,128)S(1)} %bitcast.8, f32[1,128]{1,0:T(1,128)S(1)} %bitcast.12, bf16[384,512]{1,0:T(8,128)(2,1)S(1)} %turn_shards.2.turned.refs_0_, bf16[3,256,128]{2,1,0:T(8,128)(2,1)S(1)} %collective-permute-done.1.refs_1_, ...), custom_call_target="tpu_custom_call" | custom-call | flops 3221225472 | bytes 1 | tf_op jit(solution)/shard_map/sensitivities/pallas_call | solution.py:288
  31.6 2.4 %sensitivities.5.refs_0_ = bf16[128,2048]{1,0:T(8,128)(2,1)S(1)} custom-call(s32[4,4096]{1,0:T(4,128)S(1)} %get-tuple-element.30.quads, f32[1,4096]{1,0:T(1,128)S(1)} %bitcast.9, bf16[16,128]{1,0:T(8,128)(2,1)S(1)} %slice.13.volume, f32[2,384,2048]{2,1,0:T(8,128)S(1)} %partial_products.3.refs_0_, bf16[3,256,128]{2,1,0:T(8,128)(2,1)S(1)} %collective-permute-done.9.refs_1_, ...), custom_call_target="tpu_custom_call" | custom-call | flops 25769803776 | bytes 1 | tf_op jit(solution)/shard_map/sensitivities/pallas_call | solution.py:288
  34.0 0.6 %early_blocks.1 = (f32[1,128,128]{2,1,0:T(8,128)S(1)}, bf16[1,128,128]{2,1,0:T(8,128)(2,1)S(1)}, bf16[256,128]{1,0:T(8,128)(2,1)S(1)}) custom-call(bf16[128,2048]{1,0:T(8,128)(2,1)S(1)} %sensitivities.3.own_send, bf16[128,2048]{1,0:T(8,128)(2,1)S(1)} %sensitivities.4.own_keep, bf16[128,2048]{1,0:T(8,128)(2,1)S(1)} %collective-permute-done.8.other_send, ...), custom_call_target="tpu_custom_call" | custom-call | flops 1000 | bytes 1 | tf_op jit(solution)/shard_map/early_blocks/pallas_call | solution.py:288
  34.6 0.5 %collective-permute-start.12 = (bf16[256,128]{1,0:T(8,128)(2,1)S(1)}, bf16[256,128]{1,0:T(8,128)(2,1)S(1)}, u32[]{:S(2)}, u32[]{:S(2)}) collective-permute-start(bf16[256,128]{1,0:T(8,128)(2,1)S(1)} %get-tuple-element.40), channel_id=1, source_target_pairs={{0,6},{1,7},{2,4},{3,5},{4,2},{5,3},{6,0},{7,1},{8,14},{9,15},{10,... | collective-permute-start | bytes 196616 | tf_op jit(solution)/shard_map/ppermute | solution.py:21
  35.1 1.1 %collective-permute-done.6.refs_0_ = bf16[128,2048]{1,0:T(8,128)(2,1)S(1)} collective-permute-done((bf16[128,2048]{1,0:T(8,128)(2,1)S(1)}, bf16[128,2048]{1,0:T(8,128)(2,1)S(1)}, u32[]{:S(2)}, u32[]{:S(2)}) %collective-permute-start.6) | collective-permute-done | bytes 524320 | tf_op jit(solution)/shard_map/ppermute | solution.py:21
  36.2 1.0 %collective-permute-done.7.refs_1_ = bf16[128,2048]{1,0:T(8,128)(2,1)S(1)} collective-permute-done((bf16[128,2048]{1,0:T(8,128)(2,1)S(1)}, bf16[128,2048]{1,0:T(8,128)(2,1)S(1)}, u32[]{:S(2)}, u32[]{:S(2)}) %collective-permute-start.7) | collective-permute-done | bytes 524320 | tf_op jit(solution)/shard_map/ppermute | solution.py:21
  37.2 0.5 %late_blocks.1 = (f32[2,128,128]{2,1,0:T(8,128)S(1)}, bf16[2,128,128]{2,1,0:T(8,128)(2,1)S(1)}, bf16[256,128]{1,0:T(8,128)(2,1)S(1)}, bf16[256,128]{1,0:T(8,128)(2,1)S(1)}) custom-call(bf16[128,2048]{1,0:T(8,128)(2,1)S(1)} %sensitivities.4.own_keep, bf16[128,2048]{1,0:T(8,128)(2,1)S(1)} %collective-permute-done.5.other_keep, ...), custom_call_target="tpu_custom_call" | custom-call | flops 1000 | bytes 1 | tf_op jit(solution)/shard_map/late_blocks/pallas_call | solution.py:288
  37.8 0.6 %collective-permute-start.14 = (bf16[256,128]{1,0:T(8,128)(2,1)S(1)}, bf16[256,128]{1,0:T(8,128)(2,1)S(1)}, u32[]{:S(2)}, u32[]{:S(2)}) collective-permute-start(bf16[256,128]{1,0:T(8,128)(2,1)S(1)} %get-tuple-element.43), channel_id=1, source_target_pairs={{0,2},{1,3},{2,0},{3,1},{4,6},{5,7},{6,4},{7,5},{8,10},{9,11},{10,... | collective-permute-start | bytes 196616 | tf_op jit(solution)/shard_map/ppermute | solution.py:21
  38.4 1.5 %collective-permute-start.15 = (bf16[256,128]{1,0:T(8,128)(2,1)S(1)}, bf16[256,128]{1,0:T(8,128)(2,1)S(1)}, u32[]{:S(2)}, u32[]{:S(2)}) collective-permute-start(bf16[256,128]{1,0:T(8,128)(2,1)S(1)} %get-tuple-element.44), channel_id=1, source_target_pairs={{0,4},{1,5},{2,6},{3,7},{4,0},{5,1},{6,2},{7,3},{8,12},{9,13},{10,... | collective-permute-start | bytes 196616 | tf_op jit(solution)/shard_map/ppermute | solution.py:21
  39.9 0.9 %own_block.1 = f32[256,128]{1,0:T(8,128)S(1)} custom-call(bf16[128,2048]{1,0:T(8,128)(2,1)S(1)} %sensitivities.3.own_send, bf16[128,2048]{1,0:T(8,128)(2,1)S(1)} %sensitivities.4.own_keep, bf16[128,2048]{1,0:T(8,128)(2,1)S(1)} %collective-permute-done.8.other_send, bf16[128,2048]{1,0:T(8,128)(2,1)S(1)} %collective-permute-done.5.other_keep), custom_call_target="tpu_custom_call" | custom-call | flops 1000 | bytes 1 | tf_op jit(solution)/shard_map/own_block/pallas_call | solution.py:288
  41.2 1.2 %collective-permute-done.14.refs_5_ = bf16[256,128]{1,0:T(8,128)(2,1)S(1)} collective-permute-done((bf16[256,128]{1,0:T(8,128)(2,1)S(1)}, bf16[256,128]{1,0:T(8,128)(2,1)S(1)}, u32[]{:S(2)}, u32[]{:S(2)}) %collective-permute-start.14) | collective-permute-done | bytes 65568 | tf_op jit(solution)/shard_map/ppermute | solution.py:21
  42.3 0.4 collective-permute-done.15.refs_6_
  42.8 1.8 %collective-permute-start.16 = (bf16[272,128]{1,0:T(8,128)(2,1)S(1)}, bf16[272,128]{1,0:T(8,128)(2,1)S(1)}, u32[]{:S(2)}, u32[]{:S(2)}) collective-permute-start(bf16[272,128]{1,0:T(8,128)(2,1)S(1)} %get-tuple-element.46), channel_id=1, source_target_pairs={{0,16},{8,24},{16,0},{24,8},{1,17},{9,25},{17,1},{25,9},{2,18},{10... | collective-permute-start | bytes 208904 | tf_op jit(solution)/shard_map/ppermute | solution.py:21
  44.6 1.9 %collective-permute-start.17 = (bf16[272,128]{1,0:T(8,128)(2,1)S(1)}, bf16[272,128]{1,0:T(8,128)(2,1)S(1)}, u32[]{:S(2)}, u32[]{:S(2)}) collective-permute-start(bf16[272,128]{1,0:T(8,128)(2,1)S(1)} %get-tuple-element.47), channel_id=1, source_target_pairs={{0,24},{8,16},{16,8},{24,0},{1,25},{9,17},{17,9},{25,1},{2,26},{10... | collective-permute-start | bytes 208904 | tf_op jit(solution)/shard_map/ppermute | solution.py:21
  46.4 0.4 collective-permute-start.18
  46.9 3.4 %collective-permute-done.16.refs_0_ = bf16[272,128]{1,0:T(8,128)(2,1)S(1)} collective-permute-done((bf16[272,128]{1,0:T(8,128)(2,1)S(1)}, bf16[272,128]{1,0:T(8,128)(2,1)S(1)}, u32[]{:S(2)}, u32[]{:S(2)}) %collective-permute-start.16) | collective-permute-done | bytes 69664 | tf_op jit(solution)/shard_map/ppermute | solution.py:21
  50.3 0.8 %collective-permute-done.17.refs_1_ = bf16[272,128]{1,0:T(8,128)(2,1)S(1)} collective-permute-done((bf16[272,128]{1,0:T(8,128)(2,1)S(1)}, bf16[272,128]{1,0:T(8,128)(2,1)S(1)}, u32[]{:S(2)}, u32[]{:S(2)}) %collective-permute-start.17) | collective-permute-done | bytes 69664 | tf_op jit(solution)/shard_map/ppermute | solution.py:21
  51.1 0.4 collective-permute-done.18.refs_2_
  51.6 0.7 %finish.1 = f32[256,128]{1,0:T(8,128)} custom-call(f32[256,128]{1,0:T(8,128)S(1)} %get-tuple-element.45.own, bf16[272,128]{1,0:T(8,128)(2,1)S(1)} %collective-permute-done.16.refs_0_, bf16[272,128]{1,0:T(8,128)(2,1)S(1)} %collective-permute-done.17.refs_1_, bf16[272,128]{1,0:T(8,128)(2,1)S(1)} %collective-permute-done.18.refs_2_), custom_call_target="tpu_custom_call" | custom-call | flops 1000 | bytes 1 | tf_op jit(solution)/shard_map/finish/pallas_call | solution.py:288
  (26 shorter events, 1.1 us)
Async XLA Ops:
  0.0 19.2 %copy-start.1 = (f32[128]{0:T(128)S(1)}, f32[128]{0:T(128)}, u32[]{:S(2)}) copy-start(f32[128]{0:T(128)} %param.6) | copy-start | bytes 1540
  0.0 19.2 %copy-start = (f32[4096]{0:T(1024)S(1)}, f32[4096]{0:T(1024)}, u32[]{:S(2)}) copy-start(f32[4096]{0:T(1024)} %param.7) | copy-start | bytes 49156
  0.0 10.8 %collective-permute-start = (bf16[3,256,128]{2,1,0:T(8,128)(2,1)}, bf16[3,256,128]{2,1,0:T(8,128)(2,1)S(1)}, u32[]{:S(2)}, u32[]{:S(2)}) collective-permute-start(bf16[3,256,128]{2,1,0:T(8,128)(2,1)} %shard.1), channel_id=1, source_target_pairs={{0,24},{8,16},{16,8},{24,0},{1,25},{9,17},{17,9},{25,1},{2,26},{10... | collective-permute-start | bytes 589832 | tf_op jit(solution)/shard_map/ppermute | solution.py:21
  6.1 13.0 %collective-permute-start.3 = (bf16[784,128]{1,0:T(8,128)(2,1)S(1)}, bf16[784,128]{1,0:T(8,128)(2,1)S(1)}, u32[]{:S(2)}, u32[]{:S(2)}) collective-permute-start(bf16[784,128]{1,0:T(8,128)(2,1)S(1)} %get-tuple-element.28), channel_id=1, source_target_pairs={{0,6},{1,7},{2,4},{3,5},{4,2},{5,3},{6,0},{7,1},{8,14},{9,15},{10,... | collective-permute-start | bytes 602120 | tf_op jit(solution)/shard_map/ppermute | solution.py:21
  8.6 10.0 %collective-permute-start.1 = (bf16[3,256,128]{2,1,0:T(8,128)(2,1)}, bf16[3,256,128]{2,1,0:T(8,128)(2,1)S(1)}, u32[]{:S(2)}, u32[]{:S(2)}) collective-permute-start(bf16[3,256,128]{2,1,0:T(8,128)(2,1)} %shard.1), channel_id=1, source_target_pairs={{0,8},{8,0},{16,24},{24,16},{1,9},{9,1},{17,25},{25,17},{2,10},{10... | collective-permute-start | bytes 589832 | tf_op jit(solution)/shard_map/ppermute | solution.py:21
  10.8 8.3 %collective-permute-start.2 = (bf16[3,256,128]{2,1,0:T(8,128)(2,1)S(1)}, bf16[3,256,128]{2,1,0:T(8,128)(2,1)S(1)}, u32[]{:S(2)}, u32[]{:S(2)}) collective-permute-start(bf16[3,256,128]{2,1,0:T(8,128)(2,1)S(1)} %collective-permute-done.refs_1_), channel_id=1, source_target_pairs={{0,8},{8,0},{16,24},{24,16},{1,9},{9,1},{17,25},{25,17},{2,10},{10... | collective-permute-start | bytes 589832 | tf_op jit(solution)/shard_map/ppermute | solution.py:21
  14.1 10.6 %collective-permute-start.4 = (bf16[3,256,128]{2,1,0:T(8,128)(2,1)S(1)}, bf16[3,256,128]{2,1,0:T(8,128)(2,1)S(1)}, u32[]{:S(2)}, u32[]{:S(2)}) collective-permute-start(bf16[3,256,128]{2,1,0:T(8,128)(2,1)S(1)} %collective-permute-done.refs_1_), channel_id=1, source_target_pairs={{0,6},{1,7},{2,4},{3,5},{4,2},{5,3},{6,0},{7,1},{8,14},{9,15},{10,... | collective-permute-start | bytes 589832 | tf_op jit(solution)/shard_map/ppermute | solution.py:21
  18.6 12.9 %collective-permute-start.9 = (bf16[3,256,128]{2,1,0:T(8,128)(2,1)S(1)}, bf16[3,256,128]{2,1,0:T(8,128)(2,1)S(1)}, u32[]{:S(2)}, u32[]{:S(2)}) collective-permute-start(bf16[3,256,128]{2,1,0:T(8,128)(2,1)S(1)} %collective-permute-done.1.refs_1_), channel_id=1, source_target_pairs={{0,6},{1,7},{2,4},{3,5},{4,2},{5,3},{6,0},{7,1},{8,14},{9,15},{10,... | collective-permute-start | bytes 589832 | tf_op jit(solution)/shard_map/ppermute | solution.py:21
  21.6 12.4 %collective-permute-start.8 = (bf16[128,2048]{1,0:T(8,128)(2,1)S(1)}, bf16[128,2048]{1,0:T(8,128)(2,1)S(1)}, u32[]{:S(2)}, u32[]{:S(2)}) collective-permute-start(bf16[128,2048]{1,0:T(8,128)(2,1)S(1)} %sensitivities.3.own_send), channel_id=1, source_target_pairs={{0,1},{1,0},{2,3},{3,2},{4,5},{5,4},{6,7},{7,6},{8,9},{9,8},{10,11... | collective-permute-start | bytes 1572872 | tf_op jit(solution)/shard_map/ppermute | solution.py:21
  21.6 14.5 %collective-permute-start.6 = (bf16[128,2048]{1,0:T(8,128)(2,1)S(1)}, bf16[128,2048]{1,0:T(8,128)(2,1)S(1)}, u32[]{:S(2)}, u32[]{:S(2)}) collective-permute-start(bf16[128,2048]{1,0:T(8,128)(2,1)S(1)} %sensitivities.3.own_send), channel_id=1, source_target_pairs={{0,2},{1,3},{2,0},{3,1},{4,6},{5,7},{6,4},{7,5},{8,10},{9,11},{10,... | collective-permute-start | bytes 1572872 | tf_op jit(solution)/shard_map/ppermute | solution.py:21
  23.2 14.0 %collective-permute-start.7 = (bf16[128,2048]{1,0:T(8,128)(2,1)S(1)}, bf16[128,2048]{1,0:T(8,128)(2,1)S(1)}, u32[]{:S(2)}, u32[]{:S(2)}) collective-permute-start(bf16[128,2048]{1,0:T(8,128)(2,1)S(1)} %sensitivities.3.own_send), channel_id=1, source_target_pairs={{0,4},{1,5},{2,6},{3,7},{4,0},{5,1},{6,2},{7,3},{8,12},{9,13},{10,... | collective-permute-start | bytes 1572872 | tf_op jit(solution)/shard_map/ppermute | solution.py:21
  24.7 6.8 %collective-permute-start.10 = (bf16[3,256,128]{2,1,0:T(8,128)(2,1)S(1)}, bf16[3,256,128]{2,1,0:T(8,128)(2,1)S(1)}, u32[]{:S(2)}, u32[]{:S(2)}) collective-permute-start(bf16[3,256,128]{2,1,0:T(8,128)(2,1)S(1)} %collective-permute-done.4.refs_1_), channel_id=1, source_target_pairs={{0,8},{8,0},{16,24},{24,16},{1,9},{9,1},{17,25},{25,17},{2,10},{10... | collective-permute-start | bytes 589832 | tf_op jit(solution)/shard_map/ppermute | solution.py:21
  31.5 2.5 %collective-permute-start.5 = (bf16[128,2048]{1,0:T(8,128)(2,1)S(1)}, bf16[128,2048]{1,0:T(8,128)(2,1)S(1)}, u32[]{:S(2)}, u32[]{:S(2)}) collective-permute-start(bf16[128,2048]{1,0:T(8,128)(2,1)S(1)} %sensitivities.4.own_keep), channel_id=1, source_target_pairs={{0,1},{1,0},{2,3},{3,2},{4,5},{5,4},{6,7},{7,6},{8,9},{9,8},{10,11... | collective-permute-start | bytes 1572872 | tf_op jit(solution)/shard_map/ppermute | solution.py:21
  34.6 6.6 %collective-permute-start.12 = (bf16[256,128]{1,0:T(8,128)(2,1)S(1)}, bf16[256,128]{1,0:T(8,128)(2,1)S(1)}, u32[]{:S(2)}, u32[]{:S(2)}) collective-permute-start(bf16[256,128]{1,0:T(8,128)(2,1)S(1)} %get-tuple-element.40), channel_id=1, source_target_pairs={{0,6},{1,7},{2,4},{3,5},{4,2},{5,3},{6,0},{7,1},{8,14},{9,15},{10,... | collective-permute-start | bytes 196616 | tf_op jit(solution)/shard_map/ppermute | solution.py:21
  37.7 3.4 %collective-permute-start.13 = (bf16[2,128,128]{2,1,0:T(8,128)(2,1)S(1)}, bf16[2,128,128]{2,1,0:T(8,128)(2,1)S(1)}, u32[]{:S(2)}, u32[]{:S(2)}) collective-permute-start(bf16[2,128,128]{2,1,0:T(8,128)(2,1)S(1)} %get-tuple-element.42), channel_id=1, source_target_pairs={{0,1},{1,0},{2,3},{3,2},{4,5},{5,4},{6,7},{7,6},{8,9},{9,8},{10,11... | collective-permute-start | bytes 196616 | tf_op jit(solution)/shard_map/ppermute | solution.py:21
  37.8 4.5 %collective-permute-start.14 = (bf16[256,128]{1,0:T(8,128)(2,1)S(1)}, bf16[256,128]{1,0:T(8,128)(2,1)S(1)}, u32[]{:S(2)}, u32[]{:S(2)}) collective-permute-start(bf16[256,128]{1,0:T(8,128)(2,1)S(1)} %get-tuple-element.43), channel_id=1, source_target_pairs={{0,2},{1,3},{2,0},{3,1},{4,6},{5,7},{6,4},{7,5},{8,10},{9,11},{10,... | collective-permute-start | bytes 196616 | tf_op jit(solution)/shard_map/ppermute | solution.py:21
  38.4 4.3 %collective-permute-start.15 = (bf16[256,128]{1,0:T(8,128)(2,1)S(1)}, bf16[256,128]{1,0:T(8,128)(2,1)S(1)}, u32[]{:S(2)}, u32[]{:S(2)}) collective-permute-start(bf16[256,128]{1,0:T(8,128)(2,1)S(1)} %get-tuple-element.44), channel_id=1, source_target_pairs={{0,4},{1,5},{2,6},{3,7},{4,0},{5,1},{6,2},{7,3},{8,12},{9,13},{10,... | collective-permute-start | bytes 196616 | tf_op jit(solution)/shard_map/ppermute | solution.py:21
  39.9 1.2 %collective-permute-start.11 = (bf16[1,128,128]{2,1,0:T(8,128)(2,1)S(1)}, bf16[1,128,128]{2,1,0:T(8,128)(2,1)S(1)}, u32[]{:S(2)}, u32[]{:S(2)}) collective-permute-start(bf16[1,128,128]{2,1,0:T(8,128)(2,1)S(1)} %get-tuple-element.39), channel_id=1, source_target_pairs={{0,1},{1,0},{2,3},{3,2},{4,5},{5,4},{6,7},{7,6},{8,9},{9,8},{10,11... | collective-permute-start | bytes 98312 | tf_op jit(solution)/shard_map/ppermute | solution.py:21
  42.8 7.5 %collective-permute-start.16 = (bf16[272,128]{1,0:T(8,128)(2,1)S(1)}, bf16[272,128]{1,0:T(8,128)(2,1)S(1)}, u32[]{:S(2)}, u32[]{:S(2)}) collective-permute-start(bf16[272,128]{1,0:T(8,128)(2,1)S(1)} %get-tuple-element.46), channel_id=1, source_target_pairs={{0,16},{8,24},{16,0},{24,8},{1,17},{9,25},{17,1},{25,9},{2,18},{10... | collective-permute-start | bytes 208904 | tf_op jit(solution)/shard_map/ppermute | solution.py:21
  44.6 6.5 %collective-permute-start.17 = (bf16[272,128]{1,0:T(8,128)(2,1)S(1)}, bf16[272,128]{1,0:T(8,128)(2,1)S(1)}, u32[]{:S(2)}, u32[]{:S(2)}) collective-permute-start(bf16[272,128]{1,0:T(8,128)(2,1)S(1)} %get-tuple-element.47), channel_id=1, source_target_pairs={{0,24},{8,16},{16,8},{24,0},{1,25},{9,17},{17,9},{25,1},{2,26},{10... | collective-permute-start | bytes 208904 | tf_op jit(solution)/shard_map/ppermute | solution.py:21
  46.4 5.1 %collective-permute-start.18 = (bf16[272,128]{1,0:T(8,128)(2,1)S(1)}, bf16[272,128]{1,0:T(8,128)(2,1)S(1)}, u32[]{:S(2)}, u32[]{:S(2)}) collective-permute-start(bf16[272,128]{1,0:T(8,128)(2,1)S(1)} %get-tuple-element.48), channel_id=1, source_target_pairs={{0,8},{8,0},{16,24},{24,16},{1,9},{9,1},{17,25},{25,17},{2,10},{10... | collective-permute-start | bytes 208904 | tf_op jit(solution)/shard_map/ppermute | solution.py:21

commit v10 on v9

--- a/solution.py
+++ b/solution.py
@@ -382,7 +382,7 @@
         [pltpu.VMEM((chips, *whole), F32)],
         own_block, *exchange(evens, *early), *exchange(odds, *late),
     )
-    arrived = [hop(parts[k], "elec", groups, k) for k in sorted(range(1, groups), key=lambda k: (k < half, k))]
+    arrived = [hop(parts[k], "elec", groups, k) for k in sorted(range(1, groups), key=lambda k: (k < half, -k))]
     return whole_call(
         functools.partial(final_kernel, float(measured * groups)),
         "finish",

time: 52.4 us -> 53 us (1.011)
  transfers between devices with their start and end apart: 19 -> 19, of which waited for: 9 -> 8; matrix products, arithmetic and copies ran while one was open for 0% -> 0% of each run, Pallas kernels for 29% -> 29%
where the time goes in v10:
time: 53 us; the launch traced here: 52.8 us
  starting transfers between devices  25.4 us (48%)
  Pallas kernels  16.1 us (30%)
  waiting for transfers between devices  11.1 us (21%)
    ppermute x19, starting transfers between devices, hop(): return lax.ppermute(x, axis, [(i, i ^ mask) for i in range(size)])  25.4 us
    pallas_call x10, Pallas kernels, whole_call(): pl.pallas_call(kernel, in_specs=[vmem] * len(arrays), out_specs=[vmem] *...  14.8 us
    ppermute x19, waiting for transfers between devices, hop(): return lax.ppermute(x, axis, [(i, i ^ mask) for i in range(size)])  11.1 us
  transfers between devices with their start and end apart: 19, of which 8 were waited for; matrix products, arithmetic and copies ran while one was open for 0% of the time, Pallas kernels for 29%

profile of v10, /device:TPU:0, one launch (start us, length us, event | category | flops | bytes accessed | tf_op | source)
XLA Modules:
  0.0 52.8 jit_solution(5106852899195714869)
XLA Ops:
  0.0 5.0 %collective-permute-start = (bf16[3,256,128]{2,1,0:T(8,128)(2,1)}, bf16[3,256,128]{2,1,0:T(8,128)(2,1)S(1)}, u32[]{:S(2)}, u32[]{:S(2)}) collective-permute-start(bf16[3,256,128]{2,1,0:T(8,128)(2,1)} %shard.1), channel_id=1, source_target_pairs={{0,24},{8,16},{16,8},{24,0},{1,25},{9,17},{17,9},{25,1},{2,26},{10... | collective-permute-start | bytes 589832 | tf_op jit(solution)/shard_map/ppermute | solution.py:21
  5.1 1.0 %pack.1 = (bf16[784,128]{1,0:T(8,128)(2,1)S(1)}, s32[4,4096]{1,0:T(4,128)S(1)}) custom-call(bf16[3,256,128]{2,1,0:T(8,128)(2,1)} %shard.1, f32[1,128]{1,0:T(1,128)} %bitcast.10, s32[4,4096]{1,0:T(4,128)} %bitcast.13), custom_call_target="tpu_custom_call" | custom-call | flops 1000 | bytes 1000 | tf_op jit(solution)/shard_map/pack/pallas_call | solution.py:102
  6.1 2.5 %collective-permute-start.3 = (bf16[784,128]{1,0:T(8,128)(2,1)S(1)}, bf16[784,128]{1,0:T(8,128)(2,1)S(1)}, u32[]{:S(2)}, u32[]{:S(2)}) collective-permute-start(bf16[784,128]{1,0:T(8,128)(2,1)S(1)} %get-tuple-element.28), channel_id=1, source_target_pairs={{0,6},{1,7},{2,4},{3,5},{4,2},{5,3},{6,0},{7,1},{8,14},{9,15},{10,... | collective-permute-start | bytes 602120 | tf_op jit(solution)/shard_map/ppermute | solution.py:21
  8.6 2.3 %collective-permute-done.refs_1_ = bf16[3,256,128]{2,1,0:T(8,128)(2,1)S(1)} collective-permute-done((bf16[3,256,128]{2,1,0:T(8,128)(2,1)}, bf16[3,256,128]{2,1,0:T(8,128)(2,1)S(1)}, u32[]{:S(2)}, u32[]{:S(2)}) %collective-permute-start) | collective-permute-done | bytes 196640 | tf_op jit(solution)/shard_map/ppermute | solution.py:21
  10.8 3.3 %collective-permute-start.2 = (bf16[3,256,128]{2,1,0:T(8,128)(2,1)S(1)}, bf16[3,256,128]{2,1,0:T(8,128)(2,1)S(1)}, u32[]{:S(2)}, u32[]{:S(2)}) collective-permute-start(bf16[3,256,128]{2,1,0:T(8,128)(2,1)S(1)} %collective-permute-done.refs_1_), channel_id=1, source_target_pairs={{0,8},{8,0},{16,24},{24,16},{1,9},{9,1},{17,25},{25,17},{2,10},{10... | collective-permute-start | bytes 589832 | tf_op jit(solution)/shard_map/ppermute | solution.py:21
  14.1 2.4 %collective-permute-start.4 = (bf16[3,256,128]{2,1,0:T(8,128)(2,1)S(1)}, bf16[3,256,128]{2,1,0:T(8,128)(2,1)S(1)}, u32[]{:S(2)}, u32[]{:S(2)}) collective-permute-start(bf16[3,256,128]{2,1,0:T(8,128)(2,1)S(1)} %collective-permute-done.refs_1_), channel_id=1, source_target_pairs={{0,6},{1,7},{2,4},{3,5},{4,2},{5,3},{6,0},{7,1},{8,14},{9,15},{10,... | collective-permute-start | bytes 589832 | tf_op jit(solution)/shard_map/ppermute | solution.py:21
  16.6 0.2 turn_shards.2.turned.refs_0_
  16.7 1.8 %partial_products.2.refs_0_ = f32[2,384,2048]{2,1,0:T(8,128)S(1)} custom-call(s32[4,4096]{1,0:T(4,128)S(1)} %get-tuple-element.30.quads, bf16[384,512]{1,0:T(8,128)(2,1)S(1)} %turn_shards.2.turned.refs_0_), custom_call_target="tpu_custom_call" | custom-call | flops 1000 | bytes 1 | tf_op jit(solution)/shard_map/partial_products/pallas_call | solution.py:288
  18.6 0.5 %collective-permute-start.9 = (bf16[3,256,128]{2,1,0:T(8,128)(2,1)S(1)}, bf16[3,256,128]{2,1,0:T(8,128)(2,1)S(1)}, u32[]{:S(2)}, u32[]{:S(2)}) collective-permute-start(bf16[3,256,128]{2,1,0:T(8,128)(2,1)S(1)} %collective-permute-done.1.refs_1_), channel_id=1, source_target_pairs={{0,6},{1,7},{2,4},{3,5},{4,2},{5,3},{6,0},{7,1},{8,14},{9,15},{10,... | collective-permute-start | bytes 589832 | tf_op jit(solution)/shard_map/ppermute | solution.py:21
  19.2 2.4 %sensitivities.3.own_send = bf16[128,2048]{1,0:T(8,128)(2,1)S(1)} custom-call(s32[4,4096]{1,0:T(4,128)S(1)} %get-tuple-element.30.quads, f32[1,4096]{1,0:T(1,128)S(1)} %bitcast.7, f32[1,128]{1,0:T(1,128)S(1)} %bitcast.11, f32[2,384,2048]{2,1,0:T(8,128)S(1)} %partial_products.2.refs_0_, bf16[3,256,128]{2,1,0:T(8,128)(2,1)S(1)} %collective-permute-done.1.refs_1_, ...), custom_call_target="tpu_custom_call" | custom-call | flops 1610612736 | bytes 1 | tf_op jit(solution)/shard_map/sensitivities/pallas_call | solution.py:288
  21.6 1.5 %collective-permute-start.6 = (bf16[128,2048]{1,0:T(8,128)(2,1)S(1)}, bf16[128,2048]{1,0:T(8,128)(2,1)S(1)}, u32[]{:S(2)}, u32[]{:S(2)}) collective-permute-start(bf16[128,2048]{1,0:T(8,128)(2,1)S(1)} %sensitivities.3.own_send), channel_id=1, source_target_pairs={{0,2},{1,3},{2,0},{3,1},{4,6},{5,7},{6,4},{7,5},{8,10},{9,11},{10,... | collective-permute-start | bytes 1572872 | tf_op jit(solution)/shard_map/ppermute | solution.py:21
  23.2 1.5 %collective-permute-start.7 = (bf16[128,2048]{1,0:T(8,128)(2,1)S(1)}, bf16[128,2048]{1,0:T(8,128)(2,1)S(1)}, u32[]{:S(2)}, u32[]{:S(2)}) collective-permute-start(bf16[128,2048]{1,0:T(8,128)(2,1)S(1)} %sensitivities.3.own_send), channel_id=1, source_target_pairs={{0,4},{1,5},{2,6},{3,7},{4,0},{5,1},{6,2},{7,3},{8,12},{9,13},{10,... | collective-permute-start | bytes 1572872 | tf_op jit(solution)/shard_map/ppermute | solution.py:21
  24.7 1.2 %collective-permute-start.10 = (bf16[3,256,128]{2,1,0:T(8,128)(2,1)S(1)}, bf16[3,256,128]{2,1,0:T(8,128)(2,1)S(1)}, u32[]{:S(2)}, u32[]{:S(2)}) collective-permute-start(bf16[3,256,128]{2,1,0:T(8,128)(2,1)S(1)} %collective-permute-done.4.refs_1_), channel_id=1, source_target_pairs={{0,8},{8,0},{16,24},{24,16},{1,9},{9,1},{17,25},{25,17},{2,10},{10... | collective-permute-start | bytes 589832 | tf_op jit(solution)/shard_map/ppermute | solution.py:21
  26.1 1.8 %partial_products.3.refs_0_ = f32[2,384,2048]{2,1,0:T(8,128)S(1)} custom-call(s32[4,4096]{1,0:T(4,128)S(1)} %get-tuple-element.30.quads, bf16[384,512]{1,0:T(8,128)(2,1)S(1)} %turn_shards.3.turned), custom_call_target="tpu_custom_call" | custom-call | flops 1000 | bytes 1 | tf_op jit(solution)/shard_map/partial_products/pallas_call | solution.py:288
  27.9 3.5 %sensitivities.4.own_keep = bf16[128,2048]{1,0:T(8,128)(2,1)S(1)} custom-call(s32[4,4096]{1,0:T(4,128)S(1)} %get-tuple-element.30.quads, f32[1,4096]{1,0:T(1,128)S(1)} %bitcast.8, f32[1,128]{1,0:T(1,128)S(1)} %bitcast.12, bf16[384,512]{1,0:T(8,128)(2,1)S(1)} %turn_shards.2.turned.refs_0_, bf16[3,256,128]{2,1,0:T(8,128)(2,1)S(1)} %collective-permute-done.1.refs_1_, ...), custom_call_target="tpu_custom_call" | custom-call | flops 3221225472 | bytes 1 | tf_op jit(solution)/shard_map/sensitivities/pallas_call | solution.py:288
  31.6 2.4 %sensitivities.5.refs_0_ = bf16[128,2048]{1,0:T(8,128)(2,1)S(1)} custom-call(s32[4,4096]{1,0:T(4,128)S(1)} %get-tuple-element.30.quads, f32[1,4096]{1,0:T(1,128)S(1)} %bitcast.9, bf16[16,128]{1,0:T(8,128)(2,1)S(1)} %slice.13.volume, f32[2,384,2048]{2,1,0:T(8,128)S(1)} %partial_products.3.refs_0_, bf16[3,256,128]{2,1,0:T(8,128)(2,1)S(1)} %collective-permute-done.9.refs_1_, ...), custom_call_target="tpu_custom_call" | custom-call | flops 25769803776 | bytes 1 | tf_op jit(solution)/shard_map/sensitivities/pallas_call | solution.py:288
  34.0 0.6 %early_blocks.1 = (f32[1,128,128]{2,1,0:T(8,128)S(1)}, bf16[1,128,128]{2,1,0:T(8,128)(2,1)S(1)}, bf16[256,128]{1,0:T(8,128)(2,1)S(1)}) custom-call(bf16[128,2048]{1,0:T(8,128)(2,1)S(1)} %sensitivities.3.own_send, bf16[128,2048]{1,0:T(8,128)(2,1)S(1)} %sensitivities.4.own_keep, bf16[128,2048]{1,0:T(8,128)(2,1)S(1)} %collective-permute-done.8.other_send, ...), custom_call_target="tpu_custom_call" | custom-call | flops 1000 | bytes 1 | tf_op jit(solution)/shard_map/early_blocks/pallas_call | solution.py:288
  34.6 0.5 collective-permute-start.12
  35.1 1.1 %collective-permute-done.6.refs_0_ = bf16[128,2048]{1,0:T(8,128)(2,1)S(1)} collective-permute-done((bf16[128,2048]{1,0:T(8,128)(2,1)S(1)}, bf16[128,2048]{1,0:T(8,128)(2,1)S(1)}, u32[]{:S(2)}, u32[]{:S(2)}) %collective-permute-start.6) | collective-permute-done | bytes 524320 | tf_op jit(solution)/shard_map/ppermute | solution.py:21
  36.2 1.0 %collective-permute-done.7.refs_1_ = bf16[128,2048]{1,0:T(8,128)(2,1)S(1)} collective-permute-done((bf16[128,2048]{1,0:T(8,128)(2,1)S(1)}, bf16[128,2048]{1,0:T(8,128)(2,1)S(1)}, u32[]{:S(2)}, u32[]{:S(2)}) %collective-permute-start.7) | collective-permute-done | bytes 524320 | tf_op jit(solution)/shard_map/ppermute | solution.py:21
  37.2 0.5 %late_blocks.1 = (f32[2,128,128]{2,1,0:T(8,128)S(1)}, bf16[2,128,128]{2,1,0:T(8,128)(2,1)S(1)}, bf16[256,128]{1,0:T(8,128)(2,1)S(1)}, bf16[256,128]{1,0:T(8,128)(2,1)S(1)}) custom-call(bf16[128,2048]{1,0:T(8,128)(2,1)S(1)} %sensitivities.4.own_keep, bf16[128,2048]{1,0:T(8,128)(2,1)S(1)} %collective-permute-done.5.other_keep, ...), custom_call_target="tpu_custom_call" | custom-call | flops 1000 | bytes 1 | tf_op jit(solution)/shard_map/late_blocks/pallas_call | solution.py:288
  37.8 0.6 %collective-permute-start.14 = (bf16[256,128]{1,0:T(8,128)(2,1)S(1)}, bf16[256,128]{1,0:T(8,128)(2,1)S(1)}, u32[]{:S(2)}, u32[]{:S(2)}) collective-permute-start(bf16[256,128]{1,0:T(8,128)(2,1)S(1)} %get-tuple-element.43), channel_id=1, source_target_pairs={{0,2},{1,3},{2,0},{3,1},{4,6},{5,7},{6,4},{7,5},{8,10},{9,11},{10,... | collective-permute-start | bytes 196616 | tf_op jit(solution)/shard_map/ppermute | solution.py:21
  38.4 1.5 %collective-permute-start.15 = (bf16[256,128]{1,0:T(8,128)(2,1)S(1)}, bf16[256,128]{1,0:T(8,128)(2,1)S(1)}, u32[]{:S(2)}, u32[]{:S(2)}) collective-permute-start(bf16[256,128]{1,0:T(8,128)(2,1)S(1)} %get-tuple-element.44), channel_id=1, source_target_pairs={{0,4},{1,5},{2,6},{3,7},{4,0},{5,1},{6,2},{7,3},{8,12},{9,13},{10,... | collective-permute-start | bytes 196616 | tf_op jit(solution)/shard_map/ppermute | solution.py:21
  39.9 0.9 %own_block.1 = f32[256,128]{1,0:T(8,128)S(1)} custom-call(bf16[128,2048]{1,0:T(8,128)(2,1)S(1)} %sensitivities.3.own_send, bf16[128,2048]{1,0:T(8,128)(2,1)S(1)} %sensitivities.4.own_keep, bf16[128,2048]{1,0:T(8,128)(2,1)S(1)} %collective-permute-done.8.other_send, bf16[128,2048]{1,0:T(8,128)(2,1)S(1)} %collective-permute-done.5.other_keep), custom_call_target="tpu_custom_call" | custom-call | flops 1000 | bytes 1 | tf_op jit(solution)/shard_map/own_block/pallas_call | solution.py:288
  40.8 0.3 collective-permute-done.11.refs_1_
  41.2 1.2 %collective-permute-done.14.refs_5_ = bf16[256,128]{1,0:T(8,128)(2,1)S(1)} collective-permute-done((bf16[256,128]{1,0:T(8,128)(2,1)S(1)}, bf16[256,128]{1,0:T(8,128)(2,1)S(1)}, u32[]{:S(2)}, u32[]{:S(2)}) %collective-permute-start.14) | collective-permute-done | bytes 65568 | tf_op jit(solution)/shard_map/ppermute | solution.py:21
  42.3 0.4 collective-permute-done.15.refs_6_
  42.8 3.5 %collective-permute-start.16 = (bf16[272,128]{1,0:T(8,128)(2,1)S(1)}, bf16[272,128]{1,0:T(8,128)(2,1)S(1)}, u32[]{:S(2)}, u32[]{:S(2)}) collective-permute-start(bf16[272,128]{1,0:T(8,128)(2,1)S(1)} %get-tuple-element.46), channel_id=1, source_target_pairs={{0,24},{8,16},{16,8},{24,0},{1,25},{9,17},{17,9},{25,1},{2,26},{10... | collective-permute-start | bytes 208904 | tf_op jit(solution)/shard_map/ppermute | solution.py:21
  46.3 1.0 %collective-permute-start.18 = (bf16[272,128]{1,0:T(8,128)(2,1)S(1)}, bf16[272,128]{1,0:T(8,128)(2,1)S(1)}, u32[]{:S(2)}, u32[]{:S(2)}) collective-permute-start(bf16[272,128]{1,0:T(8,128)(2,1)S(1)} %get-tuple-element.48), channel_id=1, source_target_pairs={{0,8},{8,0},{16,24},{24,16},{1,9},{9,1},{17,25},{25,17},{2,10},{10... | collective-permute-start | bytes 208904 | tf_op jit(solution)/shard_map/ppermute | solution.py:21
  47.2 2.0 %collective-permute-done.16.refs_0_ = bf16[272,128]{1,0:T(8,128)(2,1)S(1)} collective-permute-done((bf16[272,128]{1,0:T(8,128)(2,1)S(1)}, bf16[272,128]{1,0:T(8,128)(2,1)S(1)}, u32[]{:S(2)}, u32[]{:S(2)}) %collective-permute-start.16) | collective-permute-done | bytes 69664 | tf_op jit(solution)/shard_map/ppermute | solution.py:21
  49.2 2.8 %collective-permute-done.17.refs_1_ = bf16[272,128]{1,0:T(8,128)(2,1)S(1)} collective-permute-done((bf16[272,128]{1,0:T(8,128)(2,1)S(1)}, bf16[272,128]{1,0:T(8,128)(2,1)S(1)}, u32[]{:S(2)}, u32[]{:S(2)}) %collective-permute-start.17) | collective-permute-done | bytes 69664 | tf_op jit(solution)/shard_map/ppermute | solution.py:21
  52.1 0.7 %finish.1 = f32[256,128]{1,0:T(8,128)} custom-call(f32[256,128]{1,0:T(8,128)S(1)} %get-tuple-element.45.own, bf16[272,128]{1,0:T(8,128)(2,1)S(1)} %collective-permute-done.16.refs_0_, bf16[272,128]{1,0:T(8,128)(2,1)S(1)} %collective-permute-done.17.refs_1_, bf16[272,128]{1,0:T(8,128)(2,1)S(1)} %collective-permute-done.18.refs_2_), custom_call_target="tpu_custom_call" | custom-call | flops 1000 | bytes 1 | tf_op jit(solution)/shard_map/finish/pallas_call | solution.py:288
  (26 shorter events, 0.6 us)
Async XLA Ops:
  0.0 19.2 %copy-start.1 = (f32[128]{0:T(128)S(1)}, f32[128]{0:T(128)}, u32[]{:S(2)}) copy-start(f32[128]{0:T(128)} %param.6) | copy-start | bytes 1540
  0.0 19.2 %copy-start = (f32[4096]{0:T(1024)S(1)}, f32[4096]{0:T(1024)}, u32[]{:S(2)}) copy-start(f32[4096]{0:T(1024)} %param.7) | copy-start | bytes 49156
  0.0 10.8 %collective-permute-start = (bf16[3,256,128]{2,1,0:T(8,128)(2,1)}, bf16[3,256,128]{2,1,0:T(8,128)(2,1)S(1)}, u32[]{:S(2)}, u32[]{:S(2)}) collective-permute-start(bf16[3,256,128]{2,1,0:T(8,128)(2,1)} %shard.1), channel_id=1, source_target_pairs={{0,24},{8,16},{16,8},{24,0},{1,25},{9,17},{17,9},{25,1},{2,26},{10... | collective-permute-start | bytes 589832 | tf_op jit(solution)/shard_map/ppermute | solution.py:21
  6.1 13.0 %collective-permute-start.3 = (bf16[784,128]{1,0:T(8,128)(2,1)S(1)}, bf16[784,128]{1,0:T(8,128)(2,1)S(1)}, u32[]{:S(2)}, u32[]{:S(2)}) collective-permute-start(bf16[784,128]{1,0:T(8,128)(2,1)S(1)} %get-tuple-element.28), channel_id=1, source_target_pairs={{0,6},{1,7},{2,4},{3,5},{4,2},{5,3},{6,0},{7,1},{8,14},{9,15},{10,... | collective-permute-start | bytes 602120 | tf_op jit(solution)/shard_map/ppermute | solution.py:21
  8.6 10.0 %collective-permute-start.1 = (bf16[3,256,128]{2,1,0:T(8,128)(2,1)}, bf16[3,256,128]{2,1,0:T(8,128)(2,1)S(1)}, u32[]{:S(2)}, u32[]{:S(2)}) collective-permute-start(bf16[3,256,128]{2,1,0:T(8,128)(2,1)} %shard.1), channel_id=1, source_target_pairs={{0,8},{8,0},{16,24},{24,16},{1,9},{9,1},{17,25},{25,17},{2,10},{10... | collective-permute-start | bytes 589832 | tf_op jit(solution)/shard_map/ppermute | solution.py:21
  10.8 8.3 %collective-permute-start.2 = (bf16[3,256,128]{2,1,0:T(8,128)(2,1)S(1)}, bf16[3,256,128]{2,1,0:T(8,128)(2,1)S(1)}, u32[]{:S(2)}, u32[]{:S(2)}) collective-permute-start(bf16[3,256,128]{2,1,0:T(8,128)(2,1)S(1)} %collective-permute-done.refs_1_), channel_id=1, source_target_pairs={{0,8},{8,0},{16,24},{24,16},{1,9},{9,1},{17,25},{25,17},{2,10},{10... | collective-permute-start | bytes 589832 | tf_op jit(solution)/shard_map/ppermute | solution.py:21
  14.1 10.6 %collective-permute-start.4 = (bf16[3,256,128]{2,1,0:T(8,128)(2,1)S(1)}, bf16[3,256,128]{2,1,0:T(8,128)(2,1)S(1)}, u32[]{:S(2)}, u32[]{:S(2)}) collective-permute-start(bf16[3,256,128]{2,1,0:T(8,128)(2,1)S(1)} %collective-permute-done.refs_1_), channel_id=1, source_target_pairs={{0,6},{1,7},{2,4},{3,5},{4,2},{5,3},{6,0},{7,1},{8,14},{9,15},{10,... | collective-permute-start | bytes 589832 | tf_op jit(solution)/shard_map/ppermute | solution.py:21
  18.6 12.9 %collective-permute-start.9 = (bf16[3,256,128]{2,1,0:T(8,128)(2,1)S(1)}, bf16[3,256,128]{2,1,0:T(8,128)(2,1)S(1)}, u32[]{:S(2)}, u32[]{:S(2)}) collective-permute-start(bf16[3,256,128]{2,1,0:T(8,128)(2,1)S(1)} %collective-permute-done.1.refs_1_), channel_id=1, source_target_pairs={{0,6},{1,7},{2,4},{3,5},{4,2},{5,3},{6,0},{7,1},{8,14},{9,15},{10,... | collective-permute-start | bytes 589832 | tf_op jit(solution)/shard_map/ppermute | solution.py:21
  21.6 12.4 %collective-permute-start.8 = (bf16[128,2048]{1,0:T(8,128)(2,1)S(1)}, bf16[128,2048]{1,0:T(8,128)(2,1)S(1)}, u32[]{:S(2)}, u32[]{:S(2)}) collective-permute-start(bf16[128,2048]{1,0:T(8,128)(2,1)S(1)} %sensitivities.3.own_send), channel_id=1, source_target_pairs={{0,1},{1,0},{2,3},{3,2},{4,5},{5,4},{6,7},{7,6},{8,9},{9,8},{10,11... | collective-permute-start | bytes 1572872 | tf_op jit(solution)/shard_map/ppermute | solution.py:21
  21.6 14.5 %collective-permute-start.6 = (bf16[128,2048]{1,0:T(8,128)(2,1)S(1)}, bf16[128,2048]{1,0:T(8,128)(2,1)S(1)}, u32[]{:S(2)}, u32[]{:S(2)}) collective-permute-start(bf16[128,2048]{1,0:T(8,128)(2,1)S(1)} %sensitivities.3.own_send), channel_id=1, source_target_pairs={{0,2},{1,3},{2,0},{3,1},{4,6},{5,7},{6,4},{7,5},{8,10},{9,11},{10,... | collective-permute-start | bytes 1572872 | tf_op jit(solution)/shard_map/ppermute | solution.py:21
  23.2 14.0 %collective-permute-start.7 = (bf16[128,2048]{1,0:T(8,128)(2,1)S(1)}, bf16[128,2048]{1,0:T(8,128)(2,1)S(1)}, u32[]{:S(2)}, u32[]{:S(2)}) collective-permute-start(bf16[128,2048]{1,0:T(8,128)(2,1)S(1)} %sensitivities.3.own_send), channel_id=1, source_target_pairs={{0,4},{1,5},{2,6},{3,7},{4,0},{5,1},{6,2},{7,3},{8,12},{9,13},{10,... | collective-permute-start | bytes 1572872 | tf_op jit(solution)/shard_map/ppermute | solution.py:21
  24.7 6.8 %collective-permute-start.10 = (bf16[3,256,128]{2,1,0:T(8,128)(2,1)S(1)}, bf16[3,256,128]{2,1,0:T(8,128)(2,1)S(1)}, u32[]{:S(2)}, u32[]{:S(2)}) collective-permute-start(bf16[3,256,128]{2,1,0:T(8,128)(2,1)S(1)} %collective-permute-done.4.refs_1_), channel_id=1, source_target_pairs={{0,8},{8,0},{16,24},{24,16},{1,9},{9,1},{17,25},{25,17},{2,10},{10... | collective-permute-start | bytes 589832 | tf_op jit(solution)/shard_map/ppermute | solution.py:21
  31.5 2.5 %collective-permute-start.5 = (bf16[128,2048]{1,0:T(8,128)(2,1)S(1)}, bf16[128,2048]{1,0:T(8,128)(2,1)S(1)}, u32[]{:S(2)}, u32[]{:S(2)}) collective-permute-start(bf16[128,2048]{1,0:T(8,128)(2,1)S(1)} %sensitivities.4.own_keep), channel_id=1, source_target_pairs={{0,1},{1,0},{2,3},{3,2},{4,5},{5,4},{6,7},{7,6},{8,9},{9,8},{10,11... | collective-permute-start | bytes 1572872 | tf_op jit(solution)/shard_map/ppermute | solution.py:21
  34.6 6.6 %collective-permute-start.12 = (bf16[256,128]{1,0:T(8,128)(2,1)S(1)}, bf16[256,128]{1,0:T(8,128)(2,1)S(1)}, u32[]{:S(2)}, u32[]{:S(2)}) collective-permute-start(bf16[256,128]{1,0:T(8,128)(2,1)S(1)} %get-tuple-element.40), channel_id=1, source_target_pairs={{0,6},{1,7},{2,4},{3,5},{4,2},{5,3},{6,0},{7,1},{8,14},{9,15},{10,... | collective-permute-start | bytes 196616 | tf_op jit(solution)/shard_map/ppermute | solution.py:21
  37.7 3.4 %collective-permute-start.13 = (bf16[2,128,128]{2,1,0:T(8,128)(2,1)S(1)}, bf16[2,128,128]{2,1,0:T(8,128)(2,1)S(1)}, u32[]{:S(2)}, u32[]{:S(2)}) collective-permute-start(bf16[2,128,128]{2,1,0:T(8,128)(2,1)S(1)} %get-tuple-element.42), channel_id=1, source_target_pairs={{0,1},{1,0},{2,3},{3,2},{4,5},{5,4},{6,7},{7,6},{8,9},{9,8},{10,11... | collective-permute-start | bytes 196616 | tf_op jit(solution)/shard_map/ppermute | solution.py:21
  37.8 4.5 %collective-permute-start.14 = (bf16[256,128]{1,0:T(8,128)(2,1)S(1)}, bf16[256,128]{1,0:T(8,128)(2,1)S(1)}, u32[]{:S(2)}, u32[]{:S(2)}) collective-permute-start(bf16[256,128]{1,0:T(8,128)(2,1)S(1)} %get-tuple-element.43), channel_id=1, source_target_pairs={{0,2},{1,3},{2,0},{3,1},{4,6},{5,7},{6,4},{7,5},{8,10},{9,11},{10,... | collective-permute-start | bytes 196616 | tf_op jit(solution)/shard_map/ppermute | solution.py:21
  38.4 4.3 %collective-permute-start.15 = (bf16[256,128]{1,0:T(8,128)(2,1)S(1)}, bf16[256,128]{1,0:T(8,128)(2,1)S(1)}, u32[]{:S(2)}, u32[]{:S(2)}) collective-permute-start(bf16[256,128]{1,0:T(8,128)(2,1)S(1)} %get-tuple-element.44), channel_id=1, source_target_pairs={{0,4},{1,5},{2,6},{3,7},{4,0},{5,1},{6,2},{7,3},{8,12},{9,13},{10,... | collective-permute-start | bytes 196616 | tf_op jit(solution)/shard_map/ppermute | solution.py:21
  39.9 1.2 %collective-permute-start.11 = (bf16[1,128,128]{2,1,0:T(8,128)(2,1)S(1)}, bf16[1,128,128]{2,1,0:T(8,128)(2,1)S(1)}, u32[]{:S(2)}, u32[]{:S(2)}) collective-permute-start(bf16[1,128,128]{2,1,0:T(8,128)(2,1)S(1)} %get-tuple-element.39), channel_id=1, source_target_pairs={{0,1},{1,0},{2,3},{3,2},{4,5},{5,4},{6,7},{7,6},{8,9},{9,8},{10,11... | collective-permute-start | bytes 98312 | tf_op jit(solution)/shard_map/ppermute | solution.py:21
  42.8 6.5 %collective-permute-start.16 = (bf16[272,128]{1,0:T(8,128)(2,1)S(1)}, bf16[272,128]{1,0:T(8,128)(2,1)S(1)}, u32[]{:S(2)}, u32[]{:S(2)}) collective-permute-start(bf16[272,128]{1,0:T(8,128)(2,1)S(1)} %get-tuple-element.46), channel_id=1, source_target_pairs={{0,24},{8,16},{16,8},{24,0},{1,25},{9,17},{17,9},{25,1},{2,26},{10... | collective-permute-start | bytes 208904 | tf_op jit(solution)/shard_map/ppermute | solution.py:21
  46.3 5.8 %collective-permute-start.17 = (bf16[272,128]{1,0:T(8,128)(2,1)S(1)}, bf16[272,128]{1,0:T(8,128)(2,1)S(1)}, u32[]{:S(2)}, u32[]{:S(2)}) collective-permute-start(bf16[272,128]{1,0:T(8,128)(2,1)S(1)} %get-tuple-element.47), channel_id=1, source_target_pairs={{0,16},{8,24},{16,0},{24,8},{1,17},{9,25},{17,1},{25,9},{2,18},{10... | collective-permute-start | bytes 208904 | tf_op jit(solution)/shard_map/ppermute | solution.py:21
  46.3 5.8 %collective-permute-start.18 = (bf16[272,128]{1,0:T(8,128)(2,1)S(1)}, bf16[272,128]{1,0:T(8,128)(2,1)S(1)}, u32[]{:S(2)}, u32[]{:S(2)}) collective-permute-start(bf16[272,128]{1,0:T(8,128)(2,1)S(1)} %get-tuple-element.48), channel_id=1, source_target_pairs={{0,8},{8,0},{16,24},{24,16},{1,9},{9,1},{17,25},{25,17},{2,10},{10... | collective-permute-start | bytes 208904 | tf_op jit(solution)/shard_map/ppermute | solution.py:21
